TPU v7x, 32 devices: a whole 2x2x4 slice. The times are simulated.
32 devices in a mesh: expert: 16 (over z, y, x), fsdp: 2 (over core).
Axes of the slice: x: 2, y: 2, z: 4, core: 2. Of those that a mesh axis runs over, the one named last changes fastest.
Arguments:
- hidden_in: bfloat16 [8192, 2048], P(('expert', 'fsdp')), may hold values from -6 to 6
- prenorm_gain: bfloat16 [2048], P(('expert', 'fsdp')), may hold values from 0.099609375 to 1.8984375
- query_weight: bfloat16 [2048, 2048], P(('expert', 'fsdp')), may hold values from -0.125 to 0.125
- key_weight: bfloat16 [2048, 2048], P(('expert', 'fsdp')), may hold values from -0.125 to 0.125
- value_weight: bfloat16 [2048, 2048], P(('expert', 'fsdp')), may hold values from -0.125 to 0.125
- querynorm_gain: bfloat16 [128], P(('expert', 'fsdp')), may hold values from 0.099609375 to 1.8984375
- keynorm_gain: bfloat16 [128], P(('expert', 'fsdp')), may hold values from 0.099609375 to 1.8984375
- output_weight: bfloat16 [2048, 2048], P(('expert', 'fsdp')), may hold values from -2 to 2
- postnorm_gain: bfloat16 [2048], P(('expert', 'fsdp')), may hold values from 0.099609375 to 1.8984375
- router_weight: bfloat16 [2048, 16], P(('expert', 'fsdp')), may hold values from -0.0625 to 0.0625
- expert_inner: bfloat16 [16, 2048, 2048], P('expert', 'fsdp'), may hold values from -0.125 to 0.125
- expert_outer: bfloat16 [16, 1024, 2048], P('expert', 'fsdp'), may hold values from -0.75 to 0.75
- expert_ids: int32 [8192, 8], P(('expert', 'fsdp')), may hold values from 0 to 15, all different within a row
- pair_order: int32 [32, 2048], P(('expert', 'fsdp')), may hold values from 0 to 2047, each once within a row
- sequence_lengths: int32 [8], replicated, may hold values from 256 to 1024, as said below
- cotangent: bfloat16 [8192, 2048], P(('expert', 'fsdp')), may hold values from -6 to 6
Outputs:
- layer_out: bfloat16 [8192, 2048], P(('expert', 'fsdp'))
- input_grad: float32 [8192, 2048], P(('expert', 'fsdp'))
- prenorm_grad: float32 [2048], P(('expert', 'fsdp'))
- query_grad: float32 [2048, 2048], P(('expert', 'fsdp'))
- key_grad: float32 [2048, 2048], P(('expert', 'fsdp'))
- value_grad: float32 [2048, 2048], P(('expert', 'fsdp'))
- querynorm_grad: float32 [128], P(('expert', 'fsdp'))
- keynorm_grad: float32 [128], P(('expert', 'fsdp'))
- output_grad: float32 [2048, 2048], P(('expert', 'fsdp'))
- postnorm_grad: float32 [2048], P(('expert', 'fsdp'))
- router_grad: float32 [2048, 16], P(('expert', 'fsdp'))
- inner_grad: float32 [16, 2048, 2048], P('expert', 'fsdp')
- outer_grad: float32 [16, 1024, 2048], P('expert', 'fsdp')
Inputs may be any that keep to these rules, and one draw needn't show every extreme that they name: `sequence_lengths`: a sequence's live tokens fill the start of its 1024 places; some sequence is 1024 long and some 1024 // 4. `expert_ids`: each row names 8 different experts. `pair_order`: each row is a permutation.
All inputs are finite; a program needn't handle non-finite values.
Results may differ from a plain program's by a relative error of at most 0.02.
Values may be sent and summed in bfloat16 or wider, within the bound.
No kernel may reach another device: no remote copies, remote signals or barrier semaphores. Data moves between devices by JAX's collectives and lax.ppermute only.
A program may use at most 320 MiB of HBM per device.

v0:
```python
import math

import jax
import jax.numpy as jnp
from jax import lax
from jax.sharding import PartitionSpec as P

HEAD = 128
EFF = 1024
TOPK = 8


epsilon = 1e-06
rope_base = 10000.0
masked = -1e30


def from_partner(block, axis, stride):
    count = lax.axis_size(axis)
    route = []
    for low in range(count):
        high = low | 1 << stride
        if high != low and high < count:
            route += [(low, high), (high, low)]
    return lax.ppermute(block, axis, route)


def contract_rows(left, right):
    return lax.dot_general(
        left, right, (((0,), (0,)), ((), ())), preferred_element_type=jnp.float32
    )


def contract_cols(left, right):
    return lax.dot_general(
        left, right, (((1,), (1,)), ((), ())), preferred_element_type=jnp.float32
    )


def rms_scale(values, gain):
    inverse = lax.rsqrt(jnp.mean(values * values, axis=-1, keepdims=True) + epsilon)
    return (values * inverse * gain, inverse)


def rms_back(values, inverse, gain, upstream):
    scaled = upstream * gain
    inner_sum = jnp.sum(scaled * values, axis=-1, keepdims=True)
    length_now = values.shape[-1]
    grad_values = inverse * scaled - values * (inverse * inverse * inverse) * (
        inner_sum / length_now
    )
    return (grad_values, upstream * values * inverse)


def rotary_tables(positions):
    half_width = HEAD // 2
    freq_steps = jnp.arange(half_width, dtype=jnp.float32)
    frequency = jnp.exp(freq_steps * (-2.0 * math.log(rope_base) / HEAD))
    angles = positions.astype(jnp.float32)[:, None] * frequency[None, :]
    return (jnp.cos(angles)[:, None, :], jnp.sin(angles)[:, None, :])


def rotate(values, cosine_table, sine_table):
    half_width = values.shape[-1] // 2
    lower_half = values[..., :half_width]
    upper_half = values[..., half_width:]
    return jnp.concatenate(
        [
            lower_half * cosine_table - upper_half * sine_table,
            upper_half * cosine_table + lower_half * sine_table,
        ],
        axis=-1,
    )


def rotate_back(upstream, cosine_table, sine_table):
    half_width = upstream.shape[-1] // 2
    lower_half = upstream[..., :half_width]
    upper_half = upstream[..., half_width:]
    return jnp.concatenate(
        [
            lower_half * cosine_table + upper_half * sine_table,
            upper_half * cosine_table - lower_half * sine_table,
        ],
        axis=-1,
    )


def softmax_rows(scores):
    peak_score = jnp.max(scores, axis=-1, keepdims=True)
    exponent = jnp.exp(scores - peak_score)
    running = jnp.sum(exponent, axis=-1, keepdims=True)
    return (exponent / running, peak_score + jnp.log(running))


def on_device(
    hidden_in,
    prenorm_gain,
    query_weight,
    key_weight,
    value_weight,
    querynorm_gain,
    keynorm_gain,
    output_weight,
    postnorm_gain,
    router_weight,
    expert_inner,
    expert_outer,
    expert_ids,
    pair_order,
    sequence_lengths,
    cotangent,
):
    tokens, model_width = hidden_in.shape
    head_count = model_width // HEAD
    owners = lax.axis_size("expert")
    sharers = lax.axis_size("fsdp")
    capacity = tokens * TOPK // owners
    slot_count = owners * capacity
    slot_span = 2 * sharers * tokens
    half_span = slot_span // 2
    pair_count = tokens * TOPK
    owner_index = lax.axis_index("expert")
    sharer_index = lax.axis_index("fsdp")
    parity = owner_index % 2
    length = lax.dynamic_index_in_dim(sequence_lengths, owner_index // 2, 0, keepdims=False)
    positions = (parity * sharers + sharer_index) * tokens + jnp.arange(tokens, dtype=jnp.int32)
    token_live = positions < length
    key_live = jnp.arange(slot_span, dtype=jnp.int32) < length
    cosine_table, sine_table = rotary_tables(positions)
    score_scale = 1.0 / math.sqrt(HEAD)
    layer_params = (
        prenorm_gain,
        query_weight,
        key_weight,
        value_weight,
        querynorm_gain,
        keynorm_gain,
        output_weight,
        postnorm_gain,
        router_weight,
    )
    gathered = (
        lax.all_gather(layer_params[0], ("expert", "fsdp"), axis=0, tiled=True),
        lax.all_gather(layer_params[1], ("expert", "fsdp"), axis=0, tiled=True),
        lax.all_gather(layer_params[2], ("expert", "fsdp"), axis=0, tiled=True),
        lax.all_gather(layer_params[3], ("expert", "fsdp"), axis=0, tiled=True),
        lax.all_gather(layer_params[4], ("expert", "fsdp"), axis=0, tiled=True),
        lax.all_gather(layer_params[5], ("expert", "fsdp"), axis=0, tiled=True),
        lax.all_gather(layer_params[6], ("expert", "fsdp"), axis=0, tiled=True),
        lax.all_gather(layer_params[7], ("expert", "fsdp"), axis=0, tiled=True),
        lax.all_gather(layer_params[8], ("expert", "fsdp"), axis=0, tiled=True),
    )
    first_gain = gathered[0].astype(jnp.float32)
    query_full, key_full, value_full = (gathered[1], gathered[2], gathered[3])
    query_scale = gathered[4].astype(jnp.float32)
    key_scale = gathered[5].astype(jnp.float32)
    output_full = gathered[6]
    second_gain = gathered[7].astype(jnp.float32)
    router_full = gathered[8]
    hidden_f = hidden_in.astype(jnp.float32)
    first_normed, first_inverse = rms_scale(hidden_f, first_gain)
    first_low = first_normed.astype(jnp.bfloat16)
    query_raw = jnp.dot(first_low, query_full, preferred_element_type=jnp.float32).reshape(
        tokens, head_count, HEAD
    )
    key_raw = jnp.dot(first_low, key_full, preferred_element_type=jnp.float32).reshape(
        tokens, head_count, HEAD
    )
    value_low = (
        jnp.dot(first_low, value_full, preferred_element_type=jnp.float32)
        .astype(jnp.bfloat16)
        .reshape(tokens, head_count, HEAD)
    )
    query_normed, query_inverse = rms_scale(query_raw, query_scale)
    key_normed, key_inverse = rms_scale(key_raw, key_scale)
    query_low = rotate(query_normed, cosine_table, sine_table).astype(jnp.bfloat16)
    key_low = rotate(key_normed, cosine_table, sine_table).astype(jnp.bfloat16)
    own_pair = jnp.stack([key_low, value_low])
    pair_block = lax.all_gather(own_pair, "fsdp", axis=1, tiled=True)
    partner_block = from_partner(pair_block, "expert", 0)
    slot_block = jnp.where(
        parity == 0,
        jnp.concatenate([pair_block, partner_block], axis=1),
        jnp.concatenate([partner_block, pair_block], axis=1),
    )
    slot_keys = slot_block[0]
    slot_values = slot_block[1]
    scores = (
        jnp.einsum("qhd,khd->hqk", query_low, slot_keys, preferred_element_type=jnp.float32)
        * score_scale
    )
    scores = jnp.where(key_live[None, None, :], scores, masked)
    attention, log_total = softmax_rows(scores)
    attended = jnp.einsum(
        "hqk,khd->qhd",
        attention.astype(jnp.bfloat16),
        slot_values,
        preferred_element_type=jnp.float32,
    )
    attended_low = attended.reshape(tokens, model_width).astype(jnp.bfloat16)
    branch = jnp.dot(attended_low, output_full, preferred_element_type=jnp.float32)
    residual = hidden_f + branch
    second_normed, second_inverse = rms_scale(residual, second_gain)
    mixed_in = second_normed.astype(jnp.bfloat16)
    logits = jnp.dot(mixed_in, router_full, preferred_element_type=jnp.float32)
    route_hot = (
        expert_ids[:, :, None] == jnp.arange(owners, dtype=jnp.int32)[None, None, :]
    ).astype(jnp.float32)
    chosen = jnp.sum(route_hot * logits[:, None, :], axis=-1)
    gate_soft, unused = softmax_rows(chosen)
    pair_expert = expert_ids.reshape(pair_count)
    pair_key = pair_order.reshape(pair_count)
    pair_live = jnp.repeat(token_live, TOPK)
    earlier = (
        (pair_expert[None, :] == pair_expert[:, None])
        & (pair_key[None, :] < pair_key[:, None])
        & pair_live[None, :]
    )
    pair_rank = jnp.sum(earlier.astype(jnp.int32), axis=1)
    pair_kept = pair_live & (pair_rank < capacity)
    pair_row = jnp.where(pair_kept, pair_expert * capacity + pair_rank, slot_count)
    row_hits = pair_row[None, :] == jnp.arange(slot_count, dtype=jnp.int32)[:, None]
    pair_token = jnp.arange(pair_count, dtype=jnp.int32) // TOPK
    row_token = jnp.sum(jnp.where(row_hits, pair_token[None, :], 0), axis=1)
    row_used = jnp.any(row_hits, axis=1)
    kept_gate = gate_soft.reshape(pair_count) * pair_kept.astype(jnp.float32)
    row_gate = jnp.sum(jnp.where(row_hits, kept_gate[None, :], 0.0), axis=1)
    send_rows = jnp.where(
        row_used[:, None], mixed_in[row_token], jnp.zeros((), jnp.bfloat16)
    ).reshape(owners, capacity, model_width)
    inner_full, outer_full = (
        lax.all_gather(expert_inner, "fsdp", axis=1, tiled=True),
        lax.all_gather(expert_outer, "fsdp", axis=1, tiled=True),
    )
    inner_now = inner_full[0]
    outer_now = outer_full[0]
    arrived_rows = lax.all_to_all(send_rows, "expert", split_axis=0, concat_axis=0, tiled=True)
    sources = arrived_rows.shape[0]
    items = arrived_rows.shape[1]
    flat_rows = arrived_rows.reshape(sources * items, model_width)
    gate_up = jnp.dot(flat_rows, inner_now, preferred_element_type=jnp.float32)
    hidden_rows = (jax.nn.silu(gate_up[:, :EFF]) * gate_up[:, EFF:]).astype(jnp.bfloat16)
    result = jnp.dot(hidden_rows, outer_now, preferred_element_type=jnp.float32).astype(
        jnp.bfloat16
    )
    returned_rows = lax.all_to_all(
        result.reshape(sources, items, model_width),
        "expert",
        split_axis=0,
        concat_axis=0,
        tiled=True,
    )
    returned = returned_rows
    kept_both = gate_up.reshape(sources, items, 2 * EFF)
    returned_rows = jnp.concatenate(
        [returned.reshape(slot_count, model_width), jnp.zeros((1, model_width), jnp.bfloat16)],
        axis=0,
    )
    pair_output = returned_rows[pair_row].reshape(tokens, TOPK, model_width).astype(jnp.float32)
    kept_soft = kept_gate.reshape(tokens, TOPK)
    mixed = jnp.sum(kept_soft[:, :, None] * pair_output, axis=1)
    layer_out = (residual + mixed).astype(jnp.bfloat16)
    upstream = cotangent.astype(jnp.float32) * token_live[:, None].astype(jnp.float32)
    late_params, upstream = lax.optimization_barrier((layer_params, upstream))
    regathered = (
        lax.all_gather(late_params[0], ("expert", "fsdp"), axis=0, tiled=True),
        lax.all_gather(late_params[1], ("expert", "fsdp"), axis=0, tiled=True),
        lax.all_gather(late_params[2], ("expert", "fsdp"), axis=0, tiled=True),
        lax.all_gather(late_params[3], ("expert", "fsdp"), axis=0, tiled=True),
        lax.all_gather(late_params[4], ("expert", "fsdp"), axis=0, tiled=True),
        lax.all_gather(late_params[5], ("expert", "fsdp"), axis=0, tiled=True),
        lax.all_gather(late_params[6], ("expert", "fsdp"), axis=0, tiled=True),
        lax.all_gather(late_params[7], ("expert", "fsdp"), axis=0, tiled=True),
        lax.all_gather(late_params[8], ("expert", "fsdp"), axis=0, tiled=True),
    )
    query_back, key_back, value_back = (regathered[1], regathered[2], regathered[3])
    output_back, router_back = (regathered[6], regathered[8])
    gate_grad = jnp.sum(pair_output * upstream[:, None, :], axis=-1) * pair_kept.reshape(
        tokens, TOPK
    ).astype(jnp.float32)
    row_upstream = jnp.where(
        row_used[:, None], upstream[row_token] * row_gate[:, None], 0.0
    ).astype(jnp.bfloat16)
    arrived_grad = lax.all_to_all(
        row_upstream.reshape(owners, capacity, model_width),
        "expert",
        split_axis=0,
        concat_axis=0,
        tiled=True,
    )
    row_inputs = arrived_rows.reshape(slot_count, model_width)
    gate_up = kept_both.reshape(slot_count, 2 * EFF)
    row_grads = arrived_grad.reshape(slot_count, model_width)
    gate_part = gate_up[:, :EFF]
    up_part = gate_up[:, EFF:]
    gate_sigmoid = jax.nn.sigmoid(gate_part)
    activated = gate_part * gate_sigmoid
    hidden_low = (activated * up_part).astype(jnp.bfloat16)
    outer_local = contract_rows(hidden_low, row_grads)
    hidden_grad = contract_cols(row_grads, outer_now)
    both_grad = jnp.concatenate(
        [
            hidden_grad * up_part * gate_sigmoid * (1.0 + gate_part * (1.0 - gate_sigmoid)),
            hidden_grad * activated,
        ],
        axis=-1,
    ).astype(jnp.bfloat16)
    inner_local = contract_rows(row_inputs, both_grad)
    input_rows_grad = contract_cols(both_grad, inner_now).astype(jnp.bfloat16)
    returned_grad = lax.all_to_all(
        input_rows_grad.reshape(owners, capacity, model_width),
        "expert",
        split_axis=0,
        concat_axis=0,
        tiled=True,
    )
    inner_grad, outer_grad = (
        lax.psum_scatter(
            inner_local[None].astype(jnp.bfloat16), "fsdp", scatter_dimension=1, tiled=True
        ).astype(jnp.float32),
        lax.psum_scatter(
            outer_local[None].astype(jnp.bfloat16), "fsdp", scatter_dimension=1, tiled=True
        ).astype(jnp.float32),
    )
    grad_rows = jnp.concatenate(
        [returned_grad.reshape(slot_count, model_width), jnp.zeros((1, model_width), jnp.bfloat16)],
        axis=0,
    )
    mixed_grad = jnp.sum(
        grad_rows[pair_row].reshape(tokens, TOPK, model_width).astype(jnp.float32), axis=1
    )
    soft_grad = gate_soft * (gate_grad - jnp.sum(gate_soft * gate_grad, axis=-1, keepdims=True))
    logit_grad = jnp.sum(route_hot * soft_grad[:, :, None], axis=1).astype(jnp.bfloat16)
    router_local = contract_rows(mixed_in, logit_grad)
    mixed_grad = mixed_grad + contract_cols(logit_grad, router_back)
    residual_part, second_terms = rms_back(residual, second_inverse, second_gain, mixed_grad)
    residual_grad = upstream + residual_part
    branch_grad = residual_grad.astype(jnp.bfloat16)
    output_local = contract_rows(attended_low, branch_grad)
    attended_grad = (
        contract_cols(branch_grad, output_back)
        .astype(jnp.bfloat16)
        .reshape(tokens, head_count, HEAD)
    )
    scores_again = (
        jnp.einsum("qhd,khd->hqk", query_low, slot_keys, preferred_element_type=jnp.float32)
        * score_scale
    )
    scores_again = jnp.where(key_live[None, None, :], scores_again, masked)
    attention_again = jnp.exp(scores_again - log_total)
    attention_grad = jnp.einsum(
        "qhd,khd->hqk", attended_grad, slot_values, preferred_element_type=jnp.float32
    )
    inner_sum = jnp.sum(attention_again * attention_grad, axis=-1, keepdims=True)
    score_grad = (attention_again * (attention_grad - inner_sum)).astype(jnp.bfloat16)
    value_slot_grad = jnp.einsum(
        "hqk,qhd->khd",
        attention_again.astype(jnp.bfloat16),
        attended_grad,
        preferred_element_type=jnp.float32,
    )
    key_slot_grad = (
        jnp.einsum("hqk,qhd->khd", score_grad, query_low, preferred_element_type=jnp.float32)
        * score_scale
    )
    query_rot_grad = (
        jnp.einsum("hqk,khd->qhd", score_grad, slot_keys, preferred_element_type=jnp.float32)
        * score_scale
    )
    slot_grads = jnp.stack([key_slot_grad, value_slot_grad])
    lower_grads = slot_grads[:, :half_span]
    upper_grads = slot_grads[:, half_span:]
    own_grads = jnp.where(parity == 0, lower_grads, upper_grads)
    other_grads = jnp.where(parity == 0, upper_grads, lower_grads)
    partner_part = from_partner(other_grads.astype(jnp.bfloat16), "expert", 0).astype(
        other_grads.dtype
    )
    pair_sums = lax.psum_scatter(
        (own_grads + partner_part).astype(jnp.bfloat16), "fsdp", scatter_dimension=1, tiled=True
    ).astype(jnp.float32)
    key_norm_grad = rotate_back(pair_sums[0], cosine_table, sine_table)
    key_raw_grad, key_terms = rms_back(key_raw, key_inverse, key_scale, key_norm_grad)
    query_norm_grad = rotate_back(query_rot_grad, cosine_table, sine_table)
    query_raw_grad, query_terms = rms_back(query_raw, query_inverse, query_scale, query_norm_grad)
    query_low_grad = query_raw_grad.reshape(tokens, model_width).astype(jnp.bfloat16)
    key_low_grad = key_raw_grad.reshape(tokens, model_width).astype(jnp.bfloat16)
    value_low_grad = pair_sums[1].reshape(tokens, model_width).astype(jnp.bfloat16)
    query_local = contract_rows(first_low, query_low_grad)
    key_local = contract_rows(first_low, key_low_grad)
    value_local = contract_rows(first_low, value_low_grad)
    normed_grad = (
        contract_cols(query_low_grad, query_back)
        + contract_cols(key_low_grad, key_back)
        + contract_cols(value_low_grad, value_back)
    )
    hidden_part, first_terms = rms_back(hidden_f, first_inverse, first_gain, normed_grad)
    input_grad = residual_grad + hidden_part
    summed = (
        lax.psum_scatter(
            jnp.sum(first_terms, axis=0), ("expert", "fsdp"), scatter_dimension=0, tiled=True
        ),
        lax.psum_scatter(query_local, ("expert", "fsdp"), scatter_dimension=0, tiled=True),
        lax.psum_scatter(key_local, ("expert", "fsdp"), scatter_dimension=0, tiled=True),
        lax.psum_scatter(value_local, ("expert", "fsdp"), scatter_dimension=0, tiled=True),
        lax.psum_scatter(
            jnp.sum(query_terms, axis=(0, 1)), ("expert", "fsdp"), scatter_dimension=0, tiled=True
        ),
        lax.psum_scatter(
            jnp.sum(key_terms, axis=(0, 1)), ("expert", "fsdp"), scatter_dimension=0, tiled=True
        ),
        lax.psum_scatter(output_local, ("expert", "fsdp"), scatter_dimension=0, tiled=True),
        lax.psum_scatter(
            jnp.sum(second_terms, axis=0), ("expert", "fsdp"), scatter_dimension=0, tiled=True
        ),
        lax.psum_scatter(router_local, ("expert", "fsdp"), scatter_dimension=0, tiled=True),
    )
    return (
        layer_out,
        input_grad,
        summed[0],
        summed[1],
        summed[2],
        summed[3],
        summed[4],
        summed[5],
        summed[6],
        summed[7],
        summed[8],
        inner_grad,
        outer_grad,
    )


def solution(mesh):
    placed = (
        P(("expert", "fsdp"), None),
        P(("expert", "fsdp")),
        P(("expert", "fsdp"), None),
        P(("expert", "fsdp"), None),
        P(("expert", "fsdp"), None),
        P(("expert", "fsdp")),
        P(("expert", "fsdp")),
        P(("expert", "fsdp"), None),
        P(("expert", "fsdp")),
        P(("expert", "fsdp"), None),
        P("expert", "fsdp", None),
        P("expert", "fsdp", None),
        P(("expert", "fsdp"), None),
        P(("expert", "fsdp"), None),
        P(),
        P(("expert", "fsdp"), None),
    )
    return jax.shard_map(
        on_device,
        mesh=mesh,
        in_specs=placed,
        out_specs=(
            P(("expert", "fsdp"), None),
            P(("expert", "fsdp"), None),
            P(("expert", "fsdp")),
            P(("expert", "fsdp"), None),
            P(("expert", "fsdp"), None),
            P(("expert", "fsdp"), None),
            P(("expert", "fsdp")),
            P(("expert", "fsdp")),
            P(("expert", "fsdp"), None),
            P(("expert", "fsdp")),
            P(("expert", "fsdp"), None),
            P("expert", "fsdp", None),
            P("expert", "fsdp", None),
        ),
        check_vma=False,
    )
```

profile of v0, /device:TPU:0, one launch (start us, length us, event | category | flops | bytes accessed | tf_op | source)
XLA Modules:
  0.0 2787.7 jit_solution(16127846858687368339)
XLA Ops:
  12.9 42.6 %all-reduce.11 = (bf16[2048]{0:T(1024)(128)(2,1)S(1)}, bf16[128]{0:T(256)(128)(2,1)S(1)}, bf16[128]{0:T(256)(128)(2,1)S(1)}, bf16[2048]{0:T(1024)(128)(2,1)S(1)}) all-reduce(bf16[2048]{0:T(1024)(128)(2,1)S(1)} %dynamic-update-slice, bf16[128]{0:T(256)(128)(2,1)S(1)} %dynamic-update-slice.1, ...), channel_id=1, replica_groups=mesh['expert'=16,'fsdp'=2] {'expert','fsdp'}, use_global_device_ids=true, to_apply=%add.2 | all-reduce | flops 4352 | bytes 17408
  58.1 33.2 %all-gather.14.cloned.1.call-done = bf16[2048,2048]{1,0:T(8,128)(2,1)} async-done(((bf16[64,2048]{1,0:T(8,128)(2,1)}), bf16[2048,2048]{1,0:T(8,128)(2,1)}) %all-gather.14.cloned.1.call-update) | async-done | bytes 8388624 | tf_op jit(solution)/shard_map/all_gather | solution.py:146
  91.3 6.1 fusion.78
  99.8 70.4 %all-gather.20.cloned.1.call-done = bf16[2048,2048]{1,0:T(8,128)(2,1)} async-done(((bf16[64,2048]{1,0:T(8,128)(2,1)}), bf16[2048,2048]{1,0:T(8,128)(2,1)}) %all-gather.20.cloned.1.call-update) | async-done | bytes 8388624 | tf_op jit(solution)/shard_map/all_gather | solution.py:145
  170.2 5.8 fusion.75
  179.6 69.5 %all-gather.16.cloned.1.call-done = bf16[2048,2048]{1,0:T(8,128)(2,1)} async-done(((bf16[64,2048]{1,0:T(8,128)(2,1)}), bf16[2048,2048]{1,0:T(8,128)(2,1)}) %all-gather.16.cloned.1.call-update) | async-done | bytes 8388624 | tf_op jit(solution)/shard_map/all_gather | solution.py:147
  249.2 5.8 fusion.46
  263.4 11.8 all-gather.18.cloned.1.call-done
  277.0 149.9 %all-gather = bf16[32,64,16]{1,2,0:T(8,128)(2,1)S(1)} all-gather(bf16[1,64,16]{1,2,0:T(8,128)(2,1)S(1)} %bitcast.242), channel_id=1, replica_groups=mesh['expert'=16,'fsdp'=2] {'expert','fsdp'}, dimensions={0}, use_global_device_ids=true | all-gather | bytes 67584 | tf_op jit(solution)/shard_map/all_gather | solution.py:152
  434.4 10.6 maximum_select_fusion
  450.5 5.8 copy-done.4
  460.0 10.1 fusion.45
  470.2 6.2 multiply_reduce_fusion.3
  483.2 11.1 gather_fusion
  494.2 7.3 broadcast_select_fusion
  506.7 12.5 gather_fusion.2
  521.0 9.3 select_convert_fusion
  530.2 135.7 %all-to-all-done = bf16[16,128,2048]{2,1,0:T(8,128)(2,1)} async-done(((bf16[16,128,2048]{2,1,0:T(8,128)(2,1)}), bf16[16,128,2048]{2,1,0:T(8,128)(2,1)}, u32[]{:S(2)}, u32[]{:S(2)}) %all-to-all-start) | async-done | bytes 8388640 | tf_op jit(solution)/shard_map/all_to_all | solution.py:238
  665.9 38.2 %all-to-all-start.2 = ((bf16[16,128,2048]{2,1,0:T(8,128)(2,1)}), bf16[16,128,2048]{2,1,0:T(8,128)(2,1)}, u32[]{:S(2)}, u32[]{:S(2)}) async-start(bf16[16,128,2048]{2,1,0:T(8,128)(2,1)} %select_convert_fusion), calls=%async_computation.2 | async-start | bytes 16777216 | tf_op jit(solution)/shard_map/all_to_all | solution.py:285
  705.4 21.9 all-gather.24.cloned.1.call-done
  727.3 24.5 fusion.10
  751.8 109.6 %all-to-all-done.2 = bf16[16,128,2048]{2,1,0:T(8,128)(2,1)} async-done(((bf16[16,128,2048]{2,1,0:T(8,128)(2,1)}), bf16[16,128,2048]{2,1,0:T(8,128)(2,1)}, u32[]{:S(2)}, u32[]{:S(2)}) %all-to-all-start.2) | async-done | bytes 8388640 | tf_op jit(solution)/shard_map/all_to_all | solution.py:285
  861.4 22.2 multiply_convert_fusion.2
  883.6 13.7 convolution_convert_fusion
  897.3 38.3 %all-to-all-start.1 = ((bf16[16,128,2048]{2,1,0:T(8,128)(2,1)}), bf16[16,128,2048]{2,1,0:T(8,128)(2,1)}, u32[]{:S(2)}, u32[]{:S(2)}) async-start(bf16[16,128,2048]{2,1,0:T(8,128)(2,1)} %bitcast.225), calls=%async_computation.1 | async-start | bytes 16777216 | tf_op jit(solution)/shard_map/all_to_all | solution.py:247
  935.6 23.7 fusion.15
  959.3 129.4 %all-to-all-done.1 = bf16[16,128,2048]{2,1,0:T(8,128)(2,1)} async-done(((bf16[16,128,2048]{2,1,0:T(8,128)(2,1)}), bf16[16,128,2048]{2,1,0:T(8,128)(2,1)}, u32[]{:S(2)}, u32[]{:S(2)}) %all-to-all-start.1) | async-done | bytes 8388640 | tf_op jit(solution)/shard_map/all_to_all | solution.py:247
  1088.7 38.5 %all-to-all-start.3 = ((bf16[16,128,2048]{2,1,0:T(8,128)(2,1)}), bf16[16,128,2048]{2,1,0:T(8,128)(2,1)}, u32[]{:S(2)}, u32[]{:S(2)}) async-start(bf16[16,128,2048]{2,1,0:T(8,128)(2,1)} %bitcast.224), calls=%async_computation.3 | async-start | bytes 16777216 | tf_op jit(solution)/shard_map/all_to_all | solution.py:311
  1128.5 191.5 %all-gather.1 = bf16[32,64,16]{1,2,0:T(8,128)(2,1)S(1)} all-gather(bf16[1,64,16]{1,2,0:T(8,128)(2,1)S(1)} %bitcast.243), channel_id=1, replica_groups=mesh['expert'=16,'fsdp'=2] {'expert','fsdp'}, dimensions={0}, use_global_device_ids=true | all-gather | bytes 67584 | tf_op jit(solution)/shard_map/all_gather | solution.py:275
  1320.6 8.4 concatenate.51
  1329.0 21.0 gather_fusion.1
  1350.0 9.5 fusion.1
  1359.5 8.4 concatenate.53
  1367.9 21.0 gather_fusion.3
  1388.9 11.3 convert_reduce_fusion
  1406.4 6.4 convolution_convert_fusion.1
  1413.3 12.8 multiply_reduce_fusion
  1426.1 9.7 fusion.23
  1435.8 15.9 multiply_convert_fusion
  1451.7 6.5 multiply_bitcast_fusion
  1462.2 48.2 %collective-permute-start.1 = (bf16[2,512,16,128]{3,1,2,0:T(8,128)(2,1)S(1)}, bf16[2,512,16,128]{3,1,2,0:T(8,128)(2,1)S(1)}, u32[]{:S(2)}, u32[]{:S(2)}) collective-permute-start(bf16[2,512,16,128]{3,1,2,0:T(8,128)(2,1)S(1)} %select_convert_fusion.1), channel_id=1, source_target_pairs={{0,2},{2,0},{4,6},{6,4},{8,10},{10,8},{12,14},{14,12},{16,18},{18,... | collective-permute-start | bytes 12582920 | tf_op jit(solution)/shard_map/ppermute | solution.py:25
  1510.4 90.9 %collective-permute-done.1 = bf16[2,512,16,128]{3,1,2,0:T(8,128)(2,1)S(1)} collective-permute-done((bf16[2,512,16,128]{3,1,2,0:T(8,128)(2,1)S(1)}, bf16[2,512,16,128]{3,1,2,0:T(8,128)(2,1)S(1)}, u32[]{:S(2)}, u32[]{:S(2)}) %collective-permute-start.1) | collective-permute-done | bytes 4194336 | tf_op jit(solution)/shard_map/ppermute | solution.py:25
  1601.3 5.6 add_convert_fusion
  1607.0 14.2 convert_bitcast_fusion.1
  1624.2 23.8 convert_bitcast_fusion
  1650.0 8.1 fusion.52
  1659.1 8.2 multiply_bitcast_fusion.1
  1682.5 8.5 fusion.71
  1704.6 8.3 fusion.73
  1714.6 8.2 fusion.69
  1727.1 52.2 %reduce-scatter.25.cloned.1.call-done = f32[64,16]{1,0:T(8,128)} async-done(((f32[2048,16]{1,0:T(8,128)}), f32[64,16]{1,0:T(8,128)}) %reduce-scatter.25.cloned.1.call-update) | async-done | bytes 4112
  1780.7 13.6 reduce-scatter.21.cloned.1.call-done
  1794.3 6.7 convert_element_type.194
  1801.0 74.9 %all-gather.30.cloned.1.call-done = bf16[2048,2048]{1,0:T(8,128)(2,1)} async-done(((bf16[64,2048]{1,0:T(8,128)(2,1)}), bf16[2048,2048]{1,0:T(8,128)(2,1)}) %all-gather.30.cloned.1.call-update) | async-done | bytes 8388624 | tf_op jit(solution)/shard_map/all_gather | solution.py:268
  1875.9 7.0 fusion.85
  1882.9 71.8 %all-gather.32.cloned.1.call-done = bf16[2048,2048]{1,0:T(8,128)(2,1)} async-done(((bf16[64,2048]{1,0:T(8,128)(2,1)}), bf16[2048,2048]{1,0:T(8,128)(2,1)}) %all-gather.32.cloned.1.call-update) | async-done | bytes 8388624 | tf_op jit(solution)/shard_map/all_gather | solution.py:269
  1954.7 7.6 convolution_add_fusion.2
  1962.3 71.1 %all-gather.34.cloned.1.call-done = bf16[2048,2048]{1,0:T(8,128)(2,1)} async-done(((bf16[64,2048]{1,0:T(8,128)(2,1)}), bf16[2048,2048]{1,0:T(8,128)(2,1)}) %all-gather.34.cloned.1.call-update) | async-done | bytes 8388624 | tf_op jit(solution)/shard_map/all_gather | solution.py:270
  2033.5 8.3 fusion.34
  2041.8 46.3 %all-reduce.10 = (f32[2048]{0:T(1024)S(1)}, f32[128]{0:T(128)S(1)}, f32[128]{0:T(128)S(1)}, f32[2048]{0:T(1024)S(1)}) all-reduce(f32[2048]{0:T(1024)S(1)} %get-tuple-element.29, f32[128]{0:T(128)S(1)} %bitcast_reduce_fusion.1, f32[128]{0:T(128)S(1)} %bitcast_reduce_fusion, ...), channel_id=3, replica_groups=mesh['expert'=16,'fsdp'=2] {'expert','fsdp'}, use_global_device_ids=true, to_apply=%region_25.26.clone | all-reduce | flops 4352 | bytes 34816
  2093.9 124.6 %reduce-scatter.19.cloned.1.call-done = f32[64,2048]{1,0:T(8,128)} async-done(((f32[2048,2048]{1,0:T(8,128)}), f32[64,2048]{1,0:T(8,128)}) %reduce-scatter.19.cloned.1.call-update) | async-done | bytes 524304 | tf_op jit(solution)/shard_map/reduce_scatter | solution.py:412
  2218.5 187.7 %reduce-scatter.15.cloned.1.call-done = f32[64,2048]{1,0:T(8,128)} async-done(((f32[2048,2048]{1,0:T(8,128)}), f32[64,2048]{1,0:T(8,128)}) %reduce-scatter.15.cloned.1.call-update) | async-done | bytes 524304 | tf_op jit(solution)/shard_map/reduce_scatter | solution.py:404
  2406.2 187.2 %reduce-scatter.13.cloned.1.call-done = f32[64,2048]{1,0:T(8,128)} async-done(((f32[2048,2048]{1,0:T(8,128)}), f32[64,2048]{1,0:T(8,128)}) %reduce-scatter.13.cloned.1.call-update) | async-done | bytes 524304 | tf_op jit(solution)/shard_map/reduce_scatter | solution.py:403
  2593.5 187.3 %reduce-scatter.17.cloned.1.call-done = f32[64,2048]{1,0:T(8,128)} async-done(((f32[2048,2048]{1,0:T(8,128)}), f32[64,2048]{1,0:T(8,128)}) %reduce-scatter.17.cloned.1.call-update) | async-done | bytes 524304 | tf_op jit(solution)/shard_map/reduce_scatter | solution.py:405
  (332 shorter events, 116.2 us)
Async XLA Ops:
  7.2 84.1 %all-gather.14.cloned.1.call-start = ((), (), s32[]{:S(2)}) async-start(), calls=%async_computation.12 | async-start | bytes 8650752 | tf_op jit(solution)/shard_map/all_gather | solution.py:146
  7.9 162.3 %all-gather.20.cloned.1.call-start = ((), (), s32[]{:S(2)}) async-start(), calls=%async_computation.15 | async-start | bytes 8650752 | tf_op jit(solution)/shard_map/all_gather | solution.py:145
  8.7 240.5 %all-gather.16.cloned.1.call-start = ((), (), s32[]{:S(2)}) async-start(), calls=%async_computation.13 | async-start | bytes 8650752 | tf_op jit(solution)/shard_map/all_gather | solution.py:147
  9.4 265.9 %all-gather.18.cloned.1.call-start = ((), (), s32[]{:S(2)}) async-start(), calls=%async_computation.14 | async-start | bytes 6291456 | tf_op jit(solution)/shard_map/all_gather | solution.py:180
  55.4 193.7 %copy-start.39 = (f32[2048]{0:T(1024)}, f32[2048]{0:T(1024)S(1)}, u32[]{:S(2)}) copy-start(f32[2048]{0:T(1024)S(1)} %convert_element_type.157) | copy-start | bytes 24580
  55.4 200.1 %copy-start.78 = (f32[128]{0:T(128)}, f32[128]{0:T(128)S(1)}, u32[]{:S(2)}) copy-start(f32[128]{0:T(128)S(1)} %convert_element_type.159) | copy-start | bytes 1540
  55.5 200.0 %copy-start.76 = (f32[128]{0:T(128)}, f32[128]{0:T(128)S(1)}, u32[]{:S(2)}) copy-start(f32[128]{0:T(128)S(1)} %convert_element_type.162) | copy-start | bytes 1540
  57.6 191.6 %copy-start.55 = (f32[256]{0:T(256)}, f32[256]{0:T(256)S(1)}, u32[]{:S(2)}) copy-start(f32[256]{0:T(256)S(1)} %get-tuple-element.77) | copy-start | bytes 3076
  58.1 200.3 %copy-start.32 = (f32[256,64]{1,0:T(8,128)}, f32[256,64]{1,0:T(8,128)S(1)}, u32[]{:S(2)}) copy-start(f32[256,64]{1,0:T(8,128)S(1)} %get-tuple-element.74) | copy-start | bytes 196612
  58.1 200.3 %copy-start.34 = (f32[256,64]{1,0:T(8,128)}, f32[256,64]{1,0:T(8,128)S(1)}, u32[]{:S(2)}) copy-start(f32[256,64]{1,0:T(8,128)S(1)} %get-tuple-element.75) | copy-start | bytes 196612
  97.4 72.8 %copy-start.5 = (bf16[256,2048]{1,0:T(8,128)(2,1)S(1)}, bf16[256,2048]{1,0:T(8,128)(2,1)}, u32[]{:S(2)}) copy-start(bf16[256,2048]{1,0:T(8,128)(2,1)} %param.16) | copy-start | bytes 3145732
  179.0 76.5 %copy-start.45 = (f32[256,16]{0,1:T(8,128)}, f32[256,16]{0,1:T(8,128)S(1)}, u32[]{:S(2)}) copy-start(f32[256,16]{0,1:T(8,128)S(1)} %get-tuple-element.71) | copy-start | bytes 49156
  179.6 75.9 %copy-start.43 = (f32[256,16]{0,1:T(8,128)}, f32[256,16]{0,1:T(8,128)S(1)}, u32[]{:S(2)}) copy-start(f32[256,16]{0,1:T(8,128)S(1)} %get-tuple-element.73) | copy-start | bytes 49156
  260.8 184.2 %copy-start.17 = (bf16[256,16,64]{2,0,1:T(8,128)(2,1)}, bf16[256,16,64]{2,0,1:T(8,128)(2,1)S(1)}, u32[]{:S(2)}) copy-start(bf16[256,16,64]{2,0,1:T(8,128)(2,1)S(1)} %get-tuple-element.58) | copy-start | bytes 1572868
  260.8 16.2 copy-start.72
  260.8 166.3 %copy-start.84 = (s32[8]{0:T(128)S(1)}, s32[8]{0:T(128)}, u32[]{:S(2)}) copy-start(s32[8]{0:T(128)} %param.30) | copy-start | bytes 100
  260.8 168.4 %copy-start.49 = (s32[256,8]{0,1:T(8,128)S(1)}, s32[256,8]{0,1:T(8,128)}, u32[]{:S(2)}) copy-start(s32[256,8]{0,1:T(8,128)} %param.28) | copy-start | bytes 24580
  260.8 169.3 %copy-start.83 = (s32[1,2048]{1,0:T(1,128)S(1)}, s32[1,2048]{1,0:T(1,128)}, u32[]{:S(2)}) copy-start(s32[1,2048]{1,0:T(1,128)} %param.29) | copy-start | bytes 24580
  262.8 207.3 %all-gather.22.cloned.1.call-start = ((), (), s32[]{:S(2)}) async-start(), calls=%async_computation.16 | async-start | bytes 8650752 | tf_op jit(solution)/shard_map/all_gather | solution.py:150
  275.3 159.2 %collective-permute-start = (bf16[2,512,16,128]{3,1,2,0:T(8,128)(2,1)}, bf16[2,512,16,128]{3,1,2,0:T(8,128)(2,1)}, u32[]{:S(2)}, u32[]{:S(2)}) collective-permute-start(bf16[2,512,16,128]{3,1,2,0:T(8,128)(2,1)} %all-gather.18.cloned.1.call-done), channel_id=1, source_target_pairs={{0,2},{2,0},{4,6},{6,4},{8,10},{10,8},{12,14},{14,12},{16,18},{18,... | collective-permute-start | bytes 12582920 | tf_op jit(solution)/shard_map/ppermute | solution.py:25
  277.0 200.0 %copy-start.51 = (f32[2048]{0:T(1024)}, f32[2048]{0:T(1024)S(1)}, u32[]{:S(2)}) copy-start(f32[2048]{0:T(1024)S(1)} %convert_element_type.168) | copy-start | bytes 24580
  428.4 16.6 copy-start.74
  434.4 44.8 %copy-start.53 = (s32[2048]{0:T(1024)}, s32[2048]{0:T(1024)S(1)}, u32[]{:S(2)}) copy-start(s32[2048]{0:T(1024)S(1)} %convert_reduce_fusion.1) | copy-start | bytes 24580
  477.9 16.3 copy-start.2
  501.6 164.3 %all-to-all-start = ((bf16[16,128,2048]{2,1,0:T(8,128)(2,1)}), bf16[16,128,2048]{2,1,0:T(8,128)(2,1)}, u32[]{:S(2)}, u32[]{:S(2)}) async-start(bf16[16,128,2048]{2,1,0:T(8,128)(2,1)} %broadcast_select_fusion), calls=%async_computation | async-start | bytes 16777216 | tf_op jit(solution)/shard_map/all_to_all | solution.py:238
  665.9 195.4 %all-to-all-start.2 = ((bf16[16,128,2048]{2,1,0:T(8,128)(2,1)}), bf16[16,128,2048]{2,1,0:T(8,128)(2,1)}, u32[]{:S(2)}, u32[]{:S(2)}) async-start(bf16[16,128,2048]{2,1,0:T(8,128)(2,1)} %select_convert_fusion), calls=%async_computation.2 | async-start | bytes 16777216 | tf_op jit(solution)/shard_map/all_to_all | solution.py:285
  704.1 23.2 all-gather.24.cloned.1.call-start
  704.7 47.1 %all-gather.26.cloned.1.call-start = ((), (), s32[]{:S(2)}) async-start(), calls=%async_computation.18 | async-start | bytes 6291456 | tf_op jit(solution)/shard_map/all_gather | solution.py:234
  861.4 22.3 copy-start.82
  897.3 191.3 %all-to-all-start.1 = ((bf16[16,128,2048]{2,1,0:T(8,128)(2,1)}), bf16[16,128,2048]{2,1,0:T(8,128)(2,1)}, u32[]{:S(2)}, u32[]{:S(2)}) async-start(bf16[16,128,2048]{2,1,0:T(8,128)(2,1)} %bitcast.225), calls=%async_computation.1 | async-start | bytes 16777216 | tf_op jit(solution)/shard_map/all_to_all | solution.py:247
  1088.6 39.4 %copy-start.42 = (pred[256,8]{1,0:T(8,128)(4,1)S(1)}, pred[256,8]{1,0:T(8,128)(4,1)}, u32[]{:S(2)}) copy-start(pred[256,8]{1,0:T(8,128)(4,1)} %copy-done.41) | copy-start | bytes 6148
  1088.6 39.6 %copy-start.50 = (s32[256,8]{0,1:T(8,128)S(1)}, s32[256,8]{0,1:T(8,128)}, u32[]{:S(2)}) copy-start(s32[256,8]{0,1:T(8,128)} %param.28) | copy-start | bytes 24580
  1088.6 39.8 %copy-start.73 = (bf16[64,16]{0,1:T(8,128)(2,1)S(1)}, bf16[64,16]{0,1:T(8,128)(2,1)}, u32[]{:S(2)}) copy-start(bf16[64,16]{0,1:T(8,128)(2,1)} %param.25) | copy-start | bytes 6148
  1088.6 231.5 %copy-start.54 = (s32[2048]{0:T(1024)S(1)}, s32[2048]{0:T(1024)}, u32[]{:S(2)}) copy-start(s32[2048]{0:T(1024)} %copy-done.53) | copy-start | bytes 24580
  1088.6 231.6 %copy-start.69 = (pred[2048]{0:T(1024)(128)(4,1)S(1)}, pred[2048]{0:T(1024)(128)(4,1)}, u32[]{:S(2)}) copy-start(pred[2048]{0:T(1024)(128)(4,1)} %copy-done.68) | copy-start | bytes 6148
  1088.6 231.8 %copy-start.38 = (f32[256,8]{0,1:T(8,128)S(1)}, f32[256,8]{0,1:T(8,128)}, u32[]{:S(2)}) copy-start(f32[256,8]{0,1:T(8,128)} %copy-done.37) | copy-start | bytes 24580
  1088.6 231.8 %copy-start.62 = (f32[256]{0:T(256)S(1)}, f32[256]{0:T(256)}, u32[]{:S(2)}) copy-start(f32[256]{0:T(256)} %copy-done.61) | copy-start | bytes 3076
  1088.7 231.8 %copy-start.67 = (f32[256]{0:T(256)S(1)}, f32[256]{0:T(256)}, u32[]{:S(2)}) copy-start(f32[256]{0:T(256)} %copy-done.66) | copy-start | bytes 3076
  1088.7 231.8 %copy-start.75 = (pred[256]{0:T(512)(128)(4,1)S(1)}, pred[256]{0:T(512)(128)(4,1)}, u32[]{:S(2)}) copy-start(pred[256]{0:T(512)(128)(4,1)} %copy-done.74) | copy-start | bytes 772
  1088.7 231.9 %copy-start.48 = (f32[16,256]{1,0:T(8,128)S(1)}, f32[16,256]{1,0:T(8,128)}, u32[]{:S(2)}) copy-start(f32[16,256]{1,0:T(8,128)} %copy-done.47) | copy-start | bytes 49156
  1088.7 231.9 %copy-start.60 = (f32[16,256]{1,0:T(8,128)S(1)}, f32[16,256]{1,0:T(8,128)}, u32[]{:S(2)}) copy-start(f32[16,256]{1,0:T(8,128)} %copy-done.59) | copy-start | bytes 49156
  1088.7 270.8 %all-to-all-start.3 = ((bf16[16,128,2048]{2,1,0:T(8,128)(2,1)}), bf16[16,128,2048]{2,1,0:T(8,128)(2,1)}, u32[]{:S(2)}, u32[]{:S(2)}) async-start(bf16[16,128,2048]{2,1,0:T(8,128)(2,1)} %bitcast.224), calls=%async_computation.3 | async-start | bytes 16777216 | tf_op jit(solution)/shard_map/all_to_all | solution.py:311
  1127.2 279.1 %all-gather.28.cloned.1.call-start = ((), (), s32[]{:S(2)}) async-start(), calls=%async_computation.19 | async-start | bytes 8650752 | tf_op jit(solution)/shard_map/all_gather | solution.py:273
  1128.0 539.4 %reduce-scatter.11.cloned.1.call-start = ((), (), s32[]{:S(2)}) async-start(), calls=%async_computation.21 | async-start | bytes 6291456 | tf_op jit(solution)/shard_map/reduce_scatter | solution.py:379
  1329.0 21.0 copy-start.1
  1435.8 15.9 copy-start.18
  1435.8 15.9 copy-start.19
  1462.2 139.1 %collective-permute-start.1 = (bf16[2,512,16,128]{3,1,2,0:T(8,128)(2,1)S(1)}, bf16[2,512,16,128]{3,1,2,0:T(8,128)(2,1)S(1)}, u32[]{:S(2)}, u32[]{:S(2)}) collective-permute-start(bf16[2,512,16,128]{3,1,2,0:T(8,128)(2,1)S(1)} %select_convert_fusion.1), channel_id=1, source_target_pairs={{0,2},{2,0},{4,6},{6,4},{8,10},{10,8},{12,14},{14,12},{16,18},{18,... | collective-permute-start | bytes 12582920 | tf_op jit(solution)/shard_map/ppermute | solution.py:25
  1606.9 116.0 %reduce-scatter.23.cloned.1.call-start = ((), (), s32[]{:S(2)}) async-start(), calls=%async_computation.29 | async-start | bytes 6291456 | tf_op jit(solution)/shard_map/reduce_scatter | solution.py:322
  1621.2 158.1 %reduce-scatter.25.cloned.1.call-start = ((), (), s32[]{:S(2)}) async-start(), calls=%async_computation.30 | async-start | bytes 1081344
  1624.2 170.1 %reduce-scatter.21.cloned.1.call-start = ((), (), s32[]{:S(2)}) async-start(), calls=%async_computation.28 | async-start | bytes 12582912 | tf_op jit(solution)/shard_map/reduce_scatter | solution.py:319
  1648.0 227.9 %all-gather.30.cloned.1.call-start = ((), (), s32[]{:S(2)}) async-start(), calls=%async_computation.20 | async-start | bytes 8650752 | tf_op jit(solution)/shard_map/all_gather | solution.py:268
  1648.8 305.9 %all-gather.32.cloned.1.call-start = ((), (), s32[]{:S(2)}) async-start(), calls=%async_computation.22 | async-start | bytes 8650752 | tf_op jit(solution)/shard_map/all_gather | solution.py:269
  1649.4 384.1 %all-gather.34.cloned.1.call-start = ((), (), s32[]{:S(2)}) async-start(), calls=%async_computation.23 | async-start | bytes 8650752 | tf_op jit(solution)/shard_map/all_gather | solution.py:270
  1649.9 568.6 %reduce-scatter.19.cloned.1.call-start = ((), (), s32[]{:S(2)}) async-start(), calls=%async_computation.27 | async-start | bytes 17301504 | tf_op jit(solution)/shard_map/reduce_scatter | solution.py:412
  1658.2 748.1 %reduce-scatter.15.cloned.1.call-start = ((), (), s32[]{:S(2)}) async-start(), calls=%async_computation.25 | async-start | bytes 17301504 | tf_op jit(solution)/shard_map/reduce_scatter | solution.py:404
  1691.0 902.4 %reduce-scatter.13.cloned.1.call-start = ((), (), s32[]{:S(2)}) async-start(), calls=%async_computation.24 | async-start | bytes 17301504 | tf_op jit(solution)/shard_map/reduce_scatter | solution.py:403
  1712.9 1067.9 %reduce-scatter.17.cloned.1.call-start = ((), (), s32[]{:S(2)}) async-start(), calls=%async_computation.26 | async-start | bytes 17301504 | tf_op jit(solution)/shard_map/reduce_scatter | solution.py:405
  1780.7 20.2 copy-start.64
  1780.7 95.2 %copy-start.31 = (bf16[256,2048]{1,0:T(8,128)(2,1)S(1)}, bf16[256,2048]{1,0:T(8,128)(2,1)}, u32[]{:S(2)}) copy-start(bf16[256,2048]{1,0:T(8,128)(2,1)} %copy-done.30) | copy-start | bytes 3145732
  1801.0 153.7 %copy-start.29 = (bf16[256,2048]{1,0:T(8,128)(2,1)S(1)}, bf16[256,2048]{1,0:T(8,128)(2,1)}, u32[]{:S(2)}) copy-start(bf16[256,2048]{1,0:T(8,128)(2,1)} %copy-done.28) | copy-start | bytes 3145732
  1962.3 79.5 %copy-start.63 = (f32[2048]{0:T(1024)S(1)}, f32[2048]{0:T(1024)}, u32[]{:S(2)}) copy-start(f32[2048]{0:T(1024)} %get-tuple-element.27) | copy-start | bytes 24580
  1962.3 128.1 %copy-start.16 = (f32[256,2048]{1,0:T(8,128)S(1)}, f32[256,2048]{1,0:T(8,128)}, u32[]{:S(2)}) copy-start(f32[256,2048]{1,0:T(8,128)} %get-tuple-element.64) | copy-start | bytes 6291460
  1962.3 128.1 %copy-start.80 = (f32[256]{0:T(256)S(1)}, f32[256]{0:T(256)}, u32[]{:S(2)}) copy-start(f32[256]{0:T(256)} %get-tuple-element.76) | copy-start | bytes 3076
  (46 other events, 180.6 us)
Sparse Core Ops, SparseCore 0:
  10.9 80.3 all-gather.13
  94.1 76.0 all-gather.19
  173.1 76.0 all-gather.15
  263.0 12.2 all-gather.17
  278.0 103.0 all-gather.21
  706.2 21.0 all-gather.23
  728.8 14.8 all-gather.25
  1130.9 195.0 all-gather.27
  1607.0 18.2 reduce-scatter.10
  1627.6 13.3 reduce-scatter.22
  1643.2 136.0 reduce-scatter.24
  1781.5 12.7 reduce-scatter.20
  1797.1 78.7 all-gather.29
  1878.6 76.0 all-gather.31
  1957.4 76.0 all-gather.33
  2036.2 182.2 reduce-scatter.18
  2221.2 184.9 reduce-scatter.14
  2409.0 184.4 reduce-scatter.12
  2596.3 184.3 reduce-scatter.16
where the time goes:
time: 2800 us; the launch traced here: 2790 us
  waiting for transfers between devices  1650 us (59%)
  blocking collectives  430 us (15%)
  matrix products  267 us (10%)
  starting transfers between devices  171 us (6%)
  other arithmetic  137 us (5%)
  local copies, waits for them, and re-layouts  118 us (4%)
    all_gather x1, blocking collectives, on_device(): lax.all_gather(late_params[8], ('expert', 'fsdp'), axis=0, tiled=True)  191 us
    reduce_scatter x1, waiting for transfers between devices, on_device(): lax.psum_scatter(key_local, ('expert', 'fsdp'), scatter_dimension=0, tile...  188 us
    reduce_scatter x1, waiting for transfers between devices, on_device(): lax.psum_scatter(value_local, ('expert', 'fsdp'), scatter_dimension=0, ti...  187 us
    reduce_scatter x1, waiting for transfers between devices, on_device(): lax.psum_scatter(query_local, ('expert', 'fsdp'), scatter_dimension=0, ti...  187 us
    all_gather x1, blocking collectives, on_device(): lax.all_gather(layer_params[8], ('expert', 'fsdp'), axis=0, tiled=True)  150 us
    all_to_all x1, waiting for transfers between devices, on_device(): lax.all_to_all(send_rows, 'expert', split_axis=0, concat_axis=0, tiled=True)  136 us
    all_to_all x1, waiting for transfers between devices, on_device(): lax.all_to_all(result.reshape(sources, items, model_width), 'expert', spl...  129 us
    reduce_scatter x1, waiting for transfers between devices, on_device(): lax.psum_scatter(output_local, ('expert', 'fsdp'), scatter_dimension=0, t...  125 us
  transfers between devices with their start and end apart: 25, of which 18 were waited for; matrix products, arithmetic and copies ran while one was open for 13% of the time, Pallas kernels for 0%

commit v1 on v0

v1 whole, which is shorter than its diff:
```python
import math

import jax
import jax.numpy as jnp
from jax import lax
from jax.experimental import pallas as pl
from jax.experimental.pallas import tpu as pltpu
from jax.sharding import PartitionSpec as P

HEAD = 128
EFF = 1024
TOPK = 8
PLANES = 4

epsilon = 1e-06
rope_base = 10000.0
masked = -1e30
bf16 = jnp.bfloat16
f32 = jnp.float32
score_scale = 1.0 / math.sqrt(HEAD)
VMEM_BYTES = 40 * 1024 * 1024


def swap(block, axis, mask):
    count = lax.axis_size(axis)
    return lax.ppermute(block, axis, [(i, i ^ mask) for i in range(count)])


def contract_rows(left, right, out=f32):
    return lax.dot_general(
        left, right, (((0,), (0,)), ((), ())), preferred_element_type=f32
    ).astype(out)


def contract_cols(left, right, out=f32):
    return lax.dot_general(
        left, right, (((1,), (1,)), ((), ())), preferred_element_type=f32
    ).astype(out)


def matmul(left, right):
    return jnp.dot(left, right, preferred_element_type=f32)


def rms_scale(values, gain):
    inverse = lax.rsqrt(jnp.mean(values * values, axis=-1, keepdims=True) + epsilon)
    return (values * inverse * gain, inverse)


def rms_back(values, inverse, gain, upstream):
    scaled = upstream * gain
    inner_sum = jnp.sum(scaled * values, axis=-1, keepdims=True)
    length_now = values.shape[-1]
    grad_values = inverse * scaled - values * (inverse * inverse * inverse) * (
        inner_sum / length_now
    )
    return (grad_values, upstream * values * inverse)


def rotary_tables(positions):
    half_width = HEAD // 2
    freq_steps = jnp.arange(half_width, dtype=f32)
    frequency = jnp.exp(freq_steps * (-2.0 * math.log(rope_base) / HEAD))
    angles = positions.astype(f32)[:, None] * frequency[None, :]
    cosine, sine = jnp.cos(angles), jnp.sin(angles)
    return jnp.stack(
        [
            jnp.concatenate([cosine, cosine], axis=-1),
            jnp.concatenate([-sine, sine], axis=-1),
        ]
    )


def unrope(upstream, cosine, sine):
    return upstream * cosine - pltpu.roll(upstream, HEAD // 2, 1) * sine


def normed_rope(values, gain, cosine, sine):
    normed, inverse = rms_scale(values, gain)
    turned = normed * cosine + pltpu.roll(normed, HEAD // 2, 1) * sine
    return turned.astype(bf16), inverse, normed


def attention_forward(query_raw, key_raw, value_low, tables, scales, live):
    queries, half = query_raw.shape
    span = key_raw.shape[0]
    heads = half // HEAD
    step = queries // 2

    def kernel(q_ref, k_ref, v_ref, table_ref, scale_ref, live_ref, out_ref, lse_ref):
        cosine, sine = table_ref[0], table_ref[1]
        key_low, _, _ = normed_rope(k_ref[...], scale_ref[1:2], cosine, sine)
        value_turned = v_ref[...].astype(f32).T.astype(bf16)
        live_now = jnp.concatenate([live_ref[...]] * (step // HEAD), axis=1) > 0.0
        for part in range(2):
            at = slice(part * step, (part + 1) * step)
            query_low, _, _ = normed_rope(q_ref[at], scale_ref[0:1], cosine[at], sine[at])
            scores = jnp.where(live_now, contract_cols(key_low, query_low), masked)
            peak = jnp.max(scores, axis=0, keepdims=True)
            exponent = jnp.exp((scores - peak) * score_scale)
            running = jnp.sum(exponent, axis=0, keepdims=True)
            turned = matmul(value_turned, exponent.astype(bf16)) / running
            out_ref[at] = turned.T.astype(bf16)
            lse_ref[0, :, at] = jnp.broadcast_to(
                peak * score_scale + jnp.log(running), (8, step)
            )

    column = lambda rows: pl.BlockSpec((rows, HEAD), lambda h: (0, h))
    return pl.pallas_call(
        kernel,
        grid=(heads,),
        in_specs=[
            column(queries),
            column(span),
            column(span),
            pl.BlockSpec((2, span, HEAD), lambda h: (0, 0, 0)),
            pl.BlockSpec((8, HEAD), lambda h: (0, 0)),
            pl.BlockSpec((span, HEAD), lambda h: (0, 0)),
        ],
        out_specs=[column(queries), pl.BlockSpec((1, 8, queries), lambda h: (h, 0, 0))],
        out_shape=[
            jax.ShapeDtypeStruct((queries, half), bf16),
            jax.ShapeDtypeStruct((heads, 8, queries), f32),
        ],
        compiler_params=pltpu.CompilerParams(vmem_limit_bytes=VMEM_BYTES),
        name="attention_forward",
    )(query_raw, key_raw, value_low, tables, scales, live)


def attention_backward(query_raw, key_raw, value_low, attended_grad, lse, tables, scales, live):
    queries, half = query_raw.shape
    span = key_raw.shape[0]
    heads = half // HEAD
    step = queries // 2

    def fold(terms):
        return jnp.sum(terms.reshape(-1, 8, HEAD), axis=0)

    def kernel(
        q_ref, k_ref, v_ref, grad_ref, lse_ref, table_ref, scale_ref, live_ref,
        dq_ref, dk_ref, dv_ref, gains_ref,
    ):
        cosine, sine = table_ref[0], table_ref[1]
        key_raw = k_ref[...]
        key_low, key_inverse, _ = normed_rope(key_raw, scale_ref[1:2], cosine, sine)
        key_turned = key_low.astype(f32).T.astype(bf16)
        live_now = jnp.concatenate([live_ref[...]] * (step // HEAD), axis=1) > 0.0
        key_grad = jnp.zeros((span, HEAD), f32)
        value_grad = jnp.zeros((span, HEAD), f32)
        query_gain = jnp.zeros((8, HEAD), f32)
        for part in range(2):
            at = slice(part * step, (part + 1) * step)
            query_raw = q_ref[at]
            query_low, query_inverse, _ = normed_rope(
                query_raw, scale_ref[0:1], cosine[at], sine[at]
            )
            upstream = grad_ref[at]
            scores = jnp.where(
                live_now, contract_cols(key_low, query_low) * score_scale, masked
            )
            probs = jnp.exp(scores - lse_ref[0, 0:1, at])
            probs_grad = contract_cols(v_ref[...], upstream)
            inner = jnp.sum(probs * probs_grad, axis=0, keepdims=True)
            score_grad = (probs * (probs_grad - inner)).astype(bf16)
            value_grad = value_grad + matmul(probs.astype(bf16), upstream)
            key_grad = key_grad + matmul(score_grad, query_low)
            query_grad = matmul(key_turned, score_grad).T * score_scale
            query_grad, terms = rms_back(
                query_raw,
                query_inverse,
                scale_ref[0:1],
                unrope(query_grad, cosine[at], sine[at]),
            )
            dq_ref[at] = query_grad.astype(bf16)
            query_gain = query_gain + fold(terms)
        dv_ref[...] = value_grad.astype(bf16)
        key_grad, terms = rms_back(
            key_raw, key_inverse, scale_ref[1:2], unrope(key_grad * score_scale, cosine, sine)
        )
        dk_ref[...] = key_grad.astype(bf16)
        gains = jnp.stack([query_gain, fold(terms)])

        @pl.when(pl.program_id(0) == 0)
        def _():
            gains_ref[...] = gains

        @pl.when(pl.program_id(0) > 0)
        def _():
            gains_ref[...] = gains_ref[...] + gains

    column = lambda rows: pl.BlockSpec((rows, HEAD), lambda h: (0, h))
    return pl.pallas_call(
        kernel,
        grid=(heads,),
        in_specs=[
            column(queries),
            column(span),
            column(span),
            column(queries),
            pl.BlockSpec((1, 8, queries), lambda h: (h, 0, 0)),
            pl.BlockSpec((2, span, HEAD), lambda h: (0, 0, 0)),
            pl.BlockSpec((8, HEAD), lambda h: (0, 0)),
            pl.BlockSpec((span, HEAD), lambda h: (0, 0)),
        ],
        out_specs=[
            column(queries),
            column(span),
            column(span),
            pl.BlockSpec((2, 8, HEAD), lambda h: (0, 0, 0)),
        ],
        out_shape=[
            jax.ShapeDtypeStruct((queries, half), bf16),
            jax.ShapeDtypeStruct((span, half), bf16),
            jax.ShapeDtypeStruct((span, half), bf16),
            jax.ShapeDtypeStruct((2, 8, HEAD), f32),
        ],
        compiler_params=pltpu.CompilerParams(vmem_limit_bytes=VMEM_BYTES),
        name="attention_backward",
    )(query_raw, key_raw, value_low, attended_grad, lse, tables, scales, live)


def in_order(flag, first, second, axis):
    return jnp.where(
        flag == 0,
        jnp.concatenate([first, second], axis=axis),
        jnp.concatenate([second, first], axis=axis),
    )


def pick(values, start, width, axis=1):
    return lax.dynamic_slice_in_dim(values, start, width, axis=axis)


def split_three(values):
    high = lax.reduce_precision(values, 8, 7)
    rest = values - high
    middle = lax.reduce_precision(rest, 8, 7)
    low = rest - middle
    return (high.astype(bf16), middle.astype(bf16), low.astype(bf16))


def on_device(
    hidden_in,
    prenorm_gain,
    query_weight,
    key_weight,
    value_weight,
    querynorm_gain,
    keynorm_gain,
    output_weight,
    postnorm_gain,
    router_weight,
    expert_inner,
    expert_outer,
    expert_ids,
    pair_order,
    sequence_lengths,
    cotangent,
):
    tokens, width = hidden_in.shape
    owners = lax.axis_size("expert")
    sharers = lax.axis_size("fsdp")
    devices = owners * sharers
    ring = owners // PLANES
    bits = ring.bit_length() - 1
    capacity = tokens * TOPK // owners
    half = width // 2
    owner = lax.axis_index("expert")
    core = lax.axis_index("fsdp")
    parity = owner % 2
    length = lax.dynamic_index_in_dim(sequence_lengths, owner // 2, 0, keepdims=False)

    plane = owner // ring

    def gather_owners(block):
        return lax.all_gather(block, "expert", axis=0, tiled=True)

    def bit_of(b):
        return (owner >> b) & 1

    def gather_planes(block):
        d1, d2, d3 = [swap(block, "expert", d * ring) for d in range(1, PLANES)]
        low, high = plane & 1, plane >> 1
        return in_order(high, in_order(low, block, d1, 0), in_order(low, d2, d3, 0), 0)

    def gather_plane(now, order):
        rows, columns = now.shape[0] // PLANES, now.shape[1]
        now = now.reshape((PLANES,) + (1,) * bits + (rows, columns))
        for b in order:
            now = in_order(bit_of(b), now, swap(now, "expert", 1 << b), bits - b)
        return now.reshape(owners * rows, columns)

    def scatter_steps(left, right, order):
        columns = right.shape[1]
        shape = [PLANES] + [2] * bits + [left.shape[1] // owners]
        axes = list(range(bits))[::-1]

        def halves(values, b, lead):
            at = lead + 1 + axes.index(b)
            return (
                lax.dynamic_index_in_dim(values, bit_of(b), at, keepdims=False),
                lax.dynamic_index_in_dim(values, 1 - bit_of(b), at, keepdims=False),
            )

        stay, go = halves(left.reshape([left.shape[0]] + shape), order[0], 1)
        sent = contract_rows(go.reshape(left.shape[0], -1), right, bf16)
        yield sent
        now = contract_rows(stay.reshape(left.shape[0], -1), right)
        now = now + swap(sent, "expert", 1 << order[0]).astype(f32)
        axes.remove(order[0])
        for b in order[1:]:
            now = now.reshape([PLANES] + [2] * len(axes) + [shape[-1], columns])
            kept, go = halves(now, b, 0)
            axes.remove(b)
            now = kept + swap(go.astype(bf16), "expert", 1 << b).astype(f32)
        now = now.reshape(PLANES, shape[-1], columns)
        total = lax.dynamic_index_in_dim(now, plane, 0, keepdims=False)
        for d in range(1, PLANES):
            sent = lax.dynamic_index_in_dim(now, plane ^ d, 0, keepdims=False)
            total = total + swap(sent.astype(bf16), "expert", d * ring).astype(f32)
        yield total

    descending = list(range(bits))[::-1]
    ascending = list(range(bits))

    def step_up(block, planes):
        return lax.ppermute(
            block, "expert", [(p * ring + i, (p + 1) * ring + i) for p in planes for i in range(ring)]
        )

    def step_down(block, planes):
        return lax.ppermute(
            block, "expert", [(p * ring + i, (p - 1) * ring + i) for p in planes for i in range(ring)]
        )

    rows_dev = width // devices
    small = jnp.concatenate(
        [
            prenorm_gain,
            postnorm_gain,
            querynorm_gain,
            keynorm_gain,
            router_weight.reshape(-1),
        ]
    )
    cut = [0]
    for piece in (prenorm_gain, postnorm_gain, querynorm_gain, keynorm_gain, router_weight):
        cut.append(cut[-1] + piece.size)
    lanes = 128
    small_rows = -(-cut[-1] // (lanes * 16)) * 16
    small = jnp.pad(small, (0, small_rows * lanes - cut[-1])).reshape(small_rows, lanes)
    small_pair = in_order(core, small, swap(small, "fsdp", 1), 0)
    small_all = gather_plane(gather_planes(small_pair), descending)
    small_all = small_all.reshape(devices, small_rows * lanes)
    first_gain = small_all[:, cut[0] : cut[1]].reshape(width).astype(f32)
    second_gain = small_all[:, cut[1] : cut[2]].reshape(width).astype(f32)
    query_scale = small_all[:, cut[2] : cut[3]].reshape(HEAD).astype(f32)
    key_scale = small_all[:, cut[3] : cut[4]].reshape(HEAD).astype(f32)
    router_full = small_all[:, cut[4] : cut[5]].reshape(width, owners)

    other_chip = swap(hidden_in, "expert", 1)
    hidden_own_peer = swap(hidden_in, "fsdp", 1)
    hidden_other_peer = swap(other_chip, "fsdp", 1)
    hidden_seq = jnp.concatenate(
        [hidden_in, hidden_own_peer, other_chip, hidden_other_peer], axis=0
    )

    stacked = jnp.stack([query_weight, key_weight, value_weight, output_weight])
    mine = pick(stacked, core * half, half, axis=2)
    theirs = swap(pick(stacked, (1 - core) * half, half, axis=2), "fsdp", 1)
    shards = in_order(core, mine, theirs, 1)
    query_own = gather_owners(shards[0])
    output_own = gather_owners(shards[3])
    key_first = gather_planes(shards[1])
    value_first = gather_planes(shards[2])

    inner_now = lax.all_gather(expert_inner, "fsdp", axis=1, tiled=True)[0]
    outer_now = lax.all_gather(expert_outer, "fsdp", axis=1, tiled=True)[0]
    extra_width = -(-3 * owners // 128) * 128
    inner_pad = jnp.pad(inner_now, ((0, extra_width), (0, 0)))

    span = 2 * sharers * tokens
    local = jnp.arange(tokens, dtype=jnp.int32)
    positions = jnp.concatenate(
        [
            ((parity ^ a) * sharers + (core ^ c)) * tokens + local
            for a in range(2)
            for c in range(2)
        ]
    )
    token_live = positions[:tokens] < length
    key_live = positions < length
    tables = rotary_tables(positions)
    live_lanes = jnp.broadcast_to(key_live.astype(f32)[:, None], (span, HEAD))
    scales = jnp.pad(jnp.stack([query_scale, key_scale]), ((0, 6), (0, 0)))
    expert_range = jnp.arange(owners, dtype=jnp.int32)
    hot = expert_ids[:, :, None] == expert_range[None, None, :]
    chosen = jnp.any(hot, axis=1)
    far = jnp.int32(1 << 30)
    order_of = jnp.sum(
        jnp.where(hot, pair_order.reshape(tokens, TOPK)[:, :, None], 0), axis=1
    )
    order_of = jnp.where(chosen & token_live[:, None], order_of, far)
    by_expert = order_of.T
    rank_of = jnp.sum(
        (by_expert[:, None, :] < by_expert[:, :, None]).astype(jnp.int32), axis=-1
    ).T
    rank_of = jnp.where(order_of == far, capacity, jnp.minimum(rank_of, capacity))
    kept = (rank_of < capacity).astype(f32)

    def widened(main, extra):
        pad = -extra.shape[1] % 128
        return jnp.concatenate([main, jnp.pad(extra, ((0, 0), (0, pad)))], axis=1)

    upstream_low = jnp.where(token_live[:, None], cotangent, jnp.zeros((), bf16))
    upstream = upstream_low.astype(f32)
    select = (expert_range[:, None] == (owner ^ jnp.arange(ring))[None, :]).astype(bf16)

    last = PLANES - 1

    def by_plane(*choices):
        out = choices[-1]
        for p in reversed(range(len(choices) - 1)):
            out = jnp.where(plane == p, choices[p], out)
        return out

    def planes_of(block):
        up1 = step_up(block, range(last))
        down1 = step_down(block, range(1, PLANES))
        up2 = step_up(up1, range(1, last))
        down2 = step_down(down1, range(1, last))
        up3 = step_up(up2, [2])
        down3 = step_down(down2, [1])
        return [
            block,
            jnp.where(plane == 0, down1, up1),
            by_plane(down2, down1, down1, up2),
            by_plane(down3, down2, up2, up3),
        ]

    def exchange(rows):
        return [rows[:capacity]] + [
            swap(rows[j * capacity : (j + 1) * capacity], "expert", j) for j in range(1, ring)
        ]

    up_wide = widened(upstream_low, rank_of.astype(bf16))
    up_wide, key_first, value_first = lax.optimization_barrier((up_wide, key_first, value_first))
    key_own = gather_plane(key_first, descending)
    value_own = gather_plane(value_first, ascending)
    output_peer = swap(output_own, "fsdp", 1)
    up_planes = planes_of(up_wide)
    up_planes, key_own, value_own = lax.optimization_barrier((up_planes, key_own, value_own))

    def exchange_all(blocks):
        got = [blocks]
        for j in range(1, ring):
            at = slice(j * capacity, (j + 1) * capacity)
            sent = jnp.concatenate([block[at] for block in blocks], axis=0)
            got.append(swap(sent, "expert", j))
        return [
            [blocks[d][:capacity]]
            + [got[j][d * capacity : (d + 1) * capacity] for j in range(1, ring)]
            for d in range(PLANES)
        ]

    pickers, up_picked = [], []
    for d in range(PLANES):
        rank_rel = matmul(up_planes[d][:, width : width + owners], select)
        hits = rank_rel[:, :, None] == jnp.arange(capacity, dtype=f32)[None, None, :]
        picker = hits.astype(bf16).reshape(tokens, ring * capacity)
        pickers.append(picker)
        up_picked.append(contract_rows(picker, up_planes[d][:, :width], bf16))
    up_rows = jnp.concatenate([p for parts in exchange_all(up_picked) for p in parts], axis=0)

    hidden_f = hidden_seq.astype(f32)
    first_normed, first_inverse = rms_scale(hidden_f, first_gain)
    first_low = first_normed.astype(bf16)
    key_raw = matmul(first_low, key_own)
    value_low = matmul(first_low, value_own).astype(bf16)
    query_raw = matmul(first_low[: 2 * tokens], query_own)
    attended, lse = attention_forward(
        query_raw, key_raw, value_low, tables, scales, live_lanes
    )
    attended_cross = swap(attended[tokens:], "fsdp", 1)
    attended_full = in_order(core, attended[:tokens], attended_cross, 1)
    attended_peer = swap(attended_full, "fsdp", 1)
    branch = in_order(
        core, matmul(attended_full, output_own), matmul(attended_full, output_peer), 1
    )
    residual = hidden_in.astype(f32) + branch
    second_normed, second_inverse = rms_scale(residual, second_gain)
    mixed_in = second_normed.astype(bf16)
    logits = matmul(mixed_in, router_full)
    shown = jnp.where(chosen, logits, masked)
    gate_exp = jnp.where(chosen, jnp.exp(shown - jnp.max(shown, axis=-1, keepdims=True)), 0.0)
    gate_soft = gate_exp / jnp.sum(gate_exp, axis=-1, keepdims=True)

    extra = jnp.concatenate(split_three(gate_soft * kept), axis=1)
    in_wide, up_rows = lax.optimization_barrier((widened(mixed_in, extra), up_rows))
    in_planes = planes_of(in_wide)
    column = jnp.arange(extra_width, dtype=jnp.int32)[None, :]
    own_column = (column % owners == owner) & (column < 3 * owners)
    plane_rows = ring * capacity

    hidden_up = contract_cols(up_rows, outer_now)
    row_inputs, hidden_gated, both_grad, rows_back = [], [], [], []
    for d in range(PLANES):
        rows = jnp.concatenate(exchange(contract_rows(pickers[d], in_planes[d], bf16)), axis=0)
        if d:
            rows, rows_back[-1] = lax.optimization_barrier((rows, rows_back[-1]))
        marks = rows[:, width:].astype(f32)
        row_gate = jnp.sum(jnp.where(own_column, marks, 0.0), axis=1, keepdims=True)
        gate_up = matmul(rows, inner_pad)
        up_back = hidden_up[d * plane_rows : (d + 1) * plane_rows]
        gate_part = gate_up[:, :EFF]
        up_part = gate_up[:, EFF:]
        gate_sigmoid = jax.nn.sigmoid(gate_part)
        activated = gate_part * gate_sigmoid
        hidden_rows = activated * up_part
        gated = (hidden_rows * row_gate).astype(bf16)
        row_gate_grad = jnp.sum(hidden_rows * up_back, axis=1, keepdims=True)
        hidden_grad = up_back * row_gate
        grads = jnp.concatenate(
            [
                hidden_grad * up_part * gate_sigmoid * (1.0 + gate_part * (1.0 - gate_sigmoid)),
                hidden_grad * activated,
            ],
            axis=-1,
        ).astype(bf16)
        part_of = jnp.concatenate(
            [jnp.broadcast_to(p, (p.shape[0], owners)) for p in split_three(row_gate_grad)],
            axis=1,
        )
        part_of = jnp.pad(part_of, ((0, 0), (0, extra_width - 3 * owners)))
        part_of = jnp.where(own_column, part_of, jnp.zeros((), bf16))
        rows_back.append(
            contract_cols(grads, inner_pad, bf16) + jnp.pad(part_of, ((0, 0), (width, 0)))
        )
        row_inputs.append(rows[:, :width])
        hidden_gated.append(gated)
        both_grad.append(grads)
    rows_back, row_inputs, hidden_gated, both_grad = lax.optimization_barrier(
        (rows_back, row_inputs, hidden_gated, both_grad)
    )
    rows_out = [matmul(gated, outer_now).astype(bf16) for gated in hidden_gated]
    row_inputs = jnp.concatenate(row_inputs, axis=0)
    hidden_gated = jnp.concatenate(hidden_gated, axis=0)
    both_grad = jnp.concatenate(both_grad, axis=0)

    def bring_back(arrived):
        parts = [None] * PLANES
        for d in reversed(range(PLANES)):
            parts[d] = matmul(pickers[d], jnp.concatenate(arrived[d], axis=0))
        near, middle, far_off = parts[1:]
        end = (plane == 0) | (plane == last)
        send = far_off.astype(bf16)
        up = step_up(send, [0]).astype(f32)
        down = step_down(send, [last]).astype(f32)
        send = jnp.where(end, middle, far_off + up + down).astype(bf16)
        up = step_up(send, [0, 1]).astype(f32)
        down = step_down(send, [2, 3]).astype(f32)
        up = step_up(jnp.where(plane == 0, near, middle + up).astype(bf16), [0, 1, 2])
        down = step_down((near + down).astype(bf16), [1, 2, 3])
        return parts[0] + up.astype(f32) + down.astype(f32)

    eff_half = EFF // 2
    inner_sent = contract_rows(pick(row_inputs, (1 - core) * half, half), both_grad, bf16)
    inner_kept = contract_rows(pick(row_inputs, core * half, half), both_grad)
    outer_sent = contract_rows(
        pick(hidden_gated, (1 - core) * eff_half, eff_half), up_rows, bf16
    )
    outer_kept = contract_rows(pick(hidden_gated, core * eff_half, eff_half), up_rows)
    back = bring_back([exchange(rows) for rows in rows_back])
    back, rows_out, inner_sent, inner_kept, outer_sent, outer_kept = lax.optimization_barrier(
        (back, rows_out, inner_sent, inner_kept, outer_sent, outer_kept)
    )
    inner_grad = inner_kept + swap(inner_sent, "fsdp", 1).astype(f32)
    outer_grad = outer_kept + swap(outer_sent, "fsdp", 1).astype(f32)
    out_arrived = exchange_all(rows_out)
    mixed_grad = back[:, :width]
    gate_grad = (
        back[:, width : width + owners]
        + back[:, width + owners : width + 2 * owners]
        + back[:, width + 2 * owners : width + 3 * owners]
    )

    soft_grad = gate_soft * (gate_grad - jnp.sum(gate_soft * gate_grad, axis=-1, keepdims=True))
    logit_grad = soft_grad.astype(bf16)
    router_local = contract_rows(mixed_in, logit_grad)
    mixed_grad = mixed_grad + contract_cols(logit_grad, router_full)
    residual_part, second_terms = rms_back(residual, second_inverse, second_gain, mixed_grad)
    residual_grad = upstream + residual_part
    branch_low = residual_grad.astype(bf16)
    branch_mine = pick(branch_low, core * half, half)
    branch_theirs = pick(branch_low, (1 - core) * half, half)
    attended_grad = (
        contract_cols(branch_mine, output_own) + contract_cols(branch_theirs, output_peer)
    ).astype(bf16)
    grad_mine = pick(attended_grad, core * half, half)
    grad_cross = swap(pick(attended_grad, (1 - core) * half, half), "fsdp", 1)
    attended_grad = jnp.concatenate([grad_mine, grad_cross], axis=0)

    attended_both = jnp.concatenate([attended_full, attended_peer], axis=0)
    branch_both = jnp.concatenate([branch_mine, swap(branch_theirs, "fsdp", 1)], axis=0)
    output_local = contract_rows(attended_both, branch_both, bf16)

    attended_grad, output_local = lax.optimization_barrier((attended_grad, output_local))
    output_block = lax.psum_scatter(output_local, "expert", scatter_dimension=0, tiled=True)
    output_block = output_block.astype(f32)
    query_low_grad, key_low_grad, value_low_grad, gain_terms = attention_backward(
        query_raw, key_raw, value_low, attended_grad, lse, tables, scales, live_lanes
    )

    out_arrived, query_low_grad, key_low_grad, value_low_grad = lax.optimization_barrier(
        (out_arrived, query_low_grad, key_low_grad, value_low_grad)
    )
    value_steps = scatter_steps(first_low, value_low_grad, descending)
    key_steps = scatter_steps(first_low, key_low_grad, ascending)
    next(value_steps)
    next(key_steps)
    quarter = half // 2
    query_left = first_low[: 2 * tokens]
    query_x = scatter_steps(query_left, query_low_grad[:, :quarter], ascending)
    query_y = scatter_steps(query_left, query_low_grad[:, quarter:], descending)
    next(query_x)
    next(query_y)
    value_block, key_block = next(value_steps), next(key_steps)
    query_block = jnp.concatenate([next(query_x), next(query_y)], axis=1)
    layer_out = (residual + bring_back(out_arrived)).astype(bf16)

    kv_grad = contract_cols(key_low_grad, key_own) + contract_cols(value_low_grad, value_own)
    q_grad = contract_cols(query_low_grad, query_own)
    own_part = kv_grad[:tokens] + q_grad[:tokens]
    peer_part = kv_grad[tokens : 2 * tokens] + q_grad[tokens:]
    far_part = kv_grad[2 * tokens : 3 * tokens]
    far_peer = kv_grad[3 * tokens :]
    crossed = swap(jnp.concatenate([peer_part, far_peer], axis=0).astype(bf16), "fsdp", 1)
    own_part = own_part + crossed[:tokens].astype(f32)
    far_part = (far_part + crossed[tokens:].astype(f32)).astype(bf16)
    far_back = swap(far_part, "expert", 1)
    normed_grad = own_part + far_back.astype(f32)
    hidden_part, first_terms = rms_back(
        hidden_f[:tokens], first_inverse[:tokens], first_gain, normed_grad
    )
    input_grad = residual_grad + hidden_part

    small_grads = jnp.concatenate(
        [
            jnp.sum(first_terms, axis=0).reshape(devices, -1),
            jnp.sum(second_terms, axis=0).reshape(devices, -1),
            jnp.sum(gain_terms[0], axis=0).reshape(devices, -1),
            jnp.sum(gain_terms[1], axis=0).reshape(devices, -1),
            router_local.reshape(devices, -1),
        ],
        axis=1,
    )
    small_grads = jnp.pad(small_grads, ((0, 0), (0, small_rows * lanes - cut[-1])))
    now = small_grads.reshape([PLANES] + [2] * bits + [2, small_rows, lanes])
    at = bits + 1
    sent = lax.dynamic_index_in_dim(now, 1 - core, at, keepdims=False)
    now = lax.dynamic_index_in_dim(now, core, at, keepdims=False) + swap(sent, "fsdp", 1)
    for b in range(bits):
        at = bits - b
        sent = lax.dynamic_index_in_dim(now, 1 - bit_of(b), at, keepdims=False)
        now = lax.dynamic_index_in_dim(now, bit_of(b), at, keepdims=False) + swap(
            sent, "expert", 1 << b
        )
    small_sum = lax.dynamic_index_in_dim(now, plane, 0, keepdims=False)
    for d in range(1, PLANES):
        sent = lax.dynamic_index_in_dim(now, plane ^ d, 0, keepdims=False)
        small_sum = small_sum + swap(sent, "expert", d * ring)
    small_sum = small_sum.reshape(-1)

    def whole_rows(block):
        keep = pick(block, core * rows_dev, rows_dev, 0)
        cross = swap(pick(block, (1 - core) * rows_dev, rows_dev, 0), "fsdp", 1)
        return in_order(core, keep, cross, 1)

    weight_grads = [whole_rows(b) for b in (query_block, key_block, value_block, output_block)]
    return (
        layer_out,
        input_grad,
        small_sum[cut[0] : cut[1]],
        weight_grads[0],
        weight_grads[1],
        weight_grads[2],
        small_sum[cut[2] : cut[3]],
        small_sum[cut[3] : cut[4]],
        weight_grads[3],
        small_sum[cut[1] : cut[2]],
        small_sum[cut[4] : cut[5]].reshape(rows_dev, owners),
        inner_grad[None],
        outer_grad[None],
    )


def solution(mesh):
    both = ("expert", "fsdp")
    placed = (
        P(both, None),
        P(both),
        P(both, None),
        P(both, None),
        P(both, None),
        P(both),
        P(both),
        P(both, None),
        P(both),
        P(both, None),
        P("expert", "fsdp", None),
        P("expert", "fsdp", None),
        P(both, None),
        P(both, None),
        P(),
        P(both, None),
    )
    return jax.shard_map(
        on_device,
        mesh=mesh,
        in_specs=placed,
        out_specs=(
            P(both, None),
            P(both, None),
            P(both),
            P(both, None),
            P(both, None),
            P(both, None),
            P(both),
            P(both),
            P(both, None),
            P(both),
            P(both, None),
            P("expert", "fsdp", None),
            P("expert", "fsdp", None),
        ),
        check_vma=False,
    )
```

time: 2800 us -> 1200 us (0.43)
  waiting for transfers between devices: 1650 us -> 429 us
  blocking collectives: 430 us -> 0 us
  Pallas kernels: 0 us -> 63.9 us
  matrix products: 267 us -> 234 us
    reduce_scatter x7 -> x1, waiting for transfers between devices: 700 us -> 0.02 us  [on_device(): lax.psum_scatter(output_local, 'expert', scatter_dimension=0, tiled=True)]
    all_gather x11 -> x4, waiting for transfers between devices: 425 us -> 0.03 us  [the longest x1 0.02 us: on_device(): inner_now = lax.all_gather(expert_inner, 'fsdp', axis=1, tiled=True)[0]]
    all_to_all x4 -> x0, waiting for transfers between devices: 375 us -> none  [the longest x1 136 us: on_device(): lax.all_to_all(send_rows, 'expert', split_axis=0, concat_axis=0, tiled=True)]
    all_gather x2 -> x0, blocking collectives: 341 us -> none  [the longest x1 191 us: on_device(): lax.all_gather(late_params[8], ('expert', 'fsdp'), axis=0, tiled=True)]
    ppermute x2 -> x113, waiting for transfers between devices: 90.9 us -> 428 us  [the longest x89 332 us: swap(): return lax.ppermute(block, axis, [(i, i ^ mask) for i in range(count)])]
    ppermute x2 -> x113, starting transfers between devices: 49.9 us -> 174 us  [the longest x89 111 us: swap(): return lax.ppermute(block, axis, [(i, i ^ mask) for i in range(count)])]
    all_to_all x4 -> x0, starting transfers between devices: 120 us -> none  [the longest x1 38.5 us: on_device(): lax.all_to_all(input_rows_grad.reshape(owners, capacity, model_width), 'e...]
    unnamed x2 -> x0, blocking collectives: 88.8 us -> none
  transfers between devices with their start and end apart: 25 -> 118, of which waited for: 18 -> 45; matrix products, arithmetic and copies ran while one was open for 13% -> 33% of each run, Pallas kernels for 0% -> 5%
where the time goes in v1:
time: 1200 us; the launch traced here: 1190 us
  waiting for transfers between devices  429 us (36%)
  matrix products  234 us (20%)
  starting transfers between devices  174 us (14%)
  local copies, waits for them, and re-layouts  141 us (12%)
  other arithmetic  133 us (11%)
  Pallas kernels  63.9 us (5%)
  between operations  17 us (1%)
    ppermute x89, waiting for transfers between devices, swap(): return lax.ppermute(block, axis, [(i, i ^ mask) for i in range(count)])  332 us
    ppermute x89, starting transfers between devices, swap(): return lax.ppermute(block, axis, [(i, i ^ mask) for i in range(count)])  111 us
    dot_general x26, matrix products, matmul(): return jnp.dot(left, right, preferred_element_type=f32)  80 us
    dot_general x22, matrix products, contract_rows(): lax.dot_general(left, right, (((0,), (0,)), ((), ())), preferred_element_...  77.2 us
    dot_general x11, matrix products, contract_cols(): lax.dot_general(left, right, (((1,), (1,)), ((), ())), preferred_element_...  76.9 us
    ppermute x12, waiting for transfers between devices, step_down(): lax.ppermute(block, 'expert', [(p * ring + i, (p - 1) * ring + i) for p i...  64.5 us
    unnamed x343, local copies, waits for them, and re-layouts  63.2 us
    ppermute x12, starting transfers between devices, step_up(): lax.ppermute(block, 'expert', [(p * ring + i, (p + 1) * ring + i) for p i...  47.5 us
  transfers between devices with their start and end apart: 118, of which 45 were waited for; matrix products, arithmetic and copies ran while one was open for 33% of the time, Pallas kernels for 5%

profile of v1, /device:TPU:0, one launch (start us, length us, event | category | flops | bytes accessed | tf_op | source)
XLA Modules:
  0.0 1193.3 jit_solution(7551411520355377041)
XLA Ops:
  37.8 5.7 collective-permute-done.12
  46.1 6.7 collective-permute-done.10
  54.0 16.6 %collective-permute-done.13 = bf16[128,1024]{1,0:T(8,128)(2,1)S(1)} collective-permute-done((bf16[128,1024]{1,0:T(8,128)(2,1)}, bf16[128,1024]{1,0:T(8,128)(2,1)S(1)}, u32[]{:S(2)}, u32[]{:S(2)}) %collective-permute-start.13) | collective-permute-done | bytes 262176 | tf_op jit(solution)/shard_map/ppermute | solution.py:26
  77.1 18.0 %collective-permute-done.14 = bf16[128,1024]{1,0:T(8,128)(2,1)S(1)} collective-permute-done((bf16[128,1024]{1,0:T(8,128)(2,1)}, bf16[128,1024]{1,0:T(8,128)(2,1)S(1)}, u32[]{:S(2)}, u32[]{:S(2)}) %collective-permute-start.14) | collective-permute-done | bytes 262176 | tf_op jit(solution)/shard_map/ppermute | solution.py:26
  107.5 5.6 collective-permute-start.17
  124.1 5.0 collective-permute-done.22
  158.7 6.3 constant_dynamic-slice_fusion.13
  167.6 13.3 %collective-permute-done.18 = bf16[256,2176]{1,0:T(8,128)(2,1)} collective-permute-done((bf16[256,2176]{1,0:T(8,128)(2,1)}, bf16[256,2176]{1,0:T(8,128)(2,1)}, u32[]{:S(2)}, u32[]{:S(2)}) %collective-permute-start.18) | collective-permute-done | bytes 1114144 | tf_op jit(solution)/shard_map/ppermute | solution.py:332
  183.5 5.1 maximum_convert_fusion
  194.2 5.4 maximum_select_fusion.1
  199.7 30.1 %collective-permute-done.20 = bf16[256,2176]{1,0:T(8,128)(2,1)S(1)} collective-permute-done((bf16[256,2176]{1,0:T(8,128)(2,1)}, bf16[256,2176]{1,0:T(8,128)(2,1)S(1)}, u32[]{:S(2)}, u32[]{:S(2)}) %collective-permute-start.20) | collective-permute-done | bytes 1114144 | tf_op jit(solution)/shard_map/ppermute | solution.py:332
  246.2 6.1 fusion.306.k_ref
  257.1 31.2 %collective-permute-done.28 = bf16[512,2048]{1,0:T(8,128)(2,1)S(1)} collective-permute-done((bf16[512,2048]{1,0:T(8,128)(2,1)S(1)}, bf16[512,2048]{1,0:T(8,128)(2,1)S(1)}, u32[]{:S(2)}, u32[]{:S(2)}) %collective-permute-start.28) | collective-permute-done | bytes 2097184 | tf_op jit(solution)/shard_map/ppermute | solution.py:26
  289.2 39.1 %collective-permute-done.29 = bf16[512,2048]{1,0:T(8,128)(2,1)S(1)} collective-permute-done((bf16[512,2048]{1,0:T(8,128)(2,1)S(1)}, bf16[512,2048]{1,0:T(8,128)(2,1)S(1)}, u32[]{:S(2)}, u32[]{:S(2)}) %collective-permute-start.29) | collective-permute-done | bytes 2097184 | tf_op jit(solution)/shard_map/ppermute | solution.py:26
  343.4 5.3 fusion.13.q_ref
  348.9 28.4 %attention_forward.1 = (bf16[512,1024]{1,0:T(8,128)(2,1)S(1)}, f32[8,8,512]{2,1,0:T(8,128)S(1)}) custom-call(f32[512,1024]{1,0:T(8,128)S(1)} %fusion.13.q_ref, f32[1024,1024]{1,0:T(8,128)S(1)} %copy-done, bf16[1024,1024]{1,0:T(8,128)(2,1)S(1)} %convolution_convert_fusion.16.v_ref, f32[2,1024,128]{2,1,0:T(8,128)S(1)} %pad_maximum_fusion.17.table_ref, ...), custom_call_target="tpu_custom_call" | custom-call | tf_op jit(solution)/shard_map/attention_forward/pallas_call | solution.py:109
  395.7 5.6 collective-permute-start.32
  408.4 14.8 %fusion.9 = f32[2048,1024]{0,1:T(8,128)} fusion(bf16[2048,2048]{1,0:T(8,128)(2,1)} %slice_dynamic-update-slice_fusion, bf16[1,1024,2048]{2,1,0:T(8,128)(2,1)} %all-gather.7.cloned.1.call-done), kind=kOutput, calls=%fused_computation.25 | convolution fusion | flops 8589934592 | bytes 20971520 | tf_op jit(solution)/shard_map/dot_general | solution.py:36
  423.2 8.9 collective-permute-done.37
  432.2 9.4 fusion.36
  442.6 5.2 multiply_convert_fusion.13
  455.3 9.9 fusion.19
  473.0 6.1 collective-permute-done.34
  479.4 8.4 fusion.33
  487.9 5.2 multiply_convert_fusion.11
  505.4 9.8 fusion.20
  519.8 7.6 collective-permute-done.42
  528.0 8.4 fusion.30
  536.5 5.2 multiply_convert_fusion.9
  550.7 9.8 fusion.21
  563.7 9.2 collective-permute-done.47
  573.7 8.6 fusion.27
  582.4 5.2 multiply_convert_fusion.7
  591.3 10.1 fusion.22
  616.6 14.1 %fusion.23 = bf16[1024,2048]{1,0:T(8,128)(2,1)} fusion(bf16[2048,2048]{0,1:T(8,128)(2,1)} %copy-done.107, bf16[2048,2048]{1,0:T(8,128)(2,1)} %constant_dynamic-update-slice_fusion, s32[]{:T(128)S(6)} %select_n.500), kind=kOutput, calls=%fused_computation.45 | convolution fusion | flops 8592031744 | bytes 16777220 | tf_op jit(solution)/shard_map/dot_general | solution.py:30
  630.6 13.5 %fusion.15 = f32[1024,2048]{1,0:T(8,128)} fusion(bf16[2048,2048]{0,1:T(8,128)(2,1)S(1)} %copy-done.108, bf16[2048,2048]{1,0:T(8,128)(2,1)} %constant_dynamic-update-slice_fusion, s32[]{:T(128)S(6)} %select_n.499), kind=kOutput, calls=%fused_computation.34 | convolution fusion | flops 8589934592 | bytes 20971524 | tf_op jit(solution)/shard_map/dot_general | solution.py:30
  652.4 6.1 fusion.142
  658.7 14.2 %collective-permute-done.60 = bf16[128,2176]{1,0:T(8,128)(2,1)S(1)} collective-permute-done((bf16[128,2176]{1,0:T(8,128)(2,1)S(1)}, bf16[128,2176]{1,0:T(8,128)(2,1)S(1)}, u32[]{:S(2)}, u32[]{:S(2)}) %collective-permute-start.60) | collective-permute-done | bytes 557088 | tf_op jit(solution)/shard_map/ppermute | solution.py:26
  674.0 21.1 %collective-permute-done.59 = bf16[128,2176]{1,0:T(8,128)(2,1)S(1)} collective-permute-done((bf16[128,2176]{1,0:T(8,128)(2,1)S(1)}, bf16[128,2176]{1,0:T(8,128)(2,1)S(1)}, u32[]{:S(2)}, u32[]{:S(2)}) %collective-permute-start.59) | collective-permute-done | bytes 557088 | tf_op jit(solution)/shard_map/ppermute | solution.py:26
  696.8 5.6 collective-permute-start.61
  702.4 5.9 convolution_convert_fusion.13
  713.0 13.3 %collective-permute-done.61 = bf16[256,2176]{1,0:T(8,128)(2,1)S(1)} collective-permute-done((bf16[256,2176]{1,0:T(8,128)(2,1)S(1)}, bf16[256,2176]{1,0:T(8,128)(2,1)S(1)}, u32[]{:S(2)}, u32[]{:S(2)}) %collective-permute-start.61) | collective-permute-done | bytes 1114144 | tf_op jit(solution)/shard_map/ppermute | solution.py:327
  744.0 14.7 %collective-permute-done.63 = bf16[256,2176]{1,0:T(8,128)(2,1)S(1)} collective-permute-done((bf16[256,2176]{1,0:T(8,128)(2,1)S(1)}, bf16[256,2176]{1,0:T(8,128)(2,1)S(1)}, u32[]{:S(2)}, u32[]{:S(2)}) %collective-permute-start.63) | collective-permute-done | bytes 1114144 | tf_op jit(solution)/shard_map/ppermute | solution.py:327
  759.1 4.9 collective-permute-start.64
  768.9 13.2 %collective-permute-done.66 = bf16[256,2176]{1,0:T(8,128)(2,1)S(1)} collective-permute-done((bf16[256,2176]{1,0:T(8,128)(2,1)S(1)}, bf16[256,2176]{1,0:T(8,128)(2,1)S(1)}, u32[]{:S(2)}, u32[]{:S(2)}) %collective-permute-start.66) | collective-permute-done | bytes 1114144 | tf_op jit(solution)/shard_map/ppermute | solution.py:332
  815.6 6.0 copy.231
  821.6 5.8 copy.230
  844.7 6.2 convolution_convert_fusion.8
  854.7 35.4 %attention_backward.1 = (bf16[512,1024]{1,0:T(8,128)(2,1)S(1)}, bf16[1024,1024]{1,0:T(8,128)(2,1)S(1)}, bf16[1024,1024]{1,0:T(8,128)(2,1)S(1)}, f32[2,8,128]{2,1,0:T(8,128)S(1)}) custom-call(f32[512,1024]{1,0:T(8,128)S(1)} %copy-done.2, f32[1024,1024]{1,0:T(8,128)} %fusion.306.k_ref, bf16[1024,1024]{1,0:T(8,128)(2,1)S(1)} %convolution_convert_fusion.16.v_ref, ...), custom_call_target="tpu_custom_call" | custom-call | tf_op jit(solution)/shard_map/attention_backward/pallas_call | solution.py:192
  906.7 5.5 collective-permute-start.73
  912.2 6.8 fusion.308
  919.0 7.4 convolution_add_fusion.1
  944.0 37.1 %collective-permute-done.87 = bf16[1024,512]{1,0:T(8,128)(2,1)S(1)} collective-permute-done((bf16[1024,512]{1,0:T(8,128)(2,1)S(1)}, bf16[1024,512]{1,0:T(8,128)(2,1)S(1)}, u32[]{:S(2)}, u32[]{:S(2)}) %collective-permute-start.87) | collective-permute-done | bytes 1048608 | tf_op jit(solution)/shard_map/ppermute | solution.py:26
  989.0 13.7 %collective-permute-done.88 = bf16[4,128,512]{2,1,0:T(8,128)(2,1)S(1)} collective-permute-done((bf16[4,128,512]{2,1,0:T(8,128)(2,1)S(1)}, bf16[4,128,512]{2,1,0:T(8,128)(2,1)S(1)}, u32[]{:S(2)}, u32[]{:S(2)}) %collective-permute-start.88) | collective-permute-done | bytes 524320 | tf_op jit(solution)/shard_map/ppermute | solution.py:26
  1005.0 13.3 %collective-permute-done.93 = bf16[4,128,512]{2,1,0:T(8,128)(2,1)S(1)} collective-permute-done((bf16[4,128,512]{2,1,0:T(8,128)(2,1)S(1)}, bf16[4,128,512]{2,1,0:T(8,128)(2,1)S(1)}, u32[]{:S(2)}, u32[]{:S(2)}) %collective-permute-start.93) | collective-permute-done | bytes 524320 | tf_op jit(solution)/shard_map/ppermute | solution.py:26
  1021.7 5.0 collective-permute-done.90
  1034.7 6.1 collective-permute-done.95
  1040.9 4.9 collective-permute-done.94
  1059.5 19.8 %collective-permute-done.98 = bf16[1024,1024]{1,0:T(8,128)(2,1)} collective-permute-done((bf16[1024,1024]{1,0:T(8,128)(2,1)S(1)}, bf16[1024,1024]{1,0:T(8,128)(2,1)}, u32[]{:S(2)}, u32[]{:S(2)}) %collective-permute-start.98) | collective-permute-done | bytes 2097184 | tf_op jit(solution)/shard_map/ppermute | solution.py:26
  1086.5 8.6 collective-permute-done.104
  1107.0 5.8 collective-permute-start.76
  1150.0 6.7 collective-permute-start.100
  1164.6 8.3 collective-permute-done.108
  1172.9 7.2 collective-permute-done.107
  (821 shorter events, 464.7 us)
Async XLA Ops:
  7.2 328.7 %all-gather.13.cloned.1.call-start = ((), (), s32[]{:S(2)}) async-start(), calls=%async_computation.5 | async-start | bytes 4456448 | tf_op jit(solution)/shard_map/all_gather | solution.py:276
  12.3 331.1 %all-gather.11.cloned.1.call-start = ((), (), s32[]{:S(2)}) async-start(), calls=%async_computation.4 | async-start | bytes 4456448 | tf_op jit(solution)/shard_map/all_gather | solution.py:276
  13.0 395.4 %all-gather.7.cloned.1.call-start = ((), (), s32[]{:S(2)}) async-start(), calls=%async_computation.1 | async-start | bytes 6291456 | tf_op jit(solution)/shard_map/all_gather | solution.py:378
  13.8 409.4 %all-gather.9.cloned.1.call-start = ((), (), s32[]{:S(2)}) async-start(), calls=%async_computation.2 | async-start | bytes 12582912 | tf_op jit(solution)/shard_map/all_gather | solution.py:377
  14.6 92.9 %collective-permute-start.1 = (bf16[256,2048]{1,0:T(8,128)(2,1)S(1)}, bf16[256,2048]{1,0:T(8,128)(2,1)S(1)}, u32[]{:S(2)}, u32[]{:S(2)}) collective-permute-start(bf16[256,2048]{1,0:T(8,128)(2,1)S(1)} %copy-done.14), channel_id=1, source_target_pairs={{0,2},{2,0},{4,6},{6,4},{8,10},{10,8},{12,14},{14,12},{16,18},{18,... | collective-permute-start | bytes 3145736 | tf_op jit(solution)/shard_map/ppermute | solution.py:26
  17.3 1164.1 %reduce-scatter.2.cloned.1.call-start = ((), (), s32[]{:S(2)}) async-start(), calls=%async_computation.3 | async-start | bytes 4456448 | tf_op jit(solution)/shard_map/reduce_scatter | solution.py:608
  35.2 35.4 %collective-permute-start.13 = (bf16[128,1024]{1,0:T(8,128)(2,1)}, bf16[128,1024]{1,0:T(8,128)(2,1)S(1)}, u32[]{:S(2)}, u32[]{:S(2)}) collective-permute-start(bf16[128,1024]{1,0:T(8,128)(2,1)} %get-tuple-element.346), channel_id=1, source_target_pairs={{0,8},{2,10},{4,12},{6,14},{8,0},{10,2},{12,4},{14,6},{16,24},{18,... | collective-permute-start | bytes 786440 | tf_op jit(solution)/shard_map/ppermute | solution.py:26
  36.8 34.9 %collective-permute-start.11 = (bf16[128,1024]{1,0:T(8,128)(2,1)}, bf16[128,1024]{1,0:T(8,128)(2,1)S(1)}, u32[]{:S(2)}, u32[]{:S(2)}) collective-permute-start(bf16[128,1024]{1,0:T(8,128)(2,1)} %get-tuple-element.347), channel_id=1, source_target_pairs={{0,16},{2,18},{4,20},{6,22},{8,24},{10,26},{12,28},{14,30},{16,0},... | collective-permute-start | bytes 786440 | tf_op jit(solution)/shard_map/ppermute | solution.py:26
  43.5 33.7 %collective-permute-start.15 = (bf16[128,1024]{1,0:T(8,128)(2,1)}, bf16[128,1024]{1,0:T(8,128)(2,1)S(1)}, u32[]{:S(2)}, u32[]{:S(2)}) collective-permute-start(bf16[128,1024]{1,0:T(8,128)(2,1)} %get-tuple-element.346), channel_id=1, source_target_pairs={{0,24},{2,26},{4,28},{6,30},{8,16},{10,18},{12,20},{14,22},{16,8},... | collective-permute-start | bytes 786440 | tf_op jit(solution)/shard_map/ppermute | solution.py:26
  52.7 42.4 %collective-permute-start.14 = (bf16[128,1024]{1,0:T(8,128)(2,1)}, bf16[128,1024]{1,0:T(8,128)(2,1)S(1)}, u32[]{:S(2)}, u32[]{:S(2)}) collective-permute-start(bf16[128,1024]{1,0:T(8,128)(2,1)} %get-tuple-element.346), channel_id=1, source_target_pairs={{0,16},{2,18},{4,20},{6,22},{8,24},{10,26},{12,28},{14,30},{16,0},... | collective-permute-start | bytes 786440 | tf_op jit(solution)/shard_map/ppermute | solution.py:26
  70.5 44.0 %collective-permute-start = (bf16[256,2048]{1,0:T(8,128)(2,1)S(1)}, bf16[256,2048]{1,0:T(8,128)(2,1)}, u32[]{:S(2)}, u32[]{:S(2)}) collective-permute-start(bf16[256,2048]{1,0:T(8,128)(2,1)S(1)} %copy-done.14), channel_id=1, source_target_pairs={{0,1},{1,0},{2,3},{3,2},{4,5},{5,4},{6,7},{7,6},{8,9},{9,8},{10,11... | collective-permute-start | bytes 3145736 | tf_op jit(solution)/shard_map/ppermute | solution.py:26
  71.7 28.1 %collective-permute-start.7 = (bf16[4,1,1,32,128]{4,3,2,1,0:T(8,128)(2,1)S(1)}, bf16[4,1,1,32,128]{4,3,2,1,0:T(8,128)(2,1)S(1)}, u32[]{:S(2)}, u32[]{:S(2)}) collective-permute-start(bf16[4,1,1,32,128]{4,3,2,1,0:T(8,128)(2,1)S(1)} %bitcast.305), channel_id=1, source_target_pairs={{0,4},{2,6},{4,0},{6,2},{8,12},{10,14},{12,8},{14,10},{16,20},{18,... | collective-permute-start | bytes 98312 | tf_op jit(solution)/shard_map/ppermute | solution.py:26
  98.2 30.9 %collective-permute-start.22 = (bf16[4,1,1,128,1024]{4,3,2,1,0:T(8,128)(2,1)}, bf16[4,1,1,128,1024]{4,3,2,1,0:T(8,128)(2,1)}, u32[]{:S(2)}, u32[]{:S(2)}) collective-permute-start(bf16[4,1,1,128,1024]{4,3,2,1,0:T(8,128)(2,1)} %bitcast.12), channel_id=1, source_target_pairs={{0,4},{2,6},{4,0},{6,2},{8,12},{10,14},{12,8},{14,10},{16,20},{18,... | collective-permute-start | bytes 3145736 | tf_op jit(solution)/shard_map/ppermute | solution.py:26
  99.9 34.6 %collective-permute-start.24 = (bf16[4,1,1,128,1024]{4,3,2,1,0:T(8,128)(2,1)}, bf16[4,1,1,128,1024]{4,3,2,1,0:T(8,128)(2,1)}, u32[]{:S(2)}, u32[]{:S(2)}) collective-permute-start(bf16[4,1,1,128,1024]{4,3,2,1,0:T(8,128)(2,1)} %bitcast.275), channel_id=1, source_target_pairs={{0,2},{2,0},{4,6},{6,4},{8,10},{10,8},{12,14},{14,12},{16,18},{18,... | collective-permute-start | bytes 3145736 | tf_op jit(solution)/shard_map/ppermute | solution.py:26
  106.2 34.8 %collective-permute-start.16 = (bf16[256,2176]{1,0:T(8,128)(2,1)}, bf16[256,2176]{1,0:T(8,128)(2,1)}, u32[]{:S(2)}, u32[]{:S(2)}) collective-permute-start(bf16[256,2176]{1,0:T(8,128)(2,1)} %fusion.152), channel_id=1, source_target_pairs={{8,0},{10,2},{12,4},{14,6},{16,8},{18,10},{20,12},{22,14},{24,16},... | collective-permute-start | bytes 3342344 | tf_op jit(solution)/shard_map/ppermute | solution.py:332
  107.5 34.8 %collective-permute-start.17 = (bf16[256,2176]{1,0:T(8,128)(2,1)}, bf16[256,2176]{1,0:T(8,128)(2,1)}, u32[]{:S(2)}, u32[]{:S(2)}) collective-permute-start(bf16[256,2176]{1,0:T(8,128)(2,1)} %fusion.152), channel_id=1, source_target_pairs={{0,8},{2,10},{4,12},{6,14},{8,16},{10,18},{12,20},{14,22},{16,24},... | collective-permute-start | bytes 3342344 | tf_op jit(solution)/shard_map/ppermute | solution.py:327
  114.5 29.8 %collective-permute-start.2 = (bf16[256,2048]{1,0:T(8,128)(2,1)S(1)}, bf16[256,2048]{1,0:T(8,128)(2,1)}, u32[]{:S(2)}, u32[]{:S(2)}) collective-permute-start(bf16[256,2048]{1,0:T(8,128)(2,1)S(1)} %collective-permute-done.1), channel_id=1, source_target_pairs={{0,1},{1,0},{2,3},{3,2},{4,5},{5,4},{6,7},{7,6},{8,9},{9,8},{10,11... | collective-permute-start | bytes 3145736 | tf_op jit(solution)/shard_map/ppermute | solution.py:26
  133.1 56.9 %collective-permute-start.23 = (bf16[4,2,1,128,1024]{4,3,2,1,0:T(8,128)(2,1)}, bf16[4,2,1,128,1024]{4,3,2,1,0:T(8,128)(2,1)}, u32[]{:S(2)}, u32[]{:S(2)}) collective-permute-start(bf16[4,2,1,128,1024]{4,3,2,1,0:T(8,128)(2,1)} %maximum_select_fusion.2), channel_id=1, source_target_pairs={{0,2},{2,0},{4,6},{6,4},{8,10},{10,8},{12,14},{14,12},{16,18},{18,... | collective-permute-start | bytes 6291464 | tf_op jit(solution)/shard_map/ppermute | solution.py:26
  137.8 56.5 %collective-permute-start.25 = (bf16[4,1,2,128,1024]{4,3,2,1,0:T(8,128)(2,1)}, bf16[4,1,2,128,1024]{4,3,2,1,0:T(8,128)(2,1)}, u32[]{:S(2)}, u32[]{:S(2)}) collective-permute-start(bf16[4,1,2,128,1024]{4,3,2,1,0:T(8,128)(2,1)} %maximum_select_fusion.3), channel_id=1, source_target_pairs={{0,4},{2,6},{4,0},{6,2},{8,12},{10,14},{12,8},{14,10},{16,20},{18,... | collective-permute-start | bytes 6291464 | tf_op jit(solution)/shard_map/ppermute | solution.py:26
  141.1 39.8 %collective-permute-start.18 = (bf16[256,2176]{1,0:T(8,128)(2,1)}, bf16[256,2176]{1,0:T(8,128)(2,1)}, u32[]{:S(2)}, u32[]{:S(2)}) collective-permute-start(bf16[256,2176]{1,0:T(8,128)(2,1)} %collective-permute-done.16), channel_id=1, source_target_pairs={{8,0},{10,2},{12,4},{14,6},{16,8},{18,10},{20,12},{22,14},{9,1},{1... | collective-permute-start | bytes 3342344 | tf_op jit(solution)/shard_map/ppermute | solution.py:332
  142.4 39.8 %collective-permute-start.19 = (bf16[256,2176]{1,0:T(8,128)(2,1)}, bf16[256,2176]{1,0:T(8,128)(2,1)}, u32[]{:S(2)}, u32[]{:S(2)}) collective-permute-start(bf16[256,2176]{1,0:T(8,128)(2,1)} %collective-permute-done.17), channel_id=1, source_target_pairs={{8,16},{10,18},{12,20},{14,22},{16,24},{18,26},{20,28},{22,30},{9,... | collective-permute-start | bytes 3342344 | tf_op jit(solution)/shard_map/ppermute | solution.py:327
  180.9 48.9 %collective-permute-start.20 = (bf16[256,2176]{1,0:T(8,128)(2,1)}, bf16[256,2176]{1,0:T(8,128)(2,1)S(1)}, u32[]{:S(2)}, u32[]{:S(2)}) collective-permute-start(bf16[256,2176]{1,0:T(8,128)(2,1)} %collective-permute-done.18), channel_id=1, source_target_pairs={{8,0},{10,2},{12,4},{14,6},{9,1},{11,3},{13,5},{15,7}} | collective-permute-start | bytes 3342344 | tf_op jit(solution)/shard_map/ppermute | solution.py:332
  182.2 47.6 %collective-permute-start.21 = (bf16[256,2176]{1,0:T(8,128)(2,1)}, bf16[256,2176]{1,0:T(8,128)(2,1)S(1)}, u32[]{:S(2)}, u32[]{:S(2)}) collective-permute-start(bf16[256,2176]{1,0:T(8,128)(2,1)} %collective-permute-done.19), channel_id=1, source_target_pairs={{16,24},{18,26},{20,28},{22,30},{17,25},{19,27},{21,29},{23,31}} | collective-permute-start | bytes 3342344 | tf_op jit(solution)/shard_map/ppermute | solution.py:327
  239.7 48.6 %collective-permute-start.28 = (bf16[512,2048]{1,0:T(8,128)(2,1)S(1)}, bf16[512,2048]{1,0:T(8,128)(2,1)S(1)}, u32[]{:S(2)}, u32[]{:S(2)}) collective-permute-start(bf16[512,2048]{1,0:T(8,128)(2,1)S(1)} %pad_maximum_fusion.4), channel_id=1, source_target_pairs={{0,2},{2,0},{4,6},{6,4},{8,10},{10,8},{12,14},{14,12},{16,18},{18,... | collective-permute-start | bytes 6291464 | tf_op jit(solution)/shard_map/ppermute | solution.py:26
  241.6 86.8 %collective-permute-start.29 = (bf16[512,2048]{1,0:T(8,128)(2,1)S(1)}, bf16[512,2048]{1,0:T(8,128)(2,1)S(1)}, u32[]{:S(2)}, u32[]{:S(2)}) collective-permute-start(bf16[512,2048]{1,0:T(8,128)(2,1)S(1)} %pad_maximum_fusion.5), channel_id=1, source_target_pairs={{0,4},{2,6},{4,0},{6,2},{8,12},{10,14},{12,8},{14,10},{16,20},{18,... | collective-permute-start | bytes 6291464 | tf_op jit(solution)/shard_map/ppermute | solution.py:26
  244.7 85.2 %collective-permute-start.30 = (bf16[512,2048]{1,0:T(8,128)(2,1)S(1)}, bf16[512,2048]{1,0:T(8,128)(2,1)S(1)}, u32[]{:S(2)}, u32[]{:S(2)}) collective-permute-start(bf16[512,2048]{1,0:T(8,128)(2,1)S(1)} %pad_maximum_fusion.6), channel_id=1, source_target_pairs={{0,6},{2,4},{4,2},{6,0},{8,14},{10,12},{12,10},{14,8},{16,22},{18,... | collective-permute-start | bytes 6291464 | tf_op jit(solution)/shard_map/ppermute | solution.py:26
  335.9 50.1 %collective-permute-start.27 = (bf16[2048,1024]{1,0:T(8,128)(2,1)}, bf16[2048,1024]{1,0:T(8,128)(2,1)}, u32[]{:S(2)}, u32[]{:S(2)}) collective-permute-start(bf16[2048,1024]{1,0:T(8,128)(2,1)} %bitcast.319), channel_id=1, source_target_pairs={{0,1},{1,0},{2,3},{3,2},{4,5},{5,4},{6,7},{7,6},{8,9},{9,8},{10,11... | collective-permute-start | bytes 12582920 | tf_op jit(solution)/shard_map/ppermute | solution.py:26
  394.4 55.0 %collective-permute-start.31 = (bf16[256,2176]{1,0:T(8,128)(2,1)}, bf16[256,2176]{1,0:T(8,128)(2,1)}, u32[]{:S(2)}, u32[]{:S(2)}) collective-permute-start(bf16[256,2176]{1,0:T(8,128)(2,1)} %pad_maximum_fusion.15), channel_id=1, source_target_pairs={{8,0},{10,2},{12,4},{14,6},{16,8},{18,10},{20,12},{22,14},{24,16},... | collective-permute-start | bytes 3342344 | tf_op jit(solution)/shard_map/ppermute | solution.py:332
  395.7 53.7 %collective-permute-start.32 = (bf16[256,2176]{1,0:T(8,128)(2,1)}, bf16[256,2176]{1,0:T(8,128)(2,1)}, u32[]{:S(2)}, u32[]{:S(2)}) collective-permute-start(bf16[256,2176]{1,0:T(8,128)(2,1)} %pad_maximum_fusion.15), channel_id=1, source_target_pairs={{0,8},{2,10},{4,12},{6,14},{8,16},{10,18},{12,20},{14,22},{16,24},... | collective-permute-start | bytes 3342344 | tf_op jit(solution)/shard_map/ppermute | solution.py:327
  469.6 29.2 %collective-permute-start.39 = (bf16[256,2176]{1,0:T(8,128)(2,1)}, bf16[256,2176]{1,0:T(8,128)(2,1)}, u32[]{:S(2)}, u32[]{:S(2)}) collective-permute-start(bf16[256,2176]{1,0:T(8,128)(2,1)} %collective-permute-done.31), channel_id=1, source_target_pairs={{8,0},{10,2},{12,4},{14,6},{16,8},{18,10},{20,12},{22,14},{9,1},{1... | collective-permute-start | bytes 3342344 | tf_op jit(solution)/shard_map/ppermute | solution.py:332
  644.4 64.2 %collective-permute-start.57 = (bf16[128,2176]{1,0:T(8,128)(2,1)S(1)}, bf16[128,2176]{1,0:T(8,128)(2,1)S(1)}, u32[]{:S(2)}, u32[]{:S(2)}) collective-permute-start(bf16[128,2176]{1,0:T(8,128)(2,1)S(1)} %get-tuple-element.254), channel_id=1, source_target_pairs={{0,6},{2,4},{4,2},{6,0},{8,14},{10,12},{12,10},{14,8},{16,22},{18,... | collective-permute-start | bytes 1671176 | tf_op jit(solution)/shard_map/ppermute | solution.py:26
  645.7 64.3 %collective-permute-start.56 = (bf16[128,2176]{1,0:T(8,128)(2,1)S(1)}, bf16[128,2176]{1,0:T(8,128)(2,1)S(1)}, u32[]{:S(2)}, u32[]{:S(2)}) collective-permute-start(bf16[128,2176]{1,0:T(8,128)(2,1)S(1)} %get-tuple-element.255), channel_id=1, source_target_pairs={{0,4},{2,6},{4,0},{6,2},{8,12},{10,14},{12,8},{14,10},{16,20},{18,... | collective-permute-start | bytes 1671176 | tf_op jit(solution)/shard_map/ppermute | solution.py:26
  649.0 46.1 %collective-permute-start.59 = (bf16[128,2176]{1,0:T(8,128)(2,1)S(1)}, bf16[128,2176]{1,0:T(8,128)(2,1)S(1)}, u32[]{:S(2)}, u32[]{:S(2)}) collective-permute-start(bf16[128,2176]{1,0:T(8,128)(2,1)S(1)} %get-tuple-element.251), channel_id=1, source_target_pairs={{0,4},{2,6},{4,0},{6,2},{8,12},{10,14},{12,8},{14,10},{16,20},{18,... | collective-permute-start | bytes 1671176 | tf_op jit(solution)/shard_map/ppermute | solution.py:26
  649.6 45.5 %collective-permute-start.58 = (bf16[128,2176]{1,0:T(8,128)(2,1)S(1)}, bf16[128,2176]{1,0:T(8,128)(2,1)S(1)}, u32[]{:S(2)}, u32[]{:S(2)}) collective-permute-start(bf16[128,2176]{1,0:T(8,128)(2,1)S(1)} %get-tuple-element.252), channel_id=1, source_target_pairs={{0,2},{2,0},{4,6},{6,4},{8,10},{10,8},{12,14},{14,12},{16,18},{18,... | collective-permute-start | bytes 1671176 | tf_op jit(solution)/shard_map/ppermute | solution.py:26
  672.9 39.0 %collective-permute-start.55 = (bf16[128,2176]{1,0:T(8,128)(2,1)S(1)}, bf16[128,2176]{1,0:T(8,128)(2,1)S(1)}, u32[]{:S(2)}, u32[]{:S(2)}) collective-permute-start(bf16[128,2176]{1,0:T(8,128)(2,1)S(1)} %get-tuple-element.256), channel_id=1, source_target_pairs={{0,2},{2,0},{4,6},{6,4},{8,10},{10,8},{12,14},{14,12},{16,18},{18,... | collective-permute-start | bytes 1671176 | tf_op jit(solution)/shard_map/ppermute | solution.py:26
  696.8 29.6 %collective-permute-start.61 = (bf16[256,2176]{1,0:T(8,128)(2,1)S(1)}, bf16[256,2176]{1,0:T(8,128)(2,1)S(1)}, u32[]{:S(2)}, u32[]{:S(2)}) collective-permute-start(bf16[256,2176]{1,0:T(8,128)(2,1)S(1)} %get-tuple-element.397), channel_id=1, source_target_pairs={{0,8},{2,10},{4,12},{6,14},{1,9},{3,11},{5,13},{7,15}} | collective-permute-start | bytes 3342344 | tf_op jit(solution)/shard_map/ppermute | solution.py:327
  708.6 29.5 %collective-permute-start.54 = (bf16[128,2176]{1,0:T(8,128)(2,1)S(1)}, bf16[128,2176]{1,0:T(8,128)(2,1)S(1)}, u32[]{:S(2)}, u32[]{:S(2)}) collective-permute-start(bf16[128,2176]{1,0:T(8,128)(2,1)S(1)} %get-tuple-element.258), channel_id=1, source_target_pairs={{0,6},{2,4},{4,2},{6,0},{8,14},{10,12},{12,10},{14,8},{16,22},{18,... | collective-permute-start | bytes 1671176 | tf_op jit(solution)/shard_map/ppermute | solution.py:26
  710.0 29.5 %collective-permute-start.53 = (bf16[128,2176]{1,0:T(8,128)(2,1)S(1)}, bf16[128,2176]{1,0:T(8,128)(2,1)S(1)}, u32[]{:S(2)}, u32[]{:S(2)}) collective-permute-start(bf16[128,2176]{1,0:T(8,128)(2,1)S(1)} %get-tuple-element.259), channel_id=1, source_target_pairs={{0,4},{2,6},{4,0},{6,2},{8,12},{10,14},{12,8},{14,10},{16,20},{18,... | collective-permute-start | bytes 1671176 | tf_op jit(solution)/shard_map/ppermute | solution.py:26
  711.9 29.5 %collective-permute-start.52 = (bf16[128,2176]{1,0:T(8,128)(2,1)S(1)}, bf16[128,2176]{1,0:T(8,128)(2,1)S(1)}, u32[]{:S(2)}, u32[]{:S(2)}) collective-permute-start(bf16[128,2176]{1,0:T(8,128)(2,1)S(1)} %get-tuple-element.260), channel_id=1, source_target_pairs={{0,2},{2,0},{4,6},{6,4},{8,10},{10,8},{12,14},{14,12},{16,18},{18,... | collective-permute-start | bytes 1671176 | tf_op jit(solution)/shard_map/ppermute | solution.py:26
  738.0 30.8 %collective-permute-start.51 = (bf16[128,2176]{1,0:T(8,128)(2,1)S(1)}, bf16[128,2176]{1,0:T(8,128)(2,1)S(1)}, u32[]{:S(2)}, u32[]{:S(2)}) collective-permute-start(bf16[128,2176]{1,0:T(8,128)(2,1)S(1)} %get-tuple-element.262), channel_id=1, source_target_pairs={{0,6},{2,4},{4,2},{6,0},{8,14},{10,12},{12,10},{14,8},{16,22},{18,... | collective-permute-start | bytes 1671176 | tf_op jit(solution)/shard_map/ppermute | solution.py:26
  739.4 29.4 %collective-permute-start.50 = (bf16[128,2176]{1,0:T(8,128)(2,1)S(1)}, bf16[128,2176]{1,0:T(8,128)(2,1)S(1)}, u32[]{:S(2)}, u32[]{:S(2)}) collective-permute-start(bf16[128,2176]{1,0:T(8,128)(2,1)S(1)} %get-tuple-element.263), channel_id=1, source_target_pairs={{0,4},{2,6},{4,0},{6,2},{8,12},{10,14},{12,8},{14,10},{16,20},{18,... | collective-permute-start | bytes 1671176 | tf_op jit(solution)/shard_map/ppermute | solution.py:26
  742.7 39.4 %collective-permute-start.66 = (bf16[256,2176]{1,0:T(8,128)(2,1)S(1)}, bf16[256,2176]{1,0:T(8,128)(2,1)S(1)}, u32[]{:S(2)}, u32[]{:S(2)}) collective-permute-start(bf16[256,2176]{1,0:T(8,128)(2,1)S(1)} %add_convert_fusion), channel_id=1, source_target_pairs={{8,0},{10,2},{12,4},{14,6},{16,8},{18,10},{20,12},{22,14},{24,16},... | collective-permute-start | bytes 3342344 | tf_op jit(solution)/shard_map/ppermute | solution.py:332
  792.3 101.7 %collective-permute-start.67 = (bf16[512,2048]{1,0:T(8,128)(2,1)}, bf16[512,2048]{1,0:T(8,128)(2,1)}, u32[]{:S(2)}, u32[]{:S(2)}) collective-permute-start(bf16[512,2048]{1,0:T(8,128)(2,1)} %pad_maximum_fusion.11), channel_id=1, source_target_pairs={{0,2},{2,0},{4,6},{6,4},{8,10},{10,8},{12,14},{14,12},{16,18},{18,... | collective-permute-start | bytes 6291464 | tf_op jit(solution)/shard_map/ppermute | solution.py:26
  795.8 100.9 %collective-permute-start.68 = (bf16[512,2048]{1,0:T(8,128)(2,1)}, bf16[512,2048]{1,0:T(8,128)(2,1)}, u32[]{:S(2)}, u32[]{:S(2)}) collective-permute-start(bf16[512,2048]{1,0:T(8,128)(2,1)} %pad_maximum_fusion.12), channel_id=1, source_target_pairs={{0,4},{2,6},{4,0},{6,2},{8,12},{10,14},{12,8},{14,10},{16,20},{18,... | collective-permute-start | bytes 6291464 | tf_op jit(solution)/shard_map/ppermute | solution.py:26
  809.3 34.9 %collective-permute-start.71 = (bf16[256,2048]{1,0:T(8,128)(2,1)}, bf16[256,2048]{1,0:T(8,128)(2,1)}, u32[]{:S(2)}, u32[]{:S(2)}) collective-permute-start(bf16[256,2048]{1,0:T(8,128)(2,1)} %maximum_select_fusion.8), channel_id=1, source_target_pairs={{0,1},{1,0},{2,3},{3,2},{4,5},{5,4},{6,7},{7,6},{8,9},{9,8},{10,11... | collective-permute-start | bytes 3145736 | tf_op jit(solution)/shard_map/ppermute | solution.py:26
  811.4 88.1 %collective-permute-start.69 = (bf16[512,2048]{1,0:T(8,128)(2,1)}, bf16[512,2048]{1,0:T(8,128)(2,1)}, u32[]{:S(2)}, u32[]{:S(2)}) collective-permute-start(bf16[512,2048]{1,0:T(8,128)(2,1)} %pad_maximum_fusion.13), channel_id=1, source_target_pairs={{0,6},{2,4},{4,2},{6,0},{8,14},{10,12},{12,10},{14,8},{16,22},{18,... | collective-permute-start | bytes 6291464 | tf_op jit(solution)/shard_map/ppermute | solution.py:26
  844.2 93.8 %collective-permute-start.112 = (bf16[512,2048]{1,0:T(8,128)(2,1)}, bf16[512,2048]{1,0:T(8,128)(2,1)}, u32[]{:S(2)}, u32[]{:S(2)}) collective-permute-start(bf16[512,2048]{1,0:T(8,128)(2,1)} %convolution_convert_fusion.13), channel_id=1, source_target_pairs={{0,1},{1,0},{2,3},{3,2},{4,5},{5,4},{6,7},{7,6},{8,9},{9,8},{10,11... | collective-permute-start | bytes 6291464 | tf_op jit(solution)/shard_map/ppermute | solution.py:26
  904.9 141.0 %collective-permute-start.74 = (bf16[256,2048]{1,0:T(8,128)(2,1)}, bf16[256,2048]{1,0:T(8,128)(2,1)}, u32[]{:S(2)}, u32[]{:S(2)}) collective-permute-start(bf16[256,2048]{1,0:T(8,128)(2,1)} %get-tuple-element.400), channel_id=1, source_target_pairs={{24,16},{26,18},{28,20},{30,22},{25,17},{27,19},{29,21},{31,23}} | collective-permute-start | bytes 3145736 | tf_op jit(solution)/shard_map/ppermute | solution.py:332
  906.7 142.1 %collective-permute-start.73 = (bf16[256,2048]{1,0:T(8,128)(2,1)}, bf16[256,2048]{1,0:T(8,128)(2,1)}, u32[]{:S(2)}, u32[]{:S(2)}) collective-permute-start(bf16[256,2048]{1,0:T(8,128)(2,1)} %get-tuple-element.400), channel_id=1, source_target_pairs={{0,8},{2,10},{4,12},{6,14},{1,9},{3,11},{5,13},{7,15}} | collective-permute-start | bytes 3145736 | tf_op jit(solution)/shard_map/ppermute | solution.py:327
  927.3 53.7 %collective-permute-start.87 = (bf16[1024,512]{1,0:T(8,128)(2,1)S(1)}, bf16[1024,512]{1,0:T(8,128)(2,1)S(1)}, u32[]{:S(2)}, u32[]{:S(2)}) collective-permute-start(bf16[1024,512]{1,0:T(8,128)(2,1)S(1)} %convolution_convert_fusion.18), channel_id=1, source_target_pairs={{0,2},{2,0},{4,6},{6,4},{8,10},{10,8},{12,14},{14,12},{16,18},{18,... | collective-permute-start | bytes 3145736 | tf_op jit(solution)/shard_map/ppermute | solution.py:26
  936.6 118.7 %collective-permute-start.79 = (bf16[512,2048]{1,0:T(8,128)(2,1)S(1)}, bf16[512,2048]{1,0:T(8,128)(2,1)S(1)}, u32[]{:S(2)}, u32[]{:S(2)}) collective-permute-start(bf16[512,2048]{1,0:T(8,128)(2,1)S(1)} %pad_maximum_fusion.14), channel_id=1, source_target_pairs={{0,1},{1,0},{2,3},{3,2},{4,5},{5,4},{6,7},{7,6},{8,9},{9,8},{10,11... | collective-permute-start | bytes 6291464 | tf_op jit(solution)/shard_map/ppermute | solution.py:26
  938.0 47.2 %collective-permute-start.92 = (bf16[1024,512]{1,0:T(8,128)(2,1)S(1)}, bf16[1024,512]{1,0:T(8,128)(2,1)S(1)}, u32[]{:S(2)}, u32[]{:S(2)}) collective-permute-start(bf16[1024,512]{1,0:T(8,128)(2,1)S(1)} %convolution_convert_fusion.17), channel_id=1, source_target_pairs={{0,4},{2,6},{4,0},{6,2},{8,12},{10,14},{12,8},{14,10},{16,20},{18,... | collective-permute-start | bytes 3145736 | tf_op jit(solution)/shard_map/ppermute | solution.py:26
  986.1 32.2 %collective-permute-start.93 = (bf16[4,128,512]{2,1,0:T(8,128)(2,1)S(1)}, bf16[4,128,512]{2,1,0:T(8,128)(2,1)S(1)}, u32[]{:S(2)}, u32[]{:S(2)}) collective-permute-start(bf16[4,128,512]{2,1,0:T(8,128)(2,1)S(1)} %fusion.174), channel_id=1, source_target_pairs={{0,2},{2,0},{4,6},{6,4},{8,10},{10,8},{12,14},{14,12},{16,18},{18,... | collective-permute-start | bytes 1572872 | tf_op jit(solution)/shard_map/ppermute | solution.py:26
  1031.0 48.3 %collective-permute-start.98 = (bf16[1024,1024]{1,0:T(8,128)(2,1)S(1)}, bf16[1024,1024]{1,0:T(8,128)(2,1)}, u32[]{:S(2)}, u32[]{:S(2)}) collective-permute-start(bf16[1024,1024]{1,0:T(8,128)(2,1)S(1)} %convolution_convert_fusion.15), channel_id=1, source_target_pairs={{0,2},{2,0},{4,6},{6,4},{8,10},{10,8},{12,14},{14,12},{16,18},{18,... | collective-permute-start | bytes 6291464 | tf_op jit(solution)/shard_map/ppermute | solution.py:26
  1045.8 61.2 %collective-permute-start.111 = (bf16[1024,2048]{1,0:T(8,128)(2,1)S(1)}, bf16[1024,2048]{1,0:T(8,128)(2,1)S(1)}, u32[]{:S(2)}, u32[]{:S(2)}) collective-permute-start(bf16[1024,2048]{1,0:T(8,128)(2,1)S(1)} %copy-done.150), channel_id=1, source_target_pairs={{0,1},{1,0},{2,3},{3,2},{4,5},{5,4},{6,7},{7,6},{8,9},{9,8},{10,11... | collective-permute-start | bytes 12582920 | tf_op jit(solution)/shard_map/ppermute | solution.py:26
  1045.9 49.2 %collective-permute-start.104 = (bf16[1024,1024]{1,0:T(8,128)(2,1)S(1)}, bf16[1024,1024]{1,0:T(8,128)(2,1)}, u32[]{:S(2)}, u32[]{:S(2)}) collective-permute-start(bf16[1024,1024]{1,0:T(8,128)(2,1)S(1)} %convolution_convert_fusion.14), channel_id=1, source_target_pairs={{0,4},{2,6},{4,0},{6,2},{8,12},{10,14},{12,8},{14,10},{16,20},{18,... | collective-permute-start | bytes 6291464 | tf_op jit(solution)/shard_map/ppermute | solution.py:26
  1053.3 49.0 %collective-permute-start.77 = (bf16[256,2048]{1,0:T(8,128)(2,1)S(1)}, bf16[256,2048]{1,0:T(8,128)(2,1)S(1)}, u32[]{:S(2)}, u32[]{:S(2)}) collective-permute-start(bf16[256,2048]{1,0:T(8,128)(2,1)S(1)} %get-tuple-element.402), channel_id=1, source_target_pairs={{16,8},{18,10},{20,12},{22,14},{24,16},{26,18},{28,20},{30,22},{17... | collective-permute-start | bytes 3145736 | tf_op jit(solution)/shard_map/ppermute | solution.py:332
  1055.3 48.9 %collective-permute-start.75 = (bf16[256,2048]{1,0:T(8,128)(2,1)S(1)}, bf16[256,2048]{1,0:T(8,128)(2,1)S(1)}, u32[]{:S(2)}, u32[]{:S(2)}) collective-permute-start(bf16[256,2048]{1,0:T(8,128)(2,1)S(1)} %get-tuple-element.402), channel_id=1, source_target_pairs={{0,8},{2,10},{4,12},{6,14},{8,16},{10,18},{12,20},{14,22},{1,9},{3... | collective-permute-start | bytes 3145736 | tf_op jit(solution)/shard_map/ppermute | solution.py:327
  1079.3 38.2 %collective-permute-start.80 = (bf16[256,2048]{1,0:T(8,128)(2,1)}, bf16[256,2048]{1,0:T(8,128)(2,1)S(1)}, u32[]{:S(2)}, u32[]{:S(2)}) collective-permute-start(bf16[256,2048]{1,0:T(8,128)(2,1)} %fusion.90), channel_id=1, source_target_pairs={{0,2},{2,0},{4,6},{6,4},{8,10},{10,8},{12,14},{14,12},{16,18},{18,... | collective-permute-start | bytes 3145736 | tf_op jit(solution)/shard_map/ppermute | solution.py:26
  1102.3 28.5 %collective-permute-start.105 = (bf16[4,128,1024]{2,1,0:T(8,128)(2,1)}, bf16[4,128,1024]{2,1,0:T(8,128)(2,1)}, u32[]{:S(2)}, u32[]{:S(2)}) collective-permute-start(bf16[4,128,1024]{2,1,0:T(8,128)(2,1)} %fusion.165), channel_id=1, source_target_pairs={{0,2},{2,0},{4,6},{6,4},{8,10},{10,8},{12,14},{14,12},{16,18},{18,... | collective-permute-start | bytes 3145736 | tf_op jit(solution)/shard_map/ppermute | solution.py:26
  1104.2 38.4 %collective-permute-start.78 = (bf16[256,2048]{1,0:T(8,128)(2,1)}, bf16[256,2048]{1,0:T(8,128)(2,1)}, u32[]{:S(2)}, u32[]{:S(2)}) collective-permute-start(bf16[256,2048]{1,0:T(8,128)(2,1)} %add_convert_fusion.1), channel_id=1, source_target_pairs={{8,0},{10,2},{12,4},{14,6},{16,8},{18,10},{20,12},{22,14},{24,16},... | collective-permute-start | bytes 3145736 | tf_op jit(solution)/shard_map/ppermute | solution.py:332
  1107.0 37.6 %collective-permute-start.76 = (bf16[256,2048]{1,0:T(8,128)(2,1)}, bf16[256,2048]{1,0:T(8,128)(2,1)}, u32[]{:S(2)}, u32[]{:S(2)}) collective-permute-start(bf16[256,2048]{1,0:T(8,128)(2,1)} %select_convert_fusion.2), channel_id=1, source_target_pairs={{0,8},{2,10},{4,12},{6,14},{8,16},{10,18},{12,20},{14,22},{16,24},... | collective-permute-start | bytes 3145736 | tf_op jit(solution)/shard_map/ppermute | solution.py:327
  1126.6 35.5 %collective-permute-start.102 = (bf16[128,1024]{1,0:T(8,128)(2,1)}, bf16[128,1024]{1,0:T(8,128)(2,1)}, u32[]{:S(2)}, u32[]{:S(2)}) collective-permute-start(bf16[128,1024]{1,0:T(8,128)(2,1)} %get-tuple-element.287), channel_id=1, source_target_pairs={{0,24},{2,26},{4,28},{6,30},{8,16},{10,18},{12,20},{14,22},{16,8},... | collective-permute-start | bytes 786440 | tf_op jit(solution)/shard_map/ppermute | solution.py:26
  1130.3 32.8 %collective-permute-start.101 = (bf16[128,1024]{1,0:T(8,128)(2,1)}, bf16[128,1024]{1,0:T(8,128)(2,1)}, u32[]{:S(2)}, u32[]{:S(2)}) collective-permute-start(bf16[128,1024]{1,0:T(8,128)(2,1)} %get-tuple-element.288), channel_id=1, source_target_pairs={{0,16},{2,18},{4,20},{6,22},{8,24},{10,26},{12,28},{14,30},{16,0},... | collective-permute-start | bytes 786440 | tf_op jit(solution)/shard_map/ppermute | solution.py:26
  (213 other events, 3393.3 us)
Sparse Core Ops, SparseCore 0:
  12.4 118.0 all-gather.12
  133.8 94.7 all-gather.10
  230.2 16.7 all-gather.6
  248.4 21.0 all-gather.8
  894.1 129.4 reduce-scatter.1

commit v2 on v1

--- a/solution.py
+++ b/solution.py
@@ -290,35 +290,40 @@
             now = in_order(bit_of(b), now, swap(now, "expert", 1 << b), bits - b)
         return now.reshape(owners * rows, columns)
 
-    def scatter_steps(left, right, order):
+    def split_columns(values, b):
+        each = values.shape[1] // owners
+
+        def side(bit):
+            return jnp.concatenate(
+                [
+                    pick(values, ((k << (b + 1)) + (bit << b)) * each, each << b)
+                    for k in range(owners >> (b + 1))
+                ],
+                axis=1,
+            )
+
+        return side(bit_of(b)), side(1 - bit_of(b))
+
+    def scatter_rest(stay, right, arrived, order):
         columns = right.shape[1]
-        shape = [PLANES] + [2] * bits + [left.shape[1] // owners]
-        axes = list(range(bits))[::-1]
-
-        def halves(values, b, lead):
-            at = lead + 1 + axes.index(b)
-            return (
-                lax.dynamic_index_in_dim(values, bit_of(b), at, keepdims=False),
-                lax.dynamic_index_in_dim(values, 1 - bit_of(b), at, keepdims=False),
-            )
-
-        stay, go = halves(left.reshape([left.shape[0]] + shape), order[0], 1)
-        sent = contract_rows(go.reshape(left.shape[0], -1), right, bf16)
-        yield sent
-        now = contract_rows(stay.reshape(left.shape[0], -1), right)
-        now = now + swap(sent, "expert", 1 << order[0]).astype(f32)
-        axes.remove(order[0])
+        now = contract_rows(stay, right) + arrived.astype(f32)
+        axes = [b for b in reversed(range(bits)) if b != order[0]]
+        rows = width // owners
         for b in order[1:]:
-            now = now.reshape([PLANES] + [2] * len(axes) + [shape[-1], columns])
-            kept, go = halves(now, b, 0)
+            now = now.reshape([PLANES] + [2] * len(axes) + [rows, columns])
+            at = 1 + axes.index(b)
+            kept = lax.dynamic_index_in_dim(now, bit_of(b), at, keepdims=False)
+            sent = lax.dynamic_index_in_dim(now, 1 - bit_of(b), at, keepdims=False)
             axes.remove(b)
-            now = kept + swap(go.astype(bf16), "expert", 1 << b).astype(f32)
-        now = now.reshape(PLANES, shape[-1], columns)
+            now = kept + swap(sent.astype(bf16), "expert", 1 << b).astype(f32)
+        return now.reshape(PLANES, rows, columns)
+
+    def scatter_planes(now):
         total = lax.dynamic_index_in_dim(now, plane, 0, keepdims=False)
         for d in range(1, PLANES):
             sent = lax.dynamic_index_in_dim(now, plane ^ d, 0, keepdims=False)
             total = total + swap(sent.astype(bf16), "expert", d * ring).astype(f32)
-        yield total
+        return total
 
     descending = list(range(bits))[::-1]
     ascending = list(range(bits))
@@ -449,7 +454,7 @@
     value_own = gather_plane(value_first, ascending)
     output_peer = swap(output_own, "fsdp", 1)
     up_planes = planes_of(up_wide)
-    up_planes, key_own, value_own = lax.optimization_barrier((up_planes, key_own, value_own))
+    up_planes, key_late, value_late = lax.optimization_barrier((up_planes, key_own, value_own))
 
     def exchange_all(blocks):
         got = [blocks]
@@ -470,7 +475,7 @@
         picker = hits.astype(bf16).reshape(tokens, ring * capacity)
         pickers.append(picker)
         up_picked.append(contract_rows(picker, up_planes[d][:, :width], bf16))
-    up_rows = jnp.concatenate([p for parts in exchange_all(up_picked) for p in parts], axis=0)
+    up_arrived = exchange_all(up_picked)
 
     hidden_f = hidden_seq.astype(f32)
     first_normed, first_inverse = rms_scale(hidden_f, first_gain)
@@ -481,6 +486,8 @@
     attended, lse = attention_forward(
         query_raw, key_raw, value_low, tables, scales, live_lanes
     )
+    left_x = split_columns(first_low, 0)
+    left_y = split_columns(first_low, bits - 1)
     attended_cross = swap(attended[tokens:], "fsdp", 1)
     attended_full = in_order(core, attended[:tokens], attended_cross, 1)
     attended_peer = swap(attended_full, "fsdp", 1)
@@ -496,8 +503,11 @@
     gate_soft = gate_exp / jnp.sum(gate_exp, axis=-1, keepdims=True)
 
     extra = jnp.concatenate(split_three(gate_soft * kept), axis=1)
-    in_wide, up_rows = lax.optimization_barrier((widened(mixed_in, extra), up_rows))
-    in_planes = planes_of(in_wide)
+    in_planes = planes_of(widened(mixed_in, extra))
+    up_arrived, mixed_late = lax.optimization_barrier((up_arrived, mixed_in))
+    up_rows = jnp.concatenate([p for parts in up_arrived for p in parts], axis=0)
+    picked = [contract_rows(pickers[d], in_planes[d], bf16) for d in range(PLANES)]
+    picked[0], up_rows = lax.optimization_barrier((picked[0], up_rows))
     column = jnp.arange(extra_width, dtype=jnp.int32)[None, :]
     own_column = (column % owners == owner) & (column < 3 * owners)
     plane_rows = ring * capacity
@@ -505,7 +515,12 @@
     hidden_up = contract_cols(up_rows, outer_now)
     row_inputs, hidden_gated, both_grad, rows_back = [], [], [], []
     for d in range(PLANES):
-        rows = jnp.concatenate(exchange(contract_rows(pickers[d], in_planes[d], bf16)), axis=0)
+        rows = exchange(picked[d])
+        if d < last:
+            rows, picked[d + 1] = lax.optimization_barrier((rows, picked[d + 1]))
+        if d == 0:
+            rows, left_x, left_y = lax.optimization_barrier((rows, left_x, left_y))
+        rows = jnp.concatenate(rows, axis=0)
         if d:
             rows, rows_back[-1] = lax.optimization_barrier((rows, rows_back[-1]))
         marks = rows[:, width:].astype(f32)
@@ -539,8 +554,14 @@
         row_inputs.append(rows[:, :width])
         hidden_gated.append(gated)
         both_grad.append(grads)
-    rows_back, row_inputs, hidden_gated, both_grad = lax.optimization_barrier(
-        (rows_back, row_inputs, hidden_gated, both_grad)
+    arrived = [None] * PLANES
+    for d in reversed(range(PLANES)):
+        block = rows_back[d]
+        if d < last:
+            block, arrived[d + 1] = lax.optimization_barrier((block, arrived[d + 1]))
+        arrived[d] = exchange(block)
+    arrived[last], row_inputs, hidden_gated, both_grad = lax.optimization_barrier(
+        (arrived[last], row_inputs, hidden_gated, both_grad)
     )
     rows_out = [matmul(gated, outer_now).astype(bf16) for gated in hidden_gated]
     row_inputs = jnp.concatenate(row_inputs, axis=0)
@@ -570,7 +591,7 @@
         pick(hidden_gated, (1 - core) * eff_half, eff_half), up_rows, bf16
     )
     outer_kept = contract_rows(pick(hidden_gated, core * eff_half, eff_half), up_rows)
-    back = bring_back([exchange(rows) for rows in rows_back])
+    back = bring_back(arrived)
     back, rows_out, inner_sent, inner_kept, outer_sent, outer_kept = lax.optimization_barrier(
         (back, rows_out, inner_sent, inner_kept, outer_sent, outer_kept)
     )
@@ -586,7 +607,7 @@
 
     soft_grad = gate_soft * (gate_grad - jnp.sum(gate_soft * gate_grad, axis=-1, keepdims=True))
     logit_grad = soft_grad.astype(bf16)
-    router_local = contract_rows(mixed_in, logit_grad)
+    router_local = contract_rows(mixed_late, logit_grad)
     mixed_grad = mixed_grad + contract_cols(logit_grad, router_full)
     residual_part, second_terms = rms_back(residual, second_inverse, second_gain, mixed_grad)
     residual_grad = upstream + residual_part
@@ -614,22 +635,47 @@
     out_arrived, query_low_grad, key_low_grad, value_low_grad = lax.optimization_barrier(
         (out_arrived, query_low_grad, key_low_grad, value_low_grad)
     )
-    value_steps = scatter_steps(first_low, value_low_grad, descending)
-    key_steps = scatter_steps(first_low, key_low_grad, ascending)
-    next(value_steps)
-    next(key_steps)
     quarter = half // 2
-    query_left = first_low[: 2 * tokens]
-    query_x = scatter_steps(query_left, query_low_grad[:, :quarter], ascending)
-    query_y = scatter_steps(query_left, query_low_grad[:, quarter:], descending)
-    next(query_x)
-    next(query_y)
-    value_block, key_block = next(value_steps), next(key_steps)
-    query_block = jnp.concatenate([next(query_x), next(query_y)], axis=1)
+    chip = 2 * tokens
+    sent = [
+        contract_rows(left_y[1], value_low_grad, bf16),
+        contract_rows(left_x[1], key_low_grad, bf16),
+    ]
+    sent, query_low_grad = lax.optimization_barrier((sent, query_low_grad))
+    sent += [
+        contract_rows(left_x[1][:chip], query_low_grad[:, :quarter], bf16),
+        contract_rows(left_y[1][:chip], query_low_grad[:, quarter:], bf16),
+    ]
+    sent, query_late, key_grad_late, value_grad_late = lax.optimization_barrier(
+        (sent, query_low_grad, key_low_grad, value_low_grad)
+    )
+    value_came = swap(sent[0], "expert", 1 << (bits - 1))
+    key_came = swap(sent[1], "expert", 1)
+    out_arrived, value_came, key_came = lax.optimization_barrier(
+        (out_arrived, value_came, key_came)
+    )
+    sent, value_came, key_came = lax.optimization_barrier((sent, value_came, key_came))
+    query_x_came = swap(sent[2], "expert", 1)
+    query_y_came = swap(sent[3], "expert", 1 << (bits - 1))
+    value_block = scatter_planes(scatter_rest(left_y[0], value_low_grad, value_came, descending))
+    key_block = scatter_planes(scatter_rest(left_x[0], key_low_grad, key_came, ascending))
+    query_block = scatter_planes(
+        jnp.concatenate(
+            [
+                scatter_rest(
+                    left_x[0][:chip], query_low_grad[:, :quarter], query_x_came, ascending
+                ),
+                scatter_rest(
+                    left_y[0][:chip], query_low_grad[:, quarter:], query_y_came, descending
+                ),
+            ],
+            axis=2,
+        )
+    )
     layer_out = (residual + bring_back(out_arrived)).astype(bf16)
 
-    kv_grad = contract_cols(key_low_grad, key_own) + contract_cols(value_low_grad, value_own)
-    q_grad = contract_cols(query_low_grad, query_own)
+    kv_grad = contract_cols(key_grad_late, key_late) + contract_cols(value_grad_late, value_late)
+    q_grad = contract_cols(query_late, query_own)
     own_part = kv_grad[:tokens] + q_grad[:tokens]
     peer_part = kv_grad[tokens : 2 * tokens] + q_grad[tokens:]
     far_part = kv_grad[2 * tokens : 3 * tokens]

time: 1200 us -> 1160 us (0.967)
  local copies, waits for them, and re-layouts: 141 us -> 97.4 us
  matrix products: 234 us -> 247 us
  waiting for transfers between devices: 429 us -> 417 us
    ppermute x12, waiting for transfers between devices: 64.5 us -> 95.4 us  [step_down(): lax.ppermute(block, 'expert', [(p * ring + i, (p - 1) * ring + i) for p i...]
    ppermute x12, waiting for transfers between devices: 31.7 us -> 3.94 us  [step_up(): lax.ppermute(block, 'expert', [(p * ring + i, (p + 1) * ring + i) for p i...]
    unnamed x343 -> x351, local copies, waits for them, and re-layouts: 63.2 us -> 39.2 us
    dynamic_slice x4 -> x0, local copies, waits for them, and re-layouts: 15.7 us -> none  [halves(): lax.dynamic_index_in_dim(values, bit_of(b), at, keepdims=False)]
    ppermute x89 -> x86, waiting for transfers between devices: 332 us -> 316 us  [swap(): return lax.ppermute(block, axis, [(i, i ^ mask) for i in range(count)])]
    ppermute x89 -> x86, starting transfers between devices: 111 us -> 119 us  [swap(): return lax.ppermute(block, axis, [(i, i ^ mask) for i in range(count)])]
  transfers between devices with their start and end apart: 118 -> 115, of which waited for: 45 -> 42; matrix products, arithmetic and copies ran while one was open for 33% -> 34% of each run, Pallas kernels for 5% -> 6%
where the time goes in v2:
time: 1160 us; the launch traced here: 1150 us
  waiting for transfers between devices  417 us (36%)
  matrix products  247 us (21%)
  starting transfers between devices  175 us (15%)
  other arithmetic  131 us (11%)
  local copies, waits for them, and re-layouts  97.4 us (8%)
  Pallas kernels  64 us (6%)
  between operations  17.2 us (1%)
    ppermute x86, waiting for transfers between devices, swap(): return lax.ppermute(block, axis, [(i, i ^ mask) for i in range(count)])  316 us
    ppermute x86, starting transfers between devices, swap(): return lax.ppermute(block, axis, [(i, i ^ mask) for i in range(count)])  119 us
    ppermute x12, waiting for transfers between devices, step_down(): lax.ppermute(block, 'expert', [(p * ring + i, (p - 1) * ring + i) for p i...  95.4 us
    dot_general x26, matrix products, matmul(): return jnp.dot(left, right, preferred_element_type=f32)  86.3 us
    dot_general x22, matrix products, contract_rows(): lax.dot_general(left, right, (((0,), (0,)), ((), ())), preferred_element_...  83.1 us
    dot_general x11, matrix products, contract_cols(): lax.dot_general(left, right, (((1,), (1,)), ((), ())), preferred_element_...  77.8 us
    ppermute x12, starting transfers between devices, step_up(): lax.ppermute(block, 'expert', [(p * ring + i, (p + 1) * ring + i) for p i...  40.2 us
    unnamed x351, local copies, waits for them, and re-layouts  39.2 us
  transfers between devices with their start and end apart: 115, of which 42 were waited for; matrix products, arithmetic and copies ran while one was open for 34% of the time, Pallas kernels for 6%

profile of v2, /device:TPU:0, one launch (start us, length us, event | category | flops | bytes accessed | tf_op | source)
XLA Modules:
  0.0 1148.0 jit_solution(7211101365153835220)
XLA Ops:
  39.4 15.7 %collective-permute-done.13 = bf16[128,1024]{1,0:T(8,128)(2,1)} collective-permute-done((bf16[128,1024]{1,0:T(8,128)(2,1)}, bf16[128,1024]{1,0:T(8,128)(2,1)}, u32[]{:S(2)}, u32[]{:S(2)}) %collective-permute-start.13) | collective-permute-done | bytes 262176 | tf_op jit(solution)/shard_map/ppermute | solution.py:26
  60.4 15.1 %collective-permute-done.11 = bf16[128,1024]{1,0:T(8,128)(2,1)} collective-permute-done((bf16[128,1024]{1,0:T(8,128)(2,1)}, bf16[128,1024]{1,0:T(8,128)(2,1)}, u32[]{:S(2)}, u32[]{:S(2)}) %collective-permute-start.11) | collective-permute-done | bytes 262176 | tf_op jit(solution)/shard_map/ppermute | solution.py:26
  78.4 12.8 %collective-permute-done.14 = bf16[128,1024]{1,0:T(8,128)(2,1)S(1)} collective-permute-done((bf16[128,1024]{1,0:T(8,128)(2,1)}, bf16[128,1024]{1,0:T(8,128)(2,1)S(1)}, u32[]{:S(2)}, u32[]{:S(2)}) %collective-permute-start.14) | collective-permute-done | bytes 262176 | tf_op jit(solution)/shard_map/ppermute | solution.py:26
  104.2 24.5 %collective-permute-done.7 = bf16[4,1,1,32,128]{4,3,2,1,0:T(8,128)(2,1)S(1)} collective-permute-done((bf16[4,1,1,32,128]{4,3,2,1,0:T(8,128)(2,1)S(1)}, bf16[4,1,1,32,128]{4,3,2,1,0:T(8,128)(2,1)S(1)}, u32[]{:S(2)}, u32[]{:S(2)}) %collective-permute-start.7) | collective-permute-done | bytes 32800 | tf_op jit(solution)/shard_map/ppermute | solution.py:26
  147.2 10.3 collective-permute-done.18
  161.0 9.0 collective-permute-done.22
  186.8 29.7 %collective-permute-done.24 = bf16[256,2176]{1,0:T(8,128)(2,1)S(1)} collective-permute-done((bf16[256,2176]{1,0:T(8,128)(2,1)}, bf16[256,2176]{1,0:T(8,128)(2,1)S(1)}, u32[]{:S(2)}, u32[]{:S(2)}) %collective-permute-start.24) | collective-permute-done | bytes 1114144 | tf_op jit(solution)/shard_map/ppermute | solution.py:337
  220.7 5.8 collective-permute-done.17
  229.8 16.0 %collective-permute-done.26 = bf16[256,2176]{1,0:T(8,128)(2,1)S(1)} collective-permute-done((bf16[256,2176]{1,0:T(8,128)(2,1)S(1)}, bf16[256,2176]{1,0:T(8,128)(2,1)S(1)}, u32[]{:S(2)}, u32[]{:S(2)}) %collective-permute-start.26) | collective-permute-done | bytes 1114144 | tf_op jit(solution)/shard_map/ppermute | solution.py:337
  258.7 6.2 fusion.307.k_ref
  269.9 8.0 convolution_convert_fusion.16.v_ref
  277.8 28.3 %collective-permute-done.28 = bf16[512,2048]{1,0:T(8,128)(2,1)} collective-permute-done((bf16[512,2048]{1,0:T(8,128)(2,1)}, bf16[512,2048]{1,0:T(8,128)(2,1)}, u32[]{:S(2)}, u32[]{:S(2)}) %collective-permute-start.28) | collective-permute-done | bytes 2097184 | tf_op jit(solution)/shard_map/ppermute | solution.py:26
  309.0 5.3 fusion.13.q_ref
  314.6 28.4 %attention_forward.1 = (bf16[512,1024]{1,0:T(8,128)(2,1)S(1)}, f32[8,8,512]{2,1,0:T(8,128)S(1)}) custom-call(f32[512,1024]{1,0:T(8,128)S(1)} %fusion.13.q_ref, f32[1024,1024]{1,0:T(8,128)S(1)} %copy-done, bf16[1024,1024]{1,0:T(8,128)(2,1)S(1)} %convolution_convert_fusion.16.v_ref, f32[2,1024,128]{2,1,0:T(8,128)S(1)} %pad_maximum_fusion.18.table_ref, ...), custom_call_target="tpu_custom_call" | custom-call | tf_op jit(solution)/shard_map/attention_forward/pallas_call | solution.py:109
  343.2 8.5 collective-permute-done.29
  367.7 5.6 collective-permute-start.35
  381.6 14.8 %fusion.9 = f32[2048,1024]{0,1:T(8,128)} fusion(bf16[2048,2048]{1,0:T(8,128)(2,1)} %copy-done.128, bf16[1,1024,2048]{2,1,0:T(8,128)(2,1)} %all-gather.7.cloned.1.call-done), kind=kOutput, calls=%fused_computation.24 | convolution fusion | flops 8589934592 | bytes 20971520 | tf_op jit(solution)/shard_map/dot_general | solution.py:36
  410.0 8.2 fusion.36
  419.2 5.2 multiply_convert_fusion.12
  428.1 10.6 fusion.19
  440.2 17.8 %collective-permute-done.39 = bf16[256,2176]{1,0:T(8,128)(2,1)} collective-permute-done((bf16[256,2176]{1,0:T(8,128)(2,1)}, bf16[256,2176]{1,0:T(8,128)(2,1)}, u32[]{:S(2)}, u32[]{:S(2)}) %collective-permute-start.39) | collective-permute-done | bytes 1114144 | tf_op jit(solution)/shard_map/ppermute | solution.py:337
  462.4 8.4 fusion.33
  475.8 5.2 multiply_convert_fusion.10
  484.5 10.5 fusion.20
  495.0 7.9 collective-permute-done.44
  507.0 8.4 fusion.30
  520.4 5.2 multiply_convert_fusion.8
  527.2 10.5 fusion.21
  539.3 8.3 fusion.27
  547.7 5.2 multiply_convert_fusion.6
  554.6 9.1 fusion.22
  570.9 7.5 collective-permute-done.49
  578.4 6.0 collective-permute-done.50
  597.4 10.7 fusion.23
  608.1 11.2 fusion.15
  624.7 9.3 convolution_convert_fusion.13
  634.0 6.3 fusion.136
  656.4 4.7 collective-permute-done.55
  661.1 7.4 collective-permute-done.56
  671.9 9.3 collective-permute-start.64
  692.0 5.9 collective-permute-done.59
  731.5 35.6 %attention_backward.1 = (bf16[512,1024]{1,0:T(8,128)(2,1)S(1)}, bf16[1024,1024]{1,0:T(8,128)(2,1)S(1)}, bf16[1024,1024]{1,0:T(8,128)(2,1)S(1)}, f32[2,8,128]{2,1,0:T(8,128)S(1)}) custom-call(f32[512,1024]{1,0:T(8,128)S(1)} %copy-done.2, f32[1024,1024]{1,0:T(8,128)} %fusion.307.k_ref, bf16[1024,1024]{1,0:T(8,128)(2,1)S(1)} %convolution_convert_fusion.16.v_ref, ...), custom_call_target="tpu_custom_call" | custom-call | tf_op jit(solution)/shard_map/attention_backward/pallas_call | solution.py:192
  771.6 23.8 %collective-permute-done.68 = bf16[512,2048]{1,0:T(8,128)(2,1)} collective-permute-done((bf16[512,2048]{1,0:T(8,128)(2,1)}, bf16[512,2048]{1,0:T(8,128)(2,1)}, u32[]{:S(2)}, u32[]{:S(2)}) %collective-permute-start.68) | collective-permute-done | bytes 2097184 | tf_op jit(solution)/shard_map/ppermute | solution.py:26
  805.2 5.3 convolution_convert_fusion.14
  817.4 6.8 fusion.309
  824.2 7.4 convolution_add_fusion.1
  838.9 5.3 maximum_convert_fusion
  847.0 5.9 add_bitcast_fusion.1
  857.1 5.7 collective-permute-start.75
  868.1 4.7 convert_add_fusion.1
  886.0 6.9 add_bitcast_fusion
  900.4 16.8 %collective-permute-done.82 = bf16[256,2048]{1,0:T(8,128)(2,1)S(1)} collective-permute-done((bf16[256,2048]{1,0:T(8,128)(2,1)}, bf16[256,2048]{1,0:T(8,128)(2,1)S(1)}, u32[]{:S(2)}, u32[]{:S(2)}) %collective-permute-start.82) | collective-permute-done | bytes 1048608 | tf_op jit(solution)/shard_map/ppermute | solution.py:26
  921.3 4.8 multiply_reduce_fusion.2
  926.4 35.7 %collective-permute-done.89 = bf16[1024,512]{1,0:T(8,128)(2,1)} collective-permute-done((bf16[1024,512]{1,0:T(8,128)(2,1)}, bf16[1024,512]{1,0:T(8,128)(2,1)}, u32[]{:S(2)}, u32[]{:S(2)}) %collective-permute-start.89) | collective-permute-done | bytes 1048608 | tf_op jit(solution)/shard_map/ppermute | solution.py:26
  966.7 4.9 collective-permute-start.90
  980.2 25.7 %collective-permute-done.102 = bf16[4,128,1024]{2,1,0:T(8,128)(2,1)} collective-permute-done((bf16[4,128,1024]{2,1,0:T(8,128)(2,1)}, bf16[4,128,1024]{2,1,0:T(8,128)(2,1)}, u32[]{:S(2)}, u32[]{:S(2)}) %collective-permute-start.102) | collective-permute-done | bytes 1048608 | tf_op jit(solution)/shard_map/ppermute | solution.py:26
  1026.0 5.8 collective-permute-done.87
  1038.2 14.2 %collective-permute-done.99 = bf16[128,1024]{1,0:T(8,128)(2,1)} collective-permute-done((bf16[128,1024]{1,0:T(8,128)(2,1)}, bf16[128,1024]{1,0:T(8,128)(2,1)}, u32[]{:S(2)}, u32[]{:S(2)}) %collective-permute-start.99) | collective-permute-done | bytes 262176 | tf_op jit(solution)/shard_map/ppermute | solution.py:26
  1052.5 7.1 collective-permute-start.103
  1062.0 7.3 collective-permute-done.104
  1073.5 7.4 collective-permute-done.92
  1085.5 18.4 %collective-permute-start.93 = (bf16[128,1024]{1,0:T(8,128)(2,1)S(1)}, bf16[128,1024]{1,0:T(8,128)(2,1)S(1)}, u32[]{:S(2)}, u32[]{:S(2)}) collective-permute-start(bf16[128,1024]{1,0:T(8,128)(2,1)S(1)} %get-tuple-element.470), channel_id=1, source_target_pairs={{0,8},{2,10},{4,12},{6,14},{8,0},{10,2},{12,4},{14,6},{16,24},{18,... | collective-permute-start | bytes 786440 | tf_op jit(solution)/shard_map/ppermute | solution.py:26
  1106.5 8.1 collective-permute-done.94
  1121.4 15.1 %collective-permute-done.80 = bf16[256,2048]{1,0:T(8,128)(2,1)} collective-permute-done((bf16[256,2048]{1,0:T(8,128)(2,1)}, bf16[256,2048]{1,0:T(8,128)(2,1)}, u32[]{:S(2)}, u32[]{:S(2)}) %collective-permute-start.80) | collective-permute-done | bytes 1048608 | tf_op jit(solution)/shard_map/ppermute | solution.py:337
  (814 shorter events, 409.1 us)
Async XLA Ops:
  7.2 262.7 %all-gather.13.cloned.1.call-start = ((), (), s32[]{:S(2)}) async-start(), calls=%async_computation.5 | async-start | bytes 4456448 | tf_op jit(solution)/shard_map/all_gather | solution.py:276
  12.3 296.8 %all-gather.11.cloned.1.call-start = ((), (), s32[]{:S(2)}) async-start(), calls=%async_computation.4 | async-start | bytes 4456448 | tf_op jit(solution)/shard_map/all_gather | solution.py:276
  13.0 368.6 %all-gather.7.cloned.1.call-start = ((), (), s32[]{:S(2)}) async-start(), calls=%async_computation.1 | async-start | bytes 6291456 | tf_op jit(solution)/shard_map/all_gather | solution.py:383
  13.8 396.2 %all-gather.9.cloned.1.call-start = ((), (), s32[]{:S(2)}) async-start(), calls=%async_computation.2 | async-start | bytes 12582912 | tf_op jit(solution)/shard_map/all_gather | solution.py:382
  14.2 80.3 %collective-permute-start.3 = (bf16[16,128]{1,0:T(8,128)(2,1)S(1)}, bf16[16,128]{1,0:T(8,128)(2,1)S(1)}, u32[]{:S(2)}, u32[]{:S(2)}) collective-permute-start(bf16[16,128]{1,0:T(8,128)(2,1)S(1)} %pad_bitcast_fusion.1), channel_id=1, source_target_pairs={{0,1},{1,0},{2,3},{3,2},{4,5},{5,4},{6,7},{7,6},{8,9},{9,8},{10,11... | collective-permute-start | bytes 12296 | tf_op jit(solution)/shard_map/ppermute | solution.py:26
  14.6 1105.1 %reduce-scatter.2.cloned.1.call-start = ((), (), s32[]{:S(2)}) async-start(), calls=%async_computation.3 | async-start | bytes 4456448 | tf_op jit(solution)/shard_map/reduce_scatter | solution.py:629
  26.0 29.1 %collective-permute-start.13 = (bf16[128,1024]{1,0:T(8,128)(2,1)}, bf16[128,1024]{1,0:T(8,128)(2,1)}, u32[]{:S(2)}, u32[]{:S(2)}) collective-permute-start(bf16[128,1024]{1,0:T(8,128)(2,1)} %get-tuple-element.535), channel_id=1, source_target_pairs={{0,8},{2,10},{4,12},{6,14},{8,0},{10,2},{12,4},{14,6},{16,24},{18,... | collective-permute-start | bytes 786440 | tf_op jit(solution)/shard_map/ppermute | solution.py:26
  27.1 33.3 %collective-permute-start.12 = (bf16[128,1024]{1,0:T(8,128)(2,1)}, bf16[128,1024]{1,0:T(8,128)(2,1)}, u32[]{:S(2)}, u32[]{:S(2)}) collective-permute-start(bf16[128,1024]{1,0:T(8,128)(2,1)} %get-tuple-element.536), channel_id=1, source_target_pairs={{0,24},{2,26},{4,28},{6,30},{8,16},{10,18},{12,20},{14,22},{16,8},... | collective-permute-start | bytes 786440 | tf_op jit(solution)/shard_map/ppermute | solution.py:26
  31.1 44.4 %collective-permute-start.11 = (bf16[128,1024]{1,0:T(8,128)(2,1)}, bf16[128,1024]{1,0:T(8,128)(2,1)}, u32[]{:S(2)}, u32[]{:S(2)}) collective-permute-start(bf16[128,1024]{1,0:T(8,128)(2,1)} %get-tuple-element.536), channel_id=1, source_target_pairs={{0,16},{2,18},{4,20},{6,22},{8,24},{10,26},{12,28},{14,30},{16,0},... | collective-permute-start | bytes 786440 | tf_op jit(solution)/shard_map/ppermute | solution.py:26
  35.7 102.3 %collective-permute-start.1 = (bf16[256,2048]{1,0:T(8,128)(2,1)S(1)}, bf16[256,2048]{1,0:T(8,128)(2,1)S(1)}, u32[]{:S(2)}, u32[]{:S(2)}) collective-permute-start(bf16[256,2048]{1,0:T(8,128)(2,1)S(1)} %copy-done.18), channel_id=1, source_target_pairs={{0,2},{2,0},{4,6},{6,4},{8,10},{10,8},{12,14},{14,12},{16,18},{18,... | collective-permute-start | bytes 3145736 | tf_op jit(solution)/shard_map/ppermute | solution.py:26
  60.4 30.9 %collective-permute-start.14 = (bf16[128,1024]{1,0:T(8,128)(2,1)}, bf16[128,1024]{1,0:T(8,128)(2,1)S(1)}, u32[]{:S(2)}, u32[]{:S(2)}) collective-permute-start(bf16[128,1024]{1,0:T(8,128)(2,1)} %get-tuple-element.535), channel_id=1, source_target_pairs={{0,16},{2,18},{4,20},{6,22},{8,24},{10,26},{12,28},{14,30},{16,0},... | collective-permute-start | bytes 786440 | tf_op jit(solution)/shard_map/ppermute | solution.py:26
  92.9 45.3 %collective-permute-start.16 = (bf16[4,1,1,128,1024]{4,3,2,1,0:T(8,128)(2,1)}, bf16[4,1,1,128,1024]{4,3,2,1,0:T(8,128)(2,1)}, u32[]{:S(2)}, u32[]{:S(2)}) collective-permute-start(bf16[4,1,1,128,1024]{4,3,2,1,0:T(8,128)(2,1)} %bitcast.12), channel_id=1, source_target_pairs={{0,4},{2,6},{4,0},{6,2},{8,12},{10,14},{12,8},{14,10},{16,20},{18,... | collective-permute-start | bytes 3145736 | tf_op jit(solution)/shard_map/ppermute | solution.py:26
  101.9 26.8 %collective-permute-start.7 = (bf16[4,1,1,32,128]{4,3,2,1,0:T(8,128)(2,1)S(1)}, bf16[4,1,1,32,128]{4,3,2,1,0:T(8,128)(2,1)S(1)}, u32[]{:S(2)}, u32[]{:S(2)}) collective-permute-start(bf16[4,1,1,32,128]{4,3,2,1,0:T(8,128)(2,1)S(1)} %bitcast.271), channel_id=1, source_target_pairs={{0,4},{2,6},{4,0},{6,2},{8,12},{10,14},{12,8},{14,10},{16,20},{18,... | collective-permute-start | bytes 98312 | tf_op jit(solution)/shard_map/ppermute | solution.py:26
  130.3 27.3 %collective-permute-start.18 = (bf16[4,1,1,128,1024]{4,3,2,1,0:T(8,128)(2,1)}, bf16[4,1,1,128,1024]{4,3,2,1,0:T(8,128)(2,1)}, u32[]{:S(2)}, u32[]{:S(2)}) collective-permute-start(bf16[4,1,1,128,1024]{4,3,2,1,0:T(8,128)(2,1)} %bitcast.251), channel_id=1, source_target_pairs={{0,2},{2,0},{4,6},{6,4},{8,10},{10,8},{12,14},{14,12},{16,18},{18,... | collective-permute-start | bytes 3145736 | tf_op jit(solution)/shard_map/ppermute | solution.py:26
  130.9 39.1 %collective-permute-start.22 = (bf16[256,2176]{1,0:T(8,128)(2,1)}, bf16[256,2176]{1,0:T(8,128)(2,1)}, u32[]{:S(2)}, u32[]{:S(2)}) collective-permute-start(bf16[256,2176]{1,0:T(8,128)(2,1)} %fusion.146), channel_id=1, source_target_pairs={{8,0},{10,2},{12,4},{14,6},{16,8},{18,10},{20,12},{22,14},{24,16},... | collective-permute-start | bytes 3342344 | tf_op jit(solution)/shard_map/ppermute | solution.py:337
  133.6 38.5 %collective-permute-start.23 = (bf16[256,2176]{1,0:T(8,128)(2,1)}, bf16[256,2176]{1,0:T(8,128)(2,1)}, u32[]{:S(2)}, u32[]{:S(2)}) collective-permute-start(bf16[256,2176]{1,0:T(8,128)(2,1)} %fusion.146), channel_id=1, source_target_pairs={{0,8},{2,10},{4,12},{6,14},{8,16},{10,18},{12,20},{14,22},{16,24},... | collective-permute-start | bytes 3342344 | tf_op jit(solution)/shard_map/ppermute | solution.py:332
  138.2 35.1 %collective-permute-start.2 = (bf16[256,2048]{1,0:T(8,128)(2,1)S(1)}, bf16[256,2048]{1,0:T(8,128)(2,1)}, u32[]{:S(2)}, u32[]{:S(2)}) collective-permute-start(bf16[256,2048]{1,0:T(8,128)(2,1)S(1)} %collective-permute-done.1), channel_id=1, source_target_pairs={{0,1},{1,0},{2,3},{3,2},{4,5},{5,4},{6,7},{7,6},{8,9},{9,8},{10,11... | collective-permute-start | bytes 3145736 | tf_op jit(solution)/shard_map/ppermute | solution.py:26
  157.6 69.0 %collective-permute-start.17 = (bf16[4,2,1,128,1024]{4,3,2,1,0:T(8,128)(2,1)S(1)}, bf16[4,2,1,128,1024]{4,3,2,1,0:T(8,128)(2,1)S(1)}, u32[]{:S(2)}, u32[]{:S(2)}) collective-permute-start(bf16[4,2,1,128,1024]{4,3,2,1,0:T(8,128)(2,1)S(1)} %maximum_select_fusion.2), channel_id=1, source_target_pairs={{0,2},{2,0},{4,6},{6,4},{8,10},{10,8},{12,14},{14,12},{16,18},{18,... | collective-permute-start | bytes 6291464 | tf_op jit(solution)/shard_map/ppermute | solution.py:26
  160.6 66.6 %collective-permute-start.19 = (bf16[4,1,2,128,1024]{4,3,2,1,0:T(8,128)(2,1)S(1)}, bf16[4,1,2,128,1024]{4,3,2,1,0:T(8,128)(2,1)S(1)}, u32[]{:S(2)}, u32[]{:S(2)}) collective-permute-start(bf16[4,1,2,128,1024]{4,3,2,1,0:T(8,128)(2,1)S(1)} %maximum_select_fusion.3), channel_id=1, source_target_pairs={{0,4},{2,6},{4,0},{6,2},{8,12},{10,14},{12,8},{14,10},{16,20},{18,... | collective-permute-start | bytes 6291464 | tf_op jit(solution)/shard_map/ppermute | solution.py:26
  170.0 46.4 %collective-permute-start.24 = (bf16[256,2176]{1,0:T(8,128)(2,1)}, bf16[256,2176]{1,0:T(8,128)(2,1)S(1)}, u32[]{:S(2)}, u32[]{:S(2)}) collective-permute-start(bf16[256,2176]{1,0:T(8,128)(2,1)} %collective-permute-done.22), channel_id=1, source_target_pairs={{8,0},{10,2},{12,4},{14,6},{16,8},{18,10},{20,12},{22,14},{9,1},{1... | collective-permute-start | bytes 3342344 | tf_op jit(solution)/shard_map/ppermute | solution.py:337
  172.1 45.6 %collective-permute-start.25 = (bf16[256,2176]{1,0:T(8,128)(2,1)}, bf16[256,2176]{1,0:T(8,128)(2,1)S(1)}, u32[]{:S(2)}, u32[]{:S(2)}) collective-permute-start(bf16[256,2176]{1,0:T(8,128)(2,1)} %collective-permute-done.23), channel_id=1, source_target_pairs={{8,16},{10,18},{12,20},{14,22},{16,24},{18,26},{20,28},{22,30},{9,... | collective-permute-start | bytes 3342344 | tf_op jit(solution)/shard_map/ppermute | solution.py:332
  216.4 29.4 %collective-permute-start.26 = (bf16[256,2176]{1,0:T(8,128)(2,1)S(1)}, bf16[256,2176]{1,0:T(8,128)(2,1)S(1)}, u32[]{:S(2)}, u32[]{:S(2)}) collective-permute-start(bf16[256,2176]{1,0:T(8,128)(2,1)S(1)} %collective-permute-done.24), channel_id=1, source_target_pairs={{8,0},{10,2},{12,4},{14,6},{9,1},{11,3},{13,5},{15,7}} | collective-permute-start | bytes 3342344 | tf_op jit(solution)/shard_map/ppermute | solution.py:337
  217.7 28.1 %collective-permute-start.27 = (bf16[256,2176]{1,0:T(8,128)(2,1)S(1)}, bf16[256,2176]{1,0:T(8,128)(2,1)S(1)}, u32[]{:S(2)}, u32[]{:S(2)}) collective-permute-start(bf16[256,2176]{1,0:T(8,128)(2,1)S(1)} %collective-permute-done.25), channel_id=1, source_target_pairs={{16,24},{18,26},{20,28},{22,30},{17,25},{19,27},{21,29},{23,31}} | collective-permute-start | bytes 3342344 | tf_op jit(solution)/shard_map/ppermute | solution.py:332
  257.3 48.9 %collective-permute-start.28 = (bf16[512,2048]{1,0:T(8,128)(2,1)}, bf16[512,2048]{1,0:T(8,128)(2,1)}, u32[]{:S(2)}, u32[]{:S(2)}) collective-permute-start(bf16[512,2048]{1,0:T(8,128)(2,1)} %pad_maximum_fusion.3), channel_id=1, source_target_pairs={{0,2},{2,0},{4,6},{6,4},{8,10},{10,8},{12,14},{14,12},{16,18},{18,... | collective-permute-start | bytes 6291464 | tf_op jit(solution)/shard_map/ppermute | solution.py:26
  266.3 85.4 %collective-permute-start.29 = (bf16[512,2048]{1,0:T(8,128)(2,1)}, bf16[512,2048]{1,0:T(8,128)(2,1)}, u32[]{:S(2)}, u32[]{:S(2)}) collective-permute-start(bf16[512,2048]{1,0:T(8,128)(2,1)} %pad_maximum_fusion.4), channel_id=1, source_target_pairs={{0,4},{2,6},{4,0},{6,2},{8,12},{10,14},{12,8},{14,10},{16,20},{18,... | collective-permute-start | bytes 6291464 | tf_op jit(solution)/shard_map/ppermute | solution.py:26
  268.3 85.2 %collective-permute-start.30 = (bf16[512,2048]{1,0:T(8,128)(2,1)}, bf16[512,2048]{1,0:T(8,128)(2,1)}, u32[]{:S(2)}, u32[]{:S(2)}) collective-permute-start(bf16[512,2048]{1,0:T(8,128)(2,1)} %pad_maximum_fusion.5), channel_id=1, source_target_pairs={{0,6},{2,4},{4,2},{6,0},{8,14},{10,12},{12,10},{14,8},{16,22},{18,... | collective-permute-start | bytes 6291464 | tf_op jit(solution)/shard_map/ppermute | solution.py:26
  269.9 87.7 %collective-permute-start.21 = (bf16[2048,1024]{1,0:T(8,128)(2,1)}, bf16[2048,1024]{1,0:T(8,128)(2,1)}, u32[]{:S(2)}, u32[]{:S(2)}) collective-permute-start(bf16[2048,1024]{1,0:T(8,128)(2,1)} %bitcast.285), channel_id=1, source_target_pairs={{0,1},{1,0},{2,3},{3,2},{4,5},{5,4},{6,7},{7,6},{8,9},{9,8},{10,11... | collective-permute-start | bytes 12582920 | tf_op jit(solution)/shard_map/ppermute | solution.py:26
  366.3 30.2 %collective-permute-start.34 = (bf16[256,2176]{1,0:T(8,128)(2,1)}, bf16[256,2176]{1,0:T(8,128)(2,1)}, u32[]{:S(2)}, u32[]{:S(2)}) collective-permute-start(bf16[256,2176]{1,0:T(8,128)(2,1)} %pad_maximum_fusion.16), channel_id=1, source_target_pairs={{8,0},{10,2},{12,4},{14,6},{16,8},{18,10},{20,12},{22,14},{24,16},... | collective-permute-start | bytes 3342344 | tf_op jit(solution)/shard_map/ppermute | solution.py:337
  367.7 28.8 %collective-permute-start.35 = (bf16[256,2176]{1,0:T(8,128)(2,1)}, bf16[256,2176]{1,0:T(8,128)(2,1)}, u32[]{:S(2)}, u32[]{:S(2)}) collective-permute-start(bf16[256,2176]{1,0:T(8,128)(2,1)} %pad_maximum_fusion.16), channel_id=1, source_target_pairs={{0,8},{2,10},{4,12},{6,14},{8,16},{10,18},{12,20},{14,22},{16,24},... | collective-permute-start | bytes 3342344 | tf_op jit(solution)/shard_map/ppermute | solution.py:332
  400.1 60.7 %collective-permute-start.36 = (bf16[128,2176]{1,0:T(8,128)(2,1)}, bf16[128,2176]{1,0:T(8,128)(2,1)}, u32[]{:S(2)}, u32[]{:S(2)}) collective-permute-start(bf16[128,2176]{1,0:T(8,128)(2,1)} %get-tuple-element.456), channel_id=1, source_target_pairs={{0,2},{2,0},{4,6},{6,4},{8,10},{10,8},{12,14},{14,12},{16,18},{18,... | collective-permute-start | bytes 1671176 | tf_op jit(solution)/shard_map/ppermute | solution.py:26
  401.6 59.2 %collective-permute-start.37 = (bf16[128,2176]{1,0:T(8,128)(2,1)}, bf16[128,2176]{1,0:T(8,128)(2,1)}, u32[]{:S(2)}, u32[]{:S(2)}) collective-permute-start(bf16[128,2176]{1,0:T(8,128)(2,1)} %get-tuple-element.455), channel_id=1, source_target_pairs={{0,4},{2,6},{4,0},{6,2},{8,12},{10,14},{12,8},{14,10},{16,20},{18,... | collective-permute-start | bytes 1671176 | tf_op jit(solution)/shard_map/ppermute | solution.py:26
  402.7 58.2 %collective-permute-start.38 = (bf16[128,2176]{1,0:T(8,128)(2,1)}, bf16[128,2176]{1,0:T(8,128)(2,1)}, u32[]{:S(2)}, u32[]{:S(2)}) collective-permute-start(bf16[128,2176]{1,0:T(8,128)(2,1)} %get-tuple-element.454), channel_id=1, source_target_pairs={{0,6},{2,4},{4,2},{6,0},{8,14},{10,12},{12,10},{14,8},{16,22},{18,... | collective-permute-start | bytes 1671176 | tf_op jit(solution)/shard_map/ppermute | solution.py:26
  424.6 33.4 %collective-permute-start.39 = (bf16[256,2176]{1,0:T(8,128)(2,1)}, bf16[256,2176]{1,0:T(8,128)(2,1)}, u32[]{:S(2)}, u32[]{:S(2)}) collective-permute-start(bf16[256,2176]{1,0:T(8,128)(2,1)} %collective-permute-done.34), channel_id=1, source_target_pairs={{8,0},{10,2},{12,4},{14,6},{16,8},{18,10},{20,12},{22,14},{9,1},{1... | collective-permute-start | bytes 3342344 | tf_op jit(solution)/shard_map/ppermute | solution.py:337
  425.9 32.1 %collective-permute-start.40 = (bf16[256,2176]{1,0:T(8,128)(2,1)}, bf16[256,2176]{1,0:T(8,128)(2,1)}, u32[]{:S(2)}, u32[]{:S(2)}) collective-permute-start(bf16[256,2176]{1,0:T(8,128)(2,1)} %collective-permute-done.35), channel_id=1, source_target_pairs={{8,16},{10,18},{12,20},{14,22},{16,24},{18,26},{20,28},{22,30},{9,... | collective-permute-start | bytes 3342344 | tf_op jit(solution)/shard_map/ppermute | solution.py:332
  472.3 33.0 %collective-permute-start.41 = (bf16[128,2176]{1,0:T(8,128)(2,1)}, bf16[128,2176]{1,0:T(8,128)(2,1)}, u32[]{:S(2)}, u32[]{:S(2)}) collective-permute-start(bf16[128,2176]{1,0:T(8,128)(2,1)} %get-tuple-element.452), channel_id=1, source_target_pairs={{0,2},{2,0},{4,6},{6,4},{8,10},{10,8},{12,14},{14,12},{16,18},{18,... | collective-permute-start | bytes 1671176 | tf_op jit(solution)/shard_map/ppermute | solution.py:26
  473.2 32.2 %collective-permute-start.42 = (bf16[128,2176]{1,0:T(8,128)(2,1)}, bf16[128,2176]{1,0:T(8,128)(2,1)}, u32[]{:S(2)}, u32[]{:S(2)}) collective-permute-start(bf16[128,2176]{1,0:T(8,128)(2,1)} %get-tuple-element.451), channel_id=1, source_target_pairs={{0,4},{2,6},{4,0},{6,2},{8,12},{10,14},{12,8},{14,10},{16,20},{18,... | collective-permute-start | bytes 1671176 | tf_op jit(solution)/shard_map/ppermute | solution.py:26
  474.4 31.0 %collective-permute-start.43 = (bf16[128,2176]{1,0:T(8,128)(2,1)}, bf16[128,2176]{1,0:T(8,128)(2,1)}, u32[]{:S(2)}, u32[]{:S(2)}) collective-permute-start(bf16[128,2176]{1,0:T(8,128)(2,1)} %get-tuple-element.450), channel_id=1, source_target_pairs={{0,6},{2,4},{4,2},{6,0},{8,14},{10,12},{12,10},{14,8},{16,22},{18,... | collective-permute-start | bytes 1671176 | tf_op jit(solution)/shard_map/ppermute | solution.py:26
  587.0 58.2 %collective-permute-start.62 = (bf16[256,2176]{1,0:T(8,128)(2,1)}, bf16[256,2176]{1,0:T(8,128)(2,1)}, u32[]{:S(2)}, u32[]{:S(2)}) collective-permute-start(bf16[256,2176]{1,0:T(8,128)(2,1)} %get-tuple-element.586), channel_id=1, source_target_pairs={{24,16},{26,18},{28,20},{30,22},{25,17},{27,19},{29,21},{31,23}} | collective-permute-start | bytes 3342344 | tf_op jit(solution)/shard_map/ppermute | solution.py:337
  588.8 56.4 %collective-permute-start.61 = (bf16[256,2176]{1,0:T(8,128)(2,1)}, bf16[256,2176]{1,0:T(8,128)(2,1)}, u32[]{:S(2)}, u32[]{:S(2)}) collective-permute-start(bf16[256,2176]{1,0:T(8,128)(2,1)} %get-tuple-element.586), channel_id=1, source_target_pairs={{0,8},{2,10},{4,12},{6,14},{1,9},{3,11},{5,13},{7,15}} | collective-permute-start | bytes 3342344 | tf_op jit(solution)/shard_map/ppermute | solution.py:332
  669.5 28.9 %collective-permute-start.66 = (bf16[256,2176]{1,0:T(8,128)(2,1)S(1)}, bf16[256,2176]{1,0:T(8,128)(2,1)S(1)}, u32[]{:S(2)}, u32[]{:S(2)}) collective-permute-start(bf16[256,2176]{1,0:T(8,128)(2,1)S(1)} %add_convert_fusion), channel_id=1, source_target_pairs={{8,0},{10,2},{12,4},{14,6},{16,8},{18,10},{20,12},{22,14},{24,16},... | collective-permute-start | bytes 3342344 | tf_op jit(solution)/shard_map/ppermute | solution.py:337
  692.0 30.6 %collective-permute-start.71 = (bf16[256,2048]{1,0:T(8,128)(2,1)S(1)}, bf16[256,2048]{1,0:T(8,128)(2,1)S(1)}, u32[]{:S(2)}, u32[]{:S(2)}) collective-permute-start(bf16[256,2048]{1,0:T(8,128)(2,1)S(1)} %copy-done.105), channel_id=1, source_target_pairs={{0,1},{1,0},{2,3},{3,2},{4,5},{5,4},{6,7},{7,6},{8,9},{9,8},{10,11... | collective-permute-start | bytes 3145736 | tf_op jit(solution)/shard_map/ppermute | solution.py:26
  705.2 61.9 %collective-permute-start.67 = (bf16[512,2048]{1,0:T(8,128)(2,1)}, bf16[512,2048]{1,0:T(8,128)(2,1)}, u32[]{:S(2)}, u32[]{:S(2)}) collective-permute-start(bf16[512,2048]{1,0:T(8,128)(2,1)} %pad_maximum_fusion.12), channel_id=1, source_target_pairs={{0,2},{2,0},{4,6},{6,4},{8,10},{10,8},{12,14},{14,12},{16,18},{18,... | collective-permute-start | bytes 6291464 | tf_op jit(solution)/shard_map/ppermute | solution.py:26
  708.3 87.2 %collective-permute-start.68 = (bf16[512,2048]{1,0:T(8,128)(2,1)}, bf16[512,2048]{1,0:T(8,128)(2,1)}, u32[]{:S(2)}, u32[]{:S(2)}) collective-permute-start(bf16[512,2048]{1,0:T(8,128)(2,1)} %pad_maximum_fusion.13), channel_id=1, source_target_pairs={{0,4},{2,6},{4,0},{6,2},{8,12},{10,14},{12,8},{14,10},{16,20},{18,... | collective-permute-start | bytes 6291464 | tf_op jit(solution)/shard_map/ppermute | solution.py:26
  719.9 78.4 %collective-permute-start.69 = (bf16[512,2048]{1,0:T(8,128)(2,1)}, bf16[512,2048]{1,0:T(8,128)(2,1)}, u32[]{:S(2)}, u32[]{:S(2)}) collective-permute-start(bf16[512,2048]{1,0:T(8,128)(2,1)} %pad_maximum_fusion.14), channel_id=1, source_target_pairs={{0,6},{2,4},{4,2},{6,0},{8,14},{10,12},{12,10},{14,8},{16,22},{18,... | collective-permute-start | bytes 6291464 | tf_op jit(solution)/shard_map/ppermute | solution.py:26
  722.6 124.4 %collective-permute-start.109 = (bf16[512,2048]{1,0:T(8,128)(2,1)}, bf16[512,2048]{1,0:T(8,128)(2,1)}, u32[]{:S(2)}, u32[]{:S(2)}) collective-permute-start(bf16[512,2048]{1,0:T(8,128)(2,1)} %convolution_convert_fusion.13), channel_id=1, source_target_pairs={{0,1},{1,0},{2,3},{3,2},{4,5},{5,4},{6,7},{7,6},{8,9},{9,8},{10,11... | collective-permute-start | bytes 6291464 | tf_op jit(solution)/shard_map/ppermute | solution.py:26
  815.4 37.5 %collective-permute-start.73 = (bf16[1024,1024]{1,0:T(8,128)(2,1)}, bf16[1024,1024]{1,0:T(8,128)(2,1)}, u32[]{:S(2)}, u32[]{:S(2)}) collective-permute-start(bf16[1024,1024]{1,0:T(8,128)(2,1)} %convolution_convert_fusion.15), channel_id=1, source_target_pairs={{0,4},{2,6},{4,0},{6,2},{8,12},{10,14},{12,8},{14,10},{16,20},{18,... | collective-permute-start | bytes 6291464 | tf_op jit(solution)/shard_map/ppermute | solution.py:26
  815.8 37.1 %collective-permute-start.74 = (bf16[1024,1024]{1,0:T(8,128)(2,1)}, bf16[1024,1024]{1,0:T(8,128)(2,1)}, u32[]{:S(2)}, u32[]{:S(2)}) collective-permute-start(bf16[1024,1024]{1,0:T(8,128)(2,1)} %convolution_convert_fusion.14), channel_id=1, source_target_pairs={{0,2},{2,0},{4,6},{6,4},{8,10},{10,8},{12,14},{14,12},{16,18},{18,... | collective-permute-start | bytes 6291464 | tf_op jit(solution)/shard_map/ppermute | solution.py:26
  838.4 46.7 %collective-permute-start.108 = (bf16[1024,2048]{1,0:T(8,128)(2,1)}, bf16[1024,2048]{1,0:T(8,128)(2,1)}, u32[]{:S(2)}, u32[]{:S(2)}) collective-permute-start(bf16[1024,2048]{1,0:T(8,128)(2,1)} %fusion.23), channel_id=1, source_target_pairs={{0,1},{1,0},{2,3},{3,2},{4,5},{5,4},{6,7},{7,6},{8,9},{9,8},{10,11... | collective-permute-start | bytes 12582920 | tf_op jit(solution)/shard_map/ppermute | solution.py:26
  855.4 37.5 %collective-permute-start.76 = (bf16[256,2048]{1,0:T(8,128)(2,1)}, bf16[256,2048]{1,0:T(8,128)(2,1)}, u32[]{:S(2)}, u32[]{:S(2)}) collective-permute-start(bf16[256,2048]{1,0:T(8,128)(2,1)} %get-tuple-element.591), channel_id=1, source_target_pairs={{24,16},{26,18},{28,20},{30,22},{25,17},{27,19},{29,21},{31,23}} | collective-permute-start | bytes 3145736 | tf_op jit(solution)/shard_map/ppermute | solution.py:337
  857.1 39.2 %collective-permute-start.75 = (bf16[256,2048]{1,0:T(8,128)(2,1)}, bf16[256,2048]{1,0:T(8,128)(2,1)}, u32[]{:S(2)}, u32[]{:S(2)}) collective-permute-start(bf16[256,2048]{1,0:T(8,128)(2,1)} %get-tuple-element.591), channel_id=1, source_target_pairs={{0,8},{2,10},{4,12},{6,14},{1,9},{3,11},{5,13},{7,15}} | collective-permute-start | bytes 3145736 | tf_op jit(solution)/shard_map/ppermute | solution.py:332
  866.0 51.1 %collective-permute-start.82 = (bf16[256,2048]{1,0:T(8,128)(2,1)}, bf16[256,2048]{1,0:T(8,128)(2,1)S(1)}, u32[]{:S(2)}, u32[]{:S(2)}) collective-permute-start(bf16[256,2048]{1,0:T(8,128)(2,1)} %fusion.83), channel_id=1, source_target_pairs={{0,2},{2,0},{4,6},{6,4},{8,10},{10,8},{12,14},{14,12},{16,18},{18,... | collective-permute-start | bytes 3145736 | tf_op jit(solution)/shard_map/ppermute | solution.py:26
  867.0 95.1 %collective-permute-start.89 = (bf16[1024,512]{1,0:T(8,128)(2,1)}, bf16[1024,512]{1,0:T(8,128)(2,1)}, u32[]{:S(2)}, u32[]{:S(2)}) collective-permute-start(bf16[1024,512]{1,0:T(8,128)(2,1)} %convolution_convert_fusion.18), channel_id=1, source_target_pairs={{0,2},{2,0},{4,6},{6,4},{8,10},{10,8},{12,14},{14,12},{16,18},{18,... | collective-permute-start | bytes 3145736 | tf_op jit(solution)/shard_map/ppermute | solution.py:26
  885.0 88.2 %collective-permute-start.91 = (bf16[1024,512]{1,0:T(8,128)(2,1)}, bf16[1024,512]{1,0:T(8,128)(2,1)}, u32[]{:S(2)}, u32[]{:S(2)}) collective-permute-start(bf16[1024,512]{1,0:T(8,128)(2,1)} %convolution_convert_fusion.17), channel_id=1, source_target_pairs={{0,4},{2,6},{4,0},{6,2},{8,12},{10,14},{12,8},{14,10},{16,20},{18,... | collective-permute-start | bytes 3145736 | tf_op jit(solution)/shard_map/ppermute | solution.py:26
  892.8 73.8 %collective-permute-start.97 = (bf16[4,128,1024]{2,1,0:T(8,128)(2,1)}, bf16[4,128,1024]{2,1,0:T(8,128)(2,1)}, u32[]{:S(2)}, u32[]{:S(2)}) collective-permute-start(bf16[4,128,1024]{2,1,0:T(8,128)(2,1)} %fusion.158), channel_id=1, source_target_pairs={{0,4},{2,6},{4,0},{6,2},{8,12},{10,14},{12,8},{14,10},{16,20},{18,... | collective-permute-start | bytes 3145736 | tf_op jit(solution)/shard_map/ppermute | solution.py:26
  896.4 109.5 %collective-permute-start.102 = (bf16[4,128,1024]{2,1,0:T(8,128)(2,1)}, bf16[4,128,1024]{2,1,0:T(8,128)(2,1)}, u32[]{:S(2)}, u32[]{:S(2)}) collective-permute-start(bf16[4,128,1024]{2,1,0:T(8,128)(2,1)} %fusion.159), channel_id=1, source_target_pairs={{0,2},{2,0},{4,6},{6,4},{8,10},{10,8},{12,14},{14,12},{16,18},{18,... | collective-permute-start | bytes 3145736 | tf_op jit(solution)/shard_map/ppermute | solution.py:26
  918.2 164.6 %collective-permute-start.77 = (bf16[256,2048]{1,0:T(8,128)(2,1)}, bf16[256,2048]{1,0:T(8,128)(2,1)}, u32[]{:S(2)}, u32[]{:S(2)}) collective-permute-start(bf16[256,2048]{1,0:T(8,128)(2,1)} %get-tuple-element.593), channel_id=1, source_target_pairs={{0,8},{2,10},{4,12},{6,14},{8,16},{10,18},{12,20},{14,22},{1,9},{3... | collective-permute-start | bytes 3145736 | tf_op jit(solution)/shard_map/ppermute | solution.py:332
  962.1 45.4 %collective-permute-start.83 = (f32[4,2,2,16,128]{4,3,2,1,0:T(8,128)S(1)}, f32[4,2,2,16,128]{4,3,2,1,0:T(8,128)S(1)}, u32[]{:S(2)}, u32[]{:S(2)}) collective-permute-start(f32[4,2,2,16,128]{4,3,2,1,0:T(8,128)S(1)} %dynamic-slice_bitcast_fusion), channel_id=1, source_target_pairs={{0,1},{1,0},{2,3},{3,2},{4,5},{5,4},{6,7},{7,6},{8,9},{9,8},{10,11... | collective-permute-start | bytes 393224 | tf_op jit(solution)/shard_map/ppermute | solution.py:26
  966.7 105.0 %collective-permute-start.90 = (bf16[4,128,512]{2,1,0:T(8,128)(2,1)}, bf16[4,128,512]{2,1,0:T(8,128)(2,1)}, u32[]{:S(2)}, u32[]{:S(2)}) collective-permute-start(bf16[4,128,512]{2,1,0:T(8,128)(2,1)} %fusion.177), channel_id=1, source_target_pairs={{0,4},{2,6},{4,0},{6,2},{8,12},{10,14},{12,8},{14,10},{16,20},{18,... | collective-permute-start | bytes 1572872 | tf_op jit(solution)/shard_map/ppermute | solution.py:26
  1033.9 27.2 %collective-permute-start.105 = (bf16[128,1024]{1,0:T(8,128)(2,1)S(1)}, bf16[128,1024]{1,0:T(8,128)(2,1)S(1)}, u32[]{:S(2)}, u32[]{:S(2)}) collective-permute-start(bf16[128,1024]{1,0:T(8,128)(2,1)S(1)} %get-tuple-element.465), channel_id=1, source_target_pairs={{0,24},{2,26},{4,28},{6,30},{8,16},{10,18},{12,20},{14,22},{16,8},... | collective-permute-start | bytes 786440 | tf_op jit(solution)/shard_map/ppermute | solution.py:26
  1070.4 46.8 %collective-permute-start.101 = (f32[64,1024]{1,0:T(8,128)S(1)}, f32[64,1024]{1,0:T(8,128)S(1)}, u32[]{:S(2)}, u32[]{:S(2)}) collective-permute-start(f32[64,1024]{1,0:T(8,128)S(1)} %get-tuple-element.547), channel_id=1, source_target_pairs={{0,1},{1,0},{2,3},{3,2},{4,5},{5,4},{6,7},{7,6},{8,9},{9,8},{10,11... | collective-permute-start | bytes 786440 | tf_op jit(solution)/shard_map/ppermute | solution.py:26
  1071.7 46.4 %collective-permute-start.106 = (f32[64,1024]{1,0:T(8,128)S(1)}, f32[64,1024]{1,0:T(8,128)S(1)}, u32[]{:S(2)}, u32[]{:S(2)}) collective-permute-start(f32[64,1024]{1,0:T(8,128)S(1)} %get-tuple-element.545), channel_id=1, source_target_pairs={{0,1},{1,0},{2,3},{3,2},{4,5},{5,4},{6,7},{7,6},{8,9},{9,8},{10,11... | collective-permute-start | bytes 786440 | tf_op jit(solution)/shard_map/ppermute | solution.py:26
  1082.8 31.8 %collective-permute-start.94 = (bf16[128,1024]{1,0:T(8,128)(2,1)S(1)}, bf16[128,1024]{1,0:T(8,128)(2,1)S(1)}, u32[]{:S(2)}, u32[]{:S(2)}) collective-permute-start(bf16[128,1024]{1,0:T(8,128)(2,1)S(1)} %get-tuple-element.471), channel_id=1, source_target_pairs={{0,16},{2,18},{4,20},{6,22},{8,24},{10,26},{12,28},{14,30},{16,0},... | collective-permute-start | bytes 786440 | tf_op jit(solution)/shard_map/ppermute | solution.py:26
  1085.5 31.4 %collective-permute-start.93 = (bf16[128,1024]{1,0:T(8,128)(2,1)S(1)}, bf16[128,1024]{1,0:T(8,128)(2,1)S(1)}, u32[]{:S(2)}, u32[]{:S(2)}) collective-permute-start(bf16[128,1024]{1,0:T(8,128)(2,1)S(1)} %get-tuple-element.470), channel_id=1, source_target_pairs={{0,8},{2,10},{4,12},{6,14},{8,0},{10,2},{12,4},{14,6},{16,24},{18,... | collective-permute-start | bytes 786440 | tf_op jit(solution)/shard_map/ppermute | solution.py:26
  1105.2 31.2 %collective-permute-start.80 = (bf16[256,2048]{1,0:T(8,128)(2,1)}, bf16[256,2048]{1,0:T(8,128)(2,1)}, u32[]{:S(2)}, u32[]{:S(2)}) collective-permute-start(bf16[256,2048]{1,0:T(8,128)(2,1)} %add_convert_fusion.1), channel_id=1, source_target_pairs={{8,0},{10,2},{12,4},{14,6},{16,8},{18,10},{20,12},{22,14},{24,16},... | collective-permute-start | bytes 3145736 | tf_op jit(solution)/shard_map/ppermute | solution.py:337
  (210 other events, 3188.3 us)
Sparse Core Ops, SparseCore 0:
  12.4 116.9 all-gather.12
  132.1 105.0 all-gather.10
  238.8 12.7 all-gather.6
  253.0 24.0 all-gather.8
  847.1 162.6 reduce-scatter.1

commit v3 on v2

--- a/solution.py
+++ b/solution.py
@@ -304,9 +304,8 @@
 
         return side(bit_of(b)), side(1 - bit_of(b))
 
-    def scatter_rest(stay, right, arrived, order):
-        columns = right.shape[1]
-        now = contract_rows(stay, right) + arrived.astype(f32)
+    def scatter_rest(now, order):
+        columns = now.shape[1]
         axes = [b for b in reversed(range(bits)) if b != order[0]]
         rows = width // owners
         for b in order[1:]:
@@ -328,16 +327,6 @@
     descending = list(range(bits))[::-1]
     ascending = list(range(bits))
 
-    def step_up(block, planes):
-        return lax.ppermute(
-            block, "expert", [(p * ring + i, (p + 1) * ring + i) for p in planes for i in range(ring)]
-        )
-
-    def step_down(block, planes):
-        return lax.ppermute(
-            block, "expert", [(p * ring + i, (p - 1) * ring + i) for p in planes for i in range(ring)]
-        )
-
     rows_dev = width // devices
     small = jnp.concatenate(
         [
@@ -354,15 +343,6 @@
     lanes = 128
     small_rows = -(-cut[-1] // (lanes * 16)) * 16
     small = jnp.pad(small, (0, small_rows * lanes - cut[-1])).reshape(small_rows, lanes)
-    small_pair = in_order(core, small, swap(small, "fsdp", 1), 0)
-    small_all = gather_plane(gather_planes(small_pair), descending)
-    small_all = small_all.reshape(devices, small_rows * lanes)
-    first_gain = small_all[:, cut[0] : cut[1]].reshape(width).astype(f32)
-    second_gain = small_all[:, cut[1] : cut[2]].reshape(width).astype(f32)
-    query_scale = small_all[:, cut[2] : cut[3]].reshape(HEAD).astype(f32)
-    key_scale = small_all[:, cut[3] : cut[4]].reshape(HEAD).astype(f32)
-    router_full = small_all[:, cut[4] : cut[5]].reshape(width, owners)
-
     other_chip = swap(hidden_in, "expert", 1)
     hidden_own_peer = swap(hidden_in, "fsdp", 1)
     hidden_other_peer = swap(other_chip, "fsdp", 1)
@@ -376,8 +356,12 @@
     shards = in_order(core, mine, theirs, 1)
     query_own = gather_owners(shards[0])
     output_own = gather_owners(shards[3])
-    key_first = gather_planes(shards[1])
-    value_first = gather_planes(shards[2])
+    small_pair = in_order(core, small, swap(small, "fsdp", 1), 0).reshape(-1, half)
+    small_tall = -(-small_pair.shape[0] // 16) * 16
+    small_pair = jnp.pad(small_pair, ((0, small_tall - small_pair.shape[0]), (0, 0)))
+    key_tall = shards.shape[1] + small_tall
+    firsts = gather_planes(jnp.concatenate([shards[1], small_pair, shards[2]], axis=0))
+    firsts = firsts.reshape(PLANES, key_tall + shards.shape[1], half)
 
     inner_now = lax.all_gather(expert_inner, "fsdp", axis=1, tiled=True)[0]
     outer_now = lax.all_gather(expert_outer, "fsdp", axis=1, tiled=True)[0]
@@ -397,7 +381,6 @@
     key_live = positions < length
     tables = rotary_tables(positions)
     live_lanes = jnp.broadcast_to(key_live.astype(f32)[:, None], (span, HEAD))
-    scales = jnp.pad(jnp.stack([query_scale, key_scale]), ((0, 6), (0, 0)))
     expert_range = jnp.arange(owners, dtype=jnp.int32)
     hot = expert_ids[:, :, None] == expert_range[None, None, :]
     chosen = jnp.any(hot, axis=1)
@@ -423,25 +406,8 @@
 
     last = PLANES - 1
 
-    def by_plane(*choices):
-        out = choices[-1]
-        for p in reversed(range(len(choices) - 1)):
-            out = jnp.where(plane == p, choices[p], out)
-        return out
-
     def planes_of(block):
-        up1 = step_up(block, range(last))
-        down1 = step_down(block, range(1, PLANES))
-        up2 = step_up(up1, range(1, last))
-        down2 = step_down(down1, range(1, last))
-        up3 = step_up(up2, [2])
-        down3 = step_down(down2, [1])
-        return [
-            block,
-            jnp.where(plane == 0, down1, up1),
-            by_plane(down2, down1, down1, up2),
-            by_plane(down3, down2, up2, up3),
-        ]
+        return [block] + [swap(block, "expert", d * ring) for d in range(1, PLANES)]
 
     def exchange(rows):
         return [rows[:capacity]] + [
@@ -449,9 +415,19 @@
         ]
 
     up_wide = widened(upstream_low, rank_of.astype(bf16))
-    up_wide, key_first, value_first = lax.optimization_barrier((up_wide, key_first, value_first))
-    key_own = gather_plane(key_first, descending)
-    value_own = gather_plane(value_first, ascending)
+    up_wide, firsts = lax.optimization_barrier((up_wide, firsts))
+    key_all = gather_plane(firsts[:, :key_tall].reshape(-1, half), descending)
+    value_own = gather_plane(firsts[:, key_tall:].reshape(-1, half), ascending)
+    key_all = key_all.reshape(owners, key_tall, half)
+    key_own = key_all[:, : shards.shape[1]].reshape(width, half)
+    small_all = key_all[:, shards.shape[1] :].reshape(owners, small_tall * half)
+    small_all = small_all[:, : sharers * small_rows * lanes].reshape(devices, -1)
+    first_gain = small_all[:, cut[0] : cut[1]].reshape(width).astype(f32)
+    second_gain = small_all[:, cut[1] : cut[2]].reshape(width).astype(f32)
+    query_scale = small_all[:, cut[2] : cut[3]].reshape(HEAD).astype(f32)
+    key_scale = small_all[:, cut[3] : cut[4]].reshape(HEAD).astype(f32)
+    router_full = small_all[:, cut[4] : cut[5]].reshape(width, owners)
+
     output_peer = swap(output_own, "fsdp", 1)
     up_planes = planes_of(up_wide)
     up_planes, key_late, value_late = lax.optimization_barrier((up_planes, key_own, value_own))
@@ -465,7 +441,7 @@
         return [
             [blocks[d][:capacity]]
             + [got[j][d * capacity : (d + 1) * capacity] for j in range(1, ring)]
-            for d in range(PLANES)
+            for d in range(len(blocks))
         ]
 
     pickers, up_picked = [], []
@@ -477,6 +453,7 @@
         up_picked.append(contract_rows(picker, up_planes[d][:, :width], bf16))
     up_arrived = exchange_all(up_picked)
 
+    scales = jnp.pad(jnp.stack([query_scale, key_scale]), ((0, 6), (0, 0)))
     hidden_f = hidden_seq.astype(f32)
     first_normed, first_inverse = rms_scale(hidden_f, first_gain)
     first_low = first_normed.astype(bf16)
@@ -513,13 +490,20 @@
     plane_rows = ring * capacity
 
     hidden_up = contract_cols(up_rows, outer_now)
-    row_inputs, hidden_gated, both_grad, rows_back = [], [], [], []
+    row_inputs, hidden_gated, both_grad, rows_back, rows_out = [], [], [], [], []
+    out_arrived = [None] * PLANES
     for d in range(PLANES):
         rows = exchange(picked[d])
         if d < last:
             rows, picked[d + 1] = lax.optimization_barrier((rows, picked[d + 1]))
         if d == 0:
-            rows, left_x, left_y = lax.optimization_barrier((rows, left_x, left_y))
+            rows, left_x, left_y, attended_peer = lax.optimization_barrier(
+                (rows, left_x, left_y, attended_peer)
+            )
+        elif d == 1 or d == last:
+            early = 0 if d == 1 else 1
+            out_rows, rows = lax.optimization_barrier((rows_out[early], rows))
+            out_arrived[early] = exchange(out_rows)
         rows = jnp.concatenate(rows, axis=0)
         if d:
             rows, rows_back[-1] = lax.optimization_barrier((rows, rows_back[-1]))
@@ -551,6 +535,7 @@
         rows_back.append(
             contract_cols(grads, inner_pad, bf16) + jnp.pad(part_of, ((0, 0), (width, 0)))
         )
+        rows_out.append(matmul(gated, outer_now).astype(bf16))
         row_inputs.append(rows[:, :width])
         hidden_gated.append(gated)
         both_grad.append(grads)
@@ -559,30 +544,28 @@
         block = rows_back[d]
         if d < last:
             block, arrived[d + 1] = lax.optimization_barrier((block, arrived[d + 1]))
+        else:
+            block, out_arrived[:2] = lax.optimization_barrier((block, out_arrived[:2]))
         arrived[d] = exchange(block)
     arrived[last], row_inputs, hidden_gated, both_grad = lax.optimization_barrier(
         (arrived[last], row_inputs, hidden_gated, both_grad)
     )
-    rows_out = [matmul(gated, outer_now).astype(bf16) for gated in hidden_gated]
     row_inputs = jnp.concatenate(row_inputs, axis=0)
     hidden_gated = jnp.concatenate(hidden_gated, axis=0)
     both_grad = jnp.concatenate(both_grad, axis=0)
 
-    def bring_back(arrived):
-        parts = [None] * PLANES
+    def at_planes(arrived):
+        came = [None] * PLANES
         for d in reversed(range(PLANES)):
-            parts[d] = matmul(pickers[d], jnp.concatenate(arrived[d], axis=0))
-        near, middle, far_off = parts[1:]
-        end = (plane == 0) | (plane == last)
-        send = far_off.astype(bf16)
-        up = step_up(send, [0]).astype(f32)
-        down = step_down(send, [last]).astype(f32)
-        send = jnp.where(end, middle, far_off + up + down).astype(bf16)
-        up = step_up(send, [0, 1]).astype(f32)
-        down = step_down(send, [2, 3]).astype(f32)
-        up = step_up(jnp.where(plane == 0, near, middle + up).astype(bf16), [0, 1, 2])
-        down = step_down((near + down).astype(bf16), [1, 2, 3])
-        return parts[0] + up.astype(f32) + down.astype(f32)
+            part = matmul(pickers[d], jnp.concatenate(arrived[d], axis=0))
+            came[d] = swap(part.astype(bf16), "expert", d * ring) if d else part
+        return came
+
+    def added(came):
+        total = came[0]
+        for part in came[1:]:
+            total = total + part.astype(f32)
+        return total
 
     eff_half = EFF // 2
     inner_sent = contract_rows(pick(row_inputs, (1 - core) * half, half), both_grad, bf16)
@@ -591,13 +574,13 @@
         pick(hidden_gated, (1 - core) * eff_half, eff_half), up_rows, bf16
     )
     outer_kept = contract_rows(pick(hidden_gated, core * eff_half, eff_half), up_rows)
-    back = bring_back(arrived)
-    back, rows_out, inner_sent, inner_kept, outer_sent, outer_kept = lax.optimization_barrier(
-        (back, rows_out, inner_sent, inner_kept, outer_sent, outer_kept)
+    back = added(at_planes(arrived))
+    back, late_out, inner_sent, inner_kept, outer_sent, outer_kept = lax.optimization_barrier(
+        (back, rows_out[2:], inner_sent, inner_kept, outer_sent, outer_kept)
     )
     inner_grad = inner_kept + swap(inner_sent, "fsdp", 1).astype(f32)
     outer_grad = outer_kept + swap(outer_sent, "fsdp", 1).astype(f32)
-    out_arrived = exchange_all(rows_out)
+    out_arrived[2:] = exchange_all(late_out)
     mixed_grad = back[:, :width]
     gate_grad = (
         back[:, width : width + owners]
@@ -637,43 +620,26 @@
     )
     quarter = half // 2
     chip = 2 * tokens
-    sent = [
-        contract_rows(left_y[1], value_low_grad, bf16),
-        contract_rows(left_x[1], key_low_grad, bf16),
+    y_bit = bits - 1
+
+    value_sent = contract_rows(left_y[1], value_low_grad, bf16)
+    key_sent = contract_rows(left_x[1], key_low_grad, bf16)
+    value_sent, key_sent, query_late, key_grad_late, value_grad_late = lax.optimization_barrier(
+        (value_sent, key_sent, query_low_grad, key_low_grad, value_low_grad)
+    )
+    value_came = swap(value_sent, "expert", 1 << y_bit)
+    key_came = swap(key_sent, "expert", 1)
+    out_came = at_planes(out_arrived)
+    query_sent = [
+        contract_rows(left_x[1][:chip], query_late[:, :quarter], bf16),
+        contract_rows(left_y[1][:chip], query_late[:, quarter:], bf16),
     ]
-    sent, query_low_grad = lax.optimization_barrier((sent, query_low_grad))
-    sent += [
-        contract_rows(left_x[1][:chip], query_low_grad[:, :quarter], bf16),
-        contract_rows(left_y[1][:chip], query_low_grad[:, quarter:], bf16),
+    value_kept = contract_rows(left_y[0], value_grad_late)
+    key_kept = contract_rows(left_x[0], key_grad_late)
+    kept = [
+        contract_rows(left_x[0][:chip], query_late[:, :quarter]),
+        contract_rows(left_y[0][:chip], query_late[:, quarter:]),
     ]
-    sent, query_late, key_grad_late, value_grad_late = lax.optimization_barrier(
-        (sent, query_low_grad, key_low_grad, value_low_grad)
-    )
-    value_came = swap(sent[0], "expert", 1 << (bits - 1))
-    key_came = swap(sent[1], "expert", 1)
-    out_arrived, value_came, key_came = lax.optimization_barrier(
-        (out_arrived, value_came, key_came)
-    )
-    sent, value_came, key_came = lax.optimization_barrier((sent, value_came, key_came))
-    query_x_came = swap(sent[2], "expert", 1)
-    query_y_came = swap(sent[3], "expert", 1 << (bits - 1))
-    value_block = scatter_planes(scatter_rest(left_y[0], value_low_grad, value_came, descending))
-    key_block = scatter_planes(scatter_rest(left_x[0], key_low_grad, key_came, ascending))
-    query_block = scatter_planes(
-        jnp.concatenate(
-            [
-                scatter_rest(
-                    left_x[0][:chip], query_low_grad[:, :quarter], query_x_came, ascending
-                ),
-                scatter_rest(
-                    left_y[0][:chip], query_low_grad[:, quarter:], query_y_came, descending
-                ),
-            ],
-            axis=2,
-        )
-    )
-    layer_out = (residual + bring_back(out_arrived)).astype(bf16)
-
     kv_grad = contract_cols(key_grad_late, key_late) + contract_cols(value_grad_late, value_late)
     q_grad = contract_cols(query_late, query_own)
     own_part = kv_grad[:tokens] + q_grad[:tokens]
@@ -683,7 +649,31 @@
     crossed = swap(jnp.concatenate([peer_part, far_peer], axis=0).astype(bf16), "fsdp", 1)
     own_part = own_part + crossed[:tokens].astype(f32)
     far_part = (far_part + crossed[tokens:].astype(f32)).astype(bf16)
+    value_came, key_came, out_came, query_sent, value_kept, key_kept, kept, far_part = (
+        lax.optimization_barrier(
+            (value_came, key_came, out_came, query_sent, value_kept, key_kept, kept, far_part)
+        )
+    )
+
+    query_came = [swap(query_sent[0], "expert", 1), swap(query_sent[1], "expert", 1 << y_bit)]
+    value_now = scatter_rest(value_kept + value_came.astype(f32), descending)
+    key_now = scatter_rest(key_kept + key_came.astype(f32), ascending)
     far_back = swap(far_part, "expert", 1)
+    query_came, value_now, key_now, far_back = lax.optimization_barrier(
+        (query_came, value_now, key_now, far_back)
+    )
+
+    query_now = [
+        scatter_rest(kept[0] + query_came[0].astype(f32), ascending),
+        scatter_rest(kept[1] + query_came[1].astype(f32), descending),
+    ]
+    pair_block = scatter_planes(jnp.concatenate([value_now, key_now], axis=2))
+    query_now, pair_block = lax.optimization_barrier((query_now, pair_block))
+
+    query_block = scatter_planes(jnp.concatenate(query_now, axis=2))
+    value_block, key_block = pair_block[:, :half], pair_block[:, half:]
+    layer_out = (residual + added(out_came)).astype(bf16)
+
     normed_grad = own_part + far_back.astype(f32)
     hidden_part, first_terms = rms_back(
         hidden_f[:tokens], first_inverse[:tokens], first_gain, normed_grad

time: 1160 us -> 1250 us (1.078)
  waiting for transfers between devices: 417 us -> 468 us
  local copies, waits for them, and re-layouts: 97.4 us -> 120 us
  starting transfers between devices: 175 us -> 193 us
    ppermute x86 -> x93, waiting for transfers between devices: 316 us -> 452 us  [swap(): return lax.ppermute(block, axis, [(i, i ^ mask) for i in range(count)])]
    ppermute x24 -> x0, waiting for transfers between devices: 99.4 us -> none  [the longest x12 95.4 us: step_down(): lax.ppermute(block, 'expert', [(p * ring + i, (p - 1) * ring + i) for p i...]
    ppermute x86 -> x93, starting transfers between devices: 119 us -> 193 us  [swap(): return lax.ppermute(block, axis, [(i, i ^ mask) for i in range(count)])]
    ppermute x24 -> x0, starting transfers between devices: 55.7 us -> none  [the longest x12 40.2 us: step_up(): lax.ppermute(block, 'expert', [(p * ring + i, (p + 1) * ring + i) for p i...]
    all_gather x2, waiting for transfers between devices: 0.01 us -> 14.1 us  [gather_owners(): return lax.all_gather(block, 'expert', axis=0, tiled=True)]
    unnamed x351 -> x382, local copies, waits for them, and re-layouts: 39.2 us -> 49.8 us
  transfers between devices with their start and end apart: 115 -> 98, of which waited for: 42 -> 36; matrix products, arithmetic and copies ran while one was open for 34% -> 32% of each run, Pallas kernels for 6% -> 5%
where the time goes in v3:
time: 1250 us; the launch traced here: 1240 us
  waiting for transfers between devices  468 us (37%)
  matrix products  254 us (20%)
  starting transfers between devices  193 us (15%)
  other arithmetic  127 us (10%)
  local copies, waits for them, and re-layouts  120 us (10%)
  Pallas kernels  64.2 us (5%)
  between operations  17.2 us (1%)
    ppermute x93, waiting for transfers between devices, swap(): return lax.ppermute(block, axis, [(i, i ^ mask) for i in range(count)])  452 us
    ppermute x93, starting transfers between devices, swap(): return lax.ppermute(block, axis, [(i, i ^ mask) for i in range(count)])  193 us
    dot_general x22, matrix products, contract_rows(): lax.dot_general(left, right, (((0,), (0,)), ((), ())), preferred_element_...  95.4 us
    dot_general x26, matrix products, matmul(): return jnp.dot(left, right, preferred_element_type=f32)  82 us
    dot_general x11, matrix products, contract_cols(): lax.dot_general(left, right, (((1,), (1,)), ((), ())), preferred_element_...  76.5 us
    unnamed x382, local copies, waits for them, and re-layouts  49.8 us
    pallas_call x1, Pallas kernels, attention_backward(): pl.pallas_call(kernel, grid=(heads,), in_specs=[column(queries), column(s...  35.8 us
    pallas_call x1, Pallas kernels, attention_forward(): pl.pallas_call(kernel, grid=(heads,), in_specs=[column(queries), column(s...  28.4 us
  transfers between devices with their start and end apart: 98, of which 36 were waited for; matrix products, arithmetic and copies ran while one was open for 32% of the time, Pallas kernels for 5%

profile of v3, /device:TPU:0, one launch (start us, length us, event | category | flops | bytes accessed | tf_op | source)
XLA Modules:
  0.0 1243.4 jit_solution(11033353826962152473)
XLA Ops:
  36.3 41.2 %collective-permute-done.6 = bf16[272,1024]{1,0:T(8,128)(2,1)} collective-permute-done((bf16[272,1024]{1,0:T(8,128)(2,1)}, bf16[272,1024]{1,0:T(8,128)(2,1)}, u32[]{:S(2)}, u32[]{:S(2)}) %collective-permute-start.6) | collective-permute-done | bytes 557088 | tf_op jit(solution)/shard_map/ppermute | solution.py:26
  86.8 34.3 %collective-permute-done.10 = bf16[4,1,1,128,1024]{4,3,0,2,1:T(8,128)(2,1)} collective-permute-done((bf16[4,1,1,128,1024]{4,3,0,2,1:T(8,128)(2,1)S(1)}, bf16[4,1,1,128,1024]{4,3,0,2,1:T(8,128)(2,1)}, u32[]{:S(2)}, u32[]{:S(2)}) %collective-permute-start.10) | collective-permute-done | bytes 1048608 | tf_op jit(solution)/shard_map/ppermute | solution.py:26
  135.1 6.9 collective-permute-start.14
  150.3 4.9 maximum_convert_fusion
  155.1 16.8 %collective-permute-done.11 = bf16[4,1,2,128,1024]{4,3,0,2,1:T(8,128)(2,1)S(1)} collective-permute-done((bf16[4,1,2,128,1024]{4,3,0,2,1:T(8,128)(2,1)S(1)}, bf16[4,1,2,128,1024]{4,3,0,2,1:T(8,128)(2,1)S(1)}, u32[]{:S(2)}, u32[]{:S(2)}) %collective-permute-start.11) | collective-permute-done | bytes 2097184 | tf_op jit(solution)/shard_map/ppermute | solution.py:26
  175.1 4.8 collective-permute-done.9
  192.4 8.0 convolution_convert_fusion.22.v_ref
  200.3 25.0 %collective-permute-done.15 = bf16[256,2176]{1,0:T(8,128)(2,1)} collective-permute-done((bf16[256,2176]{1,0:T(8,128)(2,1)}, bf16[256,2176]{1,0:T(8,128)(2,1)}, u32[]{:S(2)}, u32[]{:S(2)}) %collective-permute-start.15) | collective-permute-done | bytes 1114144 | tf_op jit(solution)/shard_map/ppermute | solution.py:26
  255.5 6.5 fusion.257.k_ref
  277.5 31.1 %collective-permute-done.19 = bf16[512,2048]{1,0:T(8,128)(2,1)} collective-permute-done((bf16[512,2048]{1,0:T(8,128)(2,1)}, bf16[512,2048]{1,0:T(8,128)(2,1)}, u32[]{:S(2)}, u32[]{:S(2)}) %collective-permute-start.19) | collective-permute-done | bytes 2097184 | tf_op jit(solution)/shard_map/ppermute | solution.py:26
  311.5 14.1 %all-gather.11.cloned.1.call-done = bf16[1,2048,1024]{2,1,0:T(8,128)(2,1)} async-done(((bf16[1,128,1024]{2,1,0:T(8,128)(2,1)}), bf16[1,2048,1024]{2,1,0:T(8,128)(2,1)}) %all-gather.11.cloned.1.call-update) | async-done | bytes 4194320 | tf_op jit(solution)/shard_map/all_gather | solution.py:276
  325.6 5.3 fusion.14.q_ref
  331.1 28.4 %attention_forward.1 = (bf16[512,1024]{1,0:T(8,128)(2,1)S(1)}, f32[8,8,512]{2,1,0:T(8,128)S(1)}) custom-call(f32[512,1024]{1,0:T(8,128)S(1)} %fusion.14.q_ref, f32[1024,1024]{1,0:T(8,128)S(1)} %copy-done, bf16[1024,1024]{1,0:T(8,128)(2,1)S(1)} %convolution_convert_fusion.22.v_ref, f32[2,1024,128]{2,1,0:T(8,128)S(1)} %pad_maximum_fusion.15.table_ref, ...), custom_call_target="tpu_custom_call" | custom-call | tf_op jit(solution)/shard_map/attention_forward/pallas_call | solution.py:109
  376.0 16.5 %collective-permute-start.23 = (bf16[256,2176]{1,0:T(8,128)(2,1)}, bf16[256,2176]{1,0:T(8,128)(2,1)}, u32[]{:S(2)}, u32[]{:S(2)}) collective-permute-start(bf16[256,2176]{1,0:T(8,128)(2,1)} %pad_maximum_fusion.13), channel_id=1, source_target_pairs={{0,8},{2,10},{4,12},{6,14},{8,0},{10,2},{12,4},{14,6},{16,24},{18,... | collective-permute-start | bytes 3342344 | tf_op jit(solution)/shard_map/ppermute | solution.py:26
  402.0 14.6 %fusion.10 = f32[2048,1024]{0,1:T(8,128)} fusion(bf16[2048,2048]{1,0:T(8,128)(2,1)} %copy-done.129, bf16[1,1024,2048]{2,1,0:T(8,128)(2,1)} %all-gather.7.cloned.1.call-done), kind=kOutput, calls=%fused_computation.25 | convolution fusion | flops 8589934592 | bytes 20971520 | tf_op jit(solution)/shard_map/dot_general | solution.py:36
  432.3 8.4 fusion.37
  441.7 5.2 multiply_convert_fusion.11
  455.8 38.7 %collective-permute-done.28 = bf16[256,2176]{1,0:T(8,128)(2,1)} collective-permute-done((bf16[256,2176]{1,0:T(8,128)(2,1)}, bf16[256,2176]{1,0:T(8,128)(2,1)}, u32[]{:S(2)}, u32[]{:S(2)}) %collective-permute-start.28) | collective-permute-done | bytes 1114144 | tf_op jit(solution)/shard_map/ppermute | solution.py:26
  499.5 10.0 fusion.20
  517.0 8.3 fusion.34
  525.5 5.2 multiply_convert_fusion.8
  534.1 10.4 fusion.21
  554.2 6.1 collective-permute-done.29
  560.3 12.0 collective-permute-done.30
  572.6 5.1 fusion.31
  577.8 5.2 multiply_convert_fusion.6
  586.4 10.2 fusion.22
  600.3 6.1 fusion.45
  606.4 6.0 collective-permute-done.33
  613.8 17.4 %collective-permute-done.34 = bf16[128,2176]{1,0:T(8,128)(2,1)S(1)} collective-permute-done((bf16[128,2176]{1,0:T(8,128)(2,1)S(1)}, bf16[128,2176]{1,0:T(8,128)(2,1)S(1)}, u32[]{:S(2)}, u32[]{:S(2)}) %collective-permute-start.34) | collective-permute-done | bytes 557088 | tf_op jit(solution)/shard_map/ppermute | solution.py:26
  631.3 5.1 fusion.28
  636.6 5.2 multiply_convert_fusion.4
  648.6 8.8 fusion.23
  658.6 14.3 %collective-permute-done.40 = bf16[128,2048]{1,0:T(8,128)(2,1)S(1)} collective-permute-done((bf16[128,2048]{1,0:T(8,128)(2,1)S(1)}, bf16[128,2048]{1,0:T(8,128)(2,1)S(1)}, u32[]{:S(2)}, u32[]{:S(2)}) %collective-permute-start.40) | collective-permute-done | bytes 524320 | tf_op jit(solution)/shard_map/ppermute | solution.py:26
  683.3 6.5 collective-permute-done.43
  700.3 13.3 %fusion.16 = f32[1024,2048]{1,0:T(8,128)} fusion(bf16[2048,2048]{0,1:T(8,128)(2,1)S(1)} %constant_dynamic-update-slice_fusion.24, bf16[2048,2048]{1,0:T(8,128)(2,1)} %copy-done.113, s32[]{:T(128)S(6)} %select_n.387), kind=kOutput, calls=%fused_computation.34 | convolution fusion | flops 8589934592 | bytes 20971524 | tf_op jit(solution)/shard_map/dot_general | solution.py:30
  713.6 12.4 %fusion.24 = bf16[1024,2048]{1,0:T(8,128)(2,1)} fusion(bf16[2048,2048]{0,1:T(8,128)(2,1)S(1)} %constant_dynamic-update-slice_fusion.24, bf16[2048,2048]{1,0:T(8,128)(2,1)} %copy-done.113, s32[]{:T(128)S(6)} %select_n.388), kind=kOutput, calls=%fused_computation.48 | convolution fusion | flops 8592031744 | bytes 16777220 | tf_op jit(solution)/shard_map/dot_general | solution.py:30
  732.4 9.4 collective-permute-done.45
  741.9 10.1 collective-permute-done.46
  755.7 9.6 fusion.119
  766.2 7.6 collective-permute-start.55
  774.6 13.4 %collective-permute-start.54 = (bf16[256,2176]{1,0:T(8,128)(2,1)S(1)}, bf16[256,2176]{1,0:T(8,128)(2,1)S(1)}, u32[]{:S(2)}, u32[]{:S(2)}) collective-permute-start(bf16[256,2176]{1,0:T(8,128)(2,1)S(1)} %convolution_convert_fusion.10), channel_id=1, source_target_pairs={{0,8},{2,10},{4,12},{6,14},{8,0},{10,2},{12,4},{14,6},{16,24},{18,... | collective-permute-start | bytes 3342344 | tf_op jit(solution)/shard_map/ppermute | solution.py:26
  791.7 5.7 convolution_convert_fusion.16
  797.5 15.6 %collective-permute-done.55 = bf16[256,2176]{1,0:T(8,128)(2,1)S(1)} collective-permute-done((bf16[256,2176]{1,0:T(8,128)(2,1)S(1)}, bf16[256,2176]{1,0:T(8,128)(2,1)S(1)}, u32[]{:S(2)}, u32[]{:S(2)}) %collective-permute-start.55) | collective-permute-done | bytes 1114144 | tf_op jit(solution)/shard_map/ppermute | solution.py:26
  813.0 7.5 collective-permute-done.54
  850.0 6.2 convolution_convert_fusion.11
  860.1 35.8 %attention_backward.1 = (bf16[512,1024]{1,0:T(8,128)(2,1)S(1)}, bf16[1024,1024]{1,0:T(8,128)(2,1)S(1)}, bf16[1024,1024]{1,0:T(8,128)(2,1)S(1)}, f32[2,8,128]{2,1,0:T(8,128)S(1)}) custom-call(f32[512,1024]{1,0:T(8,128)S(1)} %copy-done.2, f32[1024,1024]{1,0:T(8,128)} %fusion.257.k_ref, bf16[1024,1024]{1,0:T(8,128)(2,1)S(1)} %convolution_convert_fusion.22.v_ref, ...), custom_call_target="tpu_custom_call" | custom-call | tf_op jit(solution)/shard_map/attention_backward/pallas_call | solution.py:192
  903.8 13.8 %collective-permute-done.57 = bf16[256,2048]{1,0:T(8,128)(2,1)} collective-permute-done((bf16[256,2048]{1,0:T(8,128)(2,1)}, bf16[256,2048]{1,0:T(8,128)(2,1)}, u32[]{:S(2)}, u32[]{:S(2)}) %collective-permute-start.57) | collective-permute-done | bytes 1048608 | tf_op jit(solution)/shard_map/ppermute | solution.py:26
  919.0 5.6 convolution_convert_fusion.20
  928.4 6.9 fusion.261
  935.3 7.3 convolution_add_fusion.1
  954.2 9.5 collective-permute-start.62
  976.4 8.6 collective-permute-done.66
  985.0 43.1 %collective-permute-start.64 = (bf16[256,2048]{1,0:T(8,128)(2,1)S(1)}, bf16[256,2048]{1,0:T(8,128)(2,1)S(1)}, u32[]{:S(2)}, u32[]{:S(2)}) collective-permute-start(bf16[256,2048]{1,0:T(8,128)(2,1)S(1)} %convolution_convert_fusion.19), channel_id=1, source_target_pairs={{0,8},{2,10},{4,12},{6,14},{8,0},{10,2},{12,4},{14,6},{16,24},{18,... | collective-permute-start | bytes 3145736 | tf_op jit(solution)/shard_map/ppermute | solution.py:26
  1035.7 13.3 %collective-permute-done.65 = bf16[256,2048]{1,0:T(8,128)(2,1)S(1)} collective-permute-done((bf16[256,2048]{1,0:T(8,128)(2,1)S(1)}, bf16[256,2048]{1,0:T(8,128)(2,1)S(1)}, u32[]{:S(2)}, u32[]{:S(2)}) %collective-permute-start.65) | collective-permute-done | bytes 1048608 | tf_op jit(solution)/shard_map/ppermute | solution.py:26
  1048.9 22.4 %collective-permute-done.64 = bf16[256,2048]{1,0:T(8,128)(2,1)S(1)} collective-permute-done((bf16[256,2048]{1,0:T(8,128)(2,1)S(1)}, bf16[256,2048]{1,0:T(8,128)(2,1)S(1)}, u32[]{:S(2)}, u32[]{:S(2)}) %collective-permute-start.64) | collective-permute-done | bytes 1048608 | tf_op jit(solution)/shard_map/ppermute | solution.py:26
  1074.9 5.3 collective-permute-start.70
  1083.8 16.0 %collective-permute-done.71 = bf16[4,128,1024]{2,1,0:T(8,128)(2,1)} collective-permute-done((bf16[4,128,1024]{2,1,0:T(8,128)(2,1)S(1)}, bf16[4,128,1024]{2,1,0:T(8,128)(2,1)}, u32[]{:S(2)}, u32[]{:S(2)}) %collective-permute-start.71) | collective-permute-done | bytes 1048608 | tf_op jit(solution)/shard_map/ppermute | solution.py:26
  1106.6 20.1 %collective-permute-done.68 = bf16[1024,512]{1,0:T(8,128)(2,1)S(1)} collective-permute-done((bf16[1024,512]{1,0:T(8,128)(2,1)}, bf16[1024,512]{1,0:T(8,128)(2,1)S(1)}, u32[]{:S(2)}, u32[]{:S(2)}) %collective-permute-start.68) | collective-permute-done | bytes 1048608 | tf_op jit(solution)/shard_map/ppermute | solution.py:26
  1127.7 20.5 %collective-permute-done.72 = bf16[256,2048]{1,0:T(8,128)(2,1)S(1)} collective-permute-done((bf16[256,2048]{1,0:T(8,128)(2,1)S(1)}, bf16[256,2048]{1,0:T(8,128)(2,1)S(1)}, u32[]{:S(2)}, u32[]{:S(2)}) %collective-permute-start.72) | collective-permute-done | bytes 1048608 | tf_op jit(solution)/shard_map/ppermute | solution.py:26
  1161.3 10.2 add_bitcast_fusion
  1191.1 7.5 collective-permute-done.80
  1203.7 7.3 collective-permute-start.84
  1218.4 12.9 %collective-permute-done.85 = bf16[128,1024]{1,0:T(8,128)(2,1)S(1)} collective-permute-done((bf16[128,1024]{1,0:T(8,128)(2,1)S(1)}, bf16[128,1024]{1,0:T(8,128)(2,1)S(1)}, u32[]{:S(2)}, u32[]{:S(2)}) %collective-permute-start.85) | collective-permute-done | bytes 262176 | tf_op jit(solution)/shard_map/ppermute | solution.py:26
  (814 shorter events, 396.9 us)
Async XLA Ops:
  7.2 254.8 %all-gather.13.cloned.1.call-start = ((), (), s32[]{:S(2)}) async-start(), calls=%async_computation.5 | async-start | bytes 4456448 | tf_op jit(solution)/shard_map/all_gather | solution.py:276
  12.2 313.4 %all-gather.11.cloned.1.call-start = ((), (), s32[]{:S(2)}) async-start(), calls=%async_computation.4 | async-start | bytes 4456448 | tf_op jit(solution)/shard_map/all_gather | solution.py:276
  13.0 389.0 %all-gather.7.cloned.1.call-start = ((), (), s32[]{:S(2)}) async-start(), calls=%async_computation.1 | async-start | bytes 6291456 | tf_op jit(solution)/shard_map/all_gather | solution.py:367
  13.7 418.6 %all-gather.9.cloned.1.call-start = ((), (), s32[]{:S(2)}) async-start(), calls=%async_computation.2 | async-start | bytes 12582912 | tf_op jit(solution)/shard_map/all_gather | solution.py:366
  14.5 71.7 %collective-permute-start.1 = (bf16[256,2048]{1,0:T(8,128)(2,1)S(1)}, bf16[256,2048]{1,0:T(8,128)(2,1)S(1)}, u32[]{:S(2)}, u32[]{:S(2)}) collective-permute-start(bf16[256,2048]{1,0:T(8,128)(2,1)S(1)} %copy-done.19), channel_id=1, source_target_pairs={{0,2},{2,0},{4,6},{6,4},{8,10},{10,8},{12,14},{14,12},{16,18},{18,... | collective-permute-start | bytes 3145736 | tf_op jit(solution)/shard_map/ppermute | solution.py:26
  29.9 47.6 %collective-permute-start.6 = (bf16[272,1024]{1,0:T(8,128)(2,1)}, bf16[272,1024]{1,0:T(8,128)(2,1)}, u32[]{:S(2)}, u32[]{:S(2)}) collective-permute-start(bf16[272,1024]{1,0:T(8,128)(2,1)} %pad_maximum_fusion.20), channel_id=1, source_target_pairs={{0,16},{2,18},{4,20},{6,22},{8,24},{10,26},{12,28},{14,30},{16,0},... | collective-permute-start | bytes 1671176 | tf_op jit(solution)/shard_map/ppermute | solution.py:26
  32.5 45.0 %collective-permute-start.7 = (bf16[272,1024]{1,0:T(8,128)(2,1)}, bf16[272,1024]{1,0:T(8,128)(2,1)}, u32[]{:S(2)}, u32[]{:S(2)}) collective-permute-start(bf16[272,1024]{1,0:T(8,128)(2,1)} %pad_maximum_fusion.20), channel_id=1, source_target_pairs={{0,24},{2,26},{4,28},{6,30},{8,16},{10,18},{12,20},{14,22},{16,8},... | collective-permute-start | bytes 1671176 | tf_op jit(solution)/shard_map/ppermute | solution.py:26
  33.8 45.7 %collective-permute-start.5 = (bf16[272,1024]{1,0:T(8,128)(2,1)}, bf16[272,1024]{1,0:T(8,128)(2,1)}, u32[]{:S(2)}, u32[]{:S(2)}) collective-permute-start(bf16[272,1024]{1,0:T(8,128)(2,1)} %pad_maximum_fusion.20), channel_id=1, source_target_pairs={{0,8},{2,10},{4,12},{6,14},{8,0},{10,2},{12,4},{14,6},{16,24},{18,... | collective-permute-start | bytes 1671176 | tf_op jit(solution)/shard_map/ppermute | solution.py:26
  82.5 38.6 %collective-permute-start.10 = (bf16[4,1,1,128,1024]{4,3,0,2,1:T(8,128)(2,1)S(1)}, bf16[4,1,1,128,1024]{4,3,0,2,1:T(8,128)(2,1)}, u32[]{:S(2)}, u32[]{:S(2)}) collective-permute-start(bf16[4,1,1,128,1024]{4,3,0,2,1:T(8,128)(2,1)S(1)} %slice_bitcast_fusion.1), channel_id=1, source_target_pairs={{0,2},{2,0},{4,6},{6,4},{8,10},{10,8},{12,14},{14,12},{16,18},{18,... | collective-permute-start | bytes 3145736 | tf_op jit(solution)/shard_map/ppermute | solution.py:26
  83.6 44.1 %collective-permute-start.8 = (bf16[4,1,1,144,1024]{4,3,2,1,0:T(8,128)(2,1)}, bf16[4,1,1,144,1024]{4,3,2,1,0:T(8,128)(2,1)}, u32[]{:S(2)}, u32[]{:S(2)}) collective-permute-start(bf16[4,1,1,144,1024]{4,3,2,1,0:T(8,128)(2,1)} %slice_bitcast_fusion), channel_id=1, source_target_pairs={{0,4},{2,6},{4,0},{6,2},{8,12},{10,14},{12,8},{14,10},{16,20},{18,... | collective-permute-start | bytes 3538952 | tf_op jit(solution)/shard_map/ppermute | solution.py:26
  85.1 56.9 %collective-permute-start = (bf16[256,2048]{1,0:T(8,128)(2,1)S(1)}, bf16[256,2048]{1,0:T(8,128)(2,1)}, u32[]{:S(2)}, u32[]{:S(2)}) collective-permute-start(bf16[256,2048]{1,0:T(8,128)(2,1)S(1)} %copy-done.19), channel_id=1, source_target_pairs={{0,1},{1,0},{2,3},{3,2},{4,5},{5,4},{6,7},{7,6},{8,9},{9,8},{10,11... | collective-permute-start | bytes 3145736 | tf_op jit(solution)/shard_map/ppermute | solution.py:26
  85.1 1147.4 %reduce-scatter.2.cloned.1.call-start = ((), (), s32[]{:S(2)}) async-start(), calls=%async_computation.3 | async-start | bytes 4456448 | tf_op jit(solution)/shard_map/reduce_scatter | solution.py:612
  86.2 60.0 %collective-permute-start.2 = (bf16[256,2048]{1,0:T(8,128)(2,1)S(1)}, bf16[256,2048]{1,0:T(8,128)(2,1)S(1)}, u32[]{:S(2)}, u32[]{:S(2)}) collective-permute-start(bf16[256,2048]{1,0:T(8,128)(2,1)S(1)} %collective-permute-done.1), channel_id=1, source_target_pairs={{0,1},{1,0},{2,3},{3,2},{4,5},{5,4},{6,7},{7,6},{8,9},{9,8},{10,11... | collective-permute-start | bytes 3145736 | tf_op jit(solution)/shard_map/ppermute | solution.py:26
  122.9 49.0 %collective-permute-start.11 = (bf16[4,1,2,128,1024]{4,3,0,2,1:T(8,128)(2,1)S(1)}, bf16[4,1,2,128,1024]{4,3,0,2,1:T(8,128)(2,1)S(1)}, u32[]{:S(2)}, u32[]{:S(2)}) collective-permute-start(bf16[4,1,2,128,1024]{4,3,0,2,1:T(8,128)(2,1)S(1)} %maximum_select_fusion.4), channel_id=1, source_target_pairs={{0,4},{2,6},{4,0},{6,2},{8,12},{10,14},{12,8},{14,10},{16,20},{18,... | collective-permute-start | bytes 6291464 | tf_op jit(solution)/shard_map/ppermute | solution.py:26
  130.6 49.3 %collective-permute-start.9 = (bf16[4,2,1,144,1024]{4,3,2,1,0:T(8,128)(2,1)S(1)}, bf16[4,2,1,144,1024]{4,3,2,1,0:T(8,128)(2,1)S(1)}, u32[]{:S(2)}, u32[]{:S(2)}) collective-permute-start(bf16[4,2,1,144,1024]{4,3,2,1,0:T(8,128)(2,1)S(1)} %maximum_select_fusion.2), channel_id=1, source_target_pairs={{0,2},{2,0},{4,6},{6,4},{8,10},{10,8},{12,14},{14,12},{16,18},{18,... | collective-permute-start | bytes 7077896 | tf_op jit(solution)/shard_map/ppermute | solution.py:26
  135.1 65.3 %collective-permute-start.14 = (bf16[256,2176]{1,0:T(8,128)(2,1)}, bf16[256,2176]{1,0:T(8,128)(2,1)}, u32[]{:S(2)}, u32[]{:S(2)}) collective-permute-start(bf16[256,2176]{1,0:T(8,128)(2,1)} %fusion.126), channel_id=1, source_target_pairs={{0,8},{2,10},{4,12},{6,14},{8,0},{10,2},{12,4},{14,6},{16,24},{18,... | collective-permute-start | bytes 3342344 | tf_op jit(solution)/shard_map/ppermute | solution.py:26
  141.9 83.4 %collective-permute-start.15 = (bf16[256,2176]{1,0:T(8,128)(2,1)}, bf16[256,2176]{1,0:T(8,128)(2,1)}, u32[]{:S(2)}, u32[]{:S(2)}) collective-permute-start(bf16[256,2176]{1,0:T(8,128)(2,1)} %fusion.126), channel_id=1, source_target_pairs={{0,16},{2,18},{4,20},{6,22},{8,24},{10,26},{12,28},{14,30},{16,0},... | collective-permute-start | bytes 3342344 | tf_op jit(solution)/shard_map/ppermute | solution.py:26
  146.2 79.1 %collective-permute-start.16 = (bf16[256,2176]{1,0:T(8,128)(2,1)}, bf16[256,2176]{1,0:T(8,128)(2,1)}, u32[]{:S(2)}, u32[]{:S(2)}) collective-permute-start(bf16[256,2176]{1,0:T(8,128)(2,1)} %fusion.126), channel_id=1, source_target_pairs={{0,24},{2,26},{4,28},{6,30},{8,16},{10,18},{12,20},{14,22},{16,8},... | collective-permute-start | bytes 3342344 | tf_op jit(solution)/shard_map/ppermute | solution.py:26
  243.9 64.7 %collective-permute-start.19 = (bf16[512,2048]{1,0:T(8,128)(2,1)}, bf16[512,2048]{1,0:T(8,128)(2,1)}, u32[]{:S(2)}, u32[]{:S(2)}) collective-permute-start(bf16[512,2048]{1,0:T(8,128)(2,1)} %pad_maximum_fusion.5), channel_id=1, source_target_pairs={{0,6},{2,4},{4,2},{6,0},{8,14},{10,12},{12,10},{14,8},{16,22},{18,... | collective-permute-start | bytes 6291464 | tf_op jit(solution)/shard_map/ppermute | solution.py:26
  245.4 114.3 %collective-permute-start.18 = (bf16[512,2048]{1,0:T(8,128)(2,1)}, bf16[512,2048]{1,0:T(8,128)(2,1)}, u32[]{:S(2)}, u32[]{:S(2)}) collective-permute-start(bf16[512,2048]{1,0:T(8,128)(2,1)} %pad_maximum_fusion.4), channel_id=1, source_target_pairs={{0,4},{2,6},{4,0},{6,2},{8,12},{10,14},{12,8},{14,10},{16,20},{18,... | collective-permute-start | bytes 6291464 | tf_op jit(solution)/shard_map/ppermute | solution.py:26
  248.5 113.1 %collective-permute-start.17 = (bf16[512,2048]{1,0:T(8,128)(2,1)}, bf16[512,2048]{1,0:T(8,128)(2,1)}, u32[]{:S(2)}, u32[]{:S(2)}) collective-permute-start(bf16[512,2048]{1,0:T(8,128)(2,1)} %pad_maximum_fusion.3), channel_id=1, source_target_pairs={{0,2},{2,0},{4,6},{6,4},{8,10},{10,8},{12,14},{14,12},{16,18},{18,... | collective-permute-start | bytes 6291464 | tf_op jit(solution)/shard_map/ppermute | solution.py:26
  262.0 105.8 %collective-permute-start.13 = (bf16[2048,1024]{1,0:T(8,128)(2,1)}, bf16[2048,1024]{1,0:T(8,128)(2,1)}, u32[]{:S(2)}, u32[]{:S(2)}) collective-permute-start(bf16[2048,1024]{1,0:T(8,128)(2,1)} %bitcast.281), channel_id=1, source_target_pairs={{0,1},{1,0},{2,3},{3,2},{4,5},{5,4},{6,7},{7,6},{8,9},{9,8},{10,11... | collective-permute-start | bytes 12582920 | tf_op jit(solution)/shard_map/ppermute | solution.py:26
  364.8 60.9 %collective-permute-start.24 = (bf16[256,2048]{1,0:T(8,128)(2,1)}, bf16[256,2048]{1,0:T(8,128)(2,1)}, u32[]{:S(2)}, u32[]{:S(2)}) collective-permute-start(bf16[256,2048]{1,0:T(8,128)(2,1)} %maximum_select_fusion.9), channel_id=1, source_target_pairs={{0,1},{1,0},{2,3},{3,2},{4,5},{5,4},{6,7},{7,6},{8,9},{9,8},{10,11... | collective-permute-start | bytes 3145736 | tf_op jit(solution)/shard_map/ppermute | solution.py:26
  376.0 42.1 %collective-permute-start.23 = (bf16[256,2176]{1,0:T(8,128)(2,1)}, bf16[256,2176]{1,0:T(8,128)(2,1)}, u32[]{:S(2)}, u32[]{:S(2)}) collective-permute-start(bf16[256,2176]{1,0:T(8,128)(2,1)} %pad_maximum_fusion.13), channel_id=1, source_target_pairs={{0,8},{2,10},{4,12},{6,14},{8,0},{10,2},{12,4},{14,6},{16,24},{18,... | collective-permute-start | bytes 3342344 | tf_op jit(solution)/shard_map/ppermute | solution.py:26
  398.5 26.8 %collective-permute-start.20 = (bf16[128,2176]{1,0:T(8,128)(2,1)}, bf16[128,2176]{1,0:T(8,128)(2,1)}, u32[]{:S(2)}, u32[]{:S(2)}) collective-permute-start(bf16[128,2176]{1,0:T(8,128)(2,1)} %get-tuple-element.485), channel_id=1, source_target_pairs={{0,2},{2,0},{4,6},{6,4},{8,10},{10,8},{12,14},{14,12},{16,18},{18,... | collective-permute-start | bytes 1671176 | tf_op jit(solution)/shard_map/ppermute | solution.py:26
  398.6 27.1 %collective-permute-start.21 = (bf16[128,2176]{1,0:T(8,128)(2,1)}, bf16[128,2176]{1,0:T(8,128)(2,1)}, u32[]{:S(2)}, u32[]{:S(2)}) collective-permute-start(bf16[128,2176]{1,0:T(8,128)(2,1)} %get-tuple-element.484), channel_id=1, source_target_pairs={{0,4},{2,6},{4,0},{6,2},{8,12},{10,14},{12,8},{14,10},{16,20},{18,... | collective-permute-start | bytes 1671176 | tf_op jit(solution)/shard_map/ppermute | solution.py:26
  401.0 24.7 %collective-permute-start.22 = (bf16[128,2176]{1,0:T(8,128)(2,1)}, bf16[128,2176]{1,0:T(8,128)(2,1)}, u32[]{:S(2)}, u32[]{:S(2)}) collective-permute-start(bf16[128,2176]{1,0:T(8,128)(2,1)} %get-tuple-element.483), channel_id=1, source_target_pairs={{0,6},{2,4},{4,2},{6,0},{8,14},{10,12},{12,10},{14,8},{16,22},{18,... | collective-permute-start | bytes 1671176 | tf_op jit(solution)/shard_map/ppermute | solution.py:26
  418.1 76.4 %collective-permute-start.28 = (bf16[256,2176]{1,0:T(8,128)(2,1)}, bf16[256,2176]{1,0:T(8,128)(2,1)}, u32[]{:S(2)}, u32[]{:S(2)}) collective-permute-start(bf16[256,2176]{1,0:T(8,128)(2,1)} %pad_maximum_fusion.13), channel_id=1, source_target_pairs={{0,16},{2,18},{4,20},{6,22},{8,24},{10,26},{12,28},{14,30},{16,0},... | collective-permute-start | bytes 3342344 | tf_op jit(solution)/shard_map/ppermute | solution.py:26
  425.3 84.2 %collective-permute-start.32 = (bf16[256,2176]{1,0:T(8,128)(2,1)}, bf16[256,2176]{1,0:T(8,128)(2,1)}, u32[]{:S(2)}, u32[]{:S(2)}) collective-permute-start(bf16[256,2176]{1,0:T(8,128)(2,1)} %pad_maximum_fusion.13), channel_id=1, source_target_pairs={{0,24},{2,26},{4,28},{6,30},{8,16},{10,18},{12,20},{14,22},{16,8},... | collective-permute-start | bytes 3342344 | tf_op jit(solution)/shard_map/ppermute | solution.py:26
  452.2 64.6 %collective-permute-start.25 = (bf16[128,2176]{1,0:T(8,128)(2,1)S(1)}, bf16[128,2176]{1,0:T(8,128)(2,1)S(1)}, u32[]{:S(2)}, u32[]{:S(2)}) collective-permute-start(bf16[128,2176]{1,0:T(8,128)(2,1)S(1)} %get-tuple-element.481), channel_id=1, source_target_pairs={{0,2},{2,0},{4,6},{6,4},{8,10},{10,8},{12,14},{14,12},{16,18},{18,... | collective-permute-start | bytes 1671176 | tf_op jit(solution)/shard_map/ppermute | solution.py:26
  453.8 63.0 %collective-permute-start.26 = (bf16[128,2176]{1,0:T(8,128)(2,1)S(1)}, bf16[128,2176]{1,0:T(8,128)(2,1)S(1)}, u32[]{:S(2)}, u32[]{:S(2)}) collective-permute-start(bf16[128,2176]{1,0:T(8,128)(2,1)S(1)} %get-tuple-element.480), channel_id=1, source_target_pairs={{0,4},{2,6},{4,0},{6,2},{8,12},{10,14},{12,8},{14,10},{16,20},{18,... | collective-permute-start | bytes 1671176 | tf_op jit(solution)/shard_map/ppermute | solution.py:26
  454.1 62.8 %collective-permute-start.27 = (bf16[128,2176]{1,0:T(8,128)(2,1)S(1)}, bf16[128,2176]{1,0:T(8,128)(2,1)S(1)}, u32[]{:S(2)}, u32[]{:S(2)}) collective-permute-start(bf16[128,2176]{1,0:T(8,128)(2,1)S(1)} %get-tuple-element.479), channel_id=1, source_target_pairs={{0,6},{2,4},{4,2},{6,0},{8,14},{10,12},{12,10},{14,8},{16,22},{18,... | collective-permute-start | bytes 1671176 | tf_op jit(solution)/shard_map/ppermute | solution.py:26
  544.8 27.5 %collective-permute-start.30 = (bf16[128,2176]{1,0:T(8,128)(2,1)S(1)}, bf16[128,2176]{1,0:T(8,128)(2,1)S(1)}, u32[]{:S(2)}, u32[]{:S(2)}) collective-permute-start(bf16[128,2176]{1,0:T(8,128)(2,1)S(1)} %get-tuple-element.476), channel_id=1, source_target_pairs={{0,4},{2,6},{4,0},{6,2},{8,12},{10,14},{12,8},{14,10},{16,20},{18,... | collective-permute-start | bytes 1671176 | tf_op jit(solution)/shard_map/ppermute | solution.py:26
  545.6 26.7 %collective-permute-start.31 = (bf16[128,2176]{1,0:T(8,128)(2,1)S(1)}, bf16[128,2176]{1,0:T(8,128)(2,1)S(1)}, u32[]{:S(2)}, u32[]{:S(2)}) collective-permute-start(bf16[128,2176]{1,0:T(8,128)(2,1)S(1)} %get-tuple-element.475), channel_id=1, source_target_pairs={{0,6},{2,4},{4,2},{6,0},{8,14},{10,12},{12,10},{14,8},{16,22},{18,... | collective-permute-start | bytes 1671176 | tf_op jit(solution)/shard_map/ppermute | solution.py:26
  549.6 98.9 %collective-permute-start.36 = (bf16[128,2048]{1,0:T(8,128)(2,1)}, bf16[128,2048]{1,0:T(8,128)(2,1)}, u32[]{:S(2)}, u32[]{:S(2)}) collective-permute-start(bf16[128,2048]{1,0:T(8,128)(2,1)} %get-tuple-element.504), channel_id=1, source_target_pairs={{0,2},{2,0},{4,6},{6,4},{8,10},{10,8},{12,14},{14,12},{16,18},{18,... | collective-permute-start | bytes 1572872 | tf_op jit(solution)/shard_map/ppermute | solution.py:26
  549.7 107.9 %collective-permute-start.37 = (bf16[128,2048]{1,0:T(8,128)(2,1)}, bf16[128,2048]{1,0:T(8,128)(2,1)}, u32[]{:S(2)}, u32[]{:S(2)}) collective-permute-start(bf16[128,2048]{1,0:T(8,128)(2,1)} %get-tuple-element.503), channel_id=1, source_target_pairs={{0,4},{2,6},{4,0},{6,2},{8,12},{10,14},{12,8},{14,10},{16,20},{18,... | collective-permute-start | bytes 1572872 | tf_op jit(solution)/shard_map/ppermute | solution.py:26
  598.8 32.4 %collective-permute-start.34 = (bf16[128,2176]{1,0:T(8,128)(2,1)S(1)}, bf16[128,2176]{1,0:T(8,128)(2,1)S(1)}, u32[]{:S(2)}, u32[]{:S(2)}) collective-permute-start(bf16[128,2176]{1,0:T(8,128)(2,1)S(1)} %get-tuple-element.472), channel_id=1, source_target_pairs={{0,4},{2,6},{4,0},{6,2},{8,12},{10,14},{12,8},{14,10},{16,20},{18,... | collective-permute-start | bytes 1671176 | tf_op jit(solution)/shard_map/ppermute | solution.py:26
  598.8 32.4 %collective-permute-start.35 = (bf16[128,2176]{1,0:T(8,128)(2,1)S(1)}, bf16[128,2176]{1,0:T(8,128)(2,1)S(1)}, u32[]{:S(2)}, u32[]{:S(2)}) collective-permute-start(bf16[128,2176]{1,0:T(8,128)(2,1)S(1)} %get-tuple-element.471), channel_id=1, source_target_pairs={{0,6},{2,4},{4,2},{6,0},{8,14},{10,12},{12,10},{14,8},{16,22},{18,... | collective-permute-start | bytes 1671176 | tf_op jit(solution)/shard_map/ppermute | solution.py:26
  612.4 45.2 %collective-permute-start.38 = (bf16[128,2048]{1,0:T(8,128)(2,1)}, bf16[128,2048]{1,0:T(8,128)(2,1)}, u32[]{:S(2)}, u32[]{:S(2)}) collective-permute-start(bf16[128,2048]{1,0:T(8,128)(2,1)} %get-tuple-element.502), channel_id=1, source_target_pairs={{0,6},{2,4},{4,2},{6,0},{8,14},{10,12},{12,10},{14,8},{16,22},{18,... | collective-permute-start | bytes 1572872 | tf_op jit(solution)/shard_map/ppermute | solution.py:26
  646.0 26.9 %collective-permute-start.40 = (bf16[128,2048]{1,0:T(8,128)(2,1)S(1)}, bf16[128,2048]{1,0:T(8,128)(2,1)S(1)}, u32[]{:S(2)}, u32[]{:S(2)}) collective-permute-start(bf16[128,2048]{1,0:T(8,128)(2,1)S(1)} %get-tuple-element.499), channel_id=1, source_target_pairs={{0,4},{2,6},{4,0},{6,2},{8,12},{10,14},{12,8},{14,10},{16,20},{18,... | collective-permute-start | bytes 1572872 | tf_op jit(solution)/shard_map/ppermute | solution.py:26
  648.5 24.3 %collective-permute-start.41 = (bf16[128,2048]{1,0:T(8,128)(2,1)S(1)}, bf16[128,2048]{1,0:T(8,128)(2,1)S(1)}, u32[]{:S(2)}, u32[]{:S(2)}) collective-permute-start(bf16[128,2048]{1,0:T(8,128)(2,1)S(1)} %get-tuple-element.498), channel_id=1, source_target_pairs={{0,6},{2,4},{4,2},{6,0},{8,14},{10,12},{12,10},{14,8},{16,22},{18,... | collective-permute-start | bytes 1572872 | tf_op jit(solution)/shard_map/ppermute | solution.py:26
  727.8 24.2 %collective-permute-start.46 = (bf16[128,2176]{1,0:T(8,128)(2,1)S(1)}, bf16[128,2176]{1,0:T(8,128)(2,1)S(1)}, u32[]{:S(2)}, u32[]{:S(2)}) collective-permute-start(bf16[128,2176]{1,0:T(8,128)(2,1)S(1)} %get-tuple-element.464), channel_id=1, source_target_pairs={{0,4},{2,6},{4,0},{6,2},{8,12},{10,14},{12,8},{14,10},{16,20},{18,... | collective-permute-start | bytes 1671176 | tf_op jit(solution)/shard_map/ppermute | solution.py:26
  730.6 59.7 %collective-permute-start.56 = (bf16[256,2176]{1,0:T(8,128)(2,1)S(1)}, bf16[256,2176]{1,0:T(8,128)(2,1)S(1)}, u32[]{:S(2)}, u32[]{:S(2)}) collective-permute-start(bf16[256,2176]{1,0:T(8,128)(2,1)S(1)} %convolution_convert_fusion.8), channel_id=1, source_target_pairs={{0,24},{2,26},{4,28},{6,30},{8,16},{10,18},{12,20},{14,22},{16,8},... | collective-permute-start | bytes 3342344 | tf_op jit(solution)/shard_map/ppermute | solution.py:26
  766.2 46.9 %collective-permute-start.55 = (bf16[256,2176]{1,0:T(8,128)(2,1)S(1)}, bf16[256,2176]{1,0:T(8,128)(2,1)S(1)}, u32[]{:S(2)}, u32[]{:S(2)}) collective-permute-start(bf16[256,2176]{1,0:T(8,128)(2,1)S(1)} %convolution_convert_fusion.9), channel_id=1, source_target_pairs={{0,16},{2,18},{4,20},{6,22},{8,24},{10,26},{12,28},{14,30},{16,0},... | collective-permute-start | bytes 3342344 | tf_op jit(solution)/shard_map/ppermute | solution.py:26
  774.6 45.9 %collective-permute-start.54 = (bf16[256,2176]{1,0:T(8,128)(2,1)S(1)}, bf16[256,2176]{1,0:T(8,128)(2,1)S(1)}, u32[]{:S(2)}, u32[]{:S(2)}) collective-permute-start(bf16[256,2176]{1,0:T(8,128)(2,1)S(1)} %convolution_convert_fusion.10), channel_id=1, source_target_pairs={{0,8},{2,10},{4,12},{6,14},{8,0},{10,2},{12,4},{14,6},{16,24},{18,... | collective-permute-start | bytes 3342344 | tf_op jit(solution)/shard_map/ppermute | solution.py:26
  788.2 24.9 %collective-permute-start.51 = (bf16[128,2176]{1,0:T(8,128)(2,1)S(1)}, bf16[128,2176]{1,0:T(8,128)(2,1)S(1)}, u32[]{:S(2)}, u32[]{:S(2)}) collective-permute-start(bf16[128,2176]{1,0:T(8,128)(2,1)S(1)} %get-tuple-element.458), channel_id=1, source_target_pairs={{0,2},{2,0},{4,6},{6,4},{8,10},{10,8},{12,14},{14,12},{16,18},{18,... | collective-permute-start | bytes 1671176 | tf_op jit(solution)/shard_map/ppermute | solution.py:26
  837.3 63.7 %collective-permute-start.59 = (bf16[256,2048]{1,0:T(8,128)(2,1)}, bf16[256,2048]{1,0:T(8,128)(2,1)}, u32[]{:S(2)}, u32[]{:S(2)}) collective-permute-start(bf16[256,2048]{1,0:T(8,128)(2,1)} %pad_maximum_fusion.18), channel_id=1, source_target_pairs={{0,6},{2,4},{4,2},{6,0},{8,14},{10,12},{12,10},{14,8},{16,22},{18,... | collective-permute-start | bytes 3145736 | tf_op jit(solution)/shard_map/ppermute | solution.py:26
  838.7 63.6 %collective-permute-start.58 = (bf16[256,2048]{1,0:T(8,128)(2,1)}, bf16[256,2048]{1,0:T(8,128)(2,1)}, u32[]{:S(2)}, u32[]{:S(2)}) collective-permute-start(bf16[256,2048]{1,0:T(8,128)(2,1)} %pad_maximum_fusion.17), channel_id=1, source_target_pairs={{0,4},{2,6},{4,0},{6,2},{8,12},{10,14},{12,8},{14,10},{16,20},{18,... | collective-permute-start | bytes 3145736 | tf_op jit(solution)/shard_map/ppermute | solution.py:26
  842.1 75.5 %collective-permute-start.57 = (bf16[256,2048]{1,0:T(8,128)(2,1)}, bf16[256,2048]{1,0:T(8,128)(2,1)}, u32[]{:S(2)}, u32[]{:S(2)}) collective-permute-start(bf16[256,2048]{1,0:T(8,128)(2,1)} %pad_maximum_fusion.16), channel_id=1, source_target_pairs={{0,2},{2,0},{4,6},{6,4},{8,10},{10,8},{12,14},{14,12},{16,18},{18,... | collective-permute-start | bytes 3145736 | tf_op jit(solution)/shard_map/ppermute | solution.py:26
  949.9 80.4 %collective-permute-start.67 = (bf16[512,2048]{1,0:T(8,128)(2,1)S(1)}, bf16[512,2048]{1,0:T(8,128)(2,1)S(1)}, u32[]{:S(2)}, u32[]{:S(2)}) collective-permute-start(bf16[512,2048]{1,0:T(8,128)(2,1)S(1)} %pad_maximum_fusion.12), channel_id=1, source_target_pairs={{0,1},{1,0},{2,3},{3,2},{4,5},{5,4},{6,7},{7,6},{8,9},{9,8},{10,11... | collective-permute-start | bytes 6291464 | tf_op jit(solution)/shard_map/ppermute | solution.py:26
  952.5 32.6 %collective-permute-start.66 = (bf16[256,2048]{1,0:T(8,128)(2,1)}, bf16[256,2048]{1,0:T(8,128)(2,1)S(1)}, u32[]{:S(2)}, u32[]{:S(2)}) collective-permute-start(bf16[256,2048]{1,0:T(8,128)(2,1)} %convolution_convert_fusion.17), channel_id=1, source_target_pairs={{0,24},{2,26},{4,28},{6,30},{8,16},{10,18},{12,20},{14,22},{16,8},... | collective-permute-start | bytes 3145736 | tf_op jit(solution)/shard_map/ppermute | solution.py:26
  953.3 95.6 %collective-permute-start.65 = (bf16[256,2048]{1,0:T(8,128)(2,1)S(1)}, bf16[256,2048]{1,0:T(8,128)(2,1)S(1)}, u32[]{:S(2)}, u32[]{:S(2)}) collective-permute-start(bf16[256,2048]{1,0:T(8,128)(2,1)S(1)} %convolution_convert_fusion.18), channel_id=1, source_target_pairs={{0,16},{2,18},{4,20},{6,22},{8,24},{10,26},{12,28},{14,30},{16,0},... | collective-permute-start | bytes 3145736 | tf_op jit(solution)/shard_map/ppermute | solution.py:26
  954.2 117.1 %collective-permute-start.62 = (bf16[1024,1024]{1,0:T(8,128)(2,1)S(1)}, bf16[1024,1024]{1,0:T(8,128)(2,1)S(1)}, u32[]{:S(2)}, u32[]{:S(2)}) collective-permute-start(bf16[1024,1024]{1,0:T(8,128)(2,1)S(1)} %copy-done.156), channel_id=1, source_target_pairs={{0,4},{2,6},{4,0},{6,2},{8,12},{10,14},{12,8},{14,10},{16,20},{18,... | collective-permute-start | bytes 6291464 | tf_op jit(solution)/shard_map/ppermute | solution.py:26
  963.7 108.6 %collective-permute-start.63 = (bf16[1024,1024]{1,0:T(8,128)(2,1)S(1)}, bf16[1024,1024]{1,0:T(8,128)(2,1)S(1)}, u32[]{:S(2)}, u32[]{:S(2)}) collective-permute-start(bf16[1024,1024]{1,0:T(8,128)(2,1)S(1)} %copy-done.155), channel_id=1, source_target_pairs={{0,2},{2,0},{4,6},{6,4},{8,10},{10,8},{12,14},{14,12},{16,18},{18,... | collective-permute-start | bytes 6291464 | tf_op jit(solution)/shard_map/ppermute | solution.py:26
  985.0 86.3 %collective-permute-start.64 = (bf16[256,2048]{1,0:T(8,128)(2,1)S(1)}, bf16[256,2048]{1,0:T(8,128)(2,1)S(1)}, u32[]{:S(2)}, u32[]{:S(2)}) collective-permute-start(bf16[256,2048]{1,0:T(8,128)(2,1)S(1)} %convolution_convert_fusion.19), channel_id=1, source_target_pairs={{0,8},{2,10},{4,12},{6,14},{8,0},{10,2},{12,4},{14,6},{16,24},{18,... | collective-permute-start | bytes 3145736 | tf_op jit(solution)/shard_map/ppermute | solution.py:26
  1030.3 50.0 %collective-permute-start.92 = (bf16[512,2048]{1,0:T(8,128)(2,1)}, bf16[512,2048]{1,0:T(8,128)(2,1)S(1)}, u32[]{:S(2)}, u32[]{:S(2)}) collective-permute-start(bf16[512,2048]{1,0:T(8,128)(2,1)} %convolution_convert_fusion.16), channel_id=1, source_target_pairs={{0,1},{1,0},{2,3},{3,2},{4,5},{5,4},{6,7},{7,6},{8,9},{9,8},{10,11... | collective-permute-start | bytes 6291464 | tf_op jit(solution)/shard_map/ppermute | solution.py:26
  1048.9 112.3 %collective-permute-start.91 = (bf16[1024,2048]{1,0:T(8,128)(2,1)}, bf16[1024,2048]{1,0:T(8,128)(2,1)}, u32[]{:S(2)}, u32[]{:S(2)}) collective-permute-start(bf16[1024,2048]{1,0:T(8,128)(2,1)} %fusion.24), channel_id=1, source_target_pairs={{0,1},{1,0},{2,3},{3,2},{4,5},{5,4},{6,7},{7,6},{8,9},{9,8},{10,11... | collective-permute-start | bytes 12582920 | tf_op jit(solution)/shard_map/ppermute | solution.py:26
  1073.5 26.2 %collective-permute-start.71 = (bf16[4,128,1024]{2,1,0:T(8,128)(2,1)S(1)}, bf16[4,128,1024]{2,1,0:T(8,128)(2,1)}, u32[]{:S(2)}, u32[]{:S(2)}) collective-permute-start(bf16[4,128,1024]{2,1,0:T(8,128)(2,1)S(1)} %fusion.128), channel_id=1, source_target_pairs={{0,4},{2,6},{4,0},{6,2},{8,12},{10,14},{12,8},{14,10},{16,20},{18,... | collective-permute-start | bytes 3145736 | tf_op jit(solution)/shard_map/ppermute | solution.py:26
  1074.9 31.4 %collective-permute-start.70 = (bf16[4,128,1024]{2,1,0:T(8,128)(2,1)S(1)}, bf16[4,128,1024]{2,1,0:T(8,128)(2,1)S(1)}, u32[]{:S(2)}, u32[]{:S(2)}) collective-permute-start(bf16[4,128,1024]{2,1,0:T(8,128)(2,1)S(1)} %fusion.127), channel_id=1, source_target_pairs={{0,2},{2,0},{4,6},{6,4},{8,10},{10,8},{12,14},{14,12},{16,18},{18,... | collective-permute-start | bytes 3145736 | tf_op jit(solution)/shard_map/ppermute | solution.py:26
  1082.9 43.8 %collective-permute-start.68 = (bf16[1024,512]{1,0:T(8,128)(2,1)}, bf16[1024,512]{1,0:T(8,128)(2,1)S(1)}, u32[]{:S(2)}, u32[]{:S(2)}) collective-permute-start(bf16[1024,512]{1,0:T(8,128)(2,1)} %convolution_convert_fusion.24), channel_id=1, source_target_pairs={{0,2},{2,0},{4,6},{6,4},{8,10},{10,8},{12,14},{14,12},{16,18},{18,... | collective-permute-start | bytes 3145736 | tf_op jit(solution)/shard_map/ppermute | solution.py:26
  1083.8 42.9 %collective-permute-start.69 = (bf16[1024,512]{1,0:T(8,128)(2,1)}, bf16[1024,512]{1,0:T(8,128)(2,1)S(1)}, u32[]{:S(2)}, u32[]{:S(2)}) collective-permute-start(bf16[1024,512]{1,0:T(8,128)(2,1)} %convolution_convert_fusion.23), channel_id=1, source_target_pairs={{0,4},{2,6},{4,0},{6,2},{8,12},{10,14},{12,8},{14,10},{16,20},{18,... | collective-permute-start | bytes 3145736 | tf_op jit(solution)/shard_map/ppermute | solution.py:26
  1099.7 48.5 %collective-permute-start.72 = (bf16[256,2048]{1,0:T(8,128)(2,1)S(1)}, bf16[256,2048]{1,0:T(8,128)(2,1)S(1)}, u32[]{:S(2)}, u32[]{:S(2)}) collective-permute-start(bf16[256,2048]{1,0:T(8,128)(2,1)S(1)} %copy-done.106), channel_id=1, source_target_pairs={{0,2},{2,0},{4,6},{6,4},{8,10},{10,8},{12,14},{14,12},{16,18},{18,... | collective-permute-start | bytes 3145736 | tf_op jit(solution)/shard_map/ppermute | solution.py:26
  1149.8 51.5 %collective-permute-start.81 = (bf16[128,2048]{1,0:T(8,128)(2,1)}, bf16[128,2048]{1,0:T(8,128)(2,1)}, u32[]{:S(2)}, u32[]{:S(2)}) collective-permute-start(bf16[128,2048]{1,0:T(8,128)(2,1)} %get-tuple-element.428), channel_id=1, source_target_pairs={{0,8},{2,10},{4,12},{6,14},{8,0},{10,2},{12,4},{14,6},{16,24},{18,... | collective-permute-start | bytes 1572872 | tf_op jit(solution)/shard_map/ppermute | solution.py:26
  1151.1 50.2 %collective-permute-start.82 = (bf16[128,2048]{1,0:T(8,128)(2,1)S(1)}, bf16[128,2048]{1,0:T(8,128)(2,1)}, u32[]{:S(2)}, u32[]{:S(2)}) collective-permute-start(bf16[128,2048]{1,0:T(8,128)(2,1)S(1)} %get-tuple-element.430), channel_id=1, source_target_pairs={{0,16},{2,18},{4,20},{6,22},{8,24},{10,26},{12,28},{14,30},{16,0},... | collective-permute-start | bytes 1572872 | tf_op jit(solution)/shard_map/ppermute | solution.py:26
  (207 other events, 2856.3 us)
Sparse Core Ops, SparseCore 0:
  12.4 119.5 all-gather.12
  134.7 190.8 all-gather.10
  327.2 14.9 all-gather.6
  343.6 21.7 all-gather.8
  856.3 117.3 reduce-scatter.1

commit v4 on v2

--- a/solution.py
+++ b/solution.py
@@ -85,14 +85,14 @@
     queries, half = query_raw.shape
     span = key_raw.shape[0]
     heads = half // HEAD
-    step = queries // 2
+    step = min(queries, 256)
 
     def kernel(q_ref, k_ref, v_ref, table_ref, scale_ref, live_ref, out_ref, lse_ref):
         cosine, sine = table_ref[0], table_ref[1]
         key_low, _, _ = normed_rope(k_ref[...], scale_ref[1:2], cosine, sine)
         value_turned = v_ref[...].astype(f32).T.astype(bf16)
         live_now = jnp.concatenate([live_ref[...]] * (step // HEAD), axis=1) > 0.0
-        for part in range(2):
+        for part in range(queries // step):
             at = slice(part * step, (part + 1) * step)
             query_low, _, _ = normed_rope(q_ref[at], scale_ref[0:1], cosine[at], sine[at])
             scores = jnp.where(live_now, contract_cols(key_low, query_low), masked)
@@ -131,7 +131,7 @@
     queries, half = query_raw.shape
     span = key_raw.shape[0]
     heads = half // HEAD
-    step = queries // 2
+    step = min(queries, 256)
 
     def fold(terms):
         return jnp.sum(terms.reshape(-1, 8, HEAD), axis=0)
@@ -148,7 +148,7 @@
         key_grad = jnp.zeros((span, HEAD), f32)
         value_grad = jnp.zeros((span, HEAD), f32)
         query_gain = jnp.zeros((8, HEAD), f32)
-        for part in range(2):
+        for part in range(queries // step):
             at = slice(part * step, (part + 1) * step)
             query_raw = q_ref[at]
             query_low, query_inverse, _ = normed_rope(
@@ -265,6 +265,8 @@
     bits = ring.bit_length() - 1
     capacity = tokens * TOPK // owners
     half = width // 2
+    quarter = width // 4
+    pair_rows = 2 * width // owners
     owner = lax.axis_index("expert")
     core = lax.axis_index("fsdp")
     parity = owner % 2
@@ -285,10 +287,10 @@
 
     def gather_plane(now, order):
         rows, columns = now.shape[0] // PLANES, now.shape[1]
-        now = now.reshape((PLANES,) + (1,) * bits + (rows, columns))
+        now = now.reshape((PLANES,) + (1,) * len(order) + (rows, columns))
         for b in order:
             now = in_order(bit_of(b), now, swap(now, "expert", 1 << b), bits - b)
-        return now.reshape(owners * rows, columns)
+        return now.reshape(-1, columns)
 
     def split_columns(values, b):
         each = values.shape[1] // owners
@@ -304,19 +306,17 @@
 
         return side(bit_of(b)), side(1 - bit_of(b))
 
-    def scatter_rest(stay, right, arrived, order):
-        columns = right.shape[1]
-        now = contract_rows(stay, right) + arrived.astype(f32)
-        axes = [b for b in reversed(range(bits)) if b != order[0]]
-        rows = width // owners
+    def scatter_rest(now, order):
+        columns = now.shape[1]
+        axes = sorted(order[1:], reverse=True)
         for b in order[1:]:
-            now = now.reshape([PLANES] + [2] * len(axes) + [rows, columns])
+            now = now.reshape([PLANES] + [2] * len(axes) + [-1, columns])
             at = 1 + axes.index(b)
             kept = lax.dynamic_index_in_dim(now, bit_of(b), at, keepdims=False)
             sent = lax.dynamic_index_in_dim(now, 1 - bit_of(b), at, keepdims=False)
             axes.remove(b)
             now = kept + swap(sent.astype(bf16), "expert", 1 << b).astype(f32)
-        return now.reshape(PLANES, rows, columns)
+        return now.reshape(PLANES, -1, columns)
 
     def scatter_planes(now):
         total = lax.dynamic_index_in_dim(now, plane, 0, keepdims=False)
@@ -354,15 +354,10 @@
     lanes = 128
     small_rows = -(-cut[-1] // (lanes * 16)) * 16
     small = jnp.pad(small, (0, small_rows * lanes - cut[-1])).reshape(small_rows, lanes)
-    small_pair = in_order(core, small, swap(small, "fsdp", 1), 0)
-    small_all = gather_plane(gather_planes(small_pair), descending)
-    small_all = small_all.reshape(devices, small_rows * lanes)
-    first_gain = small_all[:, cut[0] : cut[1]].reshape(width).astype(f32)
-    second_gain = small_all[:, cut[1] : cut[2]].reshape(width).astype(f32)
-    query_scale = small_all[:, cut[2] : cut[3]].reshape(HEAD).astype(f32)
-    key_scale = small_all[:, cut[3] : cut[4]].reshape(HEAD).astype(f32)
-    router_full = small_all[:, cut[4] : cut[5]].reshape(width, owners)
-
+    small_two = in_order(parity, small, swap(small, "expert", 1), 0).reshape(2, 1, -1)
+    small_four = in_order(core, small_two, swap(small_two, "fsdp", 1), 1).reshape(-1, quarter)
+    small_tall = -(-small_four.shape[0] // 16) * 16
+    small_four = jnp.pad(small_four, ((0, small_tall - small_four.shape[0]), (0, 0)))
     other_chip = swap(hidden_in, "expert", 1)
     hidden_own_peer = swap(hidden_in, "fsdp", 1)
     hidden_other_peer = swap(other_chip, "fsdp", 1)
@@ -370,14 +365,19 @@
         [hidden_in, hidden_own_peer, other_chip, hidden_other_peer], axis=0
     )
 
-    stacked = jnp.stack([query_weight, key_weight, value_weight, output_weight])
-    mine = pick(stacked, core * half, half, axis=2)
-    theirs = swap(pick(stacked, (1 - core) * half, half, axis=2), "fsdp", 1)
-    shards = in_order(core, mine, theirs, 1)
-    query_own = gather_owners(shards[0])
-    output_own = gather_owners(shards[3])
-    key_first = gather_planes(shards[1])
-    value_first = gather_planes(shards[2])
+    stacked = jnp.stack([key_weight, value_weight, query_weight])
+    mine = pick(stacked, parity * half, half, axis=2)
+    theirs = swap(pick(stacked, (1 - parity) * half, half, axis=2), "expert", 1)
+    shards = in_order(parity, mine, theirs, 1)
+    mine = pick(shards, core * quarter, quarter, axis=2).reshape(3, 2, 1, -1, quarter)
+    theirs = swap(pick(shards, (1 - core) * quarter, quarter, axis=2), "fsdp", 1)
+    shards = in_order(core, mine, theirs.reshape(mine.shape), 2).reshape(3, pair_rows, quarter)
+    key_first = gather_planes(jnp.concatenate([shards[0], small_four], axis=0))
+    value_first = gather_planes(shards[1])
+    query_first = gather_planes(shards[2])
+    mine = pick(output_weight, core * half, half)
+    theirs = swap(pick(output_weight, (1 - core) * half, half), "fsdp", 1)
+    output_shard = in_order(core, mine, theirs, 0)
 
     inner_now = lax.all_gather(expert_inner, "fsdp", axis=1, tiled=True)[0]
     outer_now = lax.all_gather(expert_outer, "fsdp", axis=1, tiled=True)[0]
@@ -397,7 +397,6 @@
     key_live = positions < length
     tables = rotary_tables(positions)
     live_lanes = jnp.broadcast_to(key_live.astype(f32)[:, None], (span, HEAD))
-    scales = jnp.pad(jnp.stack([query_scale, key_scale]), ((0, 6), (0, 0)))
     expert_range = jnp.arange(owners, dtype=jnp.int32)
     hot = expert_ids[:, :, None] == expert_range[None, None, :]
     chosen = jnp.any(hot, axis=1)
@@ -449,12 +448,34 @@
         ]
 
     up_wide = widened(upstream_low, rank_of.astype(bf16))
-    up_wide, key_first, value_first = lax.optimization_barrier((up_wide, key_first, value_first))
-    key_own = gather_plane(key_first, descending)
-    value_own = gather_plane(value_first, ascending)
+    pair_order_bits = descending[:-1]
+    key_all = gather_plane(key_first, pair_order_bits).reshape(-1, pair_rows + small_tall, quarter)
+    value_own = gather_plane(value_first, pair_order_bits)
+    key_own = key_all[:, :pair_rows].reshape(width, quarter)
+    small_all = key_all[:, pair_rows:].reshape(-1, small_tall * quarter)
+    small_all = small_all[:, : 2 * sharers * small_rows * lanes].reshape(devices, -1)
+    first_gain = small_all[:, cut[0] : cut[1]].reshape(width).astype(f32)
+    second_gain = small_all[:, cut[1] : cut[2]].reshape(width).astype(f32)
+    query_scale = small_all[:, cut[2] : cut[3]].reshape(HEAD).astype(f32)
+    key_scale = small_all[:, cut[3] : cut[4]].reshape(HEAD).astype(f32)
+    router_full = small_all[:, cut[4] : cut[5]].reshape(width, owners)
+
+    output_shard, up_wide, query_first = lax.optimization_barrier(
+        (output_shard, up_wide, query_first)
+    )
+    query_own = gather_plane(query_first, pair_order_bits)
+    output_own = gather_plane(gather_planes(output_shard), descending)
     output_peer = swap(output_own, "fsdp", 1)
-    up_planes = planes_of(up_wide)
-    up_planes, key_late, value_late = lax.optimization_barrier((up_planes, key_own, value_own))
+    d1, d2, d3 = [swap(up_wide, "expert", d * ring) for d in range(1, PLANES)]
+    up_planes = [
+        up_wide,
+        by_plane(d1, d1, d3, d1),
+        by_plane(d2, d3, d1, d2),
+        by_plane(d3, d2, d2, d3),
+    ]
+    up_planes, key_late, value_late, query_late = lax.optimization_barrier(
+        (up_planes, key_own, value_own, query_own)
+    )
 
     def exchange_all(blocks):
         got = [blocks]
@@ -475,22 +496,32 @@
         picker = hits.astype(bf16).reshape(tokens, ring * capacity)
         pickers.append(picker)
         up_picked.append(contract_rows(picker, up_planes[d][:, :width], bf16))
-    up_arrived = exchange_all(up_picked)
-
+
+    scales = jnp.pad(jnp.stack([query_scale, key_scale]), ((0, 6), (0, 0)))
     hidden_f = hidden_seq.astype(f32)
     first_normed, first_inverse = rms_scale(hidden_f, first_gain)
     first_low = first_normed.astype(bf16)
     key_raw = matmul(first_low, key_own)
     value_low = matmul(first_low, value_own).astype(bf16)
-    query_raw = matmul(first_low[: 2 * tokens], query_own)
+    query_raw = matmul(first_low, query_own)
+    key_raw, up_picked = lax.optimization_barrier((key_raw, up_picked))
+    up_arrived = exchange_all(up_picked)
     attended, lse = attention_forward(
         query_raw, key_raw, value_low, tables, scales, live_lanes
     )
-    left_x = split_columns(first_low, 0)
     left_y = split_columns(first_low, bits - 1)
-    attended_cross = swap(attended[tokens:], "fsdp", 1)
-    attended_full = in_order(core, attended[:tokens], attended_cross, 1)
+    far_heads = swap(attended[2 * tokens :], "expert", 1)
+    crossed = jnp.concatenate([attended[tokens : 2 * tokens], far_heads[tokens:]], axis=1)
+    crossed = swap(crossed, "fsdp", 1)
+    attended_full = in_order(
+        parity,
+        in_order(core, attended[:tokens], crossed[:, :quarter], 1),
+        in_order(core, far_heads[:tokens], crossed[:, quarter:], 1),
+        1,
+    )
     attended_peer = swap(attended_full, "fsdp", 1)
+    attended_both = jnp.concatenate([attended_full, attended_peer], axis=0)
+    attended_x = split_columns(attended_both, 0)
     branch = in_order(
         core, matmul(attended_full, output_own), matmul(attended_full, output_peer), 1
     )
@@ -519,7 +550,7 @@
         if d < last:
             rows, picked[d + 1] = lax.optimization_barrier((rows, picked[d + 1]))
         if d == 0:
-            rows, left_x, left_y = lax.optimization_barrier((rows, left_x, left_y))
+            rows, left_y, attended_x = lax.optimization_barrier((rows, left_y, attended_x))
         rows = jnp.concatenate(rows, axis=0)
         if d:
             rows, rows_back[-1] = lax.optimization_barrier((rows, rows_back[-1]))
@@ -617,17 +648,17 @@
     attended_grad = (
         contract_cols(branch_mine, output_own) + contract_cols(branch_theirs, output_peer)
     ).astype(bf16)
-    grad_mine = pick(attended_grad, core * half, half)
-    grad_cross = swap(pick(attended_grad, (1 - core) * half, half), "fsdp", 1)
-    attended_grad = jnp.concatenate([grad_mine, grad_cross], axis=0)
-
-    attended_both = jnp.concatenate([attended_full, attended_peer], axis=0)
+    far_grad = swap(pick(attended_grad, (1 - parity) * half, half), "expert", 1)
+    chip_grad = jnp.stack([pick(attended_grad, parity * half, half), far_grad])
+    crossed = swap(pick(chip_grad, (1 - core) * quarter, quarter, 2), "fsdp", 1)
+    kept_grad = pick(chip_grad, core * quarter, quarter, 2)
+    attended_grad = jnp.concatenate([kept_grad[0], crossed[0], kept_grad[1], crossed[1]], axis=0)
+
     branch_both = jnp.concatenate([branch_mine, swap(branch_theirs, "fsdp", 1)], axis=0)
-    output_local = contract_rows(attended_both, branch_both, bf16)
-
-    attended_grad, output_local = lax.optimization_barrier((attended_grad, output_local))
-    output_block = lax.psum_scatter(output_local, "expert", scatter_dimension=0, tiled=True)
-    output_block = output_block.astype(f32)
+    output_sent = contract_rows(attended_x[1], branch_both, bf16)
+
+    attended_grad, output_sent = lax.optimization_barrier((attended_grad, output_sent))
+    output_came = swap(output_sent, "expert", 1)
     query_low_grad, key_low_grad, value_low_grad, gain_terms = attention_backward(
         query_raw, key_raw, value_low, attended_grad, lse, tables, scales, live_lanes
     )
@@ -635,51 +666,34 @@
     out_arrived, query_low_grad, key_low_grad, value_low_grad = lax.optimization_barrier(
         (out_arrived, query_low_grad, key_low_grad, value_low_grad)
     )
-    quarter = half // 2
-    chip = 2 * tokens
-    sent = [
-        contract_rows(left_y[1], value_low_grad, bf16),
-        contract_rows(left_x[1], key_low_grad, bf16),
+    y_bit = bits - 1
+    steps = [key_low_grad, value_low_grad, query_low_grad]
+    grads_late = lax.optimization_barrier(
+        (steps, [contract_rows(left_y[1], right, bf16) for right in steps])
+    )
+    steps, sent = grads_late
+    key_came = swap(sent[0], "expert", 1 << y_bit)
+    output_now = contract_rows(attended_x[0], branch_both) + output_came.astype(f32)
+    output_now = scatter_rest(output_now, ascending)
+    sent[1], key_came = lax.optimization_barrier((sent[1], key_came))
+    value_came = swap(sent[1], "expert", 1 << y_bit)
+    sent[2], value_came = lax.optimization_barrier((sent[2], value_came))
+    query_came = swap(sent[2], "expert", 1 << y_bit)
+    kept = [contract_rows(left_y[0], right) for right in steps]
+    blocks = [
+        scatter_planes(scatter_rest(k + c.astype(f32), pair_order_bits))
+        for k, c in zip(kept, (key_came, value_came, query_came))
     ]
-    sent, query_low_grad = lax.optimization_barrier((sent, query_low_grad))
-    sent += [
-        contract_rows(left_x[1][:chip], query_low_grad[:, :quarter], bf16),
-        contract_rows(left_y[1][:chip], query_low_grad[:, quarter:], bf16),
-    ]
-    sent, query_late, key_grad_late, value_grad_late = lax.optimization_barrier(
-        (sent, query_low_grad, key_low_grad, value_low_grad)
-    )
-    value_came = swap(sent[0], "expert", 1 << (bits - 1))
-    key_came = swap(sent[1], "expert", 1)
-    out_arrived, value_came, key_came = lax.optimization_barrier(
-        (out_arrived, value_came, key_came)
-    )
-    sent, value_came, key_came = lax.optimization_barrier((sent, value_came, key_came))
-    query_x_came = swap(sent[2], "expert", 1)
-    query_y_came = swap(sent[3], "expert", 1 << (bits - 1))
-    value_block = scatter_planes(scatter_rest(left_y[0], value_low_grad, value_came, descending))
-    key_block = scatter_planes(scatter_rest(left_x[0], key_low_grad, key_came, ascending))
-    query_block = scatter_planes(
-        jnp.concatenate(
-            [
-                scatter_rest(
-                    left_x[0][:chip], query_low_grad[:, :quarter], query_x_came, ascending
-                ),
-                scatter_rest(
-                    left_y[0][:chip], query_low_grad[:, quarter:], query_y_came, descending
-                ),
-            ],
-            axis=2,
-        )
-    )
+    output_block = scatter_planes(output_now)
+    key_late_grad, value_late_grad, query_late_grad = steps
     layer_out = (residual + bring_back(out_arrived)).astype(bf16)
 
-    kv_grad = contract_cols(key_grad_late, key_late) + contract_cols(value_grad_late, value_late)
-    q_grad = contract_cols(query_late, query_own)
-    own_part = kv_grad[:tokens] + q_grad[:tokens]
-    peer_part = kv_grad[tokens : 2 * tokens] + q_grad[tokens:]
-    far_part = kv_grad[2 * tokens : 3 * tokens]
-    far_peer = kv_grad[3 * tokens :]
+    all_grad = (
+        contract_cols(key_late_grad, key_late)
+        + contract_cols(value_late_grad, value_late)
+        + contract_cols(query_late_grad, query_late)
+    )
+    own_part, peer_part, far_part, far_peer = jnp.split(all_grad, 4, axis=0)
     crossed = swap(jnp.concatenate([peer_part, far_peer], axis=0).astype(bf16), "fsdp", 1)
     own_part = own_part + crossed[:tokens].astype(f32)
     far_part = (far_part + crossed[tokens:].astype(f32)).astype(bf16)
@@ -722,7 +736,15 @@
         cross = swap(pick(block, (1 - core) * rows_dev, rows_dev, 0), "fsdp", 1)
         return in_order(core, keep, cross, 1)
 
-    weight_grads = [whole_rows(b) for b in (query_block, key_block, value_block, output_block)]
+    blocks = jnp.stack(blocks).reshape(3, 2, 2, rows_dev, quarter)
+    kept = lax.dynamic_index_in_dim(blocks, core, 2, keepdims=False)
+    cross = swap(lax.dynamic_index_in_dim(blocks, 1 - core, 2, keepdims=False), "fsdp", 1)
+    blocks = in_order(core, kept, cross, 3)
+    kept = lax.dynamic_index_in_dim(blocks, parity, 1, keepdims=False)
+    cross = lax.dynamic_index_in_dim(blocks, 1 - parity, 1, keepdims=False)
+    cross = swap(cross.astype(bf16), "expert", 1).astype(f32)
+    key_grad, value_grad, query_grad = in_order(parity, kept, cross, 2)
+    weight_grads = [query_grad, key_grad, value_grad, whole_rows(output_block)]
     return (
         layer_out,
         input_grad,

time: 1160 us -> 1180 us (1.017)
  starting transfers between devices: 175 us -> 216 us
  Pallas kernels: 64 us -> 49.4 us
    ppermute x12 -> x9, waiting for transfers between devices: 95.4 us -> 8.7 us  [step_down(): lax.ppermute(block, 'expert', [(p * ring + i, (p - 1) * ring + i) for p i...]
    ppermute x86 -> x95, waiting for transfers between devices: 316 us -> 389 us  [swap(): return lax.ppermute(block, axis, [(i, i ^ mask) for i in range(count)])]
    ppermute x86 -> x95, starting transfers between devices: 119 us -> 169 us  [swap(): return lax.ppermute(block, axis, [(i, i ^ mask) for i in range(count)])]
    dot_general x22 -> x21, matrix products: 83.1 us -> 77.5 us  [contract_rows(): lax.dot_general(left, right, (((0,), (0,)), ((), ())), preferred_element_...]
    ppermute x12 -> x9, starting transfers between devices: 40.2 us -> 35 us  [step_up(): lax.ppermute(block, 'expert', [(p * ring + i, (p + 1) * ring + i) for p i...]
    select_n x22 -> x27, other arithmetic: 20.4 us -> 24 us  [in_order(): jnp.where(flag == 0, jnp.concatenate([first, second], axis=axis), jnp.con...]
    unnamed x351 -> x436, local copies, waits for them, and re-layouts: 39.2 us -> 39.3 us
  transfers between devices with their start and end apart: 115 -> 115, of which waited for: 42 -> 42; matrix products, arithmetic and copies ran while one was open for 34% -> 32% of each run, Pallas kernels for 6% -> 4%
where the time goes in v4:
time: 1180 us; the launch traced here: 1160 us
  waiting for transfers between devices  414 us (35%)
  matrix products  236 us (20%)
  starting transfers between devices  216 us (18%)
  other arithmetic  130 us (11%)
  local copies, waits for them, and re-layouts  101 us (9%)
  Pallas kernels  49.4 us (4%)
  between operations  18.2 us (2%)
    ppermute x95, waiting for transfers between devices, swap(): return lax.ppermute(block, axis, [(i, i ^ mask) for i in range(count)])  389 us
    ppermute x95, starting transfers between devices, swap(): return lax.ppermute(block, axis, [(i, i ^ mask) for i in range(count)])  169 us
    dot_general x11, matrix products, contract_cols(): lax.dot_general(left, right, (((1,), (1,)), ((), ())), preferred_element_...  81.4 us
    dot_general x21, matrix products, contract_rows(): lax.dot_general(left, right, (((0,), (0,)), ((), ())), preferred_element_...  77.5 us
    dot_general x26, matrix products, matmul(): return jnp.dot(left, right, preferred_element_type=f32)  76.8 us
    unnamed x436, local copies, waits for them, and re-layouts  39.3 us
    ppermute x9, starting transfers between devices, step_up(): lax.ppermute(block, 'expert', [(p * ring + i, (p + 1) * ring + i) for p i...  35 us
    pallas_call x1, Pallas kernels, attention_backward(): pl.pallas_call(kernel, grid=(heads,), in_specs=[column(queries), column(s...  29 us
  transfers between devices with their start and end apart: 115, of which 42 were waited for; matrix products, arithmetic and copies ran while one was open for 32% of the time, Pallas kernels for 4%

profile of v4, /device:TPU:0, one launch (start us, length us, event | category | flops | bytes accessed | tf_op | source)
XLA Modules:
  0.0 1164.9 jit_solution(17996662424343209192)
XLA Ops:
  31.2 12.5 %collective-permute-done.3 = bf16[3,64,1024]{2,1,0:T(8,128)(2,1)} collective-permute-done((bf16[3,64,1024]{2,1,0:T(8,128)(2,1)}, bf16[3,64,1024]{2,1,0:T(8,128)(2,1)}, u32[]{:S(2)}, u32[]{:S(2)}) %collective-permute-start.3) | collective-permute-done | bytes 393248 | tf_op jit(solution)/shard_map/ppermute | solution.py:26
  57.1 8.4 collective-permute-start.21
  65.8 13.7 %collective-permute-start.20 = (bf16[256,512]{1,0:T(8,128)(2,1)}, bf16[256,512]{1,0:T(8,128)(2,1)S(1)}, u32[]{:S(2)}, u32[]{:S(2)}) collective-permute-start(bf16[256,512]{1,0:T(8,128)(2,1)} %bitcast.22), channel_id=1, source_target_pairs={{0,16},{2,18},{4,20},{6,22},{8,24},{10,26},{12,28},{14,30},{16,0},... | collective-permute-start | bytes 786440 | tf_op jit(solution)/shard_map/ppermute | solution.py:26
  79.5 8.9 collective-permute-done.13
  89.2 16.8 %collective-permute-done.19 = bf16[256,512]{1,0:T(8,128)(2,1)S(1)} collective-permute-done((bf16[256,512]{1,0:T(8,128)(2,1)}, bf16[256,512]{1,0:T(8,128)(2,1)S(1)}, u32[]{:S(2)}, u32[]{:S(2)}) %collective-permute-start.19) | collective-permute-done | bytes 262176 | tf_op jit(solution)/shard_map/ppermute | solution.py:26
  111.5 5.3 collective-permute-done.7
  116.7 6.1 collective-permute-start.27
  123.1 20.4 %collective-permute-start.26 = (bf16[128,1024]{1,0:T(8,128)(2,1)S(1)}, bf16[128,1024]{1,0:T(8,128)(2,1)S(1)}, u32[]{:S(2)}, u32[]{:S(2)}) collective-permute-start(bf16[128,1024]{1,0:T(8,128)(2,1)S(1)} %maximum_select_fusion.26), channel_id=1, source_target_pairs={{0,16},{2,18},{4,20},{6,22},{8,24},{10,26},{12,28},{14,30},{16,0},... | collective-permute-start | bytes 786440 | tf_op jit(solution)/shard_map/ppermute | solution.py:26
  143.5 9.4 collective-permute-done.8
  153.6 7.4 collective-permute-done.25
  162.8 21.2 %collective-permute-done.26 = bf16[128,1024]{1,0:T(8,128)(2,1)S(1)} collective-permute-done((bf16[128,1024]{1,0:T(8,128)(2,1)S(1)}, bf16[128,1024]{1,0:T(8,128)(2,1)S(1)}, u32[]{:S(2)}, u32[]{:S(2)}) %collective-permute-start.26) | collective-permute-done | bytes 262176 | tf_op jit(solution)/shard_map/ppermute | solution.py:26
  194.6 5.3 maximum_convert_fusion
  199.9 14.3 %collective-permute-done.22 = bf16[4,1,256,512]{3,2,1,0:T(8,128)(2,1)S(1)} collective-permute-done((bf16[4,1,256,512]{3,2,1,0:T(8,128)(2,1)S(1)}, bf16[4,1,256,512]{3,2,1,0:T(8,128)(2,1)S(1)}, u32[]{:S(2)}, u32[]{:S(2)}) %collective-permute-start.22) | collective-permute-done | bytes 1048608 | tf_op jit(solution)/shard_map/ppermute | solution.py:26
  217.8 24.4 %collective-permute-done.18 = bf16[256,2176]{0,1:T(8,128)(2,1)S(1)} collective-permute-done((bf16[256,2176]{0,1:T(8,128)(2,1)S(1)}, bf16[256,2176]{0,1:T(8,128)(2,1)S(1)}, u32[]{:S(2)}, u32[]{:S(2)}) %collective-permute-start.18) | collective-permute-done | bytes 1114144 | tf_op jit(solution)/shard_map/ppermute | solution.py:26
  268.3 5.4 convolution_convert_fusion.17.v_ref
  273.9 20.5 %attention_forward.1 = (bf16[1024,512]{1,0:T(8,128)(2,1)S(1)}, f32[4,8,1024]{2,1,0:T(8,128)S(1)}) custom-call(f32[1024,512]{1,0:T(8,128)S(1)} %fusion.316.q_ref, f32[1024,512]{1,0:T(8,128)S(1)} %copy-done, bf16[1024,512]{1,0:T(8,128)(2,1)S(1)} %convolution_convert_fusion.17.v_ref, f32[2,1024,128]{2,1,0:T(8,128)S(1)} %pad_maximum_fusion.18.table_ref, ...), custom_call_target="tpu_custom_call" | custom-call | tf_op jit(solution)/shard_map/attention_forward/pallas_call | solution.py:109
  318.3 36.1 %collective-permute-done.29 = bf16[4,2,1,128,1024]{4,3,2,1,0:T(8,128)(2,1)} collective-permute-done((bf16[4,2,1,128,1024]{4,3,2,1,0:T(8,128)(2,1)}, bf16[4,2,1,128,1024]{4,3,2,1,0:T(8,128)(2,1)}, u32[]{:S(2)}, u32[]{:S(2)}) %collective-permute-start.29) | collective-permute-done | bytes 2097184 | tf_op jit(solution)/shard_map/ppermute | solution.py:26
  364.2 35.0 %collective-permute-done.31 = bf16[512,2048]{1,0:T(8,128)(2,1)S(1)} collective-permute-done((bf16[512,2048]{1,0:T(8,128)(2,1)S(1)}, bf16[512,2048]{1,0:T(8,128)(2,1)S(1)}, u32[]{:S(2)}, u32[]{:S(2)}) %collective-permute-start.31) | collective-permute-done | bytes 2097184 | tf_op jit(solution)/shard_map/ppermute | solution.py:26
  399.7 40.7 %collective-permute-done.33 = bf16[512,2048]{1,0:T(8,128)(2,1)S(1)} collective-permute-done((bf16[512,2048]{1,0:T(8,128)(2,1)S(1)}, bf16[512,2048]{1,0:T(8,128)(2,1)S(1)}, u32[]{:S(2)}, u32[]{:S(2)}) %collective-permute-start.33) | collective-permute-done | bytes 2097184 | tf_op jit(solution)/shard_map/ppermute | solution.py:26
  450.0 5.6 collective-permute-start.38
  466.5 14.8 %fusion.9 = f32[2048,1024]{0,1:T(8,128)} fusion(bf16[2048,2048]{1,0:T(8,128)(2,1)} %copy-done.158, bf16[1,1024,2048]{2,1,0:T(8,128)(2,1)} %all-gather.3.cloned.1.call-done), kind=kOutput, calls=%fused_computation.56 | convolution fusion | flops 8589934592 | bytes 20971520 | tf_op jit(solution)/shard_map/dot_general | solution.py:36
  497.4 8.2 fusion.32
  506.7 5.2 multiply_convert_fusion.12
  515.3 10.6 fusion.15
  527.3 4.7 collective-permute-done.42
  536.5 8.4 fusion.29
  549.9 5.2 multiply_convert_fusion.10
  558.8 10.5 fusion.16
  577.4 8.3 fusion.26
  590.8 5.3 multiply_convert_fusion.8
  597.7 10.5 fusion.17
  609.8 8.3 fusion.23
  618.3 5.2 multiply_convert_fusion.6
  625.1 9.1 fusion.18
  644.3 6.3 collective-permute-done.55
  664.4 10.5 fusion.19
  674.9 11.1 fusion.11
  688.7 9.3 convolution_convert_fusion.12
  698.0 6.3 fusion.126
  718.0 8.8 collective-permute-done.58
  741.2 15.7 %collective-permute-done.60 = bf16[128,2176]{1,0:T(8,128)(2,1)S(1)} collective-permute-done((bf16[128,2176]{1,0:T(8,128)(2,1)S(1)}, bf16[128,2176]{1,0:T(8,128)(2,1)S(1)}, u32[]{:S(2)}, u32[]{:S(2)}) %collective-permute-start.60) | collective-permute-done | bytes 557088 | tf_op jit(solution)/shard_map/ppermute | solution.py:26
  760.0 5.2 collective-permute-start.68
  772.4 7.9 collective-permute-done.64
  780.3 6.0 collective-permute-done.63
  786.2 6.0 collective-permute-done.62
  801.7 4.4 collective-permute-start.72
  826.6 20.1 %collective-permute-done.74 = bf16[256,1024]{1,0:T(8,128)(2,1)} collective-permute-done((bf16[256,1024]{1,0:T(8,128)(2,1)}, bf16[256,1024]{1,0:T(8,128)(2,1)}, u32[]{:S(2)}, u32[]{:S(2)}) %collective-permute-start.74) | collective-permute-done | bytes 524320 | tf_op jit(solution)/shard_map/ppermute | solution.py:26
  854.2 29.0 %attention_backward.1 = (bf16[1024,512]{1,0:T(8,128)(2,1)S(1)}, bf16[1024,512]{1,0:T(8,128)(2,1)S(1)}, bf16[1024,512]{1,0:T(8,128)(2,1)S(1)}, f32[2,8,128]{2,1,0:T(8,128)S(1)}) custom-call(f32[1024,512]{1,0:T(8,128)S(1)} %fusion.316.q_ref, f32[1024,512]{1,0:T(8,128)S(1)} %copy-done.1, bf16[1024,512]{1,0:T(8,128)(2,1)S(1)} %copy-done.5, ...), custom_call_target="tpu_custom_call" | custom-call | tf_op jit(solution)/shard_map/attention_backward/pallas_call | solution.py:192
  909.4 5.9 fusion.321
  915.3 5.7 fusion.322
  921.1 8.4 fusion.314
  929.6 4.5 collective-permute-start.91
  941.6 15.8 %collective-permute-done.91 = bf16[1024,512]{1,0:T(8,128)(2,1)S(1)} collective-permute-done((bf16[1024,512]{1,0:T(8,128)(2,1)}, bf16[1024,512]{1,0:T(8,128)(2,1)S(1)}, u32[]{:S(2)}, u32[]{:S(2)}) %collective-permute-start.91) | collective-permute-done | bytes 1048608 | tf_op jit(solution)/shard_map/ppermute | solution.py:26
  969.8 15.6 %collective-permute-done.77 = bf16[256,2048]{0,1:T(8,128)(2,1)S(1)} collective-permute-done((bf16[256,2048]{0,1:T(8,128)(2,1)}, bf16[256,2048]{0,1:T(8,128)(2,1)S(1)}, u32[]{:S(2)}, u32[]{:S(2)}) %collective-permute-start.77) | collective-permute-done | bytes 1048608 | tf_op jit(solution)/shard_map/ppermute | solution.py:332
  1000.3 5.4 collective-permute-start.79
  1009.5 7.5 collective-permute-done.106
  1024.1 10.1 add_bitcast_fusion
  1034.2 4.7 collective-permute-start.108
  1050.0 5.8 collective-permute-start.97
  1056.3 8.3 collective-permute-start.96
  1069.9 5.8 collective-permute-start.80
  1084.2 16.8 %collective-permute-done.99 = bf16[1024,512]{1,0:T(8,128)(2,1)} collective-permute-done((bf16[1024,512]{1,0:T(8,128)(2,1)}, bf16[1024,512]{1,0:T(8,128)(2,1)}, u32[]{:S(2)}, u32[]{:S(2)}) %collective-permute-start.99) | collective-permute-done | bytes 1048608 | tf_op jit(solution)/shard_map/ppermute | solution.py:26
  1118.8 11.4 collective-permute-done.101
  1149.2 7.0 collective-permute-done.104
  (923 shorter events, 429.4 us)
Async XLA Ops:
  7.3 459.2 %all-gather.3.cloned.1.call-start = ((), (), s32[]{:S(2)}) async-start(), calls=%async_computation | async-start | bytes 6291456 | tf_op jit(solution)/shard_map/all_gather | solution.py:383
  8.0 489.4 %all-gather.5.cloned.1.call-start = ((), (), s32[]{:S(2)}) async-start(), calls=%async_computation.1 | async-start | bytes 12582912 | tf_op jit(solution)/shard_map/all_gather | solution.py:382
  9.0 98.3 %collective-permute-start.1 = (bf16[256,2048]{0,1:T(8,128)(2,1)S(1)}, bf16[256,2048]{0,1:T(8,128)(2,1)}, u32[]{:S(2)}, u32[]{:S(2)}) collective-permute-start(bf16[256,2048]{0,1:T(8,128)(2,1)S(1)} %copy.189), channel_id=1, source_target_pairs={{0,2},{2,0},{4,6},{6,4},{8,10},{10,8},{12,14},{14,12},{16,18},{18,... | collective-permute-start | bytes 3145736 | tf_op jit(solution)/shard_map/ppermute | solution.py:26
  12.0 173.6 %collective-permute-start = (bf16[256,2048]{0,1:T(8,128)(2,1)S(1)}, bf16[256,2048]{0,1:T(8,128)(2,1)}, u32[]{:S(2)}, u32[]{:S(2)}) collective-permute-start(bf16[256,2048]{0,1:T(8,128)(2,1)S(1)} %copy.189), channel_id=1, source_target_pairs={{0,1},{1,0},{2,3},{3,2},{4,5},{5,4},{6,7},{7,6},{8,9},{9,8},{10,11... | collective-permute-start | bytes 3145736 | tf_op jit(solution)/shard_map/ppermute | solution.py:26
  12.9 33.5 %collective-permute-start.5 = (bf16[16,128]{1,0:T(8,128)(2,1)}, bf16[16,128]{1,0:T(8,128)(2,1)}, u32[]{:S(2)}, u32[]{:S(2)}) collective-permute-start(bf16[16,128]{1,0:T(8,128)(2,1)} %pad_bitcast_fusion.1), channel_id=1, source_target_pairs={{0,2},{2,0},{4,6},{6,4},{8,10},{10,8},{12,14},{14,12},{16,18},{18,... | collective-permute-start | bytes 12296 | tf_op jit(solution)/shard_map/ppermute | solution.py:26
  13.9 29.8 %collective-permute-start.3 = (bf16[3,64,1024]{2,1,0:T(8,128)(2,1)}, bf16[3,64,1024]{2,1,0:T(8,128)(2,1)}, u32[]{:S(2)}, u32[]{:S(2)}) collective-permute-start(bf16[3,64,1024]{2,1,0:T(8,128)(2,1)} %get-tuple-element.518), channel_id=1, source_target_pairs={{0,2},{2,0},{4,6},{6,4},{8,10},{10,8},{12,14},{14,12},{16,18},{18,... | collective-permute-start | bytes 1179656 | tf_op jit(solution)/shard_map/ppermute | solution.py:26
  16.5 36.5 %collective-permute-start.11 = (bf16[64,1024]{1,0:T(8,128)(2,1)}, bf16[64,1024]{1,0:T(8,128)(2,1)}, u32[]{:S(2)}, u32[]{:S(2)}) collective-permute-start(bf16[64,1024]{1,0:T(8,128)(2,1)} %get-tuple-element.530), channel_id=1, source_target_pairs={{0,1},{1,0},{2,3},{3,2},{4,5},{5,4},{6,7},{7,6},{8,9},{9,8},{10,11... | collective-permute-start | bytes 393224 | tf_op jit(solution)/shard_map/ppermute | solution.py:26
  53.0 35.4 %collective-permute-start.13 = (bf16[256,512]{1,0:T(8,128)(2,1)S(1)}, bf16[256,512]{1,0:T(8,128)(2,1)S(1)}, u32[]{:S(2)}, u32[]{:S(2)}) collective-permute-start(bf16[256,512]{1,0:T(8,128)(2,1)S(1)} %bitcast.302), channel_id=1, source_target_pairs={{0,16},{2,18},{4,20},{6,22},{8,24},{10,26},{12,28},{14,30},{16,0},... | collective-permute-start | bytes 786440 | tf_op jit(solution)/shard_map/ppermute | solution.py:26
  57.1 51.4 %collective-permute-start.21 = (bf16[256,512]{1,0:T(8,128)(2,1)}, bf16[256,512]{1,0:T(8,128)(2,1)S(1)}, u32[]{:S(2)}, u32[]{:S(2)}) collective-permute-start(bf16[256,512]{1,0:T(8,128)(2,1)} %bitcast.22), channel_id=1, source_target_pairs={{0,24},{2,26},{4,28},{6,30},{8,16},{10,18},{12,20},{14,22},{16,8},... | collective-permute-start | bytes 786440 | tf_op jit(solution)/shard_map/ppermute | solution.py:26
  65.8 45.0 %collective-permute-start.20 = (bf16[256,512]{1,0:T(8,128)(2,1)}, bf16[256,512]{1,0:T(8,128)(2,1)S(1)}, u32[]{:S(2)}, u32[]{:S(2)}) collective-permute-start(bf16[256,512]{1,0:T(8,128)(2,1)} %bitcast.22), channel_id=1, source_target_pairs={{0,16},{2,18},{4,20},{6,22},{8,24},{10,26},{12,28},{14,30},{16,0},... | collective-permute-start | bytes 786440 | tf_op jit(solution)/shard_map/ppermute | solution.py:26
  108.5 44.4 %collective-permute-start.8 = (bf16[272,512]{1,0:T(8,128)(2,1)S(1)}, bf16[272,512]{1,0:T(8,128)(2,1)S(1)}, u32[]{:S(2)}, u32[]{:S(2)}) collective-permute-start(bf16[272,512]{1,0:T(8,128)(2,1)S(1)} %pad_maximum_fusion.25), channel_id=1, source_target_pairs={{0,16},{2,18},{4,20},{6,22},{8,24},{10,26},{12,28},{14,30},{16,0},... | collective-permute-start | bytes 835592 | tf_op jit(solution)/shard_map/ppermute | solution.py:26
  110.8 76.8 %collective-permute-start.2 = (bf16[256,2048]{0,1:T(8,128)(2,1)}, bf16[256,2048]{0,1:T(8,128)(2,1)S(1)}, u32[]{:S(2)}, u32[]{:S(2)}) collective-permute-start(bf16[256,2048]{0,1:T(8,128)(2,1)} %collective-permute-done.1), channel_id=1, source_target_pairs={{0,1},{1,0},{2,3},{3,2},{4,5},{5,4},{6,7},{7,6},{8,9},{9,8},{10,11... | collective-permute-start | bytes 3145736 | tf_op jit(solution)/shard_map/ppermute | solution.py:26
  116.7 45.9 %collective-permute-start.27 = (bf16[128,1024]{1,0:T(8,128)(2,1)S(1)}, bf16[128,1024]{1,0:T(8,128)(2,1)S(1)}, u32[]{:S(2)}, u32[]{:S(2)}) collective-permute-start(bf16[128,1024]{1,0:T(8,128)(2,1)S(1)} %maximum_select_fusion.26), channel_id=1, source_target_pairs={{0,24},{2,26},{4,28},{6,30},{8,16},{10,18},{12,20},{14,22},{16,8},... | collective-permute-start | bytes 786440 | tf_op jit(solution)/shard_map/ppermute | solution.py:26
  123.1 60.8 %collective-permute-start.26 = (bf16[128,1024]{1,0:T(8,128)(2,1)S(1)}, bf16[128,1024]{1,0:T(8,128)(2,1)S(1)}, u32[]{:S(2)}, u32[]{:S(2)}) collective-permute-start(bf16[128,1024]{1,0:T(8,128)(2,1)S(1)} %maximum_select_fusion.26), channel_id=1, source_target_pairs={{0,16},{2,18},{4,20},{6,22},{8,24},{10,26},{12,28},{14,30},{16,0},... | collective-permute-start | bytes 786440 | tf_op jit(solution)/shard_map/ppermute | solution.py:26
  161.0 31.3 %collective-permute-start.15 = (bf16[4,1,256,512]{3,2,1,0:T(8,128)(2,1)S(1)}, bf16[4,1,256,512]{3,2,1,0:T(8,128)(2,1)S(1)}, u32[]{:S(2)}, u32[]{:S(2)}) collective-permute-start(bf16[4,1,256,512]{3,2,1,0:T(8,128)(2,1)S(1)} %bitcast.278), channel_id=1, source_target_pairs={{0,4},{2,6},{4,0},{6,2},{8,12},{10,14},{12,8},{14,10},{16,20},{18,... | collective-permute-start | bytes 3145736 | tf_op jit(solution)/shard_map/ppermute | solution.py:26
  162.7 55.1 %collective-permute-start.17 = (bf16[256,2176]{0,1:T(8,128)(2,1)S(1)}, bf16[256,2176]{0,1:T(8,128)(2,1)S(1)}, u32[]{:S(2)}, u32[]{:S(2)}) collective-permute-start(bf16[256,2176]{0,1:T(8,128)(2,1)S(1)} %copy-done.48), channel_id=1, source_target_pairs={{0,24},{2,26},{4,28},{6,30},{8,16},{10,18},{12,20},{14,22},{16,8},... | collective-permute-start | bytes 3342344 | tf_op jit(solution)/shard_map/ppermute | solution.py:26
  184.0 58.3 %collective-permute-start.18 = (bf16[256,2176]{0,1:T(8,128)(2,1)S(1)}, bf16[256,2176]{0,1:T(8,128)(2,1)S(1)}, u32[]{:S(2)}, u32[]{:S(2)}) collective-permute-start(bf16[256,2176]{0,1:T(8,128)(2,1)S(1)} %copy-done.48), channel_id=1, source_target_pairs={{0,16},{2,18},{4,20},{6,22},{8,24},{10,26},{12,28},{14,30},{16,0},... | collective-permute-start | bytes 3342344 | tf_op jit(solution)/shard_map/ppermute | solution.py:26
  185.6 56.6 %collective-permute-start.16 = (bf16[256,2176]{0,1:T(8,128)(2,1)S(1)}, bf16[256,2176]{0,1:T(8,128)(2,1)S(1)}, u32[]{:S(2)}, u32[]{:S(2)}) collective-permute-start(bf16[256,2176]{0,1:T(8,128)(2,1)S(1)} %copy-done.48), channel_id=1, source_target_pairs={{0,8},{2,10},{4,12},{6,14},{8,0},{10,2},{12,4},{14,6},{16,24},{18,... | collective-permute-start | bytes 3342344 | tf_op jit(solution)/shard_map/ppermute | solution.py:26
  187.6 26.6 %collective-permute-start.22 = (bf16[4,1,256,512]{3,2,1,0:T(8,128)(2,1)S(1)}, bf16[4,1,256,512]{3,2,1,0:T(8,128)(2,1)S(1)}, u32[]{:S(2)}, u32[]{:S(2)}) collective-permute-start(bf16[4,1,256,512]{3,2,1,0:T(8,128)(2,1)S(1)} %bitcast.280), channel_id=1, source_target_pairs={{0,4},{2,6},{4,0},{6,2},{8,12},{10,14},{12,8},{14,10},{16,20},{18,... | collective-permute-start | bytes 3145736 | tf_op jit(solution)/shard_map/ppermute | solution.py:26
  192.3 51.9 %collective-permute-start.10 = (bf16[4,1,272,512]{3,2,1,0:T(8,128)(2,1)S(1)}, bf16[4,1,272,512]{3,2,1,0:T(8,128)(2,1)S(1)}, u32[]{:S(2)}, u32[]{:S(2)}) collective-permute-start(bf16[4,1,272,512]{3,2,1,0:T(8,128)(2,1)S(1)} %bitcast.276), channel_id=1, source_target_pairs={{0,4},{2,6},{4,0},{6,2},{8,12},{10,14},{12,8},{14,10},{16,20},{18,... | collective-permute-start | bytes 3342344 | tf_op jit(solution)/shard_map/ppermute | solution.py:26
  214.2 84.7 %collective-permute-start.28 = (bf16[4,1,1,128,1024]{4,3,2,1,0:T(8,128)(2,1)}, bf16[4,1,1,128,1024]{4,3,2,1,0:T(8,128)(2,1)}, u32[]{:S(2)}, u32[]{:S(2)}) collective-permute-start(bf16[4,1,1,128,1024]{4,3,2,1,0:T(8,128)(2,1)} %bitcast.31), channel_id=1, source_target_pairs={{0,4},{2,6},{4,0},{6,2},{8,12},{10,14},{12,8},{14,10},{16,20},{18,... | collective-permute-start | bytes 3145736 | tf_op jit(solution)/shard_map/ppermute | solution.py:26
  302.9 51.5 %collective-permute-start.29 = (bf16[4,2,1,128,1024]{4,3,2,1,0:T(8,128)(2,1)}, bf16[4,2,1,128,1024]{4,3,2,1,0:T(8,128)(2,1)}, u32[]{:S(2)}, u32[]{:S(2)}) collective-permute-start(bf16[4,2,1,128,1024]{4,3,2,1,0:T(8,128)(2,1)} %maximum_select_fusion.4), channel_id=1, source_target_pairs={{0,2},{2,0},{4,6},{6,4},{8,10},{10,8},{12,14},{14,12},{16,18},{18,... | collective-permute-start | bytes 6291464 | tf_op jit(solution)/shard_map/ppermute | solution.py:26
  311.8 87.4 %collective-permute-start.31 = (bf16[512,2048]{1,0:T(8,128)(2,1)S(1)}, bf16[512,2048]{1,0:T(8,128)(2,1)S(1)}, u32[]{:S(2)}, u32[]{:S(2)}) collective-permute-start(bf16[512,2048]{1,0:T(8,128)(2,1)S(1)} %pad_maximum_fusion.3), channel_id=1, source_target_pairs={{0,2},{2,0},{4,6},{6,4},{8,10},{10,8},{12,14},{14,12},{16,18},{18,... | collective-permute-start | bytes 6291464 | tf_op jit(solution)/shard_map/ppermute | solution.py:26
  313.7 85.7 %collective-permute-start.32 = (bf16[512,2048]{1,0:T(8,128)(2,1)S(1)}, bf16[512,2048]{1,0:T(8,128)(2,1)S(1)}, u32[]{:S(2)}, u32[]{:S(2)}) collective-permute-start(bf16[512,2048]{1,0:T(8,128)(2,1)S(1)} %pad_maximum_fusion.4), channel_id=1, source_target_pairs={{0,4},{2,6},{4,0},{6,2},{8,12},{10,14},{12,8},{14,10},{16,20},{18,... | collective-permute-start | bytes 6291464 | tf_op jit(solution)/shard_map/ppermute | solution.py:26
  316.1 46.2 %collective-permute-start.44 = (bf16[256,2048]{1,0:T(8,128)(2,1)S(1)}, bf16[256,2048]{1,0:T(8,128)(2,1)S(1)}, u32[]{:S(2)}, u32[]{:S(2)}) collective-permute-start(bf16[256,2048]{1,0:T(8,128)(2,1)S(1)} %maximum_select_fusion.11), channel_id=1, source_target_pairs={{0,1},{1,0},{2,3},{3,2},{4,5},{5,4},{6,7},{7,6},{8,9},{9,8},{10,11... | collective-permute-start | bytes 3145736 | tf_op jit(solution)/shard_map/ppermute | solution.py:26
  317.2 123.3 %collective-permute-start.33 = (bf16[512,2048]{1,0:T(8,128)(2,1)S(1)}, bf16[512,2048]{1,0:T(8,128)(2,1)S(1)}, u32[]{:S(2)}, u32[]{:S(2)}) collective-permute-start(bf16[512,2048]{1,0:T(8,128)(2,1)S(1)} %pad_maximum_fusion.5), channel_id=1, source_target_pairs={{0,6},{2,4},{4,2},{6,0},{8,14},{10,12},{12,10},{14,8},{16,22},{18,... | collective-permute-start | bytes 6291464 | tf_op jit(solution)/shard_map/ppermute | solution.py:26
  358.8 83.7 %collective-permute-start.30 = (bf16[2048,1024]{1,0:T(8,128)(2,1)S(1)}, bf16[2048,1024]{1,0:T(8,128)(2,1)S(1)}, u32[]{:S(2)}, u32[]{:S(2)}) collective-permute-start(bf16[2048,1024]{1,0:T(8,128)(2,1)S(1)} %bitcast.282), channel_id=1, source_target_pairs={{0,1},{1,0},{2,3},{3,2},{4,5},{5,4},{6,7},{7,6},{8,9},{9,8},{10,11... | collective-permute-start | bytes 12582920 | tf_op jit(solution)/shard_map/ppermute | solution.py:26
  448.7 32.6 %collective-permute-start.37 = (bf16[256,2176]{0,1:T(8,128)(2,1)}, bf16[256,2176]{0,1:T(8,128)(2,1)}, u32[]{:S(2)}, u32[]{:S(2)}) collective-permute-start(bf16[256,2176]{0,1:T(8,128)(2,1)} %pad_maximum_fusion.17), channel_id=1, source_target_pairs={{8,0},{10,2},{12,4},{14,6},{16,8},{18,10},{20,12},{22,14},{24,16},... | collective-permute-start | bytes 3342344 | tf_op jit(solution)/shard_map/ppermute | solution.py:337
  450.0 31.3 %collective-permute-start.38 = (bf16[256,2176]{0,1:T(8,128)(2,1)}, bf16[256,2176]{0,1:T(8,128)(2,1)}, u32[]{:S(2)}, u32[]{:S(2)}) collective-permute-start(bf16[256,2176]{0,1:T(8,128)(2,1)} %pad_maximum_fusion.17), channel_id=1, source_target_pairs={{0,8},{2,10},{4,12},{6,14},{8,16},{10,18},{12,20},{14,22},{16,24},... | collective-permute-start | bytes 3342344 | tf_op jit(solution)/shard_map/ppermute | solution.py:332
  487.4 47.5 %collective-permute-start.39 = (bf16[128,2176]{1,0:T(8,128)(2,1)}, bf16[128,2176]{1,0:T(8,128)(2,1)}, u32[]{:S(2)}, u32[]{:S(2)}) collective-permute-start(bf16[128,2176]{1,0:T(8,128)(2,1)} %get-tuple-element.420), channel_id=1, source_target_pairs={{0,2},{2,0},{4,6},{6,4},{8,10},{10,8},{12,14},{14,12},{16,18},{18,... | collective-permute-start | bytes 1671176 | tf_op jit(solution)/shard_map/ppermute | solution.py:26
  488.7 46.2 %collective-permute-start.40 = (bf16[128,2176]{1,0:T(8,128)(2,1)}, bf16[128,2176]{1,0:T(8,128)(2,1)}, u32[]{:S(2)}, u32[]{:S(2)}) collective-permute-start(bf16[128,2176]{1,0:T(8,128)(2,1)} %get-tuple-element.419), channel_id=1, source_target_pairs={{0,4},{2,6},{4,0},{6,2},{8,12},{10,14},{12,8},{14,10},{16,20},{18,... | collective-permute-start | bytes 1671176 | tf_op jit(solution)/shard_map/ppermute | solution.py:26
  490.5 44.4 %collective-permute-start.41 = (bf16[128,2176]{1,0:T(8,128)(2,1)}, bf16[128,2176]{1,0:T(8,128)(2,1)}, u32[]{:S(2)}, u32[]{:S(2)}) collective-permute-start(bf16[128,2176]{1,0:T(8,128)(2,1)} %get-tuple-element.418), channel_id=1, source_target_pairs={{0,6},{2,4},{4,2},{6,0},{8,14},{10,12},{12,10},{14,8},{16,22},{18,... | collective-permute-start | bytes 1671176 | tf_op jit(solution)/shard_map/ppermute | solution.py:26
  546.4 29.5 %collective-permute-start.45 = (bf16[128,2176]{1,0:T(8,128)(2,1)}, bf16[128,2176]{1,0:T(8,128)(2,1)}, u32[]{:S(2)}, u32[]{:S(2)}) collective-permute-start(bf16[128,2176]{1,0:T(8,128)(2,1)} %get-tuple-element.416), channel_id=1, source_target_pairs={{0,2},{2,0},{4,6},{6,4},{8,10},{10,8},{12,14},{14,12},{16,18},{18,... | collective-permute-start | bytes 1671176 | tf_op jit(solution)/shard_map/ppermute | solution.py:26
  546.7 29.1 %collective-permute-start.46 = (bf16[128,2176]{1,0:T(8,128)(2,1)}, bf16[128,2176]{1,0:T(8,128)(2,1)}, u32[]{:S(2)}, u32[]{:S(2)}) collective-permute-start(bf16[128,2176]{1,0:T(8,128)(2,1)} %get-tuple-element.415), channel_id=1, source_target_pairs={{0,4},{2,6},{4,0},{6,2},{8,12},{10,14},{12,8},{14,10},{16,20},{18,... | collective-permute-start | bytes 1671176 | tf_op jit(solution)/shard_map/ppermute | solution.py:26
  548.2 27.7 %collective-permute-start.47 = (bf16[128,2176]{1,0:T(8,128)(2,1)}, bf16[128,2176]{1,0:T(8,128)(2,1)}, u32[]{:S(2)}, u32[]{:S(2)}) collective-permute-start(bf16[128,2176]{1,0:T(8,128)(2,1)} %get-tuple-element.414), channel_id=1, source_target_pairs={{0,6},{2,4},{4,2},{6,0},{8,14},{10,12},{12,10},{14,8},{16,22},{18,... | collective-permute-start | bytes 1671176 | tf_op jit(solution)/shard_map/ppermute | solution.py:26
  653.1 73.8 %collective-permute-start.66 = (bf16[256,2176]{0,1:T(8,128)(2,1)S(1)}, bf16[256,2176]{0,1:T(8,128)(2,1)}, u32[]{:S(2)}, u32[]{:S(2)}) collective-permute-start(bf16[256,2176]{0,1:T(8,128)(2,1)S(1)} %get-tuple-element.567), channel_id=1, source_target_pairs={{24,16},{26,18},{28,20},{30,22},{25,17},{27,19},{29,21},{31,23}} | collective-permute-start | bytes 3342344 | tf_op jit(solution)/shard_map/ppermute | solution.py:337
  654.9 72.0 %collective-permute-start.65 = (bf16[256,2176]{0,1:T(8,128)(2,1)S(1)}, bf16[256,2176]{0,1:T(8,128)(2,1)}, u32[]{:S(2)}, u32[]{:S(2)}) collective-permute-start(bf16[256,2176]{0,1:T(8,128)(2,1)S(1)} %get-tuple-element.567), channel_id=1, source_target_pairs={{0,8},{2,10},{4,12},{6,14},{1,9},{3,11},{5,13},{7,15}} | collective-permute-start | bytes 3342344 | tf_op jit(solution)/shard_map/ppermute | solution.py:332
  729.8 28.1 %collective-permute-start.69 = (bf16[256,2176]{0,1:T(8,128)(2,1)S(1)}, bf16[256,2176]{0,1:T(8,128)(2,1)S(1)}, u32[]{:S(2)}, u32[]{:S(2)}) collective-permute-start(bf16[256,2176]{0,1:T(8,128)(2,1)S(1)} %get-tuple-element.569), channel_id=1, source_target_pairs={{16,8},{18,10},{20,12},{22,14},{24,16},{26,18},{28,20},{30,22},{17... | collective-permute-start | bytes 3342344 | tf_op jit(solution)/shard_map/ppermute | solution.py:337
  735.2 24.3 %collective-permute-start.67 = (bf16[256,2176]{0,1:T(8,128)(2,1)S(1)}, bf16[256,2176]{0,1:T(8,128)(2,1)S(1)}, u32[]{:S(2)}, u32[]{:S(2)}) collective-permute-start(bf16[256,2176]{0,1:T(8,128)(2,1)S(1)} %get-tuple-element.569), channel_id=1, source_target_pairs={{0,8},{2,10},{4,12},{6,14},{8,16},{10,18},{12,20},{14,22},{1,9},{3... | collective-permute-start | bytes 3342344 | tf_op jit(solution)/shard_map/ppermute | solution.py:332
  758.2 34.0 %collective-permute-start.70 = (bf16[256,2176]{0,1:T(8,128)(2,1)S(1)}, bf16[256,2176]{0,1:T(8,128)(2,1)S(1)}, u32[]{:S(2)}, u32[]{:S(2)}) collective-permute-start(bf16[256,2176]{0,1:T(8,128)(2,1)S(1)} %add_convert_fusion), channel_id=1, source_target_pairs={{8,0},{10,2},{12,4},{14,6},{16,8},{18,10},{20,12},{22,14},{24,16},... | collective-permute-start | bytes 3342344 | tf_op jit(solution)/shard_map/ppermute | solution.py:337
  760.0 32.2 %collective-permute-start.68 = (bf16[256,2176]{0,1:T(8,128)(2,1)S(1)}, bf16[256,2176]{0,1:T(8,128)(2,1)S(1)}, u32[]{:S(2)}, u32[]{:S(2)}) collective-permute-start(bf16[256,2176]{0,1:T(8,128)(2,1)S(1)} %select_convert_fusion), channel_id=1, source_target_pairs={{0,8},{2,10},{4,12},{6,14},{8,16},{10,18},{12,20},{14,22},{16,24},... | collective-permute-start | bytes 3342344 | tf_op jit(solution)/shard_map/ppermute | solution.py:332
  799.3 88.3 %collective-permute-start.71 = (bf16[512,2048]{1,0:T(8,128)(2,1)}, bf16[512,2048]{1,0:T(8,128)(2,1)}, u32[]{:S(2)}, u32[]{:S(2)}) collective-permute-start(bf16[512,2048]{1,0:T(8,128)(2,1)} %pad_maximum_fusion.12), channel_id=1, source_target_pairs={{0,2},{2,0},{4,6},{6,4},{8,10},{10,8},{12,14},{14,12},{16,18},{18,... | collective-permute-start | bytes 6291464 | tf_op jit(solution)/shard_map/ppermute | solution.py:26
  801.7 90.8 %collective-permute-start.72 = (bf16[512,2048]{1,0:T(8,128)(2,1)}, bf16[512,2048]{1,0:T(8,128)(2,1)}, u32[]{:S(2)}, u32[]{:S(2)}) collective-permute-start(bf16[512,2048]{1,0:T(8,128)(2,1)} %pad_maximum_fusion.13), channel_id=1, source_target_pairs={{0,4},{2,6},{4,0},{6,2},{8,12},{10,14},{12,8},{14,10},{16,20},{18,... | collective-permute-start | bytes 6291464 | tf_op jit(solution)/shard_map/ppermute | solution.py:26
  810.2 38.0 %collective-permute-start.76 = (bf16[256,1024]{0,1:T(8,128)(2,1)}, bf16[256,1024]{0,1:T(8,128)(2,1)}, u32[]{:S(2)}, u32[]{:S(2)}) collective-permute-start(bf16[256,1024]{0,1:T(8,128)(2,1)} %get-tuple-element.509), channel_id=1, source_target_pairs={{0,1},{1,0},{2,3},{3,2},{4,5},{5,4},{6,7},{7,6},{8,9},{9,8},{10,11... | collective-permute-start | bytes 1572872 | tf_op jit(solution)/shard_map/ppermute | solution.py:26
  816.4 30.4 %collective-permute-start.74 = (bf16[256,1024]{1,0:T(8,128)(2,1)}, bf16[256,1024]{1,0:T(8,128)(2,1)}, u32[]{:S(2)}, u32[]{:S(2)}) collective-permute-start(bf16[256,1024]{1,0:T(8,128)(2,1)} %get-tuple-element.506), channel_id=1, source_target_pairs={{0,2},{2,0},{4,6},{6,4},{8,10},{10,8},{12,14},{14,12},{16,18},{18,... | collective-permute-start | bytes 1572872 | tf_op jit(solution)/shard_map/ppermute | solution.py:26
  818.0 77.2 %collective-permute-start.73 = (bf16[512,2048]{1,0:T(8,128)(2,1)}, bf16[512,2048]{1,0:T(8,128)(2,1)}, u32[]{:S(2)}, u32[]{:S(2)}) collective-permute-start(bf16[512,2048]{1,0:T(8,128)(2,1)} %pad_maximum_fusion.14), channel_id=1, source_target_pairs={{0,6},{2,4},{4,2},{6,0},{8,14},{10,12},{12,10},{14,8},{16,22},{18,... | collective-permute-start | bytes 6291464 | tf_op jit(solution)/shard_map/ppermute | solution.py:26
  848.2 171.7 %collective-permute-start.111 = (bf16[1024,2048]{1,0:T(8,128)(2,1)}, bf16[1024,2048]{1,0:T(8,128)(2,1)}, u32[]{:S(2)}, u32[]{:S(2)}) collective-permute-start(bf16[1024,2048]{1,0:T(8,128)(2,1)} %fusion.19), channel_id=1, source_target_pairs={{0,1},{1,0},{2,3},{3,2},{4,5},{5,4},{6,7},{7,6},{8,9},{9,8},{10,11... | collective-permute-start | bytes 12582920 | tf_op jit(solution)/shard_map/ppermute | solution.py:26
  852.9 81.4 %collective-permute-start.112 = (bf16[512,2048]{1,0:T(8,128)(2,1)}, bf16[512,2048]{1,0:T(8,128)(2,1)}, u32[]{:S(2)}, u32[]{:S(2)}) collective-permute-start(bf16[512,2048]{1,0:T(8,128)(2,1)} %convolution_convert_fusion.12), channel_id=1, source_target_pairs={{0,1},{1,0},{2,3},{3,2},{4,5},{5,4},{6,7},{7,6},{8,9},{9,8},{10,11... | collective-permute-start | bytes 6291464 | tf_op jit(solution)/shard_map/ppermute | solution.py:26
  887.6 75.5 %collective-permute-start.105 = (bf16[1024,1024]{1,0:T(8,128)(2,1)}, bf16[1024,1024]{1,0:T(8,128)(2,1)}, u32[]{:S(2)}, u32[]{:S(2)}) collective-permute-start(bf16[1024,1024]{1,0:T(8,128)(2,1)} %convolution_convert_fusion.13), channel_id=1, source_target_pairs={{0,2},{2,0},{4,6},{6,4},{8,10},{10,8},{12,14},{14,12},{16,18},{18,... | collective-permute-start | bytes 6291464 | tf_op jit(solution)/shard_map/ppermute | solution.py:26
  900.6 69.1 %collective-permute-start.78 = (bf16[256,2048]{0,1:T(8,128)(2,1)}, bf16[256,2048]{0,1:T(8,128)(2,1)}, u32[]{:S(2)}, u32[]{:S(2)}) collective-permute-start(bf16[256,2048]{0,1:T(8,128)(2,1)} %get-tuple-element.572), channel_id=1, source_target_pairs={{24,16},{26,18},{28,20},{30,22},{25,17},{27,19},{29,21},{31,23}} | collective-permute-start | bytes 3145736 | tf_op jit(solution)/shard_map/ppermute | solution.py:337
  929.6 27.8 %collective-permute-start.91 = (bf16[1024,512]{1,0:T(8,128)(2,1)}, bf16[1024,512]{1,0:T(8,128)(2,1)S(1)}, u32[]{:S(2)}, u32[]{:S(2)}) collective-permute-start(bf16[1024,512]{1,0:T(8,128)(2,1)} %convolution_convert_fusion.16), channel_id=1, source_target_pairs={{0,4},{2,6},{4,0},{6,2},{8,12},{10,14},{12,8},{14,10},{16,20},{18,... | collective-permute-start | bytes 3145736 | tf_op jit(solution)/shard_map/ppermute | solution.py:26
  934.4 72.2 %collective-permute-start.83 = (bf16[512,2048]{0,1:T(8,128)(2,1)S(1)}, bf16[512,2048]{0,1:T(8,128)(2,1)S(1)}, u32[]{:S(2)}, u32[]{:S(2)}) collective-permute-start(bf16[512,2048]{0,1:T(8,128)(2,1)S(1)} %pad_maximum_fusion.15), channel_id=1, source_target_pairs={{0,1},{1,0},{2,3},{3,2},{4,5},{5,4},{6,7},{7,6},{8,9},{9,8},{10,11... | collective-permute-start | bytes 6291464 | tf_op jit(solution)/shard_map/ppermute | solution.py:26
  957.4 28.0 %collective-permute-start.77 = (bf16[256,2048]{0,1:T(8,128)(2,1)}, bf16[256,2048]{0,1:T(8,128)(2,1)S(1)}, u32[]{:S(2)}, u32[]{:S(2)}) collective-permute-start(bf16[256,2048]{0,1:T(8,128)(2,1)} %get-tuple-element.572), channel_id=1, source_target_pairs={{0,8},{2,10},{4,12},{6,14},{1,9},{3,11},{5,13},{7,15}} | collective-permute-start | bytes 3145736 | tf_op jit(solution)/shard_map/ppermute | solution.py:332
  963.2 27.8 %collective-permute-start.94 = (bf16[256,512]{1,0:T(8,128)(2,1)S(1)}, bf16[256,512]{1,0:T(8,128)(2,1)S(1)}, u32[]{:S(2)}, u32[]{:S(2)}) collective-permute-start(bf16[256,512]{1,0:T(8,128)(2,1)S(1)} %get-tuple-element.433), channel_id=1, source_target_pairs={{0,24},{2,26},{4,28},{6,30},{8,16},{10,18},{12,20},{14,22},{16,8},... | collective-permute-start | bytes 786440 | tf_op jit(solution)/shard_map/ppermute | solution.py:26
  969.7 26.8 %collective-permute-start.93 = (bf16[256,512]{1,0:T(8,128)(2,1)S(1)}, bf16[256,512]{1,0:T(8,128)(2,1)S(1)}, u32[]{:S(2)}, u32[]{:S(2)}) collective-permute-start(bf16[256,512]{1,0:T(8,128)(2,1)S(1)} %get-tuple-element.434), channel_id=1, source_target_pairs={{0,16},{2,18},{4,20},{6,22},{8,24},{10,26},{12,28},{14,30},{16,0},... | collective-permute-start | bytes 786440 | tf_op jit(solution)/shard_map/ppermute | solution.py:26
  990.9 26.1 %collective-permute-start.106 = (bf16[4,128,1024]{2,1,0:T(8,128)(2,1)S(1)}, bf16[4,128,1024]{2,1,0:T(8,128)(2,1)S(1)}, u32[]{:S(2)}, u32[]{:S(2)}) collective-permute-start(bf16[4,128,1024]{2,1,0:T(8,128)(2,1)S(1)} %fusion.148), channel_id=1, source_target_pairs={{0,4},{2,6},{4,0},{6,2},{8,12},{10,14},{12,8},{14,10},{16,20},{18,... | collective-permute-start | bytes 3145736 | tf_op jit(solution)/shard_map/ppermute | solution.py:26
  996.5 69.4 %collective-permute-start.81 = (bf16[256,2048]{0,1:T(8,128)(2,1)}, bf16[256,2048]{0,1:T(8,128)(2,1)}, u32[]{:S(2)}, u32[]{:S(2)}) collective-permute-start(bf16[256,2048]{0,1:T(8,128)(2,1)} %get-tuple-element.574), channel_id=1, source_target_pairs={{16,8},{18,10},{20,12},{22,14},{24,16},{26,18},{28,20},{30,22},{17... | collective-permute-start | bytes 3145736 | tf_op jit(solution)/shard_map/ppermute | solution.py:337
  1000.3 33.9 %collective-permute-start.79 = (bf16[256,2048]{0,1:T(8,128)(2,1)}, bf16[256,2048]{0,1:T(8,128)(2,1)}, u32[]{:S(2)}, u32[]{:S(2)}) collective-permute-start(bf16[256,2048]{0,1:T(8,128)(2,1)} %get-tuple-element.574), channel_id=1, source_target_pairs={{0,8},{2,10},{4,12},{6,14},{8,16},{10,18},{12,20},{14,22},{1,9},{3... | collective-permute-start | bytes 3145736 | tf_op jit(solution)/shard_map/ppermute | solution.py:332
  1006.6 35.7 %collective-permute-start.95 = (bf16[1024,512]{1,0:T(8,128)(2,1)}, bf16[1024,512]{1,0:T(8,128)(2,1)}, u32[]{:S(2)}, u32[]{:S(2)}) collective-permute-start(bf16[1024,512]{1,0:T(8,128)(2,1)} %convolution_convert_fusion.15), channel_id=1, source_target_pairs={{0,4},{2,6},{4,0},{6,2},{8,12},{10,14},{12,8},{14,10},{16,20},{18,... | collective-permute-start | bytes 3145736 | tf_op jit(solution)/shard_map/ppermute | solution.py:26
  1017.0 61.2 %collective-permute-start.84 = (bf16[256,2048]{0,1:T(8,128)(2,1)}, bf16[256,2048]{0,1:T(8,128)(2,1)S(1)}, u32[]{:S(2)}, u32[]{:S(2)}) collective-permute-start(bf16[256,2048]{0,1:T(8,128)(2,1)} %fusion.79), channel_id=1, source_target_pairs={{0,2},{2,0},{4,6},{6,4},{8,10},{10,8},{12,14},{14,12},{16,18},{18,... | collective-permute-start | bytes 3145736 | tf_op jit(solution)/shard_map/ppermute | solution.py:26
  1019.9 25.1 %collective-permute-start.109 = (bf16[128,1024]{1,0:T(8,128)(2,1)}, bf16[128,1024]{1,0:T(8,128)(2,1)}, u32[]{:S(2)}, u32[]{:S(2)}) collective-permute-start(bf16[128,1024]{1,0:T(8,128)(2,1)} %get-tuple-element.430), channel_id=1, source_target_pairs={{0,24},{2,26},{4,28},{6,30},{8,16},{10,18},{12,20},{14,22},{16,8},... | collective-permute-start | bytes 786440 | tf_op jit(solution)/shard_map/ppermute | solution.py:26
  1068.5 65.8 %collective-permute-start.82 = (bf16[256,2048]{0,1:T(8,128)(2,1)}, bf16[256,2048]{0,1:T(8,128)(2,1)}, u32[]{:S(2)}, u32[]{:S(2)}) collective-permute-start(bf16[256,2048]{0,1:T(8,128)(2,1)} %add_convert_fusion.1), channel_id=1, source_target_pairs={{8,0},{10,2},{12,4},{14,6},{16,8},{18,10},{20,12},{22,14},{24,16},... | collective-permute-start | bytes 3145736 | tf_op jit(solution)/shard_map/ppermute | solution.py:337
  1069.9 67.6 %collective-permute-start.80 = (bf16[256,2048]{0,1:T(8,128)(2,1)}, bf16[256,2048]{0,1:T(8,128)(2,1)}, u32[]{:S(2)}, u32[]{:S(2)}) collective-permute-start(bf16[256,2048]{0,1:T(8,128)(2,1)} %select_convert_fusion.2), channel_id=1, source_target_pairs={{0,8},{2,10},{4,12},{6,14},{8,16},{10,18},{12,20},{14,22},{16,24},... | collective-permute-start | bytes 3145736 | tf_op jit(solution)/shard_map/ppermute | solution.py:332
  1075.7 25.4 %collective-permute-start.99 = (bf16[1024,512]{1,0:T(8,128)(2,1)}, bf16[1024,512]{1,0:T(8,128)(2,1)}, u32[]{:S(2)}, u32[]{:S(2)}) collective-permute-start(bf16[1024,512]{1,0:T(8,128)(2,1)} %convolution_convert_fusion.14), channel_id=1, source_target_pairs={{0,4},{2,6},{4,0},{6,2},{8,12},{10,14},{12,8},{14,10},{16,20},{18,... | collective-permute-start | bytes 3145736 | tf_op jit(solution)/shard_map/ppermute | solution.py:26
  (253 other events, 3587.2 us)
Sparse Core Ops, SparseCore 0:
  9.7 16.3 all-gather.2
  27.6 21.5 all-gather.4

commit v5 on v4

--- a/solution.py
+++ b/solution.py
@@ -486,7 +486,7 @@
         return [
             [blocks[d][:capacity]]
             + [got[j][d * capacity : (d + 1) * capacity] for j in range(1, ring)]
-            for d in range(PLANES)
+            for d in range(len(blocks))
         ]
 
     pickers, up_picked = [], []
@@ -510,6 +510,7 @@
         query_raw, key_raw, value_low, tables, scales, live_lanes
     )
     left_y = split_columns(first_low, bits - 1)
+    attended, up_arrived = lax.optimization_barrier((attended, up_arrived))
     far_heads = swap(attended[2 * tokens :], "expert", 1)
     crossed = jnp.concatenate([attended[tokens : 2 * tokens], far_heads[tokens:]], axis=1)
     crossed = swap(crossed, "fsdp", 1)
@@ -535,7 +536,6 @@
 
     extra = jnp.concatenate(split_three(gate_soft * kept), axis=1)
     in_planes = planes_of(widened(mixed_in, extra))
-    up_arrived, mixed_late = lax.optimization_barrier((up_arrived, mixed_in))
     up_rows = jnp.concatenate([p for parts in up_arrived for p in parts], axis=0)
     picked = [contract_rows(pickers[d], in_planes[d], bf16) for d in range(PLANES)]
     picked[0], up_rows = lax.optimization_barrier((picked[0], up_rows))
@@ -591,15 +591,18 @@
         if d < last:
             block, arrived[d + 1] = lax.optimization_barrier((block, arrived[d + 1]))
         arrived[d] = exchange(block)
-    arrived[last], row_inputs, hidden_gated, both_grad = lax.optimization_barrier(
-        (arrived[last], row_inputs, hidden_gated, both_grad)
-    )
-    rows_out = [matmul(gated, outer_now).astype(bf16) for gated in hidden_gated]
+    arrived[3], row_inputs, both_grad = lax.optimization_barrier(
+        (arrived[3], row_inputs, both_grad)
+    )
     row_inputs = jnp.concatenate(row_inputs, axis=0)
-    hidden_gated = jnp.concatenate(hidden_gated, axis=0)
     both_grad = jnp.concatenate(both_grad, axis=0)
-
-    def bring_back(arrived):
+    inner_local = contract_rows(row_inputs, both_grad, bf16)
+    arrived[2], gated_rows = lax.optimization_barrier((arrived[2], hidden_gated))
+    outer_local = contract_rows(jnp.concatenate(gated_rows, axis=0), up_rows, bf16)
+    arrived[1], late_gated = lax.optimization_barrier((arrived[1], gated_rows))
+    rows_out = [matmul(gated, outer_now).astype(bf16) for gated in late_gated]
+
+    def relayed(arrived):
         parts = [None] * PLANES
         for d in reversed(range(PLANES)):
             parts[d] = matmul(pickers[d], jnp.concatenate(arrived[d], axis=0))
@@ -615,20 +618,16 @@
         down = step_down((near + down).astype(bf16), [1, 2, 3])
         return parts[0] + up.astype(f32) + down.astype(f32)
 
-    eff_half = EFF // 2
-    inner_sent = contract_rows(pick(row_inputs, (1 - core) * half, half), both_grad, bf16)
-    inner_kept = contract_rows(pick(row_inputs, core * half, half), both_grad)
-    outer_sent = contract_rows(
-        pick(hidden_gated, (1 - core) * eff_half, eff_half), up_rows, bf16
-    )
-    outer_kept = contract_rows(pick(hidden_gated, core * eff_half, eff_half), up_rows)
-    back = bring_back(arrived)
-    back, rows_out, inner_sent, inner_kept, outer_sent, outer_kept = lax.optimization_barrier(
-        (back, rows_out, inner_sent, inner_kept, outer_sent, outer_kept)
-    )
-    inner_grad = inner_kept + swap(inner_sent, "fsdp", 1).astype(f32)
-    outer_grad = outer_kept + swap(outer_sent, "fsdp", 1).astype(f32)
-    out_arrived = exchange_all(rows_out)
+    back = relayed(arrived)
+    back, rows_out, inner_local, outer_local = lax.optimization_barrier(
+        (back, rows_out, inner_local, outer_local)
+    )
+    inner_grad = lax.psum_scatter(
+        inner_local, "fsdp", scatter_dimension=0, tiled=True
+    ).astype(f32)
+    outer_grad = lax.psum_scatter(
+        outer_local, "fsdp", scatter_dimension=0, tiled=True
+    ).astype(f32)
     mixed_grad = back[:, :width]
     gate_grad = (
         back[:, width : width + owners]
@@ -638,7 +637,7 @@
 
     soft_grad = gate_soft * (gate_grad - jnp.sum(gate_soft * gate_grad, axis=-1, keepdims=True))
     logit_grad = soft_grad.astype(bf16)
-    router_local = contract_rows(mixed_late, logit_grad)
+    router_local = contract_rows(mixed_in, logit_grad)
     mixed_grad = mixed_grad + contract_cols(logit_grad, router_full)
     residual_part, second_terms = rms_back(residual, second_inverse, second_gain, mixed_grad)
     residual_grad = upstream + residual_part
@@ -649,6 +648,8 @@
         contract_cols(branch_mine, output_own) + contract_cols(branch_theirs, output_peer)
     ).astype(bf16)
     far_grad = swap(pick(attended_grad, (1 - parity) * half, half), "expert", 1)
+    rows_out, far_grad = lax.optimization_barrier((rows_out, far_grad))
+    out_arrived = exchange_all(rows_out)
     chip_grad = jnp.stack([pick(attended_grad, parity * half, half), far_grad])
     crossed = swap(pick(chip_grad, (1 - core) * quarter, quarter, 2), "fsdp", 1)
     kept_grad = pick(chip_grad, core * quarter, quarter, 2)
@@ -663,41 +664,35 @@
         query_raw, key_raw, value_low, attended_grad, lse, tables, scales, live_lanes
     )
 
-    out_arrived, query_low_grad, key_low_grad, value_low_grad = lax.optimization_barrier(
-        (out_arrived, query_low_grad, key_low_grad, value_low_grad)
-    )
     y_bit = bits - 1
-    steps = [key_low_grad, value_low_grad, query_low_grad]
-    grads_late = lax.optimization_barrier(
-        (steps, [contract_rows(left_y[1], right, bf16) for right in steps])
-    )
-    steps, sent = grads_late
-    key_came = swap(sent[0], "expert", 1 << y_bit)
-    output_now = contract_rows(attended_x[0], branch_both) + output_came.astype(f32)
-    output_now = scatter_rest(output_now, ascending)
-    sent[1], key_came = lax.optimization_barrier((sent[1], key_came))
-    value_came = swap(sent[1], "expert", 1 << y_bit)
-    sent[2], value_came = lax.optimization_barrier((sent[2], value_came))
-    query_came = swap(sent[2], "expert", 1 << y_bit)
-    kept = [contract_rows(left_y[0], right) for right in steps]
-    blocks = [
-        scatter_planes(scatter_rest(k + c.astype(f32), pair_order_bits))
-        for k, c in zip(kept, (key_came, value_came, query_came))
-    ]
-    output_block = scatter_planes(output_now)
-    key_late_grad, value_late_grad, query_late_grad = steps
-    layer_out = (residual + bring_back(out_arrived)).astype(bf16)
-
-    all_grad = (
-        contract_cols(key_late_grad, key_late)
-        + contract_cols(value_late_grad, value_late)
-        + contract_cols(query_late_grad, query_late)
+    steps = jnp.concatenate([key_low_grad, value_low_grad, query_low_grad], axis=1)
+    sent = contract_rows(left_y[1], steps, bf16)
+    sent, steps = lax.optimization_barrier((sent, steps))
+    weights_came = swap(sent, "expert", 1 << y_bit)
+    all_grad = sum(
+        contract_cols(steps[:, i * quarter : (i + 1) * quarter], weight)
+        for i, weight in enumerate((key_own, value_own, query_own))
     )
     own_part, peer_part, far_part, far_peer = jnp.split(all_grad, 4, axis=0)
     crossed = swap(jnp.concatenate([peer_part, far_peer], axis=0).astype(bf16), "fsdp", 1)
     own_part = own_part + crossed[:tokens].astype(f32)
     far_part = (far_part + crossed[tokens:].astype(f32)).astype(bf16)
     far_back = swap(far_part, "expert", 1)
+    weights_came, output_came = lax.optimization_barrier((weights_came, output_came))
+    output_now = contract_rows(attended_x[0], branch_both) + output_came.astype(f32)
+    output_now = scatter_rest(output_now, ascending)
+    weights_now = contract_rows(left_y[0], steps) + weights_came.astype(f32)
+    weights_now = scatter_rest(weights_now, pair_order_bits)
+    output_now, far_back, inner_grad, outer_grad = lax.optimization_barrier(
+        (output_now, far_back, inner_grad, outer_grad)
+    )
+    blocks = scatter_planes(weights_now)
+    output_block = scatter_planes(output_now)
+    mixed = relayed(out_arrived)
+    blocks, mixed = lax.optimization_barrier((blocks, mixed))
+    layer_out = residual + mixed
+    layer_out = layer_out.astype(bf16)
+
     normed_grad = own_part + far_back.astype(f32)
     hidden_part, first_terms = rms_back(
         hidden_f[:tokens], first_inverse[:tokens], first_gain, normed_grad
@@ -736,7 +731,7 @@
         cross = swap(pick(block, (1 - core) * rows_dev, rows_dev, 0), "fsdp", 1)
         return in_order(core, keep, cross, 1)
 
-    blocks = jnp.stack(blocks).reshape(3, 2, 2, rows_dev, quarter)
+    blocks = blocks.reshape(2, 2, rows_dev, 3, quarter).transpose(3, 0, 1, 2, 4)
     kept = lax.dynamic_index_in_dim(blocks, core, 2, keepdims=False)
     cross = swap(lax.dynamic_index_in_dim(blocks, 1 - core, 2, keepdims=False), "fsdp", 1)
     blocks = in_order(core, kept, cross, 3)

time: 1180 us -> 1180 us (level)
  waiting for transfers between devices: 414 us -> 483 us
  starting transfers between devices: 216 us -> 168 us
  matrix products: 236 us -> 220 us
    ppermute x95 -> x85, starting transfers between devices: 169 us -> 126 us  [swap(): return lax.ppermute(block, axis, [(i, i ^ mask) for i in range(count)])]
    ppermute x95 -> x85, waiting for transfers between devices: 389 us -> 415 us  [swap(): return lax.ppermute(block, axis, [(i, i ^ mask) for i in range(count)])]
    ppermute x9, waiting for transfers between devices: 15.6 us -> 40.3 us  [step_up(): lax.ppermute(block, 'expert', [(p * ring + i, (p + 1) * ring + i) for p i...]
    ppermute x9, waiting for transfers between devices: 8.7 us -> 27.2 us  [step_down(): lax.ppermute(block, 'expert', [(p * ring + i, (p - 1) * ring + i) for p i...]
    broadcast_in_dim x2 -> x0, other arithmetic: 14.3 us -> none  [the longest x1 10.1 us: on_device(): inner_grad[None]]
    dot_general x21 -> x15, matrix products: 77.5 us -> 67.3 us  [contract_rows(): lax.dot_general(left, right, (((0,), (0,)), ((), ())), preferred_element_...]
    unnamed x436 -> x352, local copies, waits for them, and re-layouts: 39.3 us -> 37.3 us
  transfers between devices with their start and end apart: 115 -> 107, of which waited for: 42 -> 42; matrix products, arithmetic and copies ran while one was open for 32% -> 29% of each run, Pallas kernels for 4% -> 4%
where the time goes in v5:
time: 1180 us; the launch traced here: 1170 us
  waiting for transfers between devices  483 us (41%)
  matrix products  220 us (19%)
  starting transfers between devices  168 us (14%)
  other arithmetic  124 us (11%)
  local copies, waits for them, and re-layouts  106 us (9%)
  Pallas kernels  49.4 us (4%)
  between operations  17.4 us (1%)
    ppermute x85, waiting for transfers between devices, swap(): return lax.ppermute(block, axis, [(i, i ^ mask) for i in range(count)])  415 us
    ppermute x85, starting transfers between devices, swap(): return lax.ppermute(block, axis, [(i, i ^ mask) for i in range(count)])  126 us
    dot_general x26, matrix products, matmul(): return jnp.dot(left, right, preferred_element_type=f32)  79.6 us
    dot_general x11, matrix products, contract_cols(): lax.dot_general(left, right, (((1,), (1,)), ((), ())), preferred_element_...  73.5 us
    dot_general x15, matrix products, contract_rows(): lax.dot_general(left, right, (((0,), (0,)), ((), ())), preferred_element_...  67.3 us
    ppermute x9, waiting for transfers between devices, step_up(): lax.ppermute(block, 'expert', [(p * ring + i, (p + 1) * ring + i) for p i...  40.3 us
    unnamed x352, local copies, waits for them, and re-layouts  37.3 us
    ppermute x9, starting transfers between devices, step_up(): lax.ppermute(block, 'expert', [(p * ring + i, (p + 1) * ring + i) for p i...  31.3 us
  transfers between devices with their start and end apart: 107, of which 42 were waited for; matrix products, arithmetic and copies ran while one was open for 29% of the time, Pallas kernels for 4%

profile of v5, /device:TPU:0, one launch (start us, length us, event | category | flops | bytes accessed | tf_op | source)
XLA Modules:
  0.0 1169.6 jit_solution(2953079099029273365)
XLA Ops:
  43.4 5.7 collective-permute-done.12
  52.1 18.1 %collective-permute-done.13 = bf16[256,512]{1,0:T(8,128)(2,1)S(1)} collective-permute-done((bf16[256,512]{1,0:T(8,128)(2,1)S(1)}, bf16[256,512]{1,0:T(8,128)(2,1)S(1)}, u32[]{:S(2)}, u32[]{:S(2)}) %collective-permute-start.13) | collective-permute-done | bytes 262176 | tf_op jit(solution)/shard_map/ppermute | solution.py:26
  70.3 7.2 collective-permute-start.8
  78.1 9.4 collective-permute-done.20
  87.5 6.2 collective-permute-start.7
  100.7 9.3 collective-permute-done.7
  118.5 12.7 %collective-permute-done.29 = bf16[128,1024]{1,0:T(8,128)(2,1)S(1)} collective-permute-done((bf16[128,1024]{1,0:T(8,128)(2,1)S(1)}, bf16[128,1024]{1,0:T(8,128)(2,1)S(1)}, u32[]{:S(2)}, u32[]{:S(2)}) %collective-permute-start.29) | collective-permute-done | bytes 262176 | tf_op jit(solution)/shard_map/ppermute | solution.py:26
  132.7 4.6 collective-permute-start.16
  146.8 10.4 collective-permute-done.22
  162.2 26.1 %collective-permute-done.17 = bf16[256,2176]{0,1:T(8,128)(2,1)S(1)} collective-permute-done((bf16[256,2176]{0,1:T(8,128)(2,1)S(1)}, bf16[256,2176]{0,1:T(8,128)(2,1)S(1)}, u32[]{:S(2)}, u32[]{:S(2)}) %collective-permute-start.17) | collective-permute-done | bytes 1114144 | tf_op jit(solution)/shard_map/ppermute | solution.py:26
  188.3 46.8 %collective-permute-done.18 = bf16[256,2176]{0,1:T(8,128)(2,1)S(1)} collective-permute-done((bf16[256,2176]{0,1:T(8,128)(2,1)S(1)}, bf16[256,2176]{0,1:T(8,128)(2,1)S(1)}, u32[]{:S(2)}, u32[]{:S(2)}) %collective-permute-start.18) | collective-permute-done | bytes 1114144 | tf_op jit(solution)/shard_map/ppermute | solution.py:26
  279.1 20.4 %attention_forward.1 = (bf16[1024,512]{1,0:T(8,128)(2,1)S(1)}, f32[4,8,1024]{2,1,0:T(8,128)S(1)}) custom-call(f32[1024,512]{1,0:T(8,128)S(1)} %copy-done, f32[1024,512]{1,0:T(8,128)S(1)} %fusion.320.k_ref, bf16[1024,512]{1,0:T(8,128)(2,1)S(1)} %copy-done.4, f32[2,1024,128]{2,1,0:T(8,128)S(1)} %pad_maximum_fusion.17.table_ref, ...), custom_call_target="tpu_custom_call" | custom-call | tf_op jit(solution)/shard_map/attention_forward/pallas_call | solution.py:109
  305.7 4.0 collective-permute-done.25
  311.4 41.3 %collective-permute-done.24 = bf16[512,2048]{1,0:T(8,128)(2,1)} collective-permute-done((bf16[512,2048]{1,0:T(8,128)(2,1)}, bf16[512,2048]{1,0:T(8,128)(2,1)}, u32[]{:S(2)}, u32[]{:S(2)}) %collective-permute-start.24) | collective-permute-done | bytes 2097184 | tf_op jit(solution)/shard_map/ppermute | solution.py:26
  358.7 40.8 %collective-permute-done.32 = bf16[4,2,1,128,1024]{4,3,2,1,0:T(8,128)(2,1)S(1)} collective-permute-done((bf16[4,2,1,128,1024]{4,3,2,1,0:T(8,128)(2,1)S(1)}, bf16[4,2,1,128,1024]{4,3,2,1,0:T(8,128)(2,1)S(1)}, u32[]{:S(2)}, u32[]{:S(2)}) %collective-permute-start.32) | collective-permute-done | bytes 2097184 | tf_op jit(solution)/shard_map/ppermute | solution.py:26
  400.4 8.5 collective-permute-done.26
  425.2 5.6 collective-permute-start.38
  436.6 14.8 %fusion.37 = f32[2048,1024]{0,1:T(8,128)} fusion(bf16[2048,2048]{1,0:T(8,128)(2,1)} %copy-done.135, bf16[1,1024,2048]{2,1,0:T(8,128)(2,1)} %all-gather.3.cloned.1.call-done), kind=kOutput, calls=%fused_computation.80 | convolution fusion | flops 8589934592 | bytes 20971520 | tf_op jit(solution)/shard_map/dot_general | solution.py:36
  466.3 8.2 fusion.56
  475.6 5.2 multiply_convert_fusion.12
  489.4 10.1 fusion.39
  501.0 11.9 %collective-permute-done.43 = bf16[256,2176]{0,1:T(8,128)(2,1)} collective-permute-done((bf16[256,2176]{0,1:T(8,128)(2,1)}, bf16[256,2176]{0,1:T(8,128)(2,1)}, u32[]{:S(2)}, u32[]{:S(2)}) %collective-permute-start.43) | collective-permute-done | bytes 1114144 | tf_op jit(solution)/shard_map/ppermute | solution.py:337
  515.9 8.4 fusion.53
  524.4 5.2 multiply_convert_fusion.10
  538.2 10.5 fusion.40
  548.7 8.5 collective-permute-done.48
  557.3 4.0 convolution_convert_fusion
  561.4 8.3 fusion.50
  569.9 5.2 multiply_convert_fusion.8
  582.2 9.9 fusion.41
  594.8 7.2 collective-permute-done.52
  602.1 8.6 fusion.47
  610.8 5.2 multiply_convert_fusion.6
  617.6 9.1 fusion.42
  642.9 7.1 collective-permute-done.54
  662.8 23.5 %fusion.15 = bf16[2048,2048]{1,0:T(8,128)(2,1)} fusion(bf16[512,2048]{0,1:T(8,128)(2,1)} %pad_maximum_fusion.11, bf16[512,2048]{0,1:T(8,128)(2,1)} %pad_maximum_fusion.10, bf16[512,2048]{0,1:T(8,128)(2,1)} %pad_maximum_fusion.9, bf16[512,2048]{0,1:T(8,128)(2,1)} %pad_maximum_fusion.8, bf16[512,2048]{1,0:T(8,128)(2,1)} %slice.575, ...), kind=kOutput, calls=%fused_computation.18 | convolution fusion | flops 17251172352 | bytes 25165824 | tf_op jit(solution)/shard_map/dot_general | solution.py:30
  693.0 12.6 %fusion.43 = bf16[1024,2048]{1,0:T(8,128)(2,1)} fusion(bf16[2048,2048]{1,0:T(8,128)(2,1)} %copy-done.135, bf16[512,1024]{0,1:T(8,128)(2,1)S(1)} %copy-done.92, bf16[512,1024]{0,1:T(8,128)(2,1)S(1)} %copy-done.90, bf16[512,1024]{0,1:T(8,128)(2,1)S(1)} %copy-done.88, bf16[512,1024]{0,1:T(8,128)(2,1)S(1)} %copy-done.86), kind=kOutput, calls=%fused_computation.89 | convolution fusion | flops 8608808960 | bytes 16777216 | tf_op jit(solution)/shard_map/dot_general | solution.py:30
  705.6 4.2 select_convert_fusion.1
  715.9 3.8 fusion.58
  719.7 3.7 fusion.61
  725.8 4.8 collective-permute-done.67
  731.0 4.9 collective-permute-start.68
  737.7 3.8 fusion.64
  745.2 5.9 collective-permute-done.68
  772.6 4.5 maximum_convert_fusion
  802.5 29.0 %attention_backward.1 = (bf16[1024,512]{1,0:T(8,128)(2,1)S(1)}, bf16[1024,512]{1,0:T(8,128)(2,1)S(1)}, bf16[1024,512]{1,0:T(8,128)(2,1)S(1)}, f32[2,8,128]{2,1,0:T(8,128)S(1)}) custom-call(f32[1024,512]{1,0:T(8,128)S(1)} %copy-done.1, f32[1024,512]{1,0:T(8,128)S(1)} %fusion.320.k_ref, bf16[1024,512]{1,0:T(8,128)(2,1)S(1)} %copy-done.5, ...), custom_call_target="tpu_custom_call" | custom-call | tf_op jit(solution)/shard_map/attention_backward/pallas_call | solution.py:192
  833.1 4.9 convolution_convert_fusion.8
  845.4 8.0 fusion.316
  855.1 32.1 %collective-permute-done.80 = bf16[512,2048]{1,0:T(8,128)(2,1)} collective-permute-done((bf16[512,2048]{1,0:T(8,128)(2,1)}, bf16[512,2048]{1,0:T(8,128)(2,1)}, u32[]{:S(2)}, u32[]{:S(2)}) %collective-permute-start.80) | collective-permute-done | bytes 2097184 | tf_op jit(solution)/shard_map/ppermute | solution.py:26
  891.6 4.5 collective-permute-start.82
  900.5 13.9 %collective-permute-done.82 = bf16[256,2048]{0,1:T(8,128)(2,1)S(1)} collective-permute-done((bf16[256,2048]{0,1:T(8,128)(2,1)S(1)}, bf16[256,2048]{0,1:T(8,128)(2,1)S(1)}, u32[]{:S(2)}, u32[]{:S(2)}) %collective-permute-start.82) | collective-permute-done | bytes 1048608 | tf_op jit(solution)/shard_map/ppermute | solution.py:332
  914.9 4.7 collective-permute-start.84
  920.3 7.6 collective-permute-done.75
  927.9 25.4 %collective-permute-done.74 = bf16[1024,1536]{1,0:T(8,128)(2,1)} collective-permute-done((bf16[1024,1536]{1,0:T(8,128)(2,1)}, bf16[1024,1536]{1,0:T(8,128)(2,1)}, u32[]{:S(2)}, u32[]{:S(2)}) %collective-permute-start.74) | collective-permute-done | bytes 3145760 | tf_op jit(solution)/shard_map/ppermute | solution.py:26
  953.3 5.3 convert_add_fusion
  968.3 25.9 %collective-permute-done.76 = bf16[256,1536]{1,0:T(8,128)(2,1)S(1)} collective-permute-done((bf16[256,1536]{1,0:T(8,128)(2,1)S(1)}, bf16[256,1536]{1,0:T(8,128)(2,1)S(1)}, u32[]{:S(2)}, u32[]{:S(2)}) %collective-permute-start.76) | collective-permute-done | bytes 786464 | tf_op jit(solution)/shard_map/ppermute | solution.py:26
  999.8 17.4 %collective-permute-done.77 = bf16[256,1536]{1,0:T(8,128)(2,1)S(1)} collective-permute-done((bf16[256,1536]{1,0:T(8,128)(2,1)S(1)}, bf16[256,1536]{1,0:T(8,128)(2,1)S(1)}, u32[]{:S(2)}, u32[]{:S(2)}) %collective-permute-start.77) | collective-permute-done | bytes 786464 | tf_op jit(solution)/shard_map/ppermute | solution.py:26
  1020.2 14.4 %collective-permute-done.85 = bf16[256,2048]{0,1:T(8,128)(2,1)S(1)} collective-permute-done((bf16[256,2048]{0,1:T(8,128)(2,1)S(1)}, bf16[256,2048]{0,1:T(8,128)(2,1)S(1)}, u32[]{:S(2)}, u32[]{:S(2)}) %collective-permute-start.85) | collective-permute-done | bytes 1048608 | tf_op jit(solution)/shard_map/ppermute | solution.py:332
  1056.6 28.3 %collective-permute-done.98 = bf16[3,64,1024]{2,0,1:T(4,128)(2,1)S(1)} collective-permute-done((bf16[3,64,1024]{2,0,1:T(4,128)(2,1)S(1)}, bf16[3,64,1024]{2,0,1:T(4,128)(2,1)S(1)}, u32[]{:S(2)}, u32[]{:S(2)}) %collective-permute-start.98) | collective-permute-done | bytes 393248 | tf_op jit(solution)/shard_map/ppermute | solution.py:26
  1086.0 4.1 convert_element_type.571
  1090.1 6.7 convert_element_type.570
  1110.3 17.8 %collective-permute-start.100 = (bf16[128,1024]{1,0:T(8,128)(2,1)}, bf16[128,1024]{1,0:T(8,128)(2,1)}, u32[]{:S(2)}, u32[]{:S(2)}) collective-permute-start(bf16[128,1024]{1,0:T(8,128)(2,1)} %get-tuple-element.420), channel_id=1, source_target_pairs={{0,16},{2,18},{4,20},{6,22},{8,24},{10,26},{12,28},{14,30},{16,0},... | collective-permute-start | bytes 786440 | tf_op jit(solution)/shard_map/ppermute | solution.py:26
  1133.6 13.7 %collective-permute-done.94 = f32[16,128]{1,0:T(8,128)S(1)} collective-permute-done((f32[16,128]{1,0:T(8,128)S(1)}, f32[16,128]{1,0:T(8,128)S(1)}, u32[]{:S(2)}, u32[]{:S(2)}) %collective-permute-start.94) | collective-permute-done | bytes 8224 | tf_op jit(solution)/shard_map/ppermute | solution.py:26
  1150.7 4.3 subtract_add_fusion
  (814 shorter events, 388.2 us)
Async XLA Ops:
  7.2 429.4 %all-gather.3.cloned.1.call-start = ((), (), s32[]{:S(2)}) async-start(), calls=%async_computation.2 | async-start | bytes 6291456 | tf_op jit(solution)/shard_map/all_gather | solution.py:383
  8.0 458.3 %all-gather.5.cloned.1.call-start = ((), (), s32[]{:S(2)}) async-start(), calls=%async_computation.3 | async-start | bytes 12582912 | tf_op jit(solution)/shard_map/all_gather | solution.py:382
  12.9 27.6 %collective-permute-start.11 = (bf16[64,1024]{1,0:T(8,128)(2,1)}, bf16[64,1024]{1,0:T(8,128)(2,1)}, u32[]{:S(2)}, u32[]{:S(2)}) collective-permute-start(bf16[64,1024]{1,0:T(8,128)(2,1)} %get-tuple-element.512), channel_id=1, source_target_pairs={{0,1},{1,0},{2,3},{3,2},{4,5},{5,4},{6,7},{7,6},{8,9},{9,8},{10,11... | collective-permute-start | bytes 393224 | tf_op jit(solution)/shard_map/ppermute | solution.py:26
  14.4 82.0 %collective-permute-start.1 = (bf16[256,2048]{0,1:T(8,128)(2,1)S(1)}, bf16[256,2048]{0,1:T(8,128)(2,1)}, u32[]{:S(2)}, u32[]{:S(2)}) collective-permute-start(bf16[256,2048]{0,1:T(8,128)(2,1)S(1)} %copy.182), channel_id=1, source_target_pairs={{0,2},{2,0},{4,6},{6,4},{8,10},{10,8},{12,14},{14,12},{16,18},{18,... | collective-permute-start | bytes 3145736 | tf_op jit(solution)/shard_map/ppermute | solution.py:26
  16.5 1069.5 %reduce-scatter.5.cloned.1.call-start = ((), (), s32[]{:S(2)}) async-start(), calls=%async_computation.5 | async-start | bytes 6291456 | tf_op jit(solution)/shard_map/reduce_scatter | solution.py:628
  37.6 32.6 %collective-permute-start.13 = (bf16[256,512]{1,0:T(8,128)(2,1)S(1)}, bf16[256,512]{1,0:T(8,128)(2,1)S(1)}, u32[]{:S(2)}, u32[]{:S(2)}) collective-permute-start(bf16[256,512]{1,0:T(8,128)(2,1)S(1)} %bitcast.261), channel_id=1, source_target_pairs={{0,16},{2,18},{4,20},{6,22},{8,24},{10,26},{12,28},{14,30},{16,0},... | collective-permute-start | bytes 786440 | tf_op jit(solution)/shard_map/ppermute | solution.py:26
  40.3 30.0 %collective-permute-start.14 = (bf16[256,512]{1,0:T(8,128)(2,1)S(1)}, bf16[256,512]{1,0:T(8,128)(2,1)S(1)}, u32[]{:S(2)}, u32[]{:S(2)}) collective-permute-start(bf16[256,512]{1,0:T(8,128)(2,1)S(1)} %bitcast.262), channel_id=1, source_target_pairs={{0,24},{2,26},{4,28},{6,30},{8,16},{10,18},{12,20},{14,22},{16,8},... | collective-permute-start | bytes 786440 | tf_op jit(solution)/shard_map/ppermute | solution.py:26
  41.6 45.9 %collective-permute-start.20 = (bf16[256,512]{1,0:T(8,128)(2,1)}, bf16[256,512]{1,0:T(8,128)(2,1)S(1)}, u32[]{:S(2)}, u32[]{:S(2)}) collective-permute-start(bf16[256,512]{1,0:T(8,128)(2,1)} %bitcast.22), channel_id=1, source_target_pairs={{0,16},{2,18},{4,20},{6,22},{8,24},{10,26},{12,28},{14,30},{16,0},... | collective-permute-start | bytes 786440 | tf_op jit(solution)/shard_map/ppermute | solution.py:26
  49.1 38.4 %collective-permute-start.21 = (bf16[256,512]{1,0:T(8,128)(2,1)}, bf16[256,512]{1,0:T(8,128)(2,1)S(1)}, u32[]{:S(2)}, u32[]{:S(2)}) collective-permute-start(bf16[256,512]{1,0:T(8,128)(2,1)} %bitcast.22), channel_id=1, source_target_pairs={{0,24},{2,26},{4,28},{6,30},{8,16},{10,18},{12,20},{14,22},{16,8},... | collective-permute-start | bytes 786440 | tf_op jit(solution)/shard_map/ppermute | solution.py:26
  70.3 30.0 %collective-permute-start.8 = (bf16[272,512]{1,0:T(8,128)(2,1)S(1)}, bf16[272,512]{1,0:T(8,128)(2,1)S(1)}, u32[]{:S(2)}, u32[]{:S(2)}) collective-permute-start(bf16[272,512]{1,0:T(8,128)(2,1)S(1)} %pad_maximum_fusion.24), channel_id=1, source_target_pairs={{0,16},{2,18},{4,20},{6,22},{8,24},{10,26},{12,28},{14,30},{16,0},... | collective-permute-start | bytes 835592 | tf_op jit(solution)/shard_map/ppermute | solution.py:26
  87.5 49.9 %collective-permute-start = (bf16[256,2048]{0,1:T(8,128)(2,1)S(1)}, bf16[256,2048]{0,1:T(8,128)(2,1)S(1)}, u32[]{:S(2)}, u32[]{:S(2)}) collective-permute-start(bf16[256,2048]{0,1:T(8,128)(2,1)S(1)} %copy.182), channel_id=1, source_target_pairs={{0,1},{1,0},{2,3},{3,2},{4,5},{5,4},{6,7},{7,6},{8,9},{9,8},{10,11... | collective-permute-start | bytes 3145736 | tf_op jit(solution)/shard_map/ppermute | solution.py:26
  93.7 45.5 %collective-permute-start.15 = (bf16[4,1,256,512]{3,2,1,0:T(8,128)(2,1)S(1)}, bf16[4,1,256,512]{3,2,1,0:T(8,128)(2,1)S(1)}, u32[]{:S(2)}, u32[]{:S(2)}) collective-permute-start(bf16[4,1,256,512]{3,2,1,0:T(8,128)(2,1)S(1)} %bitcast.239), channel_id=1, source_target_pairs={{0,4},{2,6},{4,0},{6,2},{8,12},{10,14},{12,8},{14,10},{16,20},{18,... | collective-permute-start | bytes 3145736 | tf_op jit(solution)/shard_map/ppermute | solution.py:26
  110.0 32.3 %collective-permute-start.2 = (bf16[256,2048]{0,1:T(8,128)(2,1)}, bf16[256,2048]{0,1:T(8,128)(2,1)S(1)}, u32[]{:S(2)}, u32[]{:S(2)}) collective-permute-start(bf16[256,2048]{0,1:T(8,128)(2,1)} %collective-permute-done.1), channel_id=1, source_target_pairs={{0,1},{1,0},{2,3},{3,2},{4,5},{5,4},{6,7},{7,6},{8,9},{9,8},{10,11... | collective-permute-start | bytes 3145736 | tf_op jit(solution)/shard_map/ppermute | solution.py:26
  131.2 26.0 %collective-permute-start.22 = (bf16[4,1,256,512]{3,2,1,0:T(8,128)(2,1)S(1)}, bf16[4,1,256,512]{3,2,1,0:T(8,128)(2,1)S(1)}, u32[]{:S(2)}, u32[]{:S(2)}) collective-permute-start(bf16[4,1,256,512]{3,2,1,0:T(8,128)(2,1)S(1)} %bitcast.241), channel_id=1, source_target_pairs={{0,4},{2,6},{4,0},{6,2},{8,12},{10,14},{12,8},{14,10},{16,20},{18,... | collective-permute-start | bytes 3145736 | tf_op jit(solution)/shard_map/ppermute | solution.py:26
  132.7 29.6 %collective-permute-start.16 = (bf16[256,2176]{0,1:T(8,128)(2,1)S(1)}, bf16[256,2176]{0,1:T(8,128)(2,1)S(1)}, u32[]{:S(2)}, u32[]{:S(2)}) collective-permute-start(bf16[256,2176]{0,1:T(8,128)(2,1)S(1)} %copy-done.40), channel_id=1, source_target_pairs={{0,8},{2,10},{4,12},{6,14},{8,0},{10,2},{12,4},{14,6},{16,24},{18,... | collective-permute-start | bytes 3342344 | tf_op jit(solution)/shard_map/ppermute | solution.py:26
  137.5 50.8 %collective-permute-start.17 = (bf16[256,2176]{0,1:T(8,128)(2,1)S(1)}, bf16[256,2176]{0,1:T(8,128)(2,1)S(1)}, u32[]{:S(2)}, u32[]{:S(2)}) collective-permute-start(bf16[256,2176]{0,1:T(8,128)(2,1)S(1)} %copy-done.40), channel_id=1, source_target_pairs={{0,24},{2,26},{4,28},{6,30},{8,16},{10,18},{12,20},{14,22},{16,8},... | collective-permute-start | bytes 3342344 | tf_op jit(solution)/shard_map/ppermute | solution.py:26
  139.2 96.0 %collective-permute-start.18 = (bf16[256,2176]{0,1:T(8,128)(2,1)S(1)}, bf16[256,2176]{0,1:T(8,128)(2,1)S(1)}, u32[]{:S(2)}, u32[]{:S(2)}) collective-permute-start(bf16[256,2176]{0,1:T(8,128)(2,1)S(1)} %copy-done.40), channel_id=1, source_target_pairs={{0,16},{2,18},{4,20},{6,22},{8,24},{10,26},{12,28},{14,30},{16,0},... | collective-permute-start | bytes 3342344 | tf_op jit(solution)/shard_map/ppermute | solution.py:26
  142.3 94.8 %collective-permute-start.10 = (bf16[4,1,272,512]{3,2,1,0:T(8,128)(2,1)S(1)}, bf16[4,1,272,512]{3,2,1,0:T(8,128)(2,1)S(1)}, u32[]{:S(2)}, u32[]{:S(2)}) collective-permute-start(bf16[4,1,272,512]{3,2,1,0:T(8,128)(2,1)S(1)} %bitcast.237), channel_id=1, source_target_pairs={{0,4},{2,6},{4,0},{6,2},{8,12},{10,14},{12,8},{14,10},{16,20},{18,... | collective-permute-start | bytes 3342344 | tf_op jit(solution)/shard_map/ppermute | solution.py:26
  157.2 145.2 %collective-permute-start.31 = (bf16[4,1,1,128,1024]{4,3,2,1,0:T(8,128)(2,1)}, bf16[4,1,1,128,1024]{4,3,2,1,0:T(8,128)(2,1)}, u32[]{:S(2)}, u32[]{:S(2)}) collective-permute-start(bf16[4,1,1,128,1024]{4,3,2,1,0:T(8,128)(2,1)} %bitcast.31), channel_id=1, source_target_pairs={{0,4},{2,6},{4,0},{6,2},{8,12},{10,14},{12,8},{14,10},{16,20},{18,... | collective-permute-start | bytes 3145736 | tf_op jit(solution)/shard_map/ppermute | solution.py:26
  259.8 49.8 %collective-permute-start.25 = (bf16[512,2048]{1,0:T(8,128)(2,1)}, bf16[512,2048]{1,0:T(8,128)(2,1)}, u32[]{:S(2)}, u32[]{:S(2)}) collective-permute-start(bf16[512,2048]{1,0:T(8,128)(2,1)} %pad_maximum_fusion.5), channel_id=1, source_target_pairs={{0,6},{2,4},{4,2},{6,0},{8,14},{10,12},{12,10},{14,8},{16,22},{18,... | collective-permute-start | bytes 6291464 | tf_op jit(solution)/shard_map/ppermute | solution.py:26
  262.8 90.0 %collective-permute-start.24 = (bf16[512,2048]{1,0:T(8,128)(2,1)}, bf16[512,2048]{1,0:T(8,128)(2,1)}, u32[]{:S(2)}, u32[]{:S(2)}) collective-permute-start(bf16[512,2048]{1,0:T(8,128)(2,1)} %pad_maximum_fusion.4), channel_id=1, source_target_pairs={{0,4},{2,6},{4,0},{6,2},{8,12},{10,14},{12,8},{14,10},{16,20},{18,... | collective-permute-start | bytes 6291464 | tf_op jit(solution)/shard_map/ppermute | solution.py:26
  269.5 85.1 %collective-permute-start.23 = (bf16[512,2048]{1,0:T(8,128)(2,1)}, bf16[512,2048]{1,0:T(8,128)(2,1)}, u32[]{:S(2)}, u32[]{:S(2)}) collective-permute-start(bf16[512,2048]{1,0:T(8,128)(2,1)} %pad_maximum_fusion.3), channel_id=1, source_target_pairs={{0,2},{2,0},{4,6},{6,4},{8,10},{10,8},{12,14},{14,12},{16,18},{18,... | collective-permute-start | bytes 6291464 | tf_op jit(solution)/shard_map/ppermute | solution.py:26
  305.1 94.4 %collective-permute-start.32 = (bf16[4,2,1,128,1024]{4,3,2,1,0:T(8,128)(2,1)S(1)}, bf16[4,2,1,128,1024]{4,3,2,1,0:T(8,128)(2,1)S(1)}, u32[]{:S(2)}, u32[]{:S(2)}) collective-permute-start(bf16[4,2,1,128,1024]{4,3,2,1,0:T(8,128)(2,1)S(1)} %maximum_select_fusion.4), channel_id=1, source_target_pairs={{0,2},{2,0},{4,6},{6,4},{8,10},{10,8},{12,14},{14,12},{16,18},{18,... | collective-permute-start | bytes 6291464 | tf_op jit(solution)/shard_map/ppermute | solution.py:26
  356.5 52.4 %collective-permute-start.26 = (bf16[512,512]{1,0:T(8,128)(2,1)S(1)}, bf16[512,512]{1,0:T(8,128)(2,1)S(1)}, u32[]{:S(2)}, u32[]{:S(2)}) collective-permute-start(bf16[512,512]{1,0:T(8,128)(2,1)S(1)} %slice.517), channel_id=1, source_target_pairs={{0,2},{2,0},{4,6},{6,4},{8,10},{10,8},{12,14},{14,12},{16,18},{18,... | collective-permute-start | bytes 1572872 | tf_op jit(solution)/shard_map/ppermute | solution.py:26
  423.9 29.0 %collective-permute-start.37 = (bf16[256,2176]{0,1:T(8,128)(2,1)}, bf16[256,2176]{0,1:T(8,128)(2,1)}, u32[]{:S(2)}, u32[]{:S(2)}) collective-permute-start(bf16[256,2176]{0,1:T(8,128)(2,1)} %pad_maximum_fusion.16), channel_id=1, source_target_pairs={{8,0},{10,2},{12,4},{14,6},{16,8},{18,10},{20,12},{22,14},{24,16},... | collective-permute-start | bytes 3342344 | tf_op jit(solution)/shard_map/ppermute | solution.py:337
  425.2 28.9 %collective-permute-start.38 = (bf16[256,2176]{0,1:T(8,128)(2,1)}, bf16[256,2176]{0,1:T(8,128)(2,1)}, u32[]{:S(2)}, u32[]{:S(2)}) collective-permute-start(bf16[256,2176]{0,1:T(8,128)(2,1)} %pad_maximum_fusion.16), channel_id=1, source_target_pairs={{0,8},{2,10},{4,12},{6,14},{8,16},{10,18},{12,20},{14,22},{16,24},... | collective-permute-start | bytes 3342344 | tf_op jit(solution)/shard_map/ppermute | solution.py:332
  433.6 26.3 %collective-permute-start.35 = (bf16[128,2176]{1,0:T(8,128)(2,1)}, bf16[128,2176]{1,0:T(8,128)(2,1)}, u32[]{:S(2)}, u32[]{:S(2)}) collective-permute-start(bf16[128,2176]{1,0:T(8,128)(2,1)} %get-tuple-element.412), channel_id=1, source_target_pairs={{0,4},{2,6},{4,0},{6,2},{8,12},{10,14},{12,8},{14,10},{16,20},{18,... | collective-permute-start | bytes 1671176 | tf_op jit(solution)/shard_map/ppermute | solution.py:26
  434.1 25.8 %collective-permute-start.36 = (bf16[128,2176]{1,0:T(8,128)(2,1)}, bf16[128,2176]{1,0:T(8,128)(2,1)}, u32[]{:S(2)}, u32[]{:S(2)}) collective-permute-start(bf16[128,2176]{1,0:T(8,128)(2,1)} %get-tuple-element.411), channel_id=1, source_target_pairs={{0,6},{2,4},{4,2},{6,0},{8,14},{10,12},{12,10},{14,8},{16,22},{18,... | collective-permute-start | bytes 1671176 | tf_op jit(solution)/shard_map/ppermute | solution.py:26
  482.9 32.9 %collective-permute-start.40 = (bf16[128,2176]{1,0:T(8,128)(2,1)S(1)}, bf16[128,2176]{1,0:T(8,128)(2,1)S(1)}, u32[]{:S(2)}, u32[]{:S(2)}) collective-permute-start(bf16[128,2176]{1,0:T(8,128)(2,1)S(1)} %get-tuple-element.409), channel_id=1, source_target_pairs={{0,2},{2,0},{4,6},{6,4},{8,10},{10,8},{12,14},{14,12},{16,18},{18,... | collective-permute-start | bytes 1671176 | tf_op jit(solution)/shard_map/ppermute | solution.py:26
  484.4 31.3 %collective-permute-start.41 = (bf16[128,2176]{1,0:T(8,128)(2,1)S(1)}, bf16[128,2176]{1,0:T(8,128)(2,1)S(1)}, u32[]{:S(2)}, u32[]{:S(2)}) collective-permute-start(bf16[128,2176]{1,0:T(8,128)(2,1)S(1)} %get-tuple-element.408), channel_id=1, source_target_pairs={{0,4},{2,6},{4,0},{6,2},{8,12},{10,14},{12,8},{14,10},{16,20},{18,... | collective-permute-start | bytes 1671176 | tf_op jit(solution)/shard_map/ppermute | solution.py:26
  484.9 30.8 %collective-permute-start.42 = (bf16[128,2176]{1,0:T(8,128)(2,1)S(1)}, bf16[128,2176]{1,0:T(8,128)(2,1)S(1)}, u32[]{:S(2)}, u32[]{:S(2)}) collective-permute-start(bf16[128,2176]{1,0:T(8,128)(2,1)S(1)} %get-tuple-element.407), channel_id=1, source_target_pairs={{0,6},{2,4},{4,2},{6,0},{8,14},{10,12},{12,10},{14,8},{16,22},{18,... | collective-permute-start | bytes 1671176 | tf_op jit(solution)/shard_map/ppermute | solution.py:26
  486.4 26.5 %collective-permute-start.43 = (bf16[256,2176]{0,1:T(8,128)(2,1)}, bf16[256,2176]{0,1:T(8,128)(2,1)}, u32[]{:S(2)}, u32[]{:S(2)}) collective-permute-start(bf16[256,2176]{0,1:T(8,128)(2,1)} %collective-permute-done.37), channel_id=1, source_target_pairs={{8,0},{10,2},{12,4},{14,6},{16,8},{18,10},{20,12},{22,14},{9,1},{1... | collective-permute-start | bytes 3342344 | tf_op jit(solution)/shard_map/ppermute | solution.py:337
  487.7 25.2 %collective-permute-start.44 = (bf16[256,2176]{0,1:T(8,128)(2,1)}, bf16[256,2176]{0,1:T(8,128)(2,1)}, u32[]{:S(2)}, u32[]{:S(2)}) collective-permute-start(bf16[256,2176]{0,1:T(8,128)(2,1)} %collective-permute-done.38), channel_id=1, source_target_pairs={{8,16},{10,18},{12,20},{14,22},{16,24},{18,26},{20,28},{22,30},{9,... | collective-permute-start | bytes 3342344 | tf_op jit(solution)/shard_map/ppermute | solution.py:332
  531.1 26.2 %collective-permute-start.48 = (bf16[256,2176]{0,1:T(8,128)(2,1)}, bf16[256,2176]{0,1:T(8,128)(2,1)}, u32[]{:S(2)}, u32[]{:S(2)}) collective-permute-start(bf16[256,2176]{0,1:T(8,128)(2,1)} %collective-permute-done.43), channel_id=1, source_target_pairs={{8,0},{10,2},{12,4},{14,6},{9,1},{11,3},{13,5},{15,7}} | collective-permute-start | bytes 3342344 | tf_op jit(solution)/shard_map/ppermute | solution.py:337
  534.6 26.6 %collective-permute-start.45 = (bf16[128,2176]{1,0:T(8,128)(2,1)}, bf16[128,2176]{1,0:T(8,128)(2,1)S(1)}, u32[]{:S(2)}, u32[]{:S(2)}) collective-permute-start(bf16[128,2176]{1,0:T(8,128)(2,1)} %get-tuple-element.405), channel_id=1, source_target_pairs={{0,2},{2,0},{4,6},{6,4},{8,10},{10,8},{12,14},{14,12},{16,18},{18,... | collective-permute-start | bytes 1671176 | tf_op jit(solution)/shard_map/ppermute | solution.py:26
  535.2 26.0 %collective-permute-start.46 = (bf16[128,2176]{1,0:T(8,128)(2,1)}, bf16[128,2176]{1,0:T(8,128)(2,1)S(1)}, u32[]{:S(2)}, u32[]{:S(2)}) collective-permute-start(bf16[128,2176]{1,0:T(8,128)(2,1)} %get-tuple-element.404), channel_id=1, source_target_pairs={{0,4},{2,6},{4,0},{6,2},{8,12},{10,14},{12,8},{14,10},{16,20},{18,... | collective-permute-start | bytes 1671176 | tf_op jit(solution)/shard_map/ppermute | solution.py:26
  652.8 52.8 %collective-permute-start.65 = (bf16[256,2176]{0,1:T(8,128)(2,1)}, bf16[256,2176]{0,1:T(8,128)(2,1)}, u32[]{:S(2)}, u32[]{:S(2)}) collective-permute-start(bf16[256,2176]{0,1:T(8,128)(2,1)} %get-tuple-element.549), channel_id=1, source_target_pairs={{0,8},{2,10},{4,12},{6,14},{1,9},{3,11},{5,13},{7,15}} | collective-permute-start | bytes 3342344 | tf_op jit(solution)/shard_map/ppermute | solution.py:332
  656.2 49.4 %collective-permute-start.66 = (bf16[256,2176]{0,1:T(8,128)(2,1)}, bf16[256,2176]{0,1:T(8,128)(2,1)}, u32[]{:S(2)}, u32[]{:S(2)}) collective-permute-start(bf16[256,2176]{0,1:T(8,128)(2,1)} %get-tuple-element.549), channel_id=1, source_target_pairs={{24,16},{26,18},{28,20},{30,22},{25,17},{27,19},{29,21},{31,23}} | collective-permute-start | bytes 3342344 | tf_op jit(solution)/shard_map/ppermute | solution.py:337
  659.3 27.0 %collective-permute-start.56 = (bf16[128,2176]{1,0:T(8,128)(2,1)}, bf16[128,2176]{1,0:T(8,128)(2,1)}, u32[]{:S(2)}, u32[]{:S(2)}) collective-permute-start(bf16[128,2176]{1,0:T(8,128)(2,1)} %get-tuple-element.393), channel_id=1, source_target_pairs={{0,2},{2,0},{4,6},{6,4},{8,10},{10,8},{12,14},{14,12},{16,18},{18,... | collective-permute-start | bytes 1671176 | tf_op jit(solution)/shard_map/ppermute | solution.py:26
  660.7 25.6 %collective-permute-start.57 = (bf16[128,2176]{1,0:T(8,128)(2,1)}, bf16[128,2176]{1,0:T(8,128)(2,1)}, u32[]{:S(2)}, u32[]{:S(2)}) collective-permute-start(bf16[128,2176]{1,0:T(8,128)(2,1)} %get-tuple-element.392), channel_id=1, source_target_pairs={{0,4},{2,6},{4,0},{6,2},{8,12},{10,14},{12,8},{14,10},{16,20},{18,... | collective-permute-start | bytes 1671176 | tf_op jit(solution)/shard_map/ppermute | solution.py:26
  661.2 25.1 %collective-permute-start.58 = (bf16[128,2176]{1,0:T(8,128)(2,1)}, bf16[128,2176]{1,0:T(8,128)(2,1)}, u32[]{:S(2)}, u32[]{:S(2)}) collective-permute-start(bf16[128,2176]{1,0:T(8,128)(2,1)} %get-tuple-element.391), channel_id=1, source_target_pairs={{0,6},{2,4},{4,2},{6,0},{8,14},{10,12},{12,10},{14,8},{16,22},{18,... | collective-permute-start | bytes 1671176 | tf_op jit(solution)/shard_map/ppermute | solution.py:26
  712.3 32.8 %collective-permute-start.62 = (bf16[128,2176]{1,0:T(8,128)(2,1)S(1)}, bf16[128,2176]{1,0:T(8,128)(2,1)S(1)}, u32[]{:S(2)}, u32[]{:S(2)}) collective-permute-start(bf16[128,2176]{1,0:T(8,128)(2,1)S(1)} %get-tuple-element.386), channel_id=1, source_target_pairs={{0,2},{2,0},{4,6},{6,4},{8,10},{10,8},{12,14},{14,12},{16,18},{18,... | collective-permute-start | bytes 1671176 | tf_op jit(solution)/shard_map/ppermute | solution.py:26
  713.8 31.4 %collective-permute-start.63 = (bf16[128,2176]{1,0:T(8,128)(2,1)S(1)}, bf16[128,2176]{1,0:T(8,128)(2,1)S(1)}, u32[]{:S(2)}, u32[]{:S(2)}) collective-permute-start(bf16[128,2176]{1,0:T(8,128)(2,1)S(1)} %get-tuple-element.385), channel_id=1, source_target_pairs={{0,4},{2,6},{4,0},{6,2},{8,12},{10,14},{12,8},{14,10},{16,20},{18,... | collective-permute-start | bytes 1671176 | tf_op jit(solution)/shard_map/ppermute | solution.py:26
  714.3 30.9 %collective-permute-start.64 = (bf16[128,2176]{1,0:T(8,128)(2,1)S(1)}, bf16[128,2176]{1,0:T(8,128)(2,1)S(1)}, u32[]{:S(2)}, u32[]{:S(2)}) collective-permute-start(bf16[128,2176]{1,0:T(8,128)(2,1)S(1)} %get-tuple-element.384), channel_id=1, source_target_pairs={{0,6},{2,4},{4,2},{6,0},{8,14},{10,12},{12,10},{14,8},{16,22},{18,... | collective-permute-start | bytes 1671176 | tf_op jit(solution)/shard_map/ppermute | solution.py:26
  756.7 333.4 %reduce-scatter.3.cloned.1.call-start = ((), (), s32[]{:S(2)}) async-start(), calls=%async_computation.4 | async-start | bytes 12582912 | tf_op jit(solution)/shard_map/reduce_scatter | solution.py:625
  790.6 62.8 %collective-permute-start.79 = (bf16[512,2048]{1,0:T(8,128)(2,1)}, bf16[512,2048]{1,0:T(8,128)(2,1)}, u32[]{:S(2)}, u32[]{:S(2)}) collective-permute-start(bf16[512,2048]{1,0:T(8,128)(2,1)} %pad_maximum_fusion.12), channel_id=1, source_target_pairs={{0,2},{2,0},{4,6},{6,4},{8,10},{10,8},{12,14},{14,12},{16,18},{18,... | collective-permute-start | bytes 6291464 | tf_op jit(solution)/shard_map/ppermute | solution.py:26
  793.4 93.8 %collective-permute-start.80 = (bf16[512,2048]{1,0:T(8,128)(2,1)}, bf16[512,2048]{1,0:T(8,128)(2,1)}, u32[]{:S(2)}, u32[]{:S(2)}) collective-permute-start(bf16[512,2048]{1,0:T(8,128)(2,1)} %pad_maximum_fusion.13), channel_id=1, source_target_pairs={{0,4},{2,6},{4,0},{6,2},{8,12},{10,14},{12,8},{14,10},{16,20},{18,... | collective-permute-start | bytes 6291464 | tf_op jit(solution)/shard_map/ppermute | solution.py:26
  796.3 92.6 %collective-permute-start.81 = (bf16[512,2048]{1,0:T(8,128)(2,1)}, bf16[512,2048]{1,0:T(8,128)(2,1)}, u32[]{:S(2)}, u32[]{:S(2)}) collective-permute-start(bf16[512,2048]{1,0:T(8,128)(2,1)} %pad_maximum_fusion.14), channel_id=1, source_target_pairs={{0,6},{2,4},{4,2},{6,0},{8,14},{10,12},{12,10},{14,8},{16,22},{18,... | collective-permute-start | bytes 6291464 | tf_op jit(solution)/shard_map/ppermute | solution.py:26
  838.0 115.3 %collective-permute-start.74 = (bf16[1024,1536]{1,0:T(8,128)(2,1)}, bf16[1024,1536]{1,0:T(8,128)(2,1)}, u32[]{:S(2)}, u32[]{:S(2)}) collective-permute-start(bf16[1024,1536]{1,0:T(8,128)(2,1)} %convolution_convert_fusion.8), channel_id=1, source_target_pairs={{0,4},{2,6},{4,0},{6,2},{8,12},{10,14},{12,8},{14,10},{16,20},{18,... | collective-permute-start | bytes 9437192 | tf_op jit(solution)/shard_map/ppermute | solution.py:26
  839.5 88.4 %collective-permute-start.75 = (bf16[1024,1024]{1,0:T(8,128)(2,1)}, bf16[1024,1024]{1,0:T(8,128)(2,1)}, u32[]{:S(2)}, u32[]{:S(2)}) collective-permute-start(bf16[1024,1024]{1,0:T(8,128)(2,1)} %convolution_convert_fusion.13), channel_id=1, source_target_pairs={{0,2},{2,0},{4,6},{6,4},{8,10},{10,8},{12,14},{14,12},{16,18},{18,... | collective-permute-start | bytes 6291464 | tf_op jit(solution)/shard_map/ppermute | solution.py:26
  898.5 146.2 %collective-permute-start.88 = (bf16[512,2048]{0,1:T(8,128)(2,1)}, bf16[512,2048]{0,1:T(8,128)(2,1)}, u32[]{:S(2)}, u32[]{:S(2)}) collective-permute-start(bf16[512,2048]{0,1:T(8,128)(2,1)} %pad_maximum_fusion.15), channel_id=1, source_target_pairs={{0,1},{1,0},{2,3},{3,2},{4,5},{5,4},{6,7},{7,6},{8,9},{9,8},{10,11... | collective-permute-start | bytes 6291464 | tf_op jit(solution)/shard_map/ppermute | solution.py:26
  914.9 47.3 %collective-permute-start.84 = (bf16[256,2048]{0,1:T(8,128)(2,1)S(1)}, bf16[256,2048]{0,1:T(8,128)(2,1)S(1)}, u32[]{:S(2)}, u32[]{:S(2)}) collective-permute-start(bf16[256,2048]{0,1:T(8,128)(2,1)S(1)} %select_convert_fusion.3), channel_id=1, source_target_pairs={{0,8},{2,10},{4,12},{6,14},{8,16},{10,18},{12,20},{14,22},{1,9},{3... | collective-permute-start | bytes 3145736 | tf_op jit(solution)/shard_map/ppermute | solution.py:332
  919.6 45.3 %collective-permute-start.86 = (bf16[256,2048]{0,1:T(8,128)(2,1)S(1)}, bf16[256,2048]{0,1:T(8,128)(2,1)S(1)}, u32[]{:S(2)}, u32[]{:S(2)}) collective-permute-start(bf16[256,2048]{0,1:T(8,128)(2,1)S(1)} %select_convert_fusion.3), channel_id=1, source_target_pairs={{16,8},{18,10},{20,12},{22,14},{24,16},{26,18},{28,20},{30,22},{17... | collective-permute-start | bytes 3145736 | tf_op jit(solution)/shard_map/ppermute | solution.py:337
  958.9 35.2 %collective-permute-start.76 = (bf16[256,1536]{1,0:T(8,128)(2,1)S(1)}, bf16[256,1536]{1,0:T(8,128)(2,1)S(1)}, u32[]{:S(2)}, u32[]{:S(2)}) collective-permute-start(bf16[256,1536]{1,0:T(8,128)(2,1)S(1)} %get-tuple-element.366), channel_id=1, source_target_pairs={{0,8},{2,10},{4,12},{6,14},{8,0},{10,2},{12,4},{14,6},{16,24},{18,... | collective-permute-start | bytes 2359304 | tf_op jit(solution)/shard_map/ppermute | solution.py:26
  962.0 55.1 %collective-permute-start.77 = (bf16[256,1536]{1,0:T(8,128)(2,1)S(1)}, bf16[256,1536]{1,0:T(8,128)(2,1)S(1)}, u32[]{:S(2)}, u32[]{:S(2)}) collective-permute-start(bf16[256,1536]{1,0:T(8,128)(2,1)S(1)} %get-tuple-element.368), channel_id=1, source_target_pairs={{0,16},{2,18},{4,20},{6,22},{8,24},{10,26},{12,28},{14,30},{16,0},... | collective-permute-start | bytes 2359304 | tf_op jit(solution)/shard_map/ppermute | solution.py:26
  962.2 56.5 %collective-permute-start.78 = (bf16[256,1536]{1,0:T(8,128)(2,1)S(1)}, bf16[256,1536]{1,0:T(8,128)(2,1)S(1)}, u32[]{:S(2)}, u32[]{:S(2)}) collective-permute-start(bf16[256,1536]{1,0:T(8,128)(2,1)S(1)} %get-tuple-element.367), channel_id=1, source_target_pairs={{0,24},{2,26},{4,28},{6,30},{8,16},{10,18},{12,20},{14,22},{16,8},... | collective-permute-start | bytes 2359304 | tf_op jit(solution)/shard_map/ppermute | solution.py:26
  964.9 69.7 %collective-permute-start.85 = (bf16[256,2048]{0,1:T(8,128)(2,1)S(1)}, bf16[256,2048]{0,1:T(8,128)(2,1)S(1)}, u32[]{:S(2)}, u32[]{:S(2)}) collective-permute-start(bf16[256,2048]{0,1:T(8,128)(2,1)S(1)} %select_convert_fusion.2), channel_id=1, source_target_pairs={{0,8},{2,10},{4,12},{6,14},{8,16},{10,18},{12,20},{14,22},{16,24},... | collective-permute-start | bytes 3145736 | tf_op jit(solution)/shard_map/ppermute | solution.py:332
  994.2 42.6 %collective-permute-start.87 = (bf16[256,2048]{0,1:T(8,128)(2,1)S(1)}, bf16[256,2048]{0,1:T(8,128)(2,1)S(1)}, u32[]{:S(2)}, u32[]{:S(2)}) collective-permute-start(bf16[256,2048]{0,1:T(8,128)(2,1)S(1)} %add_convert_fusion.2), channel_id=1, source_target_pairs={{8,0},{10,2},{12,4},{14,6},{16,8},{18,10},{20,12},{22,14},{24,16},... | collective-permute-start | bytes 3145736 | tf_op jit(solution)/shard_map/ppermute | solution.py:337
  1017.2 37.6 %collective-permute-start.89 = (bf16[4,128,1024]{2,1,0:T(8,128)(2,1)}, bf16[4,128,1024]{2,1,0:T(8,128)(2,1)}, u32[]{:S(2)}, u32[]{:S(2)}) collective-permute-start(bf16[4,128,1024]{2,1,0:T(8,128)(2,1)} %fusion.159), channel_id=1, source_target_pairs={{0,4},{2,6},{4,0},{6,2},{8,12},{10,14},{12,8},{14,10},{16,20},{18,... | collective-permute-start | bytes 3145736 | tf_op jit(solution)/shard_map/ppermute | solution.py:26
  1047.9 48.9 %collective-permute-start.90 = (bf16[256,2048]{0,1:T(8,128)(2,1)}, bf16[256,2048]{0,1:T(8,128)(2,1)}, u32[]{:S(2)}, u32[]{:S(2)}) collective-permute-start(bf16[256,2048]{0,1:T(8,128)(2,1)} %fusion.104), channel_id=1, source_target_pairs={{0,2},{2,0},{4,6},{6,4},{8,10},{10,8},{12,14},{14,12},{16,18},{18,... | collective-permute-start | bytes 3145736 | tf_op jit(solution)/shard_map/ppermute | solution.py:26
  1053.5 31.4 %collective-permute-start.98 = (bf16[3,64,1024]{2,0,1:T(4,128)(2,1)S(1)}, bf16[3,64,1024]{2,0,1:T(4,128)(2,1)S(1)}, u32[]{:S(2)}, u32[]{:S(2)}) collective-permute-start(bf16[3,64,1024]{2,0,1:T(4,128)(2,1)S(1)} %fusion.172), channel_id=1, source_target_pairs={{0,2},{2,0},{4,6},{6,4},{8,10},{10,8},{12,14},{14,12},{16,18},{18,... | collective-permute-start | bytes 1179656 | tf_op jit(solution)/shard_map/ppermute | solution.py:26
  1110.3 48.0 %collective-permute-start.100 = (bf16[128,1024]{1,0:T(8,128)(2,1)}, bf16[128,1024]{1,0:T(8,128)(2,1)}, u32[]{:S(2)}, u32[]{:S(2)}) collective-permute-start(bf16[128,1024]{1,0:T(8,128)(2,1)} %get-tuple-element.420), channel_id=1, source_target_pairs={{0,16},{2,18},{4,20},{6,22},{8,24},{10,26},{12,28},{14,30},{16,0},... | collective-permute-start | bytes 786440 | tf_op jit(solution)/shard_map/ppermute | solution.py:26
  1128.1 30.2 %collective-permute-start.101 = (bf16[128,1024]{1,0:T(8,128)(2,1)}, bf16[128,1024]{1,0:T(8,128)(2,1)}, u32[]{:S(2)}, u32[]{:S(2)}) collective-permute-start(bf16[128,1024]{1,0:T(8,128)(2,1)} %get-tuple-element.419), channel_id=1, source_target_pairs={{0,24},{2,26},{4,28},{6,30},{8,16},{10,18},{12,20},{14,22},{16,8},... | collective-permute-start | bytes 786440 | tf_op jit(solution)/shard_map/ppermute | solution.py:26
  1131.5 26.8 %collective-permute-start.99 = (bf16[128,1024]{1,0:T(8,128)(2,1)S(1)}, bf16[128,1024]{1,0:T(8,128)(2,1)}, u32[]{:S(2)}, u32[]{:S(2)}) collective-permute-start(bf16[128,1024]{1,0:T(8,128)(2,1)S(1)} %get-tuple-element.418), channel_id=1, source_target_pairs={{0,8},{2,10},{4,12},{6,14},{8,0},{10,2},{12,4},{14,6},{16,24},{18,... | collective-permute-start | bytes 786440 | tf_op jit(solution)/shard_map/ppermute | solution.py:26
  (203 other events, 3224.7 us)
Sparse Core Ops, SparseCore 0:
  9.6 16.3 all-gather.2
  27.5 21.0 all-gather.4
  756.9 12.3 reduce-scatter.4
  777.2 17.4 reduce-scatter.2
